TPU v7x, 128 devices: a whole 4x4x4 slice. The times are simulated.
128 devices in a mesh: grp: 16 (over x, z_hi, core), seq: 8 (over y, z_lo).
Axes of the slice: x: 4, y: 4, z: 4 (z_hi: 2, z_lo: 2; z = z_hi * 2 + z_lo), core: 2. Of those that a mesh axis runs over, the one named last changes fastest.
Arguments:
- prompt_hidden: bfloat16 [16, 8192, 5120], P('grp', 'seq'), may hold values from -6 to 6
- resp_hidden: bfloat16 [16, 1024, 5120], P('grp', 'seq'), may hold values from -6 to 6
- queries: bfloat16 [16, 1024, 1024], P('grp', 'seq'), may hold values from -180 to 180
- grad_out: bfloat16 [16, 1024, 1024], P('grp', 'seq'), may hold values from -6 to 6
- kv_weight: bfloat16 [5120, 256], P(('grp', 'seq')), may hold values from -0.078125 to 0.078125
- prompt_lengths: int32 [16], P('grp'), may hold values from 4096 to 8192
- response_lengths: int32 [16, 8], P('grp'), may hold values from 1 to 128, 640 in all within a row
Outputs:
- attended: bfloat16 [16, 1024, 1024], P('grp', 'seq')
- query_grad: bfloat16 [16, 1024, 1024], P('grp', 'seq')
- prompt_kv_grad: bfloat16 [16, 8192, 256], P('grp', 'seq')
- weight_grad: float32 [5120, 256], P(('grp', 'seq'))
Inputs may be any that keep to these rules, and one draw needn't show every extreme that they name: `response_lengths`: every prompt has one response of exactly 128 live tokens.
All inputs are finite; a program needn't handle non-finite values.
Results may differ from a plain program's by a relative error of at most 0.025.
The roundings to bfloat16 on the way count: a program that leaves them out, or rounds other values in their place, can miss the bound.
Values may be sent and summed in bfloat16 or wider, within the bound.
No kernel may reach another device: no remote copies, remote signals or barrier semaphores. Data moves between devices by JAX's collectives and lax.ppermute only.
A program may use at most 128 MiB of HBM per device.

v0:
```python
import jax
import jax.numpy as jnp
from jax import lax
from jax.sharding import PartitionSpec as P


def per_device(
    prompt_hidden, resp_hidden, queries, grad_out, kv_weight, prompt_lengths, response_lengths
):
    seq_rank = lax.axis_index("seq")
    head_dim = kv_weight.shape[1] // 2
    rt_dev = resp_hidden.shape[1]
    width = queries.shape[2]
    heads = width // head_dim
    group_heads = 2
    blocks = heads // group_heads
    scale = head_dim ** (-0.5)
    prompt_rows = prompt_hidden[0]
    resp_rows = resp_hidden[0]
    piece = lax.all_gather(kv_weight, ("grp", "seq"), axis=0, tiled=True)
    left = prompt_rows
    right = resp_rows
    own_kv = jnp.dot(left, piece, preferred_element_type=jnp.float32)
    resp_kv = jnp.dot(right, piece, preferred_element_type=jnp.float32)
    own_kv = own_kv.astype(jnp.bfloat16)
    resp_kv = resp_kv.astype(jnp.bfloat16)
    prompt_kv = lax.all_gather(own_kv, "seq", axis=0, tiled=True)
    plen_all = prompt_kv.shape[0]
    prompt_len = prompt_lengths[0]
    lengths_row = response_lengths[0]
    members = jnp.arange(lengths_row.shape[0])
    resp_len = jnp.sum(jnp.where(members == seq_rank, lengths_row, 0))
    position = jnp.arange(rt_dev)
    live = position < resp_len
    prompt_ok = jnp.arange(plen_all) < prompt_len
    allowed = jnp.concatenate(
        [
            jnp.broadcast_to(prompt_ok[None, :], (rt_dev, plen_all)),
            position[None, :] <= position[:, None],
        ],
        1,
    )
    keys = jnp.concatenate([prompt_kv[:, :head_dim], resp_kv[:, :head_dim]], 0)
    values = jnp.concatenate([prompt_kv[:, head_dim:], resp_kv[:, head_dim:]], 0)
    grad_live = jnp.where(live[:, None], grad_out[0], jnp.zeros_like(grad_out[0]))
    q_blocks = queries[0].reshape(rt_dev, blocks, group_heads, head_dim).transpose(1, 0, 2, 3)
    g_blocks = grad_live.reshape(rt_dev, blocks, group_heads, head_dim).transpose(1, 0, 2, 3)

    def attend_block(pieces):
        q_part, g_part = pieces
        scores = jnp.einsum("thd,kd->htk", q_part, keys, preferred_element_type=jnp.float32) * scale
        scores = jnp.where(allowed[None], scores, -jnp.inf)
        top = jnp.max(scores, 2, keepdims=True)
        expo = jnp.exp(scores - top)
        total = jnp.sum(expo, 2, keepdims=True)
        probs = expo / total
        probs_b = probs.astype(jnp.bfloat16)
        out_part = jnp.einsum("htk,kd->thd", probs_b, values, preferred_element_type=jnp.float32)
        out_part = jnp.where(live[:, None, None], out_part, jnp.zeros_like(out_part)).astype(
            jnp.bfloat16
        )
        delta = jnp.sum(g_part.astype(jnp.float32) * out_part.astype(jnp.float32), 2).T
        dprob = jnp.einsum("thd,kd->htk", g_part, values, preferred_element_type=jnp.float32)
        dscore = (probs * (dprob - delta[:, :, None]) * scale).astype(jnp.bfloat16)
        q_grad = jnp.einsum("htk,kd->thd", dscore, keys, preferred_element_type=jnp.float32).astype(
            jnp.bfloat16
        )
        key_grad = jnp.einsum("htk,thd->kd", dscore, q_part, preferred_element_type=jnp.float32)
        value_grad = jnp.einsum("htk,thd->kd", probs_b, g_part, preferred_element_type=jnp.float32)
        return (out_part, q_grad, key_grad, value_grad, top[:, :, 0], total[:, :, 0], delta)

    out_b, qg_b, key_grad, value_grad, tops, totals, deltas = lax.map(
        attend_block, (q_blocks, g_blocks)
    )
    attended = out_b.transpose(1, 0, 2, 3).reshape(rt_dev, width)
    query_grad = qg_b.transpose(1, 0, 2, 3).reshape(rt_dev, width)
    kv_grad = jnp.concatenate([jnp.sum(key_grad, 0), jnp.sum(value_grad, 0)], 1)
    resp_grad = kv_grad[plen_all:]
    prompt_grad = lax.psum_scatter(
        kv_grad[None, :plen_all], "seq", scatter_dimension=1, tiled=True
    )[0]
    prompt_grad = prompt_grad.astype(jnp.bfloat16)
    resp_grad = resp_grad.astype(jnp.bfloat16)
    contract = (((0,), (0,)), ((), ()))
    left = prompt_rows
    right = resp_rows
    term = lax.dot_general(left, prompt_grad, contract, preferred_element_type=jnp.float32)
    weight_grad = lax.psum_scatter(
        term + lax.dot_general(right, resp_grad, contract, preferred_element_type=jnp.float32),
        ("grp", "seq"),
        scatter_dimension=0,
        tiled=True,
    )
    return (attended[None], query_grad[None], prompt_grad[None], weight_grad)


def solution(mesh):
    return jax.shard_map(
        per_device,
        mesh=mesh,
        in_specs=(
            P("grp", "seq", None),
            P("grp", "seq", None),
            P("grp", "seq", None),
            P("grp", "seq", None),
            P(("grp", "seq"), None),
            P("grp"),
            P("grp", None),
        ),
        out_specs=(
            P("grp", "seq", None),
            P("grp", "seq", None),
            P("grp", "seq", None),
            P(("grp", "seq"), None),
        ),
        check_vma=False,
    )
```

profile of v0, /device:TPU:0, one launch (start us, length us, event | category | flops | bytes accessed | tf_op | source)
XLA Modules:
  0.0 1376.8 jit_solution(18195348858659832953)
XLA Ops:
  8.0 307.9 %all-gather.3.cloned.1.call-done = bf16[5120,256]{1,0:T(8,128)(2,1)} async-done(((bf16[40,256]{1,0:T(8,128)(2,1)}), bf16[5120,256]{1,0:T(8,128)(2,1)}) %all-gather.3.cloned.1.call-update) | async-done | bytes 2621456 | tf_op jit(solution)/shard_map/all_gather | solution.py:20
  315.9 8.4 fusion.56
  331.7 84.0 %all-gather.5.cloned.1.call-done = bf16[8192,256]{1,0:T(8,128)(2,1)} async-done(((bf16[1024,256]{1,0:T(8,128)(2,1)}), bf16[8192,256]{1,0:T(8,128)(2,1)}) %all-gather.5.cloned.1.call-update) | async-done | bytes 4194320 | tf_op jit(solution)/shard_map/all_gather | solution.py:27
  418.2 5.0 pad_maximum_fusion
  423.2 87.4 %while.17 = (s32[]{:T(128)}, bf16[4,128,2,128]{1,3,2,0:T(8,128)(2,1)}, bf16[4,128,2,128]{3,1,2,0:T(8,128)(2,1)}, f32[4,8320,128]{2,1,0:T(8,128)}, f32[4,8320,128...) while((s32[]{:T(128)}, ...), condition=%wide.region_5.6_spmd.clone, body=%wide.region_1.5_spmd.clone.sunk | while | flops 3301604864 | bytes 87911880 | solution.py:72
  432.3 3.4 fusion.104
  437.6 4.1 fusion.106
  441.7 3.3 fusion.107
  454.1 3.4 fusion.104
  459.4 4.2 fusion.106
  463.5 3.4 fusion.107
  476.0 3.4 fusion.104
  481.3 4.2 fusion.106
  485.4 3.4 fusion.107
  497.8 3.4 fusion.104
  503.1 4.1 fusion.106
  507.2 3.3 fusion.107
  510.6 8.9 reduce_sum.47
  519.5 8.8 reduce_sum.46
  528.2 5.7 fusion.51
  534.0 171.8 %reduce-scatter.5.cloned.1.call-done = f32[1,1024,256]{2,1,0:T(8,128)} async-done(((f32[1,8192,256]{2,1,0:T(8,128)}), f32[1,1024,256]{2,1,0:T(8,128)}) %reduce-scatter.5.cloned.1.call-update) | async-done | bytes 1048592 | tf_op jit(solution)/shard_map/reduce_scatter | solution.py:79
  707.3 6.6 fusion.46
  717.2 5.9 copy.52
  726.1 644.2 %reduce-scatter.7.cloned.1.call-done = f32[40,256]{1,0:T(8,128)} async-done(((f32[5120,256]{1,0:T(8,128)}), f32[40,256]{1,0:T(8,128)}) %reduce-scatter.7.cloned.1.call-update) | async-done | bytes 40976
  (97 shorter events, 61.5 us)
Async XLA Ops:
  7.2 322.3 %copy-start = (bf16[1,128,5120]{2,1,0:T(8,128)(2,1)S(1)}, bf16[1,128,5120]{2,1,0:T(8,128)(2,1)}, u32[]{:S(2)}) copy-start(bf16[1,128,5120]{2,1,0:T(8,128)(2,1)} %param.10) | copy-start | bytes 3932164
  7.2 308.7 %all-gather.3.cloned.1.call-start = ((), (), s32[]{:S(2)}) async-start(), calls=%async_computation.2 | async-start | bytes 2641920 | tf_op jit(solution)/shard_map/all_gather | solution.py:20
  7.9 317.1 %copy-start.4 = (bf16[1,128,1024]{2,1,0:T(8,128)(2,1)S(1)}, bf16[1,128,1024]{2,1,0:T(8,128)(2,1)}, u32[]{:S(2)}) copy-start(bf16[1,128,1024]{2,1,0:T(8,128)(2,1)} %param.11) | copy-start | bytes 786436
  7.9 317.9 %copy-start.5 = (bf16[1,128,1024]{2,1,0:T(8,128)(2,1)S(1)}, bf16[1,128,1024]{2,1,0:T(8,128)(2,1)}, u32[]{:S(2)}) copy-start(bf16[1,128,1024]{2,1,0:T(8,128)(2,1)} %param.12) | copy-start | bytes 786436
  7.9 318.1 %copy-start.8 = (s32[1,8]{1,0:T(1,128)S(1)}, s32[1,8]{1,0:T(1,128)}, u32[]{:S(2)}) copy-start(s32[1,8]{1,0:T(1,128)} %param.15) | copy-start | bytes 100
  7.9 407.8 %all-gather.5.cloned.1.call-start = ((), (), s32[]{:S(2)}) async-start(), calls=%async_computation.3 | async-start | bytes 4718592 | tf_op jit(solution)/shard_map/all_gather | solution.py:27
  324.3 381.6 %reduce-scatter.5.cloned.1.call-start = ((), (), s32[]{:S(2)}) async-start(), calls=%async_computation.4 | async-start | bytes 9437184 | tf_op jit(solution)/shard_map/reduce_scatter | solution.py:79
  428.4 1.6 copy-start.1
  430.0 2.2 copy-start.2
  450.2 1.6 copy-start.1
  451.9 2.2 copy-start.2
  472.1 1.6 copy-start.1
  473.8 2.2 copy-start.2
  494.0 1.6 copy-start.1
  495.6 2.2 copy-start.2
  534.0 836.3 %reduce-scatter.7.cloned.1.call-start = ((), (), s32[]{:S(2)}) async-start(), calls=%async_computation.5 | async-start | bytes 5283840
  705.8 8.1 slice-start
  705.8 8.1 slice-start.2
  707.3 6.7 copy-start.3
  707.3 6.7 slice-start.1
  707.3 6.7 slice-start.3
  723.1 0.9 copy-start.7
  723.1 1.8 copy-start.6
Sparse Core Ops, SparseCore 0:
  9.7 306.1 all-gather.2
  324.4 91.2 all-gather.4
  534.1 171.6 reduce-scatter.4
  723.3 646.9 reduce-scatter.6
where the time goes:
time: 1380 us
  waiting for transfers between devices  1210 us (88%)
  matrix products  92.9 us (7%)
  other arithmetic  47.3 us (3%)
  between operations  14.6 us (1%)
    unnamed x5, waiting for transfers between devices  645 us
    all_gather x1, waiting for transfers between devices, per_device(): piece = lax.all_gather(kv_weight, ('grp', 'seq'), axis=0, tiled=True)  308 us
    reduce_scatter x1, waiting for transfers between devices, per_device(): lax.psum_scatter(kv_grad[None, :plen_all], 'seq', scatter_dimension=1, ti...  172 us
    all_gather x1, waiting for transfers between devices, per_device(): prompt_kv = lax.all_gather(own_kv, 'seq', axis=0, tiled=True)  84 us
  transfers between devices with their start and end apart: 4, of which 4 were waited for; matrix products, arithmetic and copies ran while one was open for 1% of the time, Pallas kernels for 0%

commit v1 on v0

v1 whole, which is shorter than its diff:
```python
import functools

import jax
import jax.numpy as jnp
from jax import lax
from jax.experimental import pallas as pl
from jax.experimental.pallas import tpu as pltpu
from jax.sharding import Mesh
from jax.sharding import PartitionSpec as P

AXES = ("x", "zh", "c", "y", "zl")
GRP = ("x", "zh", "c")
SEQ = ("y", "zl")
CHIPS = ("x", "zh", "y", "zl")
N_SEQ = 8
HEADS = 8
DH = 128
SLOTS = 64
ROWS = SLOTS * HEADS
NEG = -1e30
LOG2E = 1.4426950408889634
NT = (((1,), (1,)), ((), ()))
F32 = jnp.float32
BF16 = jnp.bfloat16


def stack_heads(block, first):
    return jnp.concatenate(
        [block[:, (first + h) * DH : (first + h + 1) * DH] for h in range(HEADS)], 0
    )


def stats_kernel(coef, valid_ref, qg_ref, kv_ref, limit_ref, out_ref, stat_ref):
    plen = kv_ref.shape[0] - DH
    valid = valid_ref[0]
    bias = jnp.where(lax.broadcasted_iota(jnp.int32, (1, plen), 1) < valid, 0.0, NEG)
    lane = lax.broadcasted_iota(jnp.int32, (SLOTS, DH), 1)
    causal = jnp.where(lane <= limit_ref[...], 0.0, NEG)
    half = HEADS // 2
    causal = jnp.concatenate([causal] * half, 0)
    columns = lax.broadcasted_iota(jnp.int32, (half * SLOTS, DH), 1)
    for part in range(2):
        base = part * half
        q = jnp.concatenate(
            [qg_ref[:, (base + h) * DH : (base + h + 1) * DH] for h in range(half)], 0
        )
        g = jnp.concatenate(
            [qg_ref[:, (HEADS + base + h) * DH : (HEADS + base + h + 1) * DH] for h in range(half)],
            0,
        )
        s = lax.dot_general(q, kv_ref[:plen, :DH], NT, preferred_element_type=F32) + bias
        sr = lax.dot_general(q, kv_ref[plen:, :DH], NT, preferred_element_type=F32) + causal
        top = jnp.maximum(jnp.max(s, 1, keepdims=True), jnp.max(sr, 1, keepdims=True))
        p = jnp.exp2((s - top) * coef)
        pr = jnp.exp2((sr - top) * coef)
        total = jnp.sum(p, 1, keepdims=True) + jnp.sum(pr, 1, keepdims=True)
        o = jnp.dot(p.astype(BF16), kv_ref[:plen, DH:], preferred_element_type=F32)
        o = o + jnp.dot(pr.astype(BF16), kv_ref[plen:, DH:], preferred_element_type=F32)
        o = o / total
        d = jnp.sum(o * g.astype(F32), 1, keepdims=True)
        for h in range(half):
            out_ref[:, (base + h) * DH : (base + h + 1) * DH] = o[
                h * SLOTS : (h + 1) * SLOTS
            ].astype(BF16)
        table = jnp.where(columns == 0, top * coef, jnp.where(columns == 1, total, d))
        stat_ref[:, part * half * SLOTS : (part + 1) * half * SLOTS] = table.T[:8]


def grad_kernel(
    coef, scale, valid_ref, qg_ref, kv_ref, limit_ref, stat_ref, out_ref,
    att_ref, qgrad_ref, kvgrad_ref, acc_ref,
):
    step = pl.program_id(0)
    plen = kv_ref.shape[0] - DH
    valid = valid_ref[0]
    top = stat_ref[0:1]
    inv = stat_ref[1:2]
    delta = stat_ref[2:3]
    mine = stat_ref[3:4]
    q = stack_heads(qg_ref, 0)
    g = stack_heads(qg_ref, HEADS)

    @pl.when(step == 0)
    def _():
        acc_ref[...] = jnp.zeros_like(acc_ref)

    weight = jnp.broadcast_to(mine, (DH, ROWS)).T
    for h in range(HEADS):
        cols = pl.ds(h * DH, DH)
        att_ref[:, cols] = (
            out_ref[:, cols].astype(F32) * weight[h * SLOTS : (h + 1) * SLOTS]
        ).astype(BF16)

    chunk = 256
    bounds = [(i, min(chunk, plen - i)) for i in range(0, plen, chunk)] + [(plen, DH)]
    dq = jnp.zeros((ROWS, DH), F32)
    for start, size in bounds:
        rows = pl.ds(start, size)
        k = kv_ref[rows, :DH]
        v = kv_ref[rows, DH:]
        s = lax.dot_general(k, q, NT, preferred_element_type=F32)
        place = lax.broadcasted_iota(jnp.int32, (size, ROWS), 0)
        if start < plen:
            seen = place < valid - start
        else:
            seen = place <= limit_ref[0:1]
        s = jnp.where(seen, s * coef - top, NEG)
        p = jnp.exp2(s) * inv
        dp = lax.dot_general(v, g, NT, preferred_element_type=F32)
        ds = (p * (dp - delta) * scale).astype(BF16)
        acc_ref[rows, :DH] += jnp.dot(ds, q, preferred_element_type=F32)
        acc_ref[rows, DH:] += jnp.dot(p.astype(BF16), g, preferred_element_type=F32)
        dq = dq + lax.dot_general(ds, k, (((0,), (0,)), ((), ())), preferred_element_type=F32)
    for h in range(HEADS):
        qgrad_ref[:, h * DH : (h + 1) * DH] = dq[h * SLOTS : (h + 1) * SLOTS].astype(BF16)

    @pl.when(step == pl.num_programs(0) - 1)
    def _():
        kvgrad_ref[...] = acc_ref[...].astype(BF16)


def spread(block, axes, count):
    copies = jnp.broadcast_to(block[None], (count,) + block.shape)
    return lax.all_to_all(copies, axes, 0, 0, tiled=True)


def per_device(
    prompt_hidden, resp_hidden, queries, grad_out, kv_weight, prompt_lengths, response_lengths
):
    rank = lax.axis_index(SEQ)
    core = lax.axis_index("c")
    slots = resp_hidden.shape[1]
    plen = prompt_hidden.shape[1]
    model = prompt_hidden.shape[2]
    width = queries.shape[2]
    scale = DH ** (-0.5)
    coef = scale * LOG2E
    prompt_rows = prompt_hidden[0]
    resp_rows = resp_hidden[0]
    swap = [(0, 1), (1, 0)]

    shard = kv_weight.shape[0]
    near = spread(kv_weight, CHIPS, 64).reshape(8, 8, shard, 2 * DH)
    far = lax.ppermute(near, "c", swap)
    first = jnp.where(core == 0, near, far)
    second = jnp.where(core == 0, far, near)
    weight = jnp.stack([first, second], 1).reshape(model, 2 * DH)

    own_kv = jnp.dot(prompt_rows, weight, preferred_element_type=F32).astype(BF16)
    resp_kv = jnp.dot(resp_rows, weight, preferred_element_type=F32).astype(BF16)
    kv = jnp.concatenate([own_kv, resp_kv], 0)

    lengths = response_lengths[0]
    live_all = slots * N_SEQ * 5 // 8
    ends = jnp.cumsum(lengths)
    starts = ends - lengths
    slot_id = jnp.arange(N_SEQ * slots)
    of_resp = slot_id // slots
    offset = slot_id % slots
    dest = jnp.where(offset < lengths[of_resp], starts[of_resp] + offset, -1)
    pick = (jnp.arange(live_all)[:, None] == dest[None, :]).astype(BF16)
    packed_id = jnp.arange(live_all)
    my_start = jnp.sum(jnp.where(jnp.arange(N_SEQ) == rank, starts, 0))
    my_len = jnp.sum(jnp.where(jnp.arange(N_SEQ) == rank, lengths, 0))
    in_mine = (packed_id >= my_start) & (packed_id < my_start + my_len)
    limit = jnp.where(in_mine, packed_id - my_start, -1).astype(jnp.int32)

    qg_own = jnp.concatenate([queries[0], grad_out[0]], 1)
    qg_all = spread(qg_own, SEQ, N_SEQ).reshape(N_SEQ * slots, 2 * width)
    qg = jnp.dot(pick, qg_all, preferred_element_type=F32).astype(BF16)

    valid = (prompt_lengths - plen * rank).astype(jnp.int32)
    steps = live_all // SLOTS
    total_rows = live_all * HEADS
    keys = plen + slots
    limit_cols = jnp.broadcast_to(limit[:, None], (live_all, DH))
    limit_rows = jnp.broadcast_to(
        limit.reshape(steps, 1, SLOTS), (steps, HEADS, SLOTS)
    ).reshape(1, total_rows)
    limit_rows = jnp.broadcast_to(limit_rows, (8, total_rows))

    smem = pl.BlockSpec(memory_space=pltpu.SMEM)
    row_block = lambda cols: pl.BlockSpec((SLOTS, cols), lambda i: (i, 0))
    lane_block = pl.BlockSpec((8, ROWS), lambda i: (0, i))
    whole = pl.BlockSpec((keys, 2 * DH), lambda i: (0, 0))
    out, stat = pl.pallas_call(
        functools.partial(stats_kernel, coef),
        grid=(steps,),
        in_specs=[smem, row_block(2 * width), whole, row_block(DH)],
        out_specs=[row_block(width), lane_block],
        out_shape=[
            jax.ShapeDtypeStruct((live_all, width), BF16),
            jax.ShapeDtypeStruct((8, total_rows), F32),
        ],
        compiler_params=pltpu.CompilerParams(vmem_limit_bytes=48 << 20),
        cost_estimate=pl.CostEstimate(
            flops=4 * total_rows * keys * DH, bytes_accessed=8 << 20, transcendentals=total_rows * keys
        ),
        name="attend_stats",
    )(valid, qg, kv, limit_cols)

    own_stat = stat[:3].reshape(3 * total_rows // DH, DH)
    stats = spread(own_stat, SEQ, N_SEQ).reshape(N_SEQ, 3, total_rows)
    top = jnp.max(stats[:, 0], 0)
    share = stats[:, 1] * jnp.exp2(stats[:, 0] - top)
    total = jnp.sum(share, 0)
    inv = 1.0 / total
    delta = jnp.sum(share * stats[:, 2], 0) * inv
    mine = stat[1] * jnp.exp2(stat[0] - top) * inv
    merged = jnp.stack([top, inv, delta, mine, mine, mine, mine, mine], 0)

    att, qgrad, kvgrad = pl.pallas_call(
        functools.partial(grad_kernel, coef, scale),
        grid=(steps,),
        in_specs=[smem, row_block(2 * width), whole, lane_block, lane_block, row_block(width)],
        out_specs=[row_block(width), row_block(width), whole],
        out_shape=[
            jax.ShapeDtypeStruct((live_all, width), BF16),
            jax.ShapeDtypeStruct((live_all, width), BF16),
            jax.ShapeDtypeStruct((keys, 2 * DH), BF16),
        ],
        scratch_shapes=[pltpu.VMEM((keys, 2 * DH), F32)],
        compiler_params=pltpu.CompilerParams(vmem_limit_bytes=48 << 20),
        cost_estimate=pl.CostEstimate(
            flops=10 * total_rows * keys * DH, bytes_accessed=8 << 20, transcendentals=total_rows * keys
        ),
        name="attend_grads",
    )(valid, qg, kv, limit_rows, merged, out)

    both = jnp.concatenate([att, qgrad], 1)
    both = lax.dot_general(
        pick, both, (((0,), (0,)), ((), ())), preferred_element_type=F32
    ).astype(BF16)
    both = lax.all_to_all(both.reshape(N_SEQ, slots, 2 * width), SEQ, 0, 0, tiled=True)
    both = jnp.sum(both.astype(F32), 0).astype(BF16)
    attended = both[:, :width]
    query_grad = both[:, width:]

    contract = (((0,), (0,)), ((), ()))
    prompt_grad = kvgrad[:plen]
    resp_grad = kvgrad[plen:]
    term = lax.dot_general(prompt_rows, prompt_grad, contract, preferred_element_type=F32)
    term = term + lax.dot_general(resp_rows, resp_grad, contract, preferred_element_type=F32)
    term = term.reshape(8, 2, 8, shard, 2 * DH)
    keep = jnp.where(core == 0, term[:, 0], term[:, 1])
    give = jnp.where(core == 0, term[:, 1], term[:, 0]).astype(BF16)
    got = lax.ppermute(give, "c", swap)
    chip_sum = (keep + got.astype(F32)).astype(BF16).reshape(64, shard, 2 * DH)
    parts = lax.all_to_all(chip_sum, CHIPS, 0, 0, tiled=True)
    weight_grad = jnp.sum(parts.astype(F32), 0)
    return attended[None], query_grad[None], prompt_grad[None], weight_grad


def solution(mesh):
    fine = Mesh(mesh.devices.reshape(4, 2, 2, 4, 2), AXES)
    return jax.shard_map(
        per_device,
        mesh=fine,
        in_specs=(
            P(GRP, SEQ, None),
            P(GRP, SEQ, None),
            P(GRP, SEQ, None),
            P(GRP, SEQ, None),
            P(AXES, None),
            P(GRP),
            P(GRP, None),
        ),
        out_specs=(
            P(GRP, SEQ, None),
            P(GRP, SEQ, None),
            P(GRP, SEQ, None),
            P(AXES, None),
        ),
        check_vma=False,
    )
```

time: 1380 us -> 287 us (0.21)
  waiting for transfers between devices: 1210 us -> 120 us
  matrix products: 92.9 us -> 28.8 us
  Pallas kernels: 0 us -> 38.6 us
  blocking collectives: 0 us -> 32.9 us
  other arithmetic: 47.3 us -> 26.6 us
  starting transfers between devices: 0.16 us -> 19.3 us
    unnamed x5 -> x0, waiting for transfers between devices: 645 us -> none
    all_gather x2 -> x0, waiting for transfers between devices: 392 us -> none  [the longest x1 308 us: per_device(): piece = lax.all_gather(kv_weight, ('grp', 'seq'), axis=0, tiled=True)]
    reduce_scatter x1 -> x0, waiting for transfers between devices: 172 us -> none  [per_device(): lax.psum_scatter(kv_grad[None, :plen_all], 'seq', scatter_dimension=1, ti...]
    all_to_all x0 -> x4, waiting for transfers between devices: none -> 117 us  [the longest x1 56.1 us: per_device(): lax.all_to_all(both.reshape(N_SEQ, slots, 2 * width), SEQ, 0, 0, tiled=True)]
    dot_general x28 -> x6, matrix products: 92.9 us -> 28.8 us  [the longest x1 6.86 us: per_device(): jnp.dot(prompt_rows, weight, preferred_element_type=F32).astype(BF16)]
    pallas_call x0 -> x2, Pallas kernels: none -> 38.6 us  [the longest x1 22.7 us: per_device(): pl.pallas_call(functools.partial(grad_kernel, coef, scale), grid=(steps,)...]
    all_to_all x0 -> x1, blocking collectives: none -> 32.9 us  [spread(): return lax.all_to_all(copies, axes, 0, 0, tiled=True)]
    all_to_all x0 -> x4, starting transfers between devices: none -> 19.2 us  [the longest x2 8.99 us: spread(): return lax.all_to_all(copies, axes, 0, 0, tiled=True)]
  transfers between devices with their start and end apart: 4 -> 6, of which waited for: 4 -> 5; matrix products, arithmetic and copies ran while one was open for 1% -> 12% of each run, Pallas kernels for 0% -> 0%
where the time goes in v1:
time: 287 us; the launch traced here: 286 us
  waiting for transfers between devices  120 us (42%)
  Pallas kernels  38.6 us (13%)
  blocking collectives  32.9 us (11%)
  matrix products  28.8 us (10%)
  other arithmetic  26.6 us (9%)
  starting transfers between devices  19.3 us (7%)
  local copies, waits for them, and re-layouts  17.3 us (6%)
  between operations  2.94 us (1%)
    all_to_all x1, waiting for transfers between devices, per_device(): lax.all_to_all(both.reshape(N_SEQ, slots, 2 * width), SEQ, 0, 0, tiled=True)  56.1 us
    all_to_all x2, waiting for transfers between devices, spread(): return lax.all_to_all(copies, axes, 0, 0, tiled=True)  44.8 us
    all_to_all x1, blocking collectives, spread(): return lax.all_to_all(copies, axes, 0, 0, tiled=True)  32.9 us
    pallas_call x1, Pallas kernels, per_device(): pl.pallas_call(functools.partial(grad_kernel, coef, scale), grid=(steps,)...  22.7 us
    pallas_call x1, Pallas kernels, per_device(): pl.pallas_call(functools.partial(stats_kernel, coef), grid=(steps,), in_s...  15.9 us
    all_to_all x1, waiting for transfers between devices, per_device(): parts = lax.all_to_all(chip_sum, CHIPS, 0, 0, tiled=True)  15.6 us
    all_to_all x2, starting transfers between devices, spread(): return lax.all_to_all(copies, axes, 0, 0, tiled=True)  8.99 us
    gather x3, other arithmetic, per_device(): dest = jnp.where(offset < lengths[of_resp], starts[of_resp] + offset, -1)  8.72 us
  transfers between devices with their start and end apart: 6, of which 5 were waited for; matrix products, arithmetic and copies ran while one was open for 12% of the time, Pallas kernels for 0%

profile of v1, /device:TPU:0, one launch (start us, length us, event | category | flops | bytes accessed | tf_op | source)
XLA Modules:
  0.0 286.1 jit_solution(6655869650194958822)
XLA Ops:
  1.6 32.9 %all_to_all.25 = bf16[64,40,256]{2,1,0:T(8,128)(2,1)S(1)} all-to-all(bf16[64,40,256]{2,1,0:T(8,128)(2,1)S(1)} %broadcast_in_dim.68), channel_id=1, replica_groups=mesh['x'=4,'zh'=2,'c'=2,'y'=4,'zl'=2] {'x','zh','y','zl'}, dimensions={0} | all-to-all | bytes 2621440 | tf_op jit(solution)/shard_map/all_to_all | solution.py:124
  34.5 2.5 broadcast_in_dim.67
  37.0 4.7 %all-to-all-start = ((bf16[8,128,2048]{2,1,0:T(8,128)(2,1)}), bf16[8,128,2048]{2,1,0:T(8,128)(2,1)}, u32[]{:S(2)}, u32[]{:S(2)}) async-start(bf16[8,128,2048]{2,1,0:T(8,128)(2,1)} %broadcast_in_dim.67), calls=%async_computation | async-start | bytes 8388608 | tf_op jit(solution)/shard_map/all_to_all | solution.py:124
  45.9 4.4 %compare_select_fusion.2 = s32[1024,1]{0,1:T(1,128)S(1)} fusion(s32[]{:T(128)} %bitcast.13, s32[]{:T(128)} %bitcast.14, s32[]{:T(128)} %bitcast.15, s32[]{:T(128)} %bitcast.16, s32[]{:T(128)} %bitcast.17, s32[]{:T(128)} %bitcast.19, s32[]{:T(128)} %bitcast.18), kind=kLoop, calls=%fused_computation.53 | loop fusion | flops 23552 | bytes 4124 | tf_op jit(solution)/shard_map/gather | solution.py:160
  50.9 4.3 %compare_select_fusion.1 = s32[1024,1]{0,1:T(1,128)S(1)} fusion(s32[]{:T(128)} %bitcast.1, s32[]{:T(128)} %bitcast.2, s32[]{:T(128)} %bitcast.3, s32[]{:T(128)} %bitcast.4, s32[]{:T(128)} %bitcast.5, s32[]{:T(128)} %bitcast.7, s32[]{:T(128)} %bitcast.6), kind=kLoop, calls=%fused_computation.52 | loop fusion | flops 23552 | bytes 4124 | tf_op jit(solution)/shard_map/gather | solution.py:160
  58.8 6.9 %fusion.20 = bf16[1024,256]{1,0:T(8,128)(2,1)S(1)} fusion(bf16[5120,256]{1,0:T(8,128)(2,1)S(1)} %bitcast.130, bf16[1,1024,5120]{2,1,0:T(8,128)(2,1)} %param.7), kind=kOutput, calls=%fused_computation.28 | convolution fusion | flops 2684616704 | bytes 13631488 | tf_op jit(solution)/shard_map/dot_general | solution.py:149
  65.8 36.4 %all-to-all-done = bf16[8,128,2048]{2,1,0:T(8,128)(2,1)} async-done(((bf16[8,128,2048]{2,1,0:T(8,128)(2,1)}), bf16[8,128,2048]{2,1,0:T(8,128)(2,1)}, u32[]{:S(2)}, u32[]{:S(2)}) %all-to-all-start) | async-done | bytes 4194336 | tf_op jit(solution)/shard_map/all_to_all | solution.py:124
  102.2 5.3 %convolution_convert_fusion.1.qg_ref = bf16[640,2048]{1,0:T(8,128)(2,1)S(1)} fusion(bf16[1024,2048]{1,0:T(8,128)(2,1)} %bitcast.24, s32[1024]{0:T(1024)S(1)} %fusion.40), kind=kOutput, calls=%fused_computation.7 | convolution fusion | flops 2686320640 | bytes 6819840 | tf_op jit(solution)/shard_map/dot_general | solution.py:170
  107.6 15.9 %attend_stats.1 = (bf16[640,1024]{1,0:T(8,128)(2,1)S(1)}, f32[8,5120]{1,0:T(8,128)S(1)}) custom-call(s32[1]{0:T(128)S(6)} %sub.46.valid_ref, bf16[640,2048]{1,0:T(8,128)(2,1)S(1)} %convolution_convert_fusion.1.qg_ref, bf16[1152,256]{1,0:T(8,128)(2,1)S(1)} %pad_maximum_fusion.1.kv_ref, s32[640,128]{1,0:T(8,128)S(1)} %broadcast_in_dim.75.limit_ref), custom_call_target="tpu_custom_call" | custom-call | flops 3019898880 | bytes 8388608 | tf_op jit(solution)/shard_map/attend_stats/pallas_call | solution.py:186
  125.5 4.3 %all-to-all-start.2 = ((f32[8,120,128]{2,1,0:T(8,128)}), f32[8,120,128]{2,1,0:T(8,128)}, u32[]{:S(2)}, u32[]{:S(2)}) async-start(f32[8,120,128]{2,1,0:T(8,128)} %broadcast_in_dim.77), calls=%async_computation.2 | async-start | bytes 983040 | tf_op jit(solution)/shard_map/all_to_all | solution.py:124
  130.5 8.4 %all-to-all-done.2 = f32[8,120,128]{2,1,0:T(8,128)} async-done(((f32[8,120,128]{2,1,0:T(8,128)}), f32[8,120,128]{2,1,0:T(8,128)}, u32[]{:S(2)}, u32[]{:S(2)}) %all-to-all-start.2) | async-done | bytes 491552 | tf_op jit(solution)/shard_map/all_to_all | solution.py:124
  142.5 22.7 %attend_grads.1 = (bf16[640,1024]{1,0:T(8,128)(2,1)S(1)}, bf16[640,1024]{1,0:T(8,128)(2,1)S(1)}, bf16[1152,256]{1,0:T(8,128)(2,1)S(1)}) custom-call(s32[1]{0:T(128)S(6)} %sub.46.valid_ref, bf16[640,2048]{1,0:T(8,128)(2,1)} %copy-done.1, bf16[1152,256]{1,0:T(8,128)(2,1)S(1)} %pad_maximum_fusion.1.kv_ref, s32[8,5120]{1,0:T(8,128)S(1)} %broadcast_in_dim.73.limit_ref, ...), custom_call_target="tpu_custom_call" | custom-call | flops 7549747200 | bytes 8388608 | tf_op jit(solution)/shard_map/attend_grads/pallas_call | solution.py:212
  165.2 6.6 %fusion = f32[256,5120]{1,0:T(8,128)S(1)} fusion(bf16[1,1024,5120]{2,1,0:T(8,128)(2,1)} %param.7, bf16[1152,256]{1,0:T(8,128)(2,1)S(1)} %get-tuple-element.13), kind=kOutput, calls=%fused_computation | convolution fusion | flops 2684354560 | bytes 16252928 | tf_op jit(solution)/shard_map/dot_general | solution.py:242
  171.8 3.2 %fusion.4 = f32[5120,256]{0,1:T(8,128)} fusion(f32[256,5120]{1,0:T(8,128)S(1)} %fusion, bf16[1,128,5120]{2,1,0:T(8,128)(2,1)S(1)} %copy-done, bf16[1152,256]{1,0:T(8,128)(2,1)S(1)} %get-tuple-element.13), kind=kOutput, calls=%fused_computation.5 | convolution fusion | flops 336855040 | bytes 11862016 | tf_op jit(solution)/shard_map/dot_general | solution.py:243
  175.1 5.9 %copy.22 = f32[5120,256]{1,0:T(8,128)} copy(f32[5120,256]{0,1:T(8,128)} %fusion.4) | data formatting | bytes 10485760 | tf_op jit(solution)/shard_map/add | solution.py:243
  181.0 2.8 fusion.11
  183.8 3.0 %collective-permute-done.1 = bf16[8,8,40,256]{3,2,1,0:T(8,128)(2,1)S(1)} collective-permute-done((bf16[8,8,40,256]{3,2,1,0:T(8,128)(2,1)S(1)}, bf16[8,8,40,256]{3,2,1,0:T(8,128)(2,1)S(1)}, u32[]{:S(2)}, u32[]{:S(2)}) %collective-permute-start.1) | collective-permute-done | bytes 1310752 | tf_op jit(solution)/shard_map/ppermute | solution.py:247
  186.8 4.1 %fusion.10 = bf16[8,8,40,256]{3,2,1,0:T(8,128)(2,1)} fusion(bf16[8,8,40,256]{3,2,1,0:T(8,128)(2,1)S(1)} %collective-permute-done.1, f32[8,2,8,40,256]{4,3,2,1,0:T(8,128)} %bitcast.128, pred[]{:T(512)S(6)} %eq.32), kind=kLoop, calls=%fused_computation.15 | loop fusion | flops 2621440 | bytes 7864321 | tf_op jit(solution)/shard_map/convert_element_type | solution.py:248
  191.0 5.6 %all-to-all-start.4 = ((bf16[64,40,256]{2,1,0:T(8,128)(2,1)}), bf16[64,40,256]{2,1,0:T(8,128)(2,1)}, u32[]{:S(2)}, u32[]{:S(2)}) async-start(bf16[64,40,256]{2,1,0:T(8,128)(2,1)} %bitcast.133), calls=%async_computation.4 | async-start | bytes 2621440 | tf_op jit(solution)/shard_map/all_to_all | solution.py:249
  196.6 6.4 %convolution_convert_fusion = bf16[1024,2048]{1,0:T(8,128)(2,1)} fusion(bf16[640,1024]{1,0:T(8,128)(2,1)} %copy-done.6, bf16[640,1024]{1,0:T(8,128)(2,1)S(1)} %copy-done.5, s32[1024]{0:T(1024)S(1)} %fusion.40), kind=kOutput, calls=%fused_computation.6 | convolution fusion | flops 2692349952 | bytes 6819840 | tf_op jit(solution)/shard_map/dot_general | solution.py:231
  203.0 15.6 %all-to-all-done.4 = bf16[64,40,256]{2,1,0:T(8,128)(2,1)} async-done(((bf16[64,40,256]{2,1,0:T(8,128)(2,1)}), bf16[64,40,256]{2,1,0:T(8,128)(2,1)}, u32[]{:S(2)}, u32[]{:S(2)}) %all-to-all-start.4) | async-done | bytes 1310752 | tf_op jit(solution)/shard_map/all_to_all | solution.py:249
  218.6 4.6 %all-to-all-start.3 = ((bf16[8,128,2048]{2,1,0:T(8,128)(2,1)}), bf16[8,128,2048]{2,1,0:T(8,128)(2,1)}, u32[]{:S(2)}, u32[]{:S(2)}) async-start(bf16[8,128,2048]{2,1,0:T(8,128)(2,1)} %bitcast.134), calls=%async_computation.3 | async-start | bytes 8388608 | tf_op jit(solution)/shard_map/all_to_all | solution.py:234
  226.2 56.1 %all-to-all-done.3 = bf16[8,128,2048]{2,1,0:T(8,128)(2,1)} async-done(((bf16[8,128,2048]{2,1,0:T(8,128)(2,1)}), bf16[8,128,2048]{2,1,0:T(8,128)(2,1)}, u32[]{:S(2)}, u32[]{:S(2)}) %all-to-all-start.3) | async-done | bytes 4194336 | tf_op jit(solution)/shard_map/all_to_all | solution.py:234
  282.3 3.0 %reduce_sum.64 = bf16[128,2048]{1,0:T(8,128)(2,1)S(1)} reduce(bf16[8,128,2048]{2,1,0:T(8,128)(2,1)} %all-to-all-done.3, bf16[]{:T(256)} %constant.74.clone.1), dimensions={0}, to_apply=%region_6.7 | reduce | flops 1835008 | bytes 4718594 | tf_op jit(solution)/shard_map/reduce_sum | solution.py:235
  (53 shorter events, 17.6 us)
Async XLA Ops:
  0.6 57.7 %copy-start = (bf16[1,128,5120]{2,1,0:T(8,128)(2,1)S(1)}, bf16[1,128,5120]{2,1,0:T(8,128)(2,1)}, u32[]{:S(2)}) copy-start(bf16[1,128,5120]{2,1,0:T(8,128)(2,1)} %param.8) | copy-start | bytes 3932164
  0.6 33.8 %copy-start.7 = (bf16[1,128,1024]{2,1,0:T(8,128)(2,1)S(1)}, bf16[1,128,1024]{2,1,0:T(8,128)(2,1)}, u32[]{:S(2)}) copy-start(bf16[1,128,1024]{2,1,0:T(8,128)(2,1)} %param.10) | copy-start | bytes 786436
  0.7 33.8 %copy-start.8 = (bf16[1,128,1024]{2,1,0:T(8,128)(2,1)S(1)}, bf16[1,128,1024]{2,1,0:T(8,128)(2,1)}, u32[]{:S(2)}) copy-start(bf16[1,128,1024]{2,1,0:T(8,128)(2,1)} %param.9) | copy-start | bytes 786436
  34.5 22.1 %collective-permute-start = (bf16[8,8,40,256]{3,2,1,0:T(8,128)(2,1)S(1)}, bf16[8,8,40,256]{3,2,1,0:T(8,128)(2,1)}, u32[]{:S(2)}, u32[]{:S(2)}) collective-permute-start(bf16[8,8,40,256]{3,2,1,0:T(8,128)(2,1)S(1)} %bitcast.131), channel_id=1, source_target_pairs={{0,8},{8,0},{1,9},{9,1},{2,10},{10,2},{3,11},{11,3},{4,12},{12,4},... | collective-permute-start | bytes 3932168 | tf_op jit(solution)/shard_map/ppermute | solution.py:144
  37.0 5.3 %copy-start.9 = (s32[1,8]{1,0:T(1,128)S(1)}, s32[1,8]{1,0:T(1,128)}, u32[]{:S(2)}) copy-start(s32[1,8]{1,0:T(1,128)} %param.13) | copy-start | bytes 100
  37.0 65.2 %all-to-all-start = ((bf16[8,128,2048]{2,1,0:T(8,128)(2,1)}), bf16[8,128,2048]{2,1,0:T(8,128)(2,1)}, u32[]{:S(2)}, u32[]{:S(2)}) async-start(bf16[8,128,2048]{2,1,0:T(8,128)(2,1)} %broadcast_in_dim.67), calls=%async_computation | async-start | bytes 8388608 | tf_op jit(solution)/shard_map/all_to_all | solution.py:124
  107.5 16.1 %copy-start.1 = (bf16[640,2048]{1,0:T(8,128)(2,1)}, bf16[640,2048]{1,0:T(8,128)(2,1)S(1)}, u32[]{:S(2)}) copy-start(bf16[640,2048]{1,0:T(8,128)(2,1)S(1)} %convolution_convert_fusion.1.qg_ref) | copy-start | bytes 7864324
  123.5 1.1 copy-start.2
  125.5 13.4 %all-to-all-start.2 = ((f32[8,120,128]{2,1,0:T(8,128)}), f32[8,120,128]{2,1,0:T(8,128)}, u32[]{:S(2)}, u32[]{:S(2)}) async-start(f32[8,120,128]{2,1,0:T(8,128)} %broadcast_in_dim.77), calls=%async_computation.2 | async-start | bytes 983040 | tf_op jit(solution)/shard_map/all_to_all | solution.py:124
  141.1 1.3 copy-start.3
  165.2 6.6 %copy-start.4 = (bf16[640,1024]{1,0:T(8,128)(2,1)}, bf16[640,1024]{1,0:T(8,128)(2,1)S(1)}, u32[]{:S(2)}) copy-start(bf16[640,1024]{1,0:T(8,128)(2,1)S(1)} %get-tuple-element.11) | copy-start | bytes 3932164
  165.2 6.6 %copy-start.6 = (bf16[640,1024]{1,0:T(8,128)(2,1)}, bf16[640,1024]{1,0:T(8,128)(2,1)S(1)}, u32[]{:S(2)}) copy-start(bf16[640,1024]{1,0:T(8,128)(2,1)S(1)} %get-tuple-element.12) | copy-start | bytes 3932164
  183.7 3.1 %collective-permute-start.1 = (bf16[8,8,40,256]{3,2,1,0:T(8,128)(2,1)S(1)}, bf16[8,8,40,256]{3,2,1,0:T(8,128)(2,1)S(1)}, u32[]{:S(2)}, u32[]{:S(2)}) collective-permute-start(bf16[8,8,40,256]{3,2,1,0:T(8,128)(2,1)S(1)} %fusion.11), channel_id=1, source_target_pairs={{0,8},{8,0},{1,9},{9,1},{2,10},{10,2},{3,11},{11,3},{4,12},{12,4},... | collective-permute-start | bytes 3932168 | tf_op jit(solution)/shard_map/ppermute | solution.py:247
  191.0 5.6 %copy-start.5 = (bf16[640,1024]{1,0:T(8,128)(2,1)S(1)}, bf16[640,1024]{1,0:T(8,128)(2,1)}, u32[]{:S(2)}) copy-start(bf16[640,1024]{1,0:T(8,128)(2,1)} %copy-done.4) | copy-start | bytes 3932164
  191.0 27.7 %all-to-all-start.4 = ((bf16[64,40,256]{2,1,0:T(8,128)(2,1)}), bf16[64,40,256]{2,1,0:T(8,128)(2,1)}, u32[]{:S(2)}, u32[]{:S(2)}) async-start(bf16[64,40,256]{2,1,0:T(8,128)(2,1)} %bitcast.133), calls=%async_computation.4 | async-start | bytes 2621440 | tf_op jit(solution)/shard_map/all_to_all | solution.py:249
  218.6 63.6 %all-to-all-start.3 = ((bf16[8,128,2048]{2,1,0:T(8,128)(2,1)}), bf16[8,128,2048]{2,1,0:T(8,128)(2,1)}, u32[]{:S(2)}, u32[]{:S(2)}) async-start(bf16[8,128,2048]{2,1,0:T(8,128)(2,1)} %bitcast.134), calls=%async_computation.3 | async-start | bytes 8388608 | tf_op jit(solution)/shard_map/all_to_all | solution.py:234

commit v2 on v1

v2 whole, which is shorter than its diff:
```python
import functools

import jax
import jax.numpy as jnp
from jax import lax
from jax.experimental import pallas as pl
from jax.experimental.pallas import tpu as pltpu
from jax.sharding import Mesh
from jax.sharding import PartitionSpec as P

AXES = ("x", "zh", "c", "y", "zl")
GRP = ("x", "zh", "c")
SEQ = ("y", "zl")
CHIPS = ("x", "zh", "y", "zl")
N_SEQ = 8
HEADS = 8
HALF = 4
DH = 128
SLOTS = 128
PAIRS = 8
NEG = -1e30
LOG2E = 1.4426950408889634
NT = (((1,), (1,)), ((), ()))
TN = (((0,), (0,)), ((), ()))
F32 = jnp.float32
BF16 = jnp.bfloat16
SWAP = [(0, 1), (1, 0)]


def params():
    return pltpu.CompilerParams(vmem_limit_bytes=48 << 20)


def stack_heads(ref, first):
    return jnp.concatenate(
        [ref[:, (first + h) * DH : (first + h + 1) * DH] for h in range(HALF)], 0
    )


def project_kernel(core_ref, near_ref, far_ref, prompt_ref, resp_ref, kv_ref, acc_ref):
    step = pl.program_id(0)
    plen = prompt_ref.shape[0]
    swapped = core_ref[0] == 1
    near = near_ref[0]
    far = far_ref[0]
    weight = jnp.concatenate(
        [jnp.where(swapped, far, near), jnp.where(swapped, near, far)], 0
    )

    @pl.when(step == 0)
    def _():
        acc_ref[...] = jnp.zeros_like(acc_ref)

    acc_ref[:plen] += jnp.dot(prompt_ref[...], weight, preferred_element_type=F32)
    acc_ref[plen:] += jnp.dot(resp_ref[...], weight, preferred_element_type=F32)

    @pl.when(step == pl.num_programs(0) - 1)
    def _():
        kv_ref[...] = acc_ref[...].astype(BF16)


def stats_kernel(coef, valid_ref, q_ref, kv_ref, limit_ref, out_ref, stat_ref):
    plen = kv_ref.shape[0] - DH
    valid = valid_ref[0]
    bias = jnp.where(lax.broadcasted_iota(jnp.int32, (1, plen), 1) < valid, 0.0, NEG)
    lane = lax.broadcasted_iota(jnp.int32, (SLOTS, DH), 1)
    causal = jnp.where(lane <= limit_ref[...], 0.0, NEG)
    causal = jnp.concatenate([causal] * HALF, 0)
    table = jnp.zeros((SLOTS, DH), F32)
    for base in (0, HALF):
        q = stack_heads(q_ref, base)
        s = lax.dot_general(q, kv_ref[:plen, :DH], NT, preferred_element_type=F32) + bias
        sr = lax.dot_general(q, kv_ref[plen:, :DH], NT, preferred_element_type=F32) + causal
        top = jnp.maximum(jnp.max(s, 1, keepdims=True), jnp.max(sr, 1, keepdims=True))
        p = jnp.exp2((s - top) * coef)
        pr = jnp.exp2((sr - top) * coef)
        total = jnp.sum(p, 1, keepdims=True) + jnp.sum(pr, 1, keepdims=True)
        o = jnp.dot(p.astype(BF16), kv_ref[:plen, DH:], preferred_element_type=F32)
        o = o + jnp.dot(pr.astype(BF16), kv_ref[plen:, DH:], preferred_element_type=F32)
        o = o / total
        top = top * coef
        for h in range(HALF):
            rows = slice(h * SLOTS, (h + 1) * SLOTS)
            head = base + h
            out_ref[:, head * DH : (head + 1) * DH] = o[rows].astype(BF16)
            table = jnp.where(lane == head, top[rows], table)
            table = jnp.where(lane == HEADS + head, total[rows], table)
    stat_ref[...] = table.T[: 2 * HEADS]


def delta_kernel(out_ref, g_ref, delta_ref):
    lane = lax.broadcasted_iota(jnp.int32, (SLOTS, DH), 1)
    table = jnp.zeros((SLOTS, DH), F32)
    for h in range(HEADS):
        cols = slice(h * DH, (h + 1) * DH)
        d = jnp.sum(out_ref[:, cols].astype(F32) * g_ref[:, cols].astype(F32), 1, keepdims=True)
        table = jnp.where(lane == h, d, table)
    delta_ref[...] = table.T[:HEADS]


def grad_kernel(
    coef, scale, valid_ref, q_ref, g_ref, kv_ref, limit_ref, stat_ref,
    qgrad_ref, kvgrad_ref, acc_ref,
):
    step = pl.program_id(0)
    plen = kv_ref.shape[0] - DH
    valid = valid_ref[0]
    tops = stat_ref[:, :HEADS]
    top_all = jnp.max(tops, 0)
    share = stat_ref[:, HEADS : 2 * HEADS] * jnp.exp2(tops - top_all)
    inv_all = 1.0 / jnp.sum(share, 0)
    delta_all = jnp.sum(share * stat_ref[:, 2 * HEADS :], 0) * inv_all

    @pl.when(step == 0)
    def _():
        acc_ref[...] = jnp.zeros_like(acc_ref)

    chunk = 256
    bounds = [(i, min(chunk, plen - i)) for i in range(0, plen, chunk)] + [(plen, DH)]
    limit = jnp.concatenate([limit_ref[0:1]] * HALF, 1)
    for base in (0, HALF):
        q = stack_heads(q_ref, base)
        g = stack_heads(g_ref, base)
        line = lambda t: jnp.concatenate([t[base + h : base + h + 1] for h in range(HALF)], 1)
        top, inv, delta = line(top_all), line(inv_all), line(delta_all)
        dq = jnp.zeros((HALF * SLOTS, DH), F32)
        for start, size in bounds:
            rows = pl.ds(start, size)
            k = kv_ref[rows, :DH]
            v = kv_ref[rows, DH:]
            s = lax.dot_general(k, q, NT, preferred_element_type=F32)
            place = lax.broadcasted_iota(jnp.int32, (size, HALF * SLOTS), 0)
            seen = place < valid - start if start < plen else place <= limit
            p = jnp.exp2(jnp.where(seen, s * coef - top, NEG)) * inv
            dp = lax.dot_general(v, g, NT, preferred_element_type=F32)
            ds = (p * (dp - delta) * scale).astype(BF16)
            acc_ref[rows, :DH] += jnp.dot(ds, q, preferred_element_type=F32)
            acc_ref[rows, DH:] += jnp.dot(p.astype(BF16), g, preferred_element_type=F32)
            dq = dq + lax.dot_general(ds, k, TN, preferred_element_type=F32)
        for h in range(HALF):
            qgrad_ref[:, (base + h) * DH : (base + h + 1) * DH] = dq[
                h * SLOTS : (h + 1) * SLOTS
            ].astype(BF16)

    @pl.when(step == pl.num_programs(0) - 1)
    def _():
        kvgrad_ref[...] = acc_ref[...].astype(BF16)


def weight_kernel(core_ref, grad_ref, prompt_ref, resp_ref, keep_ref, give_ref):
    plen = prompt_ref.shape[0]
    part = prompt_ref.shape[1] // 2
    swapped = core_ref[0] == 1
    t = lax.dot_general(grad_ref[:plen], prompt_ref[...], TN, preferred_element_type=F32)
    t = t + lax.dot_general(grad_ref[plen:], resp_ref[...], TN, preferred_element_type=F32)
    t = t.T
    keep_ref[0] = jnp.where(swapped, t[part:], t[:part])
    give_ref[0] = jnp.where(swapped, t[:part], t[part:]).astype(BF16)


def spread(block, axes, count):
    copies = jnp.broadcast_to(block[None], (count,) + block.shape)
    return lax.all_to_all(copies, axes, 0, 0, tiled=True)


def per_device(
    prompt_hidden, resp_hidden, queries, grad_out, kv_weight, prompt_lengths, response_lengths
):
    rank = lax.axis_index(SEQ)
    core = lax.axis_index("c")
    core_id = core.astype(jnp.int32).reshape(1)
    slots = resp_hidden.shape[1]
    plen = prompt_hidden.shape[1]
    model = prompt_hidden.shape[2]
    width = queries.shape[2]
    scale = DH ** (-0.5)
    coef = scale * LOG2E
    prompt_rows = prompt_hidden[0]
    resp_rows = resp_hidden[0]
    keys = plen + slots
    smem = pl.BlockSpec(memory_space=pltpu.SMEM)

    q_all = spread(queries[0], SEQ, N_SEQ).reshape(N_SEQ * slots, width)
    g_all = spread(grad_out[0], SEQ, N_SEQ).reshape(N_SEQ * slots, width)

    shard = kv_weight.shape[0]
    near = spread(kv_weight, CHIPS, 64).reshape(PAIRS, 8 * shard, 2 * DH)
    far = lax.ppermute(near, "c", SWAP)
    wide = model // PAIRS
    kv = pl.pallas_call(
        project_kernel,
        grid=(PAIRS,),
        in_specs=[
            smem,
            pl.BlockSpec((1, 8 * shard, 2 * DH), lambda i: (i, 0, 0)),
            pl.BlockSpec((1, 8 * shard, 2 * DH), lambda i: (i, 0, 0)),
            pl.BlockSpec((plen, wide), lambda i: (0, i)),
            pl.BlockSpec((slots, wide), lambda i: (0, i)),
        ],
        out_specs=pl.BlockSpec((keys, 2 * DH), lambda i: (0, 0)),
        out_shape=jax.ShapeDtypeStruct((keys, 2 * DH), BF16),
        scratch_shapes=[pltpu.VMEM((keys, 2 * DH), F32)],
        compiler_params=params(),
        cost_estimate=pl.CostEstimate(
            flops=2 * keys * model * 2 * DH, bytes_accessed=2 * keys * model, transcendentals=0
        ),
        name="project",
    )(core_id, near, far, prompt_rows, resp_rows)

    lengths = response_lengths[0]
    live_all = slots * N_SEQ * 5 // 8
    ends = jnp.cumsum(lengths)
    packed = jnp.arange(live_all)
    past = packed[:, None] >= ends[None, :]
    source = packed + jnp.sum(jnp.where(past, slots - lengths[None, :], 0), 1)
    pick = (source[:, None] == jnp.arange(N_SEQ * slots)[None, :]).astype(BF16)
    offset = source - rank * slots
    limit = jnp.where((offset >= 0) & (offset < slots), offset, -1).astype(jnp.int32)
    limit_cols = jnp.broadcast_to(limit[:, None], (live_all, DH))
    limit_rows = jnp.broadcast_to(limit[None, :], (8, live_all))
    valid = (prompt_lengths - plen * rank).astype(jnp.int32)

    q = jnp.dot(pick, q_all, preferred_element_type=F32).astype(BF16)
    steps = live_all // SLOTS
    rows = live_all * HEADS
    row_block = pl.BlockSpec((SLOTS, width), lambda i: (i, 0))
    whole = pl.BlockSpec((keys, 2 * DH), lambda i: (0, 0))
    out, stat = pl.pallas_call(
        functools.partial(stats_kernel, coef),
        grid=(steps,),
        in_specs=[smem, row_block, whole, pl.BlockSpec((SLOTS, DH), lambda i: (i, 0))],
        out_specs=[row_block, pl.BlockSpec((2 * HEADS, SLOTS), lambda i: (0, i))],
        out_shape=[
            jax.ShapeDtypeStruct((live_all, width), BF16),
            jax.ShapeDtypeStruct((2 * HEADS, live_all), F32),
        ],
        compiler_params=params(),
        cost_estimate=pl.CostEstimate(
            flops=4 * rows * keys * DH, bytes_accessed=4 << 20, transcendentals=rows * keys
        ),
        name="attend_stats",
    )(valid, q, kv, limit_cols)

    g = jnp.dot(pick, g_all, preferred_element_type=F32).astype(BF16)
    delta = pl.pallas_call(
        delta_kernel,
        grid=(steps,),
        in_specs=[row_block, row_block],
        out_specs=pl.BlockSpec((HEADS, SLOTS), lambda i: (0, i)),
        out_shape=jax.ShapeDtypeStruct((HEADS, live_all), F32),
        compiler_params=params(),
        name="partial_delta",
    )(out, g)
    stats = spread(jnp.concatenate([stat, delta], 0), SEQ, N_SEQ)

    parts = lax.dot_general(pick, out, TN, preferred_element_type=F32).astype(BF16)
    parts = lax.all_to_all(parts.reshape(N_SEQ, slots, width), SEQ, 0, 0, tiled=True)

    qgrad, kvgrad = pl.pallas_call(
        functools.partial(grad_kernel, coef, scale),
        grid=(steps,),
        in_specs=[
            smem, row_block, row_block, whole,
            pl.BlockSpec((8, SLOTS), lambda i: (0, i)),
            pl.BlockSpec((N_SEQ, 3 * HEADS, SLOTS), lambda i: (0, 0, i)),
        ],
        out_specs=[row_block, whole],
        out_shape=[
            jax.ShapeDtypeStruct((live_all, width), BF16),
            jax.ShapeDtypeStruct((keys, 2 * DH), BF16),
        ],
        scratch_shapes=[pltpu.VMEM((keys, 2 * DH), F32)],
        compiler_params=params(),
        cost_estimate=pl.CostEstimate(
            flops=10 * rows * keys * DH, bytes_accessed=8 << 20, transcendentals=rows * keys
        ),
        name="attend_grads",
    )(valid, q, g, kv, limit_rows, stats)

    back = lax.dot_general(pick, qgrad, TN, preferred_element_type=F32).astype(BF16)
    back = lax.all_to_all(back.reshape(N_SEQ, slots, width), SEQ, 0, 0, tiled=True)
    query_grad = jnp.sum(back.astype(F32), 0).astype(BF16)

    keep, give = pl.pallas_call(
        weight_kernel,
        grid=(PAIRS,),
        in_specs=[
            smem,
            whole,
            pl.BlockSpec((plen, wide), lambda i: (0, i)),
            pl.BlockSpec((slots, wide), lambda i: (0, i)),
        ],
        out_specs=[
            pl.BlockSpec((1, 8 * shard, 2 * DH), lambda i: (i, 0, 0)),
            pl.BlockSpec((1, 8 * shard, 2 * DH), lambda i: (i, 0, 0)),
        ],
        out_shape=[
            jax.ShapeDtypeStruct((PAIRS, 8 * shard, 2 * DH), F32),
            jax.ShapeDtypeStruct((PAIRS, 8 * shard, 2 * DH), BF16),
        ],
        compiler_params=params(),
        cost_estimate=pl.CostEstimate(
            flops=2 * keys * model * 2 * DH, bytes_accessed=2 * keys * model, transcendentals=0
        ),
        name="weight_grad",
    )(core_id, kvgrad, prompt_rows, resp_rows)
    got = lax.ppermute(give, "c", SWAP)
    chip_sum = (keep + got.astype(F32)).astype(BF16).reshape(64, shard, 2 * DH)
    shares = lax.all_to_all(chip_sum, CHIPS, 0, 0, tiled=True)
    weight_grad = jnp.sum(shares.astype(F32), 0)

    top = jnp.max(stats[:, :HEADS], 0)
    share = stats[:, HEADS : 2 * HEADS] * jnp.exp2(stats[:, :HEADS] - top)
    share = share / jnp.sum(share, 0)
    my_len = jnp.sum(jnp.where(jnp.arange(N_SEQ) == rank, lengths, 0))
    my_start = jnp.sum(jnp.where(jnp.arange(N_SEQ) == rank, ends, 0)) - my_len
    share = lax.dynamic_slice_in_dim(
        jnp.pad(share, ((0, 0), (0, 0), (0, slots))), my_start, slots, 2
    )
    share = jnp.where(jnp.arange(slots) < my_len, share, 0.0).transpose(0, 2, 1)
    parts = parts.astype(F32).reshape(N_SEQ, slots, HEADS, DH) * share[..., None]
    attended = jnp.sum(parts, 0).astype(BF16).reshape(slots, width)
    return attended[None], query_grad[None], kvgrad[None, :plen], weight_grad


def solution(mesh):
    fine = Mesh(mesh.devices.reshape(4, 2, 2, 4, 2), AXES)
    return jax.shard_map(
        per_device,
        mesh=fine,
        in_specs=(
            P(GRP, SEQ, None),
            P(GRP, SEQ, None),
            P(GRP, SEQ, None),
            P(GRP, SEQ, None),
            P(AXES, None),
            P(GRP),
            P(GRP, None),
        ),
        out_specs=(
            P(GRP, SEQ, None),
            P(GRP, SEQ, None),
            P(GRP, SEQ, None),
            P(AXES, None),
        ),
        check_vma=False,
    )
```

time: 287 us -> 227 us (0.79)
  waiting for transfers between devices: 120 us -> 38.2 us
  blocking collectives: 32.9 us -> 61.6 us
  Pallas kernels: 38.6 us -> 53.7 us
  matrix products: 28.8 us -> 15.3 us
  other arithmetic: 26.6 us -> 13.4 us
  starting transfers between devices: 19.3 us -> 23.2 us
    all_to_all x2 -> x3, waiting for transfers between devices: 71.7 us -> 12.8 us  [the longest x1 8.67 us: per_device(): lax.all_to_all(back.reshape(N_SEQ, slots, width), SEQ, 0, 0, tiled=True)]
    all_to_all x1 -> x2, blocking collectives: 32.9 us -> 61.6 us  [spread(): return lax.all_to_all(copies, axes, 0, 0, tiled=True)]
    pallas_call x0 -> x3, Pallas kernels: none -> 21.5 us  [the longest x1 10.3 us: per_device(): pl.pallas_call(weight_kernel, grid=(PAIRS,), in_specs=[smem, whole, pl.Bl...]
    all_to_all x2, waiting for transfers between devices: 44.8 us -> 25.4 us  [spread(): return lax.all_to_all(copies, axes, 0, 0, tiled=True)]
    dot_general x6 -> x4, matrix products: 28.8 us -> 15.3 us  [the longest x1 4.58 us: per_device(): lax.dot_general(pick, out, TN, preferred_element_type=F32).astype(BF16)]
    gather x3 -> x0, other arithmetic: 8.72 us -> none  [per_device(): dest = jnp.where(offset < lengths[of_resp], starts[of_resp] + offset, -1)]
    mul x0 -> x2, local copies, waits for them, and re-layouts: none -> 7.47 us  [per_device(): parts.astype(F32).reshape(N_SEQ, slots, HEADS, DH) * share[..., None]]
    add x1 -> x0, local copies, waits for them, and re-layouts: 5.9 us -> none  [per_device(): term + lax.dot_general(resp_rows, resp_grad, contract, preferred_element_...]
  transfers between devices with their start and end apart: 6 -> 7, of which waited for: 5 -> 5; matrix products, arithmetic and copies ran while one was open for 12% -> 16% of each run, Pallas kernels for 0% -> 14%
where the time goes in v2:
time: 227 us; the launch traced here: 226 us
  blocking collectives  61.6 us (27%)
  Pallas kernels  53.7 us (24%)
  waiting for transfers between devices  38.2 us (17%)
  starting transfers between devices  23.2 us (10%)
  local copies, waits for them, and re-layouts  17.6 us (8%)
  matrix products  15.3 us (7%)
  other arithmetic  13.4 us (6%)
  between operations  2.85 us (1%)
    all_to_all x2, blocking collectives, spread(): return lax.all_to_all(copies, axes, 0, 0, tiled=True)  61.6 us
    all_to_all x2, waiting for transfers between devices, spread(): return lax.all_to_all(copies, axes, 0, 0, tiled=True)  25.4 us
    pallas_call x1, Pallas kernels, per_device(): pl.pallas_call(functools.partial(grad_kernel, coef, scale), grid=(steps,)...  20.4 us
    pallas_call x1, Pallas kernels, per_device(): pl.pallas_call(functools.partial(stats_kernel, coef), grid=(steps,), in_s...  11.7 us
    pallas_call x1, Pallas kernels, per_device(): pl.pallas_call(weight_kernel, grid=(PAIRS,), in_specs=[smem, whole, pl.Bl...  10.3 us
    pallas_call x1, Pallas kernels, per_device(): pl.pallas_call(project_kernel, grid=(PAIRS,), in_specs=[smem, pl.BlockSpe...  9.89 us
    all_to_all x1, waiting for transfers between devices, per_device(): lax.all_to_all(back.reshape(N_SEQ, slots, width), SEQ, 0, 0, tiled=True)  8.67 us
    mul x2, local copies, waits for them, and re-layouts, per_device(): parts.astype(F32).reshape(N_SEQ, slots, HEADS, DH) * share[..., None]  7.47 us
  transfers between devices with their start and end apart: 7, of which 5 were waited for; matrix products, arithmetic and copies ran while one was open for 16% of the time, Pallas kernels for 14%

profile of v2, /device:TPU:0, one launch (start us, length us, event | category | flops | bytes accessed | tf_op | source)
XLA Modules:
  0.0 225.8 jit_solution(11032878580527147972)
XLA Ops:
  1.5 32.9 %all_to_all.35 = bf16[64,40,256]{2,1,0:T(8,128)(2,1)S(1)} all-to-all(bf16[64,40,256]{2,1,0:T(8,128)(2,1)S(1)} %broadcast_in_dim.87), channel_id=1, replica_groups=mesh['x'=4,'zh'=2,'c'=2,'y'=4,'zl'=2] {'x','zh','y','zl'}, dimensions={0} | all-to-all | bytes 2621440 | tf_op jit(solution)/shard_map/all_to_all | solution.py:163
  34.6 28.7 %all_to_all.36 = bf16[8,128,1024]{2,1,0:T(8,128)(2,1)} all-to-all(bf16[8,128,1024]{2,1,0:T(8,128)(2,1)S(1)} %broadcast_in_dim.86), channel_id=1, replica_groups=mesh['x'=4,'zh'=2,'c'=2,'y'=4,'zl'=2] {'y','zl'}, dimensions={0} | all-to-all | bytes 4194304 | tf_op jit(solution)/shard_map/all_to_all | solution.py:163
  64.9 3.7 %all-to-all-start.3 = ((bf16[8,128,1024]{2,1,0:T(8,128)(2,1)}), bf16[8,128,1024]{2,1,0:T(8,128)(2,1)S(1)}, u32[]{:S(2)}, u32[]{:S(2)}) async-start(bf16[8,128,1024]{2,1,0:T(8,128)(2,1)} %broadcast_in_dim.93), calls=%async_computation.3 | async-start | bytes 4194304 | tf_op jit(solution)/shard_map/all_to_all | solution.py:163
  69.7 4.2 %fusion.6.q_ref = bf16[640,1024]{1,0:T(8,128)(2,1)} fusion(bf16[1024,1024]{1,0:T(8,128)(2,1)} %bitcast.40, s32[640]{0:T(1024)S(1)} %get-tuple-element.17), kind=kOutput, calls=%fused_computation.10 | convolution fusion | flops 1343488000 | bytes 3410432 | tf_op jit(solution)/shard_map/dot_general | solution.py:223
  73.9 22.1 %all-to-all-done.3 = bf16[8,128,1024]{2,1,0:T(8,128)(2,1)S(1)} async-done(((bf16[8,128,1024]{2,1,0:T(8,128)(2,1)}), bf16[8,128,1024]{2,1,0:T(8,128)(2,1)S(1)}, u32[]{:S(2)}, u32[]{:S(2)}) %all-to-all-start.3) | async-done | bytes 2097184 | tf_op jit(solution)/shard_map/all_to_all | solution.py:163
  97.3 3.3 %fusion.7.g_ref = bf16[640,1024]{1,0:T(8,128)(2,1)S(1)} fusion(bf16[1024,1024]{1,0:T(8,128)(2,1)} %bitcast.39, s32[640]{0:T(1024)S(1)} %get-tuple-element.17), kind=kOutput, calls=%fused_computation.11 | convolution fusion | flops 1343488000 | bytes 3410432 | tf_op jit(solution)/shard_map/dot_general | solution.py:244
  100.6 9.9 %project.1.kv_ref = bf16[1152,256]{1,0:T(8,128)(2,1)S(1)} custom-call(s32[1]{0:T(128)} %bitcast.6.core_ref, bf16[8,320,256]{2,1,0:T(8,128)(2,1)S(1)} %bitcast.36, bf16[8,320,256]{2,1,0:T(8,128)(2,1)} %collective-permute-done.far_ref, bf16[1024,5120]{1,0:T(8,128)(2,1)} %bitcast.37, bf16[128,5120]{1,0:T(8,128)(2,1)S(1)} %bitcast.33), custom_call_target="tpu_custom_call" | custom-call | flops 3019898880 | bytes 11796480 | tf_op jit(solution)/shard_map/project/pallas_call | solution.py:190
  110.7 11.7 %attend_stats.1 = (bf16[640,1024]{1,0:T(8,128)(2,1)S(1)}, f32[16,640]{1,0:T(8,128)S(1)}) custom-call(s32[1]{0:T(128)S(6)} %sub.36.valid_ref, bf16[640,1024]{1,0:T(8,128)(2,1)S(1)} %copy-done.5, bf16[1152,256]{1,0:T(8,128)(2,1)S(1)} %project.1.kv_ref, s32[640,128]{1,0:T(8,128)S(1)} %broadcast_in_dim.89.limit_ref), custom_call_target="tpu_custom_call" | custom-call | flops 3019898880 | bytes 4194304 | tf_op jit(solution)/shard_map/attend_stats/pallas_call | solution.py:228
  124.5 3.5 %all-to-all-start.4 = ((f32[8,24,640]{2,1,0:T(8,128)}), f32[8,24,640]{2,1,0:T(8,128)S(1)}, u32[]{:S(2)}, u32[]{:S(2)}) async-start(f32[8,24,640]{2,1,0:T(8,128)} %broadcast_in_dim.94), calls=%async_computation.4 | async-start | bytes 983040 | tf_op jit(solution)/shard_map/all_to_all | solution.py:163
  128.0 4.6 %fusion.4 = bf16[1024,1024]{1,0:T(8,128)(2,1)} fusion(bf16[640,1024]{1,0:T(8,128)(2,1)} %copy-done.4, s32[640]{0:T(1024)S(1)} %get-tuple-element.17), kind=kOutput, calls=%fused_computation.8 | convolution fusion | flops 1343881216 | bytes 3410432 | tf_op jit(solution)/shard_map/dot_general | solution.py:256
  132.6 3.3 %all-to-all-done.4.stat_ref = f32[8,24,640]{2,1,0:T(8,128)S(1)} async-done(((f32[8,24,640]{2,1,0:T(8,128)}), f32[8,24,640]{2,1,0:T(8,128)S(1)}, u32[]{:S(2)}, u32[]{:S(2)}) %all-to-all-start.4) | async-done | bytes 491552 | tf_op jit(solution)/shard_map/all_to_all | solution.py:163
  135.9 4.6 %all-to-all-start.2 = ((bf16[8,128,1024]{2,1,0:T(8,128)(2,1)}), bf16[8,128,1024]{2,1,0:T(8,128)(2,1)}, u32[]{:S(2)}, u32[]{:S(2)}) async-start(bf16[8,128,1024]{2,1,0:T(8,128)(2,1)} %bitcast.42), calls=%async_computation.2 | async-start | bytes 4194304 | tf_op jit(solution)/shard_map/all_to_all | solution.py:257
  143.1 20.4 %attend_grads.1 = (bf16[640,1024]{1,0:T(8,128)(2,1)S(1)}, bf16[1152,256]{1,0:T(8,128)(2,1)S(1)}) custom-call(s32[1]{0:T(128)S(6)} %sub.36.valid_ref, bf16[640,1024]{1,0:T(8,128)(2,1)S(1)} %copy-done.6, bf16[640,1024]{1,0:T(8,128)(2,1)S(1)} %copy-done.3, bf16[1152,256]{1,0:T(8,128)(2,1)S(1)} %project.1.kv_ref, s32[8,640]{1,0:T(8,128)S(1)} %broadcast_in_dim.96.limit_ref, ...), custom_call_target="tpu_custom_call" | custom-call | flops 7549747200 | bytes 8388608 | tf_op jit(solution)/shard_map/attend_grads/pallas_call | solution.py:259
  163.6 3.2 %fusion.5 = bf16[1024,1024]{1,0:T(8,128)(2,1)} fusion(bf16[640,1024]{1,0:T(8,128)(2,1)S(1)} %get-tuple-element.12, s32[640]{0:T(1024)S(1)} %get-tuple-element.17), kind=kOutput, calls=%fused_computation.9 | convolution fusion | flops 1343881216 | bytes 3410432 | tf_op jit(solution)/shard_map/dot_general | solution.py:280
  167.1 5.2 %all-to-all-start.5 = ((bf16[8,128,1024]{2,1,0:T(8,128)(2,1)}), bf16[8,128,1024]{2,1,0:T(8,128)(2,1)}, u32[]{:S(2)}, u32[]{:S(2)}) async-start(bf16[8,128,1024]{2,1,0:T(8,128)(2,1)} %bitcast.41), calls=%async_computation.5 | async-start | bytes 4194304 | tf_op jit(solution)/shard_map/all_to_all | solution.py:281
  172.2 10.3 %weight_grad.1 = (f32[8,320,256]{2,1,0:T(8,128)S(1)}, bf16[8,320,256]{2,1,0:T(8,128)(2,1)}) custom-call(s32[1]{0:T(128)} %bitcast.6.core_ref, bf16[1152,256]{1,0:T(8,128)(2,1)S(1)} %get-tuple-element.13.grad_ref, bf16[1024,5120]{1,0:T(8,128)(2,1)} %bitcast.38, bf16[128,5120]{1,0:T(8,128)(2,1)S(1)} %bitcast.34), custom_call_target="tpu_custom_call" | custom-call | flops 3019898880 | bytes 11796480 | tf_op jit(solution)/shard_map/weight_grad/pallas_call | solution.py:284
  187.3 3.2 %add_convert_fusion = bf16[8,320,256]{2,1,0:T(8,128)(2,1)} fusion(f32[8,320,256]{2,1,0:T(8,128)} %copy-done.1, bf16[8,320,256]{2,1,0:T(8,128)(2,1)S(1)} %collective-permute-done.1), kind=kLoop, calls=%fused_computation.2 | loop fusion | flops 1966080 | bytes 5242880 | tf_op jit(solution)/shard_map/convert_element_type | solution.py:308
  190.5 8.7 %all-to-all-done.5 = bf16[8,128,1024]{2,1,0:T(8,128)(2,1)} async-done(((bf16[8,128,1024]{2,1,0:T(8,128)(2,1)}), bf16[8,128,1024]{2,1,0:T(8,128)(2,1)}, u32[]{:S(2)}, u32[]{:S(2)}) %all-to-all-start.5) | async-done | bytes 2097184 | tf_op jit(solution)/shard_map/all_to_all | solution.py:281
  199.2 6.2 %all-to-all-start.6 = ((bf16[64,40,256]{2,1,0:T(8,128)(2,1)}), bf16[64,40,256]{2,1,0:T(8,128)(2,1)S(1)}, u32[]{:S(2)}, u32[]{:S(2)}) async-start(bf16[64,40,256]{2,1,0:T(8,128)(2,1)} %bitcast.19), calls=%async_computation.6 | async-start | bytes 2621440 | tf_op jit(solution)/shard_map/all_to_all | solution.py:309
  205.8 2.6 %mul.23 = f32[8,128,8,128]{3,2,1,0:T(8,128)} broadcast(f32[8,128,8]{2,1,0:T(8,128)S(1)} %copy.12), dimensions={0,1,2} | broadcast | bytes 4227072 | tf_op jit(solution)/shard_map/mul | solution.py:321
  208.4 4.9 %mul.24 = f32[8,128,1024]{2,1,0:T(8,128)} reshape(f32[8,128,8,128]{3,2,1,0:T(8,128)} %mul.23) | data formatting | bytes 8388608 | tf_op jit(solution)/shard_map/mul | solution.py:321
  214.1 4.3 %multiply_reduce_fusion = bf16[128,1024]{1,0:T(8,128)(2,1)} fusion(f32[8,128,1024]{2,1,0:T(8,128)} %mul.24, bf16[8,128,1024]{2,1,0:T(8,128)(2,1)} %all-to-all-done.2), kind=kLoop, calls=%fused_computation | loop fusion | flops 3014656 | bytes 6553600 | tf_op jit(solution)/shard_map/reduce_sum | solution.py:322
  218.4 2.7 %reduce_sum.71 = bf16[128,1024]{1,0:T(8,128)(2,1)} reduce(bf16[8,128,1024]{2,1,0:T(8,128)(2,1)} %all-to-all-done.5, bf16[]{:T(256)} %constant.37.clone.1), dimensions={0}, to_apply=%region_7.8 | reduce | flops 917504 | bytes 2359298 | tf_op jit(solution)/shard_map/reduce_sum | solution.py:282
  221.1 3.8 %all-to-all-done.6 = bf16[64,40,256]{2,1,0:T(8,128)(2,1)S(1)} async-done(((bf16[64,40,256]{2,1,0:T(8,128)(2,1)}), bf16[64,40,256]{2,1,0:T(8,128)(2,1)S(1)}, u32[]{:S(2)}, u32[]{:S(2)}) %all-to-all-start.6) | async-done | bytes 1310752 | tf_op jit(solution)/shard_map/all_to_all | solution.py:309
  (49 shorter events, 14.9 us)
Async XLA Ops:
  0.6 33.7 %copy-start.8 = (bf16[1,128,1024]{2,1,0:T(8,128)(2,1)S(1)}, bf16[1,128,1024]{2,1,0:T(8,128)(2,1)}, u32[]{:S(2)}) copy-start(bf16[1,128,1024]{2,1,0:T(8,128)(2,1)} %param.9) | copy-start | bytes 786436
  34.6 28.7 %copy-start.9 = (bf16[1,128,1024]{2,1,0:T(8,128)(2,1)S(1)}, bf16[1,128,1024]{2,1,0:T(8,128)(2,1)}, u32[]{:S(2)}) copy-start(bf16[1,128,1024]{2,1,0:T(8,128)(2,1)} %param.10) | copy-start | bytes 786436
  64.9 4.4 %copy-start.10 = (s32[1,8]{1,0:T(1,128)S(1)}, s32[1,8]{1,0:T(1,128)}, u32[]{:S(2)}) copy-start(s32[1,8]{1,0:T(1,128)} %param.13) | copy-start | bytes 100
  64.9 31.0 %all-to-all-start.3 = ((bf16[8,128,1024]{2,1,0:T(8,128)(2,1)}), bf16[8,128,1024]{2,1,0:T(8,128)(2,1)S(1)}, u32[]{:S(2)}, u32[]{:S(2)}) async-start(bf16[8,128,1024]{2,1,0:T(8,128)(2,1)} %broadcast_in_dim.93), calls=%async_computation.3 | async-start | bytes 4194304 | tf_op jit(solution)/shard_map/all_to_all | solution.py:163
  69.5 31.1 %collective-permute-start = (bf16[8,320,256]{2,1,0:T(8,128)(2,1)S(1)}, bf16[8,320,256]{2,1,0:T(8,128)(2,1)}, u32[]{:S(2)}, u32[]{:S(2)}) collective-permute-start(bf16[8,320,256]{2,1,0:T(8,128)(2,1)S(1)} %bitcast.35), channel_id=1, source_target_pairs={{0,8},{8,0},{1,9},{9,1},{2,10},{10,2},{3,11},{11,3},{4,12},{12,4},... | collective-permute-start | bytes 3932168 | tf_op jit(solution)/shard_map/ppermute | solution.py:188
  96.0 1.3 copy-start.7
  97.3 3.3 %copy-start = (bf16[1,128,5120]{2,1,0:T(8,128)(2,1)S(1)}, bf16[1,128,5120]{2,1,0:T(8,128)(2,1)}, u32[]{:S(2)}) copy-start(bf16[1,128,5120]{2,1,0:T(8,128)(2,1)} %param.8) | copy-start | bytes 3932164
  100.6 21.9 %copy-start.2 = (bf16[640,1024]{1,0:T(8,128)(2,1)}, bf16[640,1024]{1,0:T(8,128)(2,1)S(1)}, u32[]{:S(2)}) copy-start(bf16[640,1024]{1,0:T(8,128)(2,1)S(1)} %fusion.7.g_ref) | copy-start | bytes 3932164
  100.6 10.1 %copy-start.5 = (bf16[640,1024]{1,0:T(8,128)(2,1)S(1)}, bf16[640,1024]{1,0:T(8,128)(2,1)}, u32[]{:S(2)}) copy-start(bf16[640,1024]{1,0:T(8,128)(2,1)} %fusion.6.q_ref) | copy-start | bytes 3932164
  122.4 1.3 copy-start.4
  124.5 11.4 %all-to-all-start.4 = ((f32[8,24,640]{2,1,0:T(8,128)}), f32[8,24,640]{2,1,0:T(8,128)S(1)}, u32[]{:S(2)}, u32[]{:S(2)}) async-start(f32[8,24,640]{2,1,0:T(8,128)} %broadcast_in_dim.94), calls=%async_computation.4 | async-start | bytes 983040 | tf_op jit(solution)/shard_map/all_to_all | solution.py:163
  135.9 31.2 %all-to-all-start.2 = ((bf16[8,128,1024]{2,1,0:T(8,128)(2,1)}), bf16[8,128,1024]{2,1,0:T(8,128)(2,1)}, u32[]{:S(2)}, u32[]{:S(2)}) async-start(bf16[8,128,1024]{2,1,0:T(8,128)(2,1)} %bitcast.42), calls=%async_computation.2 | async-start | bytes 4194304 | tf_op jit(solution)/shard_map/all_to_all | solution.py:257
  140.5 1.3 copy-start.3
  141.8 1.3 copy-start.6
  167.1 32.1 %all-to-all-start.5 = ((bf16[8,128,1024]{2,1,0:T(8,128)(2,1)}), bf16[8,128,1024]{2,1,0:T(8,128)(2,1)}, u32[]{:S(2)}, u32[]{:S(2)}) async-start(bf16[8,128,1024]{2,1,0:T(8,128)(2,1)} %bitcast.41), calls=%async_computation.5 | async-start | bytes 4194304 | tf_op jit(solution)/shard_map/all_to_all | solution.py:281
  182.6 1.5 copy-start.1
  184.1 3.2 %collective-permute-start.1 = (bf16[8,320,256]{2,1,0:T(8,128)(2,1)}, bf16[8,320,256]{2,1,0:T(8,128)(2,1)S(1)}, u32[]{:S(2)}, u32[]{:S(2)}) collective-permute-start(bf16[8,320,256]{2,1,0:T(8,128)(2,1)} %get-tuple-element.15), channel_id=1, source_target_pairs={{0,8},{8,0},{1,9},{9,1},{2,10},{10,2},{3,11},{11,3},{4,12},{12,4},... | collective-permute-start | bytes 3932168 | tf_op jit(solution)/shard_map/ppermute | solution.py:307
  199.2 25.8 %all-to-all-start.6 = ((bf16[64,40,256]{2,1,0:T(8,128)(2,1)}), bf16[64,40,256]{2,1,0:T(8,128)(2,1)S(1)}, u32[]{:S(2)}, u32[]{:S(2)}) async-start(bf16[64,40,256]{2,1,0:T(8,128)(2,1)} %bitcast.19), calls=%async_computation.6 | async-start | bytes 2621440 | tf_op jit(solution)/shard_map/all_to_all | solution.py:309

commit v3 on v2

--- a/solution.py
+++ b/solution.py
@@ -27,8 +27,12 @@
 SWAP = [(0, 1), (1, 0)]
 
 
-def params():
-    return pltpu.CompilerParams(vmem_limit_bytes=48 << 20)
+def params(mib):
+    return pltpu.CompilerParams(vmem_limit_bytes=mib << 20)
+
+
+def shift(k):
+    return [((i + k) % 4, i) for i in range(4)]
 
 
 def stack_heads(ref, first):
@@ -37,26 +41,48 @@
     )
 
 
-def project_kernel(core_ref, near_ref, far_ref, prompt_ref, resp_ref, kv_ref, acc_ref):
-    step = pl.program_id(0)
-    plen = prompt_ref.shape[0]
+def fetch(source_a, source_b, buf, sems, order_ref, wide):
+    split = source_a.shape[0]
+    copies = []
+    for i in range(PAIRS):
+        there = pl.ds(pl.multiple_of(order_ref[i] * wide, DH), wide)
+        here = pl.ds(i * wide, wide)
+        pair = (
+            pltpu.make_async_copy(source_a.at[:, there], buf.at[:split, here], sems.at[i, 0]),
+            pltpu.make_async_copy(source_b.at[:, there], buf.at[split:, here], sems.at[i, 1]),
+        )
+        for copy in pair:
+            copy.start()
+        copies.append(pair)
+    return copies
+
+
+def project_kernel(core_ref, order_ref, *refs):
+    nears, fars = refs[:4], refs[4:8]
+    prompt_ref, resp_ref, kv_ref, buf, weight, acc, sems = refs[8:]
+    wide = weight.shape[0] // PAIRS
+    half = wide // 2
+    copies = fetch(prompt_ref, resp_ref, buf, sems, order_ref, wide)
     swapped = core_ref[0] == 1
-    near = near_ref[0]
-    far = far_ref[0]
-    weight = jnp.concatenate(
-        [jnp.where(swapped, far, near), jnp.where(swapped, near, far)], 0
-    )
-
-    @pl.when(step == 0)
-    def _():
-        acc_ref[...] = jnp.zeros_like(acc_ref)
-
-    acc_ref[:plen] += jnp.dot(prompt_ref[...], weight, preferred_element_type=F32)
-    acc_ref[plen:] += jnp.dot(resp_ref[...], weight, preferred_element_type=F32)
-
-    @pl.when(step == pl.num_programs(0) - 1)
-    def _():
-        kv_ref[...] = acc_ref[...].astype(BF16)
+    for i in range(PAIRS):
+        near = nears[i // 2][i % 2]
+        far = fars[i // 2][i % 2]
+        weight[i * wide : i * wide + half] = jnp.where(swapped, far, near)
+        weight[i * wide + half : (i + 1) * wide] = jnp.where(swapped, near, far)
+    groups = 4
+    each = PAIRS // groups
+    for part in range(groups):
+        for pair in copies[part * each : (part + 1) * each]:
+            for copy in pair:
+                copy.wait()
+        cols = slice(part * each * wide, (part + 1) * each * wide)
+        t = jnp.dot(buf[:, cols], weight[cols], preferred_element_type=F32)
+        if part == 0:
+            acc[...] = t
+        elif part < groups - 1:
+            acc[...] += t
+        else:
+            kv_ref[...] = (acc[...] + t).astype(BF16)
 
 
 def stats_kernel(coef, valid_ref, q_ref, kv_ref, limit_ref, out_ref, stat_ref):
@@ -147,15 +173,29 @@
         kvgrad_ref[...] = acc_ref[...].astype(BF16)
 
 
-def weight_kernel(core_ref, grad_ref, prompt_ref, resp_ref, keep_ref, give_ref):
-    plen = prompt_ref.shape[0]
-    part = prompt_ref.shape[1] // 2
+def weight_kernel(core_ref, order_ref, grad_ref, prompt_ref, resp_ref, keep_ref, give_ref, buf, sems):
+    wide = buf.shape[1] // PAIRS
+    half = wide // 2
+    copies = fetch(prompt_ref, resp_ref, buf, sems, order_ref, wide)
     swapped = core_ref[0] == 1
-    t = lax.dot_general(grad_ref[:plen], prompt_ref[...], TN, preferred_element_type=F32)
-    t = t + lax.dot_general(grad_ref[plen:], resp_ref[...], TN, preferred_element_type=F32)
-    t = t.T
-    keep_ref[0] = jnp.where(swapped, t[part:], t[:part])
-    give_ref[0] = jnp.where(swapped, t[:part], t[part:]).astype(BF16)
+    grad = grad_ref[...].T
+    for i in range(PAIRS):
+        for copy in copies[i]:
+            copy.wait()
+        t = jnp.dot(grad, buf[:, i * wide : (i + 1) * wide], preferred_element_type=F32).T
+        keep_ref[i // 2, i % 2] = jnp.where(swapped, t[half:], t[:half])
+        give_ref[i // 2, i % 2] = jnp.where(swapped, t[:half], t[half:]).astype(BF16)
+
+
+def weigh_kernel(parts_ref, share_ref, out_ref):
+    share = share_ref[...].T
+    for h in range(HEADS):
+        cols = slice(h * DH, (h + 1) * DH)
+        total = jnp.zeros((out_ref.shape[0], DH), F32)
+        for j in range(N_SEQ):
+            column = j * HEADS + h
+            total = total + parts_ref[j, :, cols].astype(F32) * share[:, column : column + 1]
+        out_ref[:, cols] = total.astype(BF16)
 
 
 def spread(block, axes, count):
@@ -184,28 +224,41 @@
     g_all = spread(grad_out[0], SEQ, N_SEQ).reshape(N_SEQ * slots, width)
 
     shard = kv_weight.shape[0]
-    near = spread(kv_weight, CHIPS, 64).reshape(PAIRS, 8 * shard, 2 * DH)
-    far = lax.ppermute(near, "c", SWAP)
+    x, zh, y, zl = (lax.axis_index(axis) for axis in ("x", "zh", "y", "zl"))
+    order = jnp.stack(
+        [((x + i // 2) % 4) * 2 + (zh + i % 2) % 2 for i in range(PAIRS)]
+    ).astype(jnp.int32)
+    other = lax.ppermute(kv_weight, "zl", SWAP)
+    pair = jnp.where(
+        zl == 0, jnp.concatenate([kv_weight, other], 0), jnp.concatenate([other, kv_weight], 0)
+    )
+    run = [pair] + [lax.ppermute(pair, "y", shift(k)) for k in range(1, 4)]
+    block = lax.dynamic_slice_in_dim(
+        jnp.concatenate(run + run, 0), ((4 - y) % 4) * 2 * shard, 8 * shard, 0
+    )
+    both = jnp.stack([block, lax.ppermute(block, "zh", SWAP)], 0)
+    nears = [both] + [lax.ppermute(both, "x", shift(k)) for k in range(1, 4)]
+    fars = [lax.ppermute(piece, "c", SWAP) for piece in nears]
     wide = model // PAIRS
+    vmem = pl.BlockSpec(memory_space=pltpu.VMEM)
+    anywhere = pl.BlockSpec(memory_space=pl.ANY)
     kv = pl.pallas_call(
         project_kernel,
-        grid=(PAIRS,),
-        in_specs=[
-            smem,
-            pl.BlockSpec((1, 8 * shard, 2 * DH), lambda i: (i, 0, 0)),
-            pl.BlockSpec((1, 8 * shard, 2 * DH), lambda i: (i, 0, 0)),
-            pl.BlockSpec((plen, wide), lambda i: (0, i)),
-            pl.BlockSpec((slots, wide), lambda i: (0, i)),
-        ],
-        out_specs=pl.BlockSpec((keys, 2 * DH), lambda i: (0, 0)),
+        in_specs=[smem, smem] + [vmem] * 8 + [anywhere] * 2,
+        out_specs=vmem,
         out_shape=jax.ShapeDtypeStruct((keys, 2 * DH), BF16),
-        scratch_shapes=[pltpu.VMEM((keys, 2 * DH), F32)],
-        compiler_params=params(),
+        scratch_shapes=[
+            pltpu.VMEM((keys, model), BF16),
+            pltpu.VMEM((model, 2 * DH), BF16),
+            pltpu.VMEM((keys, 2 * DH), F32),
+            pltpu.SemaphoreType.DMA((PAIRS, 2)),
+        ],
+        compiler_params=params(32),
         cost_estimate=pl.CostEstimate(
             flops=2 * keys * model * 2 * DH, bytes_accessed=2 * keys * model, transcendentals=0
         ),
         name="project",
-    )(core_id, near, far, prompt_rows, resp_rows)
+    )(core_id, order, *nears, *fars, prompt_rows, resp_rows)
 
     lengths = response_lengths[0]
     live_all = slots * N_SEQ * 5 // 8
@@ -234,7 +287,7 @@
             jax.ShapeDtypeStruct((live_all, width), BF16),
             jax.ShapeDtypeStruct((2 * HEADS, live_all), F32),
         ],
-        compiler_params=params(),
+        compiler_params=params(24),
         cost_estimate=pl.CostEstimate(
             flops=4 * rows * keys * DH, bytes_accessed=4 << 20, transcendentals=rows * keys
         ),
@@ -248,7 +301,7 @@
         in_specs=[row_block, row_block],
         out_specs=pl.BlockSpec((HEADS, SLOTS), lambda i: (0, i)),
         out_shape=jax.ShapeDtypeStruct((HEADS, live_all), F32),
-        compiler_params=params(),
+        compiler_params=params(24),
         name="partial_delta",
     )(out, g)
     stats = spread(jnp.concatenate([stat, delta], 0), SEQ, N_SEQ)
@@ -270,7 +323,7 @@
             jax.ShapeDtypeStruct((keys, 2 * DH), BF16),
         ],
         scratch_shapes=[pltpu.VMEM((keys, 2 * DH), F32)],
-        compiler_params=params(),
+        compiler_params=params(24),
         cost_estimate=pl.CostEstimate(
             flops=10 * rows * keys * DH, bytes_accessed=8 << 20, transcendentals=rows * keys
         ),
@@ -283,30 +336,30 @@
 
     keep, give = pl.pallas_call(
         weight_kernel,
-        grid=(PAIRS,),
-        in_specs=[
-            smem,
-            whole,
-            pl.BlockSpec((plen, wide), lambda i: (0, i)),
-            pl.BlockSpec((slots, wide), lambda i: (0, i)),
-        ],
-        out_specs=[
-            pl.BlockSpec((1, 8 * shard, 2 * DH), lambda i: (i, 0, 0)),
-            pl.BlockSpec((1, 8 * shard, 2 * DH), lambda i: (i, 0, 0)),
-        ],
+        in_specs=[smem, smem, vmem, anywhere, anywhere],
+        out_specs=[vmem, vmem],
         out_shape=[
-            jax.ShapeDtypeStruct((PAIRS, 8 * shard, 2 * DH), F32),
-            jax.ShapeDtypeStruct((PAIRS, 8 * shard, 2 * DH), BF16),
-        ],
-        compiler_params=params(),
+            jax.ShapeDtypeStruct((4, 2, 8 * shard, 2 * DH), F32),
+            jax.ShapeDtypeStruct((4, 2, 8 * shard, 2 * DH), BF16),
+        ],
+        scratch_shapes=[
+            pltpu.VMEM((keys, model), BF16),
+            pltpu.SemaphoreType.DMA((PAIRS, 2)),
+        ],
+        compiler_params=params(32),
         cost_estimate=pl.CostEstimate(
             flops=2 * keys * model * 2 * DH, bytes_accessed=2 * keys * model, transcendentals=0
         ),
         name="weight_grad",
-    )(core_id, kvgrad, prompt_rows, resp_rows)
-    got = lax.ppermute(give, "c", SWAP)
-    chip_sum = (keep + got.astype(F32)).astype(BF16).reshape(64, shard, 2 * DH)
-    shares = lax.all_to_all(chip_sum, CHIPS, 0, 0, tiled=True)
+    )(core_id, order, kvgrad, prompt_rows, resp_rows)
+    got = [lax.ppermute(give[k], "c", SWAP) for k in range(4)]
+    line = keep[0] + got[0].astype(F32)
+    for k in range(1, 4):
+        piece = (keep[k] + got[k].astype(F32)).astype(BF16)
+        line = line + lax.ppermute(piece, "x", shift(-k)).astype(F32)
+    line = line.astype(BF16)
+    line = jnp.where(zh == 0, line, line[::-1]).reshape(16, shard, 2 * DH)
+    shares = lax.all_to_all(line, ("zh", "y", "zl"), 0, 0, tiled=True)
     weight_grad = jnp.sum(shares.astype(F32), 0)
 
     top = jnp.max(stats[:, :HEADS], 0)
@@ -317,9 +370,15 @@
     share = lax.dynamic_slice_in_dim(
         jnp.pad(share, ((0, 0), (0, 0), (0, slots))), my_start, slots, 2
     )
-    share = jnp.where(jnp.arange(slots) < my_len, share, 0.0).transpose(0, 2, 1)
-    parts = parts.astype(F32).reshape(N_SEQ, slots, HEADS, DH) * share[..., None]
-    attended = jnp.sum(parts, 0).astype(BF16).reshape(slots, width)
+    share = jnp.where(jnp.arange(slots) < my_len, share, 0.0).reshape(N_SEQ * HEADS, slots)
+    attended = pl.pallas_call(
+        weigh_kernel,
+        in_specs=[vmem, vmem],
+        out_specs=vmem,
+        out_shape=jax.ShapeDtypeStruct((slots, width), BF16),
+        compiler_params=params(16),
+        name="weigh",
+    )(parts, share)
     return attended[None], query_grad[None], kvgrad[None, :plen], weight_grad
 
 

time: 227 us -> 286 us (1.26)
  waiting for transfers between devices: 38.2 us -> 123 us
  blocking collectives: 61.6 us -> 15.7 us
  starting transfers between devices: 23.2 us -> 52.5 us
  local copies, waits for them, and re-layouts: 17.6 us -> 11.9 us
  other arithmetic: 13.4 us -> 9.17 us
    ppermute x2 -> x19, waiting for transfers between devices: 0.02 us -> 71.2 us  [the longest x1 24.7 us: per_device(): both = jnp.stack([block, lax.ppermute(block, 'zh', SWAP)], 0)]
    all_to_all x2 -> x1, blocking collectives: 61.6 us -> 15.7 us  [spread(): return lax.all_to_all(copies, axes, 0, 0, tiled=True)]
    ppermute x2 -> x19, starting transfers between devices: 0.01 us -> 30.4 us  [the longest x3 11.8 us: per_device(): run = [pair] + [lax.ppermute(pair, 'y', shift(k)) for k in range(1, 4)]]
    all_to_all x2, waiting for transfers between devices: 25.4 us -> 0.01 us  [spread(): return lax.all_to_all(copies, axes, 0, 0, tiled=True)]
    all_to_all x1, waiting for transfers between devices: 0.25 us -> 24.1 us  [per_device(): lax.all_to_all(parts.reshape(N_SEQ, slots, width), SEQ, 0, 0, tiled=True)]
    all_to_all x1, waiting for transfers between devices: 8.67 us -> 21.8 us  [per_device(): lax.all_to_all(back.reshape(N_SEQ, slots, width), SEQ, 0, 0, tiled=True)]
    mul x2 -> x0, local copies, waits for them, and re-layouts: 7.47 us -> none  [per_device(): parts.astype(F32).reshape(N_SEQ, slots, HEADS, DH) * share[..., None]]
    reduce_sum x1 -> x0, other arithmetic: 4.33 us -> none  [per_device(): attended = jnp.sum(parts, 0).astype(BF16).reshape(slots, width)]
  transfers between devices with their start and end apart: 7 -> 24, of which waited for: 5 -> 19; matrix products, arithmetic and copies ran while one was open for 16% -> 6% of each run, Pallas kernels for 14% -> 4%
where the time goes in v3:
time: 286 us; the launch traced here: 283 us
  waiting for transfers between devices  123 us (43%)
  Pallas kernels  54 us (19%)
  starting transfers between devices  52.5 us (18%)
  blocking collectives  15.7 us (5%)
  matrix products  13.8 us (5%)
  local copies, waits for them, and re-layouts  11.9 us (4%)
  other arithmetic  9.17 us (3%)
  between operations  2.96 us (1%)
    ppermute x1, waiting for transfers between devices, per_device(): both = jnp.stack([block, lax.ppermute(block, 'zh', SWAP)], 0)  24.7 us
    all_to_all x1, waiting for transfers between devices, per_device(): lax.all_to_all(parts.reshape(N_SEQ, slots, width), SEQ, 0, 0, tiled=True)  24.1 us
    all_to_all x1, waiting for transfers between devices, per_device(): lax.all_to_all(back.reshape(N_SEQ, slots, width), SEQ, 0, 0, tiled=True)  21.8 us
    pallas_call x1, Pallas kernels, per_device(): pl.pallas_call(functools.partial(grad_kernel, coef, scale), grid=(steps,)...  20.5 us
    all_to_all x1, blocking collectives, spread(): return lax.all_to_all(copies, axes, 0, 0, tiled=True)  15.7 us
    ppermute x1, waiting for transfers between devices, per_device(): other = lax.ppermute(kv_weight, 'zl', SWAP)  15.4 us
    ppermute x3, waiting for transfers between devices, per_device(): line = line + lax.ppermute(piece, 'x', shift(-k)).astype(F32)  13.9 us
    ppermute x3, starting transfers between devices, per_device(): run = [pair] + [lax.ppermute(pair, 'y', shift(k)) for k in range(1, 4)]  11.8 us
  transfers between devices with their start and end apart: 24, of which 19 were waited for; matrix products, arithmetic and copies ran while one was open for 6% of the time, Pallas kernels for 4%

profile of v3, /device:TPU:0, one launch (start us, length us, event | category | flops | bytes accessed | tf_op | source)
XLA Modules:
  0.0 282.8 jit_solution(8533554966171074898)
XLA Ops:
  3.2 6.0 %all-to-all-start = ((bf16[8,128,1024]{2,1,0:T(8,128)(2,1)}), bf16[8,128,1024]{2,1,0:T(8,128)(2,1)S(1)}, u32[]{:S(2)}, u32[]{:S(2)}) async-start(bf16[8,128,1024]{2,1,0:T(8,128)(2,1)} %broadcast_in_dim.82), calls=%async_computation | async-start | bytes 4194304 | tf_op jit(solution)/shard_map/all_to_all | solution.py:203
  11.3 15.4 %collective-permute-done = bf16[40,256]{1,0:T(8,128)(2,1)S(1)} collective-permute-done((bf16[40,256]{1,0:T(8,128)(2,1)S(1)}, bf16[40,256]{1,0:T(8,128)(2,1)S(1)}, u32[]{:S(2)}, u32[]{:S(2)}) %collective-permute-start) | collective-permute-done | bytes 20512 | tf_op jit(solution)/shard_map/ppermute | solution.py:231
  26.7 10.6 %collective-permute-start.1 = (bf16[80,256]{1,0:T(8,128)(2,1)S(1)}, bf16[80,256]{1,0:T(8,128)(2,1)S(1)}, u32[]{:S(2)}, u32[]{:S(2)}) collective-permute-start(bf16[80,256]{1,0:T(8,128)(2,1)S(1)} %get-tuple-element.17), channel_id=1, source_target_pairs={{2,0},{4,2},{6,4},{0,6},{3,1},{5,3},{7,5},{1,7},{10,8},{12,10},{14... | collective-permute-start | bytes 122888 | tf_op jit(solution)/shard_map/ppermute | solution.py:235
  39.0 3.8 %collective-permute-done.2 = bf16[80,256]{1,0:T(8,128)(2,1)S(1)} collective-permute-done((bf16[80,256]{1,0:T(8,128)(2,1)S(1)}, bf16[80,256]{1,0:T(8,128)(2,1)S(1)}, u32[]{:S(2)}, u32[]{:S(2)}) %collective-permute-start.2) | collective-permute-done | bytes 40992 | tf_op jit(solution)/shard_map/ppermute | solution.py:235
  46.4 4.5 %all-to-all-start.2 = ((bf16[8,128,1024]{2,1,0:T(8,128)(2,1)}), bf16[8,128,1024]{2,1,0:T(8,128)(2,1)}, u32[]{:S(2)}, u32[]{:S(2)}) async-start(bf16[8,128,1024]{2,1,0:T(8,128)(2,1)} %broadcast_in_dim.88), calls=%async_computation.2 | async-start | bytes 4194304 | tf_op jit(solution)/shard_map/all_to_all | solution.py:203
  50.9 3.7 %collective-permute-start.4 = (bf16[320,256]{1,0:T(8,128)(2,1)S(1)}, bf16[320,256]{1,0:T(8,128)(2,1)S(1)}, u32[]{:S(2)}, u32[]{:S(2)}) collective-permute-start(bf16[320,256]{1,0:T(8,128)(2,1)S(1)} %constant_dynamic-slice_fusion), channel_id=1, source_target_pairs={{0,16},{16,0},{1,17},{17,1},{2,18},{18,2},{3,19},{19,3},{4,20},{20... | collective-permute-start | bytes 491528 | tf_op jit(solution)/shard_map/ppermute | solution.py:239
  54.6 24.7 %collective-permute-done.4 = bf16[320,256]{1,0:T(8,128)(2,1)S(1)} collective-permute-done((bf16[320,256]{1,0:T(8,128)(2,1)S(1)}, bf16[320,256]{1,0:T(8,128)(2,1)S(1)}, u32[]{:S(2)}, u32[]{:S(2)}) %collective-permute-start.4) | collective-permute-done | bytes 163872 | tf_op jit(solution)/shard_map/ppermute | solution.py:239
  86.6 4.9 %collective-permute-done.6.refs_2_ = bf16[2,320,256]{2,1,0:T(8,128)(2,1)S(1)} collective-permute-done((bf16[2,320,256]{2,1,0:T(8,128)(2,1)S(1)}, bf16[2,320,256]{2,1,0:T(8,128)(2,1)S(1)}, u32[]{:S(2)}, u32[]{:S(2)}) %collective-permute-start.6) | collective-permute-done | bytes 327712 | tf_op jit(solution)/shard_map/ppermute | solution.py:240
  91.5 4.4 %collective-permute-done.7.refs_3_ = bf16[2,320,256]{2,1,0:T(8,128)(2,1)S(1)} collective-permute-done((bf16[2,320,256]{2,1,0:T(8,128)(2,1)S(1)}, bf16[2,320,256]{2,1,0:T(8,128)(2,1)S(1)}, u32[]{:S(2)}, u32[]{:S(2)}) %collective-permute-start.7) | collective-permute-done | bytes 327712 | tf_op jit(solution)/shard_map/ppermute | solution.py:240
  98.0 4.0 %copy-done = bf16[1,1024,5120]{2,1,0:T(8,128)(2,1)S(1)} copy-done((bf16[1,1024,5120]{2,1,0:T(8,128)(2,1)S(1)}, bf16[1,1024,5120]{2,1,0:T(8,128)(2,1)}, u32[]{:S(2)}) %copy-start) | copy-done | bytes 10485784
  102.0 9.4 %project.1.kv_ref = bf16[1152,256]{1,0:T(8,128)(2,1)S(1)} custom-call(s32[1]{0:T(128)} %bitcast.6.core_ref, s32[8]{0:T(128)S(1)} %stack.44.order_ref, bf16[2,320,256]{2,1,0:T(8,128)(2,1)S(1)} %pad_maximum_fusion.refs_0_, bf16[2,320,256]{2,1,0:T(8,128)(2,1)S(1)} %collective-permute-done.5.refs_1_, bf16[2,320,256]{2,1,0:T(8,128)(2,1)S(1)} %collective-permute-done.6.refs_2_, ...), custom_call_target="tpu_custom_call" | custom-call | flops 3019898880 | bytes 11796480 | tf_op jit(solution)/shard_map/project/pallas_call | solution.py:245
  117.6 11.7 %attend_stats.1 = (bf16[640,1024]{1,0:T(8,128)(2,1)S(1)}, f32[16,640]{1,0:T(8,128)S(1)}) custom-call(s32[1]{0:T(128)S(6)} %sub.39.valid_ref, bf16[640,1024]{1,0:T(8,128)(2,1)S(1)} %copy-done.7, bf16[1152,256]{1,0:T(8,128)(2,1)S(1)} %project.1.kv_ref, s32[640,128]{1,0:T(8,128)S(1)} %broadcast_in_dim.84.limit_ref), custom_call_target="tpu_custom_call" | custom-call | flops 3019898880 | bytes 4194304 | tf_op jit(solution)/shard_map/attend_stats/pallas_call | solution.py:281
  130.7 15.7 %all_to_all.30.stat_ref = f32[8,24,640]{2,1,0:T(8,128)S(1)} all-to-all(f32[8,24,640]{2,1,0:T(8,128)S(1)} %broadcast_in_dim.89), channel_id=1, replica_groups=mesh['x'=4,'zh'=2,'c'=2,'y'=4,'zl'=2] {'y','zl'}, dimensions={0} | all-to-all | bytes 983040 | tf_op jit(solution)/shard_map/all_to_all | solution.py:203
  146.5 20.5 %attend_grads.1 = (bf16[640,1024]{1,0:T(8,128)(2,1)S(1)}, bf16[1152,256]{1,0:T(8,128)(2,1)S(1)}) custom-call(s32[1]{0:T(128)S(6)} %sub.39.valid_ref, bf16[640,1024]{1,0:T(8,128)(2,1)S(1)} %copy-done.7, bf16[640,1024]{1,0:T(8,128)(2,1)S(1)} %fusion.7.g_ref, bf16[1152,256]{1,0:T(8,128)(2,1)S(1)} %copy-done.6, s32[8,640]{1,0:T(8,128)S(1)} %broadcast_in_dim.92.limit_ref, ...), custom_call_target="tpu_custom_call" | custom-call | flops 7549747200 | bytes 8388608 | tf_op jit(solution)/shard_map/attend_grads/pallas_call | solution.py:312
  168.1 9.0 %weight_grad.1 = (f32[4,2,320,256]{3,2,1,0:T(8,128)S(1)}, bf16[4,2,320,256]{3,2,1,0:T(8,128)(2,1)S(1)}) custom-call(s32[1]{0:T(128)} %bitcast.6.core_ref, s32[8]{0:T(128)S(1)} %stack.44.order_ref, bf16[1152,256]{1,0:T(8,128)(2,1)S(1)} %get-tuple-element.13.grad_ref, bf16[1024,5120]{1,0:T(8,128)(2,1)S(1)} %bitcast.72, bf16[128,5120]{1,0:T(8,128)(2,1)S(1)} %bitcast.74), custom_call_target="tpu_custom_call" | custom-call | flops 3019898880 | bytes 11796480 | tf_op jit(solution)/shard_map/weight_grad/pallas_call | solution.py:337
  186.0 6.4 %collective-permute-done.14 = bf16[2,320,256]{2,1,0:T(8,128)(2,1)S(1)} collective-permute-done((bf16[2,320,256]{2,1,0:T(8,128)(2,1)}, bf16[2,320,256]{2,1,0:T(8,128)(2,1)S(1)}, u32[]{:S(2)}, u32[]{:S(2)}) %collective-permute-start.14) | collective-permute-done | bytes 327712 | tf_op jit(solution)/shard_map/ppermute | solution.py:359
  192.4 7.4 %collective-permute-done.16 = bf16[2,320,256]{2,1,0:T(8,128)(2,1)} collective-permute-done((bf16[2,320,256]{2,1,0:T(8,128)(2,1)}, bf16[2,320,256]{2,1,0:T(8,128)(2,1)}, u32[]{:S(2)}, u32[]{:S(2)}) %collective-permute-start.16) | collective-permute-done | bytes 327712 | tf_op jit(solution)/shard_map/ppermute | solution.py:359
  202.2 3.5 %all-to-all-start.5 = ((bf16[16,40,256]{2,1,0:T(8,128)(2,1)}), bf16[16,40,256]{2,1,0:T(8,128)(2,1)S(1)}, u32[]{:S(2)}, u32[]{:S(2)}) async-start(bf16[16,40,256]{2,1,0:T(8,128)(2,1)} %bitcast.36), calls=%async_computation.5 | async-start | bytes 655360 | tf_op jit(solution)/shard_map/all_to_all | solution.py:362
  209.0 5.6 %all-to-all-done.5 = bf16[16,40,256]{2,1,0:T(8,128)(2,1)S(1)} async-done(((bf16[16,40,256]{2,1,0:T(8,128)(2,1)}), bf16[16,40,256]{2,1,0:T(8,128)(2,1)S(1)}, u32[]{:S(2)}, u32[]{:S(2)}) %all-to-all-start.5) | async-done | bytes 327712 | tf_op jit(solution)/shard_map/all_to_all | solution.py:362
  214.6 3.6 %all-to-all-start.1 = ((bf16[8,128,1024]{2,1,0:T(8,128)(2,1)}), bf16[8,128,1024]{2,1,0:T(8,128)(2,1)S(1)}, u32[]{:S(2)}, u32[]{:S(2)}) async-start(bf16[8,128,1024]{2,1,0:T(8,128)(2,1)} %bitcast.77), calls=%async_computation.1 | async-start | bytes 4194304 | tf_op jit(solution)/shard_map/all_to_all | solution.py:310
  218.2 4.6 %fusion.5 = bf16[1024,1024]{1,0:T(8,128)(2,1)} fusion(bf16[640,1024]{1,0:T(8,128)(2,1)} %copy-done.8, s32[640]{0:T(1024)S(1)} %get-tuple-element.26), kind=kOutput, calls=%fused_computation.6 | convolution fusion | flops 1343881216 | bytes 3410432 | tf_op jit(solution)/shard_map/dot_general | solution.py:333
  222.8 24.1 %all-to-all-done.1.parts_ref = bf16[8,128,1024]{2,1,0:T(8,128)(2,1)S(1)} async-done(((bf16[8,128,1024]{2,1,0:T(8,128)(2,1)}), bf16[8,128,1024]{2,1,0:T(8,128)(2,1)S(1)}, u32[]{:S(2)}, u32[]{:S(2)}) %all-to-all-start.1) | async-done | bytes 2097184 | tf_op jit(solution)/shard_map/all_to_all | solution.py:310
  246.9 4.4 %all-to-all-start.4 = ((bf16[8,128,1024]{2,1,0:T(8,128)(2,1)}), bf16[8,128,1024]{2,1,0:T(8,128)(2,1)}, u32[]{:S(2)}, u32[]{:S(2)}) async-start(bf16[8,128,1024]{2,1,0:T(8,128)(2,1)} %bitcast.76), calls=%async_computation.4 | async-start | bytes 4194304 | tf_op jit(solution)/shard_map/all_to_all | solution.py:334
  258.3 21.8 %all-to-all-done.4 = bf16[8,128,1024]{2,1,0:T(8,128)(2,1)} async-done(((bf16[8,128,1024]{2,1,0:T(8,128)(2,1)}), bf16[8,128,1024]{2,1,0:T(8,128)(2,1)}, u32[]{:S(2)}, u32[]{:S(2)}) %all-to-all-start.4) | async-done | bytes 2097184 | tf_op jit(solution)/shard_map/all_to_all | solution.py:334
  (106 shorter events, 50.1 us)
Async XLA Ops:
  3.2 40.2 %all-to-all-start = ((bf16[8,128,1024]{2,1,0:T(8,128)(2,1)}), bf16[8,128,1024]{2,1,0:T(8,128)(2,1)S(1)}, u32[]{:S(2)}, u32[]{:S(2)}) async-start(bf16[8,128,1024]{2,1,0:T(8,128)(2,1)} %broadcast_in_dim.82), calls=%async_computation | async-start | bytes 4194304 | tf_op jit(solution)/shard_map/all_to_all | solution.py:203
  9.3 17.4 %collective-permute-start = (bf16[40,256]{1,0:T(8,128)(2,1)S(1)}, bf16[40,256]{1,0:T(8,128)(2,1)S(1)}, u32[]{:S(2)}, u32[]{:S(2)}) collective-permute-start(bf16[40,256]{1,0:T(8,128)(2,1)S(1)} %copy-done.12), channel_id=1, source_target_pairs={{0,1},{1,0},{2,3},{3,2},{4,5},{5,4},{6,7},{7,6},{8,9},{9,8},{10,11... | collective-permute-start | bytes 61448 | tf_op jit(solution)/shard_map/ppermute | solution.py:231
  26.7 12.2 %collective-permute-start.1 = (bf16[80,256]{1,0:T(8,128)(2,1)S(1)}, bf16[80,256]{1,0:T(8,128)(2,1)S(1)}, u32[]{:S(2)}, u32[]{:S(2)}) collective-permute-start(bf16[80,256]{1,0:T(8,128)(2,1)S(1)} %get-tuple-element.17), channel_id=1, source_target_pairs={{2,0},{4,2},{6,4},{0,6},{3,1},{5,3},{7,5},{1,7},{10,8},{12,10},{14... | collective-permute-start | bytes 122888 | tf_op jit(solution)/shard_map/ppermute | solution.py:235
  37.3 5.5 %collective-permute-start.2 = (bf16[80,256]{1,0:T(8,128)(2,1)S(1)}, bf16[80,256]{1,0:T(8,128)(2,1)S(1)}, u32[]{:S(2)}, u32[]{:S(2)}) collective-permute-start(bf16[80,256]{1,0:T(8,128)(2,1)S(1)} %get-tuple-element.17), channel_id=1, source_target_pairs={{4,0},{6,2},{0,4},{2,6},{5,1},{7,3},{1,5},{3,7},{12,8},{14,10},{8,... | collective-permute-start | bytes 122888 | tf_op jit(solution)/shard_map/ppermute | solution.py:235
  38.1 5.2 %collective-permute-start.3 = (bf16[80,256]{1,0:T(8,128)(2,1)S(1)}, bf16[80,256]{1,0:T(8,128)(2,1)S(1)}, u32[]{:S(2)}, u32[]{:S(2)}) collective-permute-start(bf16[80,256]{1,0:T(8,128)(2,1)S(1)} %get-tuple-element.17), channel_id=1, source_target_pairs={{6,0},{0,2},{2,4},{4,6},{7,1},{1,3},{3,5},{5,7},{14,8},{8,10},{10,... | collective-permute-start | bytes 122888 | tf_op jit(solution)/shard_map/ppermute | solution.py:235
  46.4 67.9 %all-to-all-start.2 = ((bf16[8,128,1024]{2,1,0:T(8,128)(2,1)}), bf16[8,128,1024]{2,1,0:T(8,128)(2,1)}, u32[]{:S(2)}, u32[]{:S(2)}) async-start(bf16[8,128,1024]{2,1,0:T(8,128)(2,1)} %broadcast_in_dim.88), calls=%async_computation.2 | async-start | bytes 4194304 | tf_op jit(solution)/shard_map/all_to_all | solution.py:203
  50.9 28.3 %collective-permute-start.4 = (bf16[320,256]{1,0:T(8,128)(2,1)S(1)}, bf16[320,256]{1,0:T(8,128)(2,1)S(1)}, u32[]{:S(2)}, u32[]{:S(2)}) collective-permute-start(bf16[320,256]{1,0:T(8,128)(2,1)S(1)} %constant_dynamic-slice_fusion), channel_id=1, source_target_pairs={{0,16},{16,0},{1,17},{17,1},{2,18},{18,2},{3,19},{19,3},{4,20},{20... | collective-permute-start | bytes 491528 | tf_op jit(solution)/shard_map/ppermute | solution.py:239
  79.2 12.3 %collective-permute-start.6 = (bf16[2,320,256]{2,1,0:T(8,128)(2,1)S(1)}, bf16[2,320,256]{2,1,0:T(8,128)(2,1)S(1)}, u32[]{:S(2)}, u32[]{:S(2)}) collective-permute-start(bf16[2,320,256]{2,1,0:T(8,128)(2,1)S(1)} %pad_maximum_fusion.refs_0_), channel_id=1, source_target_pairs={{64,0},{96,32},{0,64},{32,96},{65,1},{97,33},{1,65},{33,97},{66,2}... | collective-permute-start | bytes 983048 | tf_op jit(solution)/shard_map/ppermute | solution.py:240
  82.4 13.6 %collective-permute-start.7 = (bf16[2,320,256]{2,1,0:T(8,128)(2,1)S(1)}, bf16[2,320,256]{2,1,0:T(8,128)(2,1)S(1)}, u32[]{:S(2)}, u32[]{:S(2)}) collective-permute-start(bf16[2,320,256]{2,1,0:T(8,128)(2,1)S(1)} %pad_maximum_fusion.refs_0_), channel_id=1, source_target_pairs={{96,0},{0,32},{32,64},{64,96},{97,1},{1,33},{33,65},{65,97},{98,2}... | collective-permute-start | bytes 983048 | tf_op jit(solution)/shard_map/ppermute | solution.py:240
  82.9 13.1 %collective-permute-start.5 = (bf16[2,320,256]{2,1,0:T(8,128)(2,1)S(1)}, bf16[2,320,256]{2,1,0:T(8,128)(2,1)S(1)}, u32[]{:S(2)}, u32[]{:S(2)}) collective-permute-start(bf16[2,320,256]{2,1,0:T(8,128)(2,1)S(1)} %pad_maximum_fusion.refs_0_), channel_id=1, source_target_pairs={{32,0},{64,32},{96,64},{0,96},{33,1},{65,33},{97,65},{1,97},{34,2}... | collective-permute-start | bytes 983048 | tf_op jit(solution)/shard_map/ppermute | solution.py:240
  86.5 10.0 %collective-permute-start.8 = (bf16[2,320,256]{2,1,0:T(8,128)(2,1)S(1)}, bf16[2,320,256]{2,1,0:T(8,128)(2,1)S(1)}, u32[]{:S(2)}, u32[]{:S(2)}) collective-permute-start(bf16[2,320,256]{2,1,0:T(8,128)(2,1)S(1)} %pad_maximum_fusion.refs_0_), channel_id=1, source_target_pairs={{0,8},{8,0},{1,9},{9,1},{2,10},{10,2},{3,11},{11,3},{4,12},{12,4},... | collective-permute-start | bytes 983048 | tf_op jit(solution)/shard_map/ppermute | solution.py:241
  91.5 5.0 %collective-permute-start.10 = (bf16[2,320,256]{2,1,0:T(8,128)(2,1)S(1)}, bf16[2,320,256]{2,1,0:T(8,128)(2,1)S(1)}, u32[]{:S(2)}, u32[]{:S(2)}) collective-permute-start(bf16[2,320,256]{2,1,0:T(8,128)(2,1)S(1)} %collective-permute-done.6.refs_2_), channel_id=1, source_target_pairs={{0,8},{8,0},{1,9},{9,1},{2,10},{10,2},{3,11},{11,3},{4,12},{12,4},... | collective-permute-start | bytes 983048 | tf_op jit(solution)/shard_map/ppermute | solution.py:241
  95.9 1.6 collective-permute-start.11
  96.1 2.0 collective-permute-start.9
  177.3 1.7 collective-permute-start.13
  177.3 2.1 collective-permute-start.15
  177.8 2.1 collective-permute-start.17
  177.9 8.1 %collective-permute-start.12 = (bf16[2,320,256]{2,1,0:T(8,128)(2,1)S(1)}, bf16[2,320,256]{2,1,0:T(8,128)(2,1)S(1)}, u32[]{:S(2)}, u32[]{:S(2)}) collective-permute-start(bf16[2,320,256]{2,1,0:T(8,128)(2,1)S(1)} %get-tuple-element.21), channel_id=1, source_target_pairs={{0,8},{8,0},{1,9},{9,1},{2,10},{10,2},{3,11},{11,3},{4,12},{12,4},... | collective-permute-start | bytes 983048 | tf_op jit(solution)/shard_map/ppermute | solution.py:355
  181.0 11.4 %collective-permute-start.14 = (bf16[2,320,256]{2,1,0:T(8,128)(2,1)}, bf16[2,320,256]{2,1,0:T(8,128)(2,1)S(1)}, u32[]{:S(2)}, u32[]{:S(2)}) collective-permute-start(bf16[2,320,256]{2,1,0:T(8,128)(2,1)} %get-tuple-element.18), channel_id=1, source_target_pairs={{96,0},{0,32},{32,64},{64,96},{97,1},{1,33},{33,65},{65,97},{98,2}... | collective-permute-start | bytes 983048 | tf_op jit(solution)/shard_map/ppermute | solution.py:359
  182.6 17.2 %collective-permute-start.16 = (bf16[2,320,256]{2,1,0:T(8,128)(2,1)}, bf16[2,320,256]{2,1,0:T(8,128)(2,1)}, u32[]{:S(2)}, u32[]{:S(2)}) collective-permute-start(bf16[2,320,256]{2,1,0:T(8,128)(2,1)} %get-tuple-element.20), channel_id=1, source_target_pairs={{64,0},{96,32},{0,64},{32,96},{65,1},{97,33},{1,65},{33,97},{66,2}... | collective-permute-start | bytes 983048 | tf_op jit(solution)/shard_map/ppermute | solution.py:359
  184.8 15.2 %collective-permute-start.18 = (bf16[2,320,256]{2,1,0:T(8,128)(2,1)}, bf16[2,320,256]{2,1,0:T(8,128)(2,1)}, u32[]{:S(2)}, u32[]{:S(2)}) collective-permute-start(bf16[2,320,256]{2,1,0:T(8,128)(2,1)} %get-tuple-element.19), channel_id=1, source_target_pairs={{32,0},{64,32},{96,64},{0,96},{33,1},{65,33},{97,65},{1,97},{34,2}... | collective-permute-start | bytes 983048 | tf_op jit(solution)/shard_map/ppermute | solution.py:359
  202.2 12.4 %all-to-all-start.5 = ((bf16[16,40,256]{2,1,0:T(8,128)(2,1)}), bf16[16,40,256]{2,1,0:T(8,128)(2,1)S(1)}, u32[]{:S(2)}, u32[]{:S(2)}) async-start(bf16[16,40,256]{2,1,0:T(8,128)(2,1)} %bitcast.36), calls=%async_computation.5 | async-start | bytes 655360 | tf_op jit(solution)/shard_map/all_to_all | solution.py:362
  214.6 32.3 %all-to-all-start.1 = ((bf16[8,128,1024]{2,1,0:T(8,128)(2,1)}), bf16[8,128,1024]{2,1,0:T(8,128)(2,1)S(1)}, u32[]{:S(2)}, u32[]{:S(2)}) async-start(bf16[8,128,1024]{2,1,0:T(8,128)(2,1)} %bitcast.77), calls=%async_computation.1 | async-start | bytes 4194304 | tf_op jit(solution)/shard_map/all_to_all | solution.py:310
  246.9 33.2 %all-to-all-start.4 = ((bf16[8,128,1024]{2,1,0:T(8,128)(2,1)}), bf16[8,128,1024]{2,1,0:T(8,128)(2,1)}, u32[]{:S(2)}, u32[]{:S(2)}) async-start(bf16[8,128,1024]{2,1,0:T(8,128)(2,1)} %bitcast.76), calls=%async_computation.4 | async-start | bytes 4194304 | tf_op jit(solution)/shard_map/all_to_all | solution.py:334
  (17 other events, 306.5 us)

commit v4 on v0

v4 whole, which is shorter than its diff:
```python
import functools

import jax
import jax.numpy as jnp
from jax import lax
from jax.experimental import pallas as pl
from jax.experimental.pallas import tpu as pltpu
from jax.sharding import Mesh
from jax.sharding import PartitionSpec as P

AXES = ("x", "zh", "c", "y", "zl")
GRP = ("x", "zh", "c")
SEQ = ("y", "zl")
PLANE = ("zh", "y", "zl")
N_SEQ = 8
NX = 4
NY = 4
HEADS = 8
HALF = 4
DH = 128
SLOTS = 128
ROWS = HALF * SLOTS
NEG = -1e30
LOG2E = 1.4426950408889634
NT = (((1,), (1,)), ((), ()))
TN = (((0,), (0,)), ((), ()))
F32 = jnp.float32
BF16 = jnp.bfloat16
SWAP = [(0, 1), (1, 0)]


def params(mib):
    return pltpu.CompilerParams(vmem_limit_bytes=mib << 20)


def shift(k):
    return [((i + k) % 4, i) for i in range(4)]


def stack_heads(ref):
    return jnp.concatenate([ref[:, h * DH : (h + 1) * DH] for h in range(HALF)], 0)


def project_kernel(place_ref, *refs):
    nears, fars = refs[:NX], refs[NX : 2 * NX]
    prompt_ref, resp_ref, kv_ref, weight, acc = refs[2 * NX :]
    plen = prompt_ref.shape[0]
    wide = weight.shape[0] // NX
    part = wide // 4
    x, core = place_ref[0], place_ref[1]
    for k in range(NX):
        for z in range(2):
            base = k * wide + z * 2 * part
            weight[pl.ds(pl.multiple_of(base + core * part, part), part)] = nears[k][z]
            weight[pl.ds(pl.multiple_of(base + (1 - core) * part, part), part)] = fars[k][z]
    for k in range(NX):
        cols = pl.ds(pl.multiple_of(lax.rem(x + k, NX) * wide, DH), wide)
        w = weight[k * wide : (k + 1) * wide]
        a = jnp.dot(prompt_ref[:, cols], w, preferred_element_type=F32)
        b = jnp.dot(resp_ref[:, cols], w, preferred_element_type=F32)
        if k == 0:
            acc[:plen], acc[plen:] = a, b
        elif k < NX - 1:
            acc[:plen] += a
            acc[plen:] += b
        else:
            kv_ref[:plen] = (acc[:plen] + a).astype(BF16)
            kv_ref[plen:] = (acc[plen:] + b).astype(BF16)


def first_pass(coef, carried, last, valid_ref, limit_ref, q_ref, kv_ref, *refs):
    refs = list(refs)
    if carried:
        prev_out_ref, prev_stat_ref = refs.pop(0), refs.pop(0)
    if last:
        g_ref = refs.pop(0)
    out_ref, stat_ref, bias, values = refs
    plen = kv_ref.shape[0] - DH

    @pl.when(pl.program_id(0) == 0)
    def _():
        place = lax.broadcasted_iota(jnp.int32, (plen, DH), 0)
        bias[...] = jnp.where(place < valid_ref[0], 0.0, NEG)
        values[...] = kv_ref[:, DH:].T

    causal = jnp.where(
        lax.broadcasted_iota(jnp.int32, (DH, SLOTS), 0) <= limit_ref[0:1], 0.0, NEG
    )
    keys = kv_ref[:, :DH]
    bias_all = jnp.concatenate([bias[...], causal], 0)
    for h in range(HALF):
        lanes = slice(h * SLOTS, (h + 1) * SLOTS)
        cols = slice(h * DH, (h + 1) * DH)
        s = lax.dot_general(keys, q_ref[:, cols], NT, preferred_element_type=F32)
        s = s * coef + bias_all
        top = jnp.max(s, 0, keepdims=True)
        if carried:
            before = prev_stat_ref[0:1, lanes]
            top = jnp.maximum(top, before)
        p = jnp.exp2(s - top)
        total = jnp.sum(p, 0, keepdims=True)
        o = jnp.dot(values[...], p.astype(BF16), preferred_element_type=F32)
        if carried:
            alpha = jnp.exp2(before - top)
            total = total + prev_stat_ref[1:2, lanes] * alpha
            o = o + prev_out_ref[:, lanes] * alpha
        if last:
            o = o / total
            stat_ref[2:3, lanes] = jnp.sum(o * g_ref[:, cols].astype(F32).T, 0, keepdims=True)
        out_ref[:, lanes] = o
        stat_ref[0:1, lanes] = top
        stat_ref[1:2, lanes] = total


def second_pass(coef, scale, last, valid_ref, limit_ref, q_ref, g_ref, kv_ref, stat_ref, *refs):
    if last:
        own_stat_ref, out_ref, prev_ref, back_ref, kvgrad_ref, acc, bias = refs
    else:
        back_ref, kvgrad_ref, acc, bias = refs
    step = pl.program_id(0)
    plen = kv_ref.shape[0] - DH
    tops = stat_ref[:, 0:1]
    top = jnp.max(tops, 0)
    share = stat_ref[:, 1:2] * jnp.exp2(tops - top)
    inv = 1.0 / jnp.sum(share, 0)
    delta = jnp.sum(share * stat_ref[:, 2:3], 0) * inv
    row = lax.broadcasted_iota(jnp.int32, (8, ROWS), 0)
    columns = jnp.where(row == 0, top, jnp.where(row == 1, inv, delta))
    columns = jnp.concatenate([columns] * 16, 0).T

    @pl.when(step == 0)
    def _():
        acc[...] = jnp.zeros_like(acc)
        place = lax.broadcasted_iota(jnp.int32, (8, plen), 1)
        bias[...] = jnp.where(place < valid_ref[0], 0.0, NEG)

    if last:
        weight = own_stat_ref[1:2] * jnp.exp2(own_stat_ref[0:1] - top) * inv
        att = (out_ref[...] * weight).T
        for h in range(HALF):
            back_ref[:, h * DH : (h + 1) * DH] = att[h * SLOTS : (h + 1) * SLOTS].astype(BF16)

    c_top, c_inv, c_delta = columns[:, 0:1], columns[:, 1:2], columns[:, 2:3]
    q = stack_heads(q_ref)
    g = stack_heads(g_ref)
    qt = q.T
    gt = g.T
    lane = lax.broadcasted_iota(jnp.int32, (SLOTS, DH), 1)
    causal = jnp.concatenate([jnp.where(lane <= limit_ref[...], 0.0, NEG)] * HALF, 0)
    dq = jnp.zeros((ROWS, DH), F32)
    chunk = 256
    for start in list(range(0, plen, chunk)) + [plen]:
        size = chunk if start < plen else DH
        keys = slice(start, start + size)
        k = kv_ref[keys, :DH]
        v = kv_ref[keys, DH:]
        s = lax.dot_general(q, k, NT, preferred_element_type=F32)
        hidden = bias[0:1, keys] if start < plen else causal
        p = jnp.exp2(s * coef - c_top + hidden) * c_inv
        dp = lax.dot_general(g, v, NT, preferred_element_type=F32)
        ds = (p * (dp - c_delta) * scale).astype(BF16)
        acc[:DH, keys] += jnp.dot(qt, ds, preferred_element_type=F32)
        acc[DH:, keys] += jnp.dot(gt, p.astype(BF16), preferred_element_type=F32)
        dq = dq + jnp.dot(ds, k, preferred_element_type=F32)
    for h in range(HALF):
        rows = slice(h * SLOTS, (h + 1) * SLOTS)
        cols = slice(h * DH, (h + 1) * DH)
        if last:
            back_ref[:, ROWS + h * DH : ROWS + (h + 1) * DH] = (
                dq[rows] + prev_ref[:, cols]
            ).astype(BF16)
        else:
            back_ref[:, cols] = dq[rows]

    @pl.when(step == pl.num_programs(0) - 1)
    def _():
        kvgrad_ref[...] = acc[...].T.astype(kvgrad_ref.dtype)


def weight_kernel(place_ref, own_ref, got_ref, prompt_ref, resp_ref, kvgrad_ref, keep_ref, give_ref, whole):
    plen = prompt_ref.shape[0]
    wide = whole.shape[0]
    part = wide // 4
    x, core = place_ref[0], place_ref[1]
    grad = (own_ref[...] + got_ref[...].astype(F32)).astype(BF16)
    kvgrad_ref[...] = grad[:plen]
    for k in range(NX):
        cols = pl.ds(pl.multiple_of(lax.rem(x + k, NX) * wide, DH), wide)
        t = lax.dot_general(prompt_ref[:, cols], grad[:plen], TN, preferred_element_type=F32)
        whole[...] = t + lax.dot_general(
            resp_ref[:, cols], grad[plen:], TN, preferred_element_type=F32
        )
        for z in range(2):
            base = z * 2 * part
            mine = pl.ds(pl.multiple_of(base + core * part, part), part)
            theirs = pl.ds(pl.multiple_of(base + (1 - core) * part, part), part)
            keep_ref[k, z] = whole[mine]
            give_ref[k, z] = whole[theirs].astype(BF16)


def spread(block, axes, count):
    copies = jnp.broadcast_to(block[None], (count,) + block.shape)
    return lax.all_to_all(copies, axes, 0, 0, tiled=True)


def per_device(
    prompt_hidden, resp_hidden, queries, grad_out, kv_weight, prompt_lengths, response_lengths
):
    rank = lax.axis_index(SEQ)
    x = lax.axis_index("x")
    place = jnp.stack([x, lax.axis_index("c")]).astype(jnp.int32)
    slots = resp_hidden.shape[1]
    plen = prompt_hidden.shape[1]
    model = prompt_hidden.shape[2]
    width = queries.shape[2]
    half = width // 2
    scale = DH ** (-0.5)
    coef = scale * LOG2E
    prompt_rows = prompt_hidden[0]
    resp_rows = resp_hidden[0]
    keys = plen + slots
    shard = kv_weight.shape[0]
    smem = pl.BlockSpec(memory_space=pltpu.SMEM)
    vmem = pl.BlockSpec(memory_space=pltpu.VMEM)

    block = spread(kv_weight, PLANE, 16).reshape(2, 8 * shard, 2 * DH)
    q_own, g_own, block = lax.optimization_barrier((queries[0], grad_out[0], block))
    nears = [block] + [lax.ppermute(block, "x", shift(k)) for k in range(1, NX)]
    fars = [lax.ppermute(piece, "c", SWAP) for piece in nears]

    def halves(t):
        t = t.reshape(slots, 2, half).transpose(1, 0, 2)[None]
        t = jnp.broadcast_to(t, (NY, 2, slots, half)).reshape(N_SEQ, slots, half)
        return lax.all_to_all(t, SEQ, 0, 0, tiled=True).reshape(N_SEQ * slots, half)

    q_all = halves(q_own)
    g_own, q_all = lax.optimization_barrier((g_own, q_all))
    g_all = halves(g_own)

    kv = pl.pallas_call(
        project_kernel,
        in_specs=[smem] + [vmem] * (2 * NX + 2),
        out_specs=vmem,
        out_shape=jax.ShapeDtypeStruct((keys, 2 * DH), BF16),
        scratch_shapes=[
            pltpu.VMEM((model, 2 * DH), BF16),
            pltpu.VMEM((keys, 2 * DH), F32),
        ],
        compiler_params=params(32),
        cost_estimate=pl.CostEstimate(
            flops=2 * keys * model * 2 * DH, bytes_accessed=2 * keys * model, transcendentals=0
        ),
        name="project",
    )(place, *nears, *fars, prompt_rows, resp_rows)
    kv_other = lax.ppermute(kv, "zl", SWAP)

    lengths = response_lengths[0]
    live_all = slots * N_SEQ * 5 // 8
    ends = jnp.cumsum(lengths)
    packed = jnp.arange(live_all)
    past = packed[:, None] >= ends[None, :]
    source = packed + jnp.sum(jnp.where(past, slots - lengths[None, :], 0), 1)
    pick = (source[:, None] == jnp.arange(N_SEQ * slots)[None, :]).astype(BF16)

    def masks(owner):
        offset = source - owner * slots
        limit = jnp.where((offset >= 0) & (offset < slots), offset, -1).astype(jnp.int32)
        return (
            (prompt_lengths - plen * owner).astype(jnp.int32),
            jnp.broadcast_to(limit[None, :], (8, live_all)),
            jnp.broadcast_to(limit[:, None], (live_all, DH)),
        )

    valid, limit_rows, limit_cols = masks(rank)
    valid_other, limit_rows_other, limit_cols_other = masks(rank ^ 1)

    steps = live_all // SLOTS
    rows = live_all * HALF
    whole = pl.BlockSpec((keys, 2 * DH), lambda i: (0, 0))
    slot_block = pl.BlockSpec((SLOTS, half), lambda i: (i, 0))
    lane_block = pl.BlockSpec((DH, ROWS), lambda i: (0, i))
    limit_lane = pl.BlockSpec((8, SLOTS), lambda i: (0, i))
    limit_slot = pl.BlockSpec((SLOTS, DH), lambda i: (i, 0))
    stat_block = pl.BlockSpec((3, ROWS), lambda i: (0, i))

    def forward(valid, limit, q, kv, state, g):
        carried, last = state is not None, g is not None
        return pl.pallas_call(
            functools.partial(first_pass, coef, carried, last),
            grid=(steps,),
            in_specs=[smem, limit_lane, slot_block, whole]
            + [lane_block, stat_block] * carried
            + [slot_block] * last,
            out_specs=[lane_block, stat_block],
            out_shape=[
                jax.ShapeDtypeStruct((DH, rows), F32),
                jax.ShapeDtypeStruct((3, rows), F32),
            ],
            scratch_shapes=[pltpu.VMEM((plen, DH), F32), pltpu.VMEM((DH, keys), BF16)],
            compiler_params=params(24),
            cost_estimate=pl.CostEstimate(
                flops=4 * rows * keys * DH, bytes_accessed=4 << 20, transcendentals=rows * keys
            ),
            name="attend_more" if carried else "attend_own",
        )(valid, limit, q, kv, *(state or ()), *([g] if last else []))

    q = jnp.dot(pick, q_all, preferred_element_type=F32).astype(BF16)
    state = forward(valid, limit_rows, q, kv, None, None)
    g = jnp.dot(pick, g_all, preferred_element_type=F32).astype(BF16)
    out, stat = forward(valid_other, limit_rows_other, q, kv_other, state, g)
    stats = spread(stat, "y", NY)

    def backward(valid, limit, kv, more):
        last = bool(more)
        return pl.pallas_call(
            functools.partial(second_pass, coef, scale, last),
            grid=(steps,),
            in_specs=[
                smem, limit_slot, slot_block, slot_block, whole,
                pl.BlockSpec((NY, 3, ROWS), lambda i: (0, 0, i)),
            ] + [stat_block, lane_block, slot_block] * last,
            out_specs=[
                pl.BlockSpec((SLOTS, 2 * half), lambda i: (i, 0)) if last else slot_block,
                whole,
            ],
            out_shape=[
                jax.ShapeDtypeStruct((live_all, 2 * half), BF16)
                if last
                else jax.ShapeDtypeStruct((live_all, half), F32),
                jax.ShapeDtypeStruct((keys, 2 * DH), F32 if last else BF16),
            ],
            scratch_shapes=[pltpu.VMEM((2 * DH, keys), F32), pltpu.VMEM((8, plen), F32)],
            compiler_params=params(24),
            cost_estimate=pl.CostEstimate(
                flops=10 * rows * keys * DH, bytes_accessed=8 << 20, transcendentals=rows * keys
            ),
            name="grads_own" if last else "grads_other",
        )(valid, limit, q, g, kv, stats, *more)

    qgrad_part, kvgrad_other = backward(valid_other, limit_cols_other, kv_other, ())
    kvgrad_got = lax.ppermute(kvgrad_other, "zl", SWAP)
    back, kvgrad_own = backward(valid, limit_cols, kv, (stat, out, qgrad_part))

    back = lax.dot_general(pick, back, TN, preferred_element_type=F32).astype(BF16)
    back, kvgrad_own = lax.optimization_barrier((back, kvgrad_own))
    back = lax.all_to_all(back.reshape(N_SEQ, slots, 2 * half), SEQ, 0, 0, tiled=True)

    prompt_grad, keep, give = pl.pallas_call(
        weight_kernel,
        in_specs=[smem] + [vmem] * 4,
        out_specs=[vmem] * 3,
        out_shape=[
            jax.ShapeDtypeStruct((plen, 2 * DH), BF16),
            jax.ShapeDtypeStruct((NX, 2, 8 * shard, 2 * DH), F32),
            jax.ShapeDtypeStruct((NX, 2, 8 * shard, 2 * DH), BF16),
        ],
        scratch_shapes=[pltpu.VMEM((model // NX, 2 * DH), F32)],
        compiler_params=params(32),
        cost_estimate=pl.CostEstimate(
            flops=2 * keys * model * 2 * DH, bytes_accessed=2 * keys * model, transcendentals=0
        ),
        name="weight_grad",
    )(place, kvgrad_own, kvgrad_got, prompt_rows, resp_rows)
    got = [lax.ppermute(give[k], "c", SWAP) for k in range(NX)]
    line = keep[0] + got[0].astype(F32)
    for k in range(1, NX):
        piece = (keep[k] + got[k].astype(F32)).astype(BF16)
        line = line + lax.ppermute(piece, "x", shift(-k)).astype(F32)
    line = line.astype(BF16).reshape(16, shard, 2 * DH)
    line, back = lax.optimization_barrier((line, back))
    shares = lax.all_to_all(line, PLANE, 0, 0, tiled=True)
    weight_grad = jnp.sum(shares.astype(F32), 0)

    back = jnp.sum(back.reshape(NY, 2, slots, 2 * half).astype(F32), 0).astype(BF16)
    attended = jnp.concatenate([back[0, :, :half], back[1, :, :half]], 1)
    query_grad = jnp.concatenate([back[0, :, half:], back[1, :, half:]], 1)
    return attended[None], query_grad[None], prompt_grad[None], weight_grad


def solution(mesh):
    fine = Mesh(mesh.devices.reshape(4, 2, 2, 4, 2), AXES)
    return jax.shard_map(
        per_device,
        mesh=fine,
        in_specs=(
            P(GRP, SEQ, None),
            P(GRP, SEQ, None),
            P(GRP, SEQ, None),
            P(GRP, SEQ, None),
            P(AXES, None),
            P(GRP),
            P(GRP, None),
        ),
        out_specs=(
            P(GRP, SEQ, None),
            P(GRP, SEQ, None),
            P(GRP, SEQ, None),
            P(AXES, None),
        ),
        check_vma=False,
    )
```

time: 1380 us -> 180 us (0.13)
  waiting for transfers between devices: 1210 us -> 34.1 us
  matrix products: 92.9 us -> 6.41 us
  Pallas kernels: 0 us -> 48.8 us
  other arithmetic: 47.3 us -> 5.17 us
  starting transfers between devices: 0.16 us -> 34.6 us
  blocking collectives: 0 us -> 27.6 us
    unnamed x5 -> x0, waiting for transfers between devices: 645 us -> none
    all_gather x2 -> x0, waiting for transfers between devices: 392 us -> none  [the longest x1 308 us: per_device(): piece = lax.all_gather(kv_weight, ('grp', 'seq'), axis=0, tiled=True)]
    reduce_scatter x1 -> x0, waiting for transfers between devices: 172 us -> none  [per_device(): lax.psum_scatter(kv_grad[None, :plen_all], 'seq', scatter_dimension=1, ti...]
    dot_general x28 -> x3, matrix products: 92.9 us -> 6.41 us  [the longest x1 3.27 us: per_device(): lax.dot_general(pick, back, TN, preferred_element_type=F32).astype(BF16)]
    pallas_call x0 -> x6, Pallas kernels: none -> 48.8 us  [the longest x2 25.9 us: backward(): pl.pallas_call(functools.partial(second_pass, coef, scale, last), grid=(s...]
    ppermute x0 -> x16, waiting for transfers between devices: none -> 28.2 us  [the longest x3 13.8 us: per_device(): line = line + lax.ppermute(piece, 'x', shift(-k)).astype(F32)]
    all_to_all x0 -> x2, blocking collectives: none -> 27.6 us  [spread(): return lax.all_to_all(copies, axes, 0, 0, tiled=True)]
    reduce_sum x11 -> x3, other arithmetic: 24.2 us -> 2.77 us  [the longest x1 2.02 us: per_device(): jnp.sum(back.reshape(NY, 2, slots, 2 * half).astype(F32), 0).astype(BF16)]
  transfers between devices with their start and end apart: 4 -> 20, of which waited for: 4 -> 10; matrix products, arithmetic and copies ran while one was open for 1% -> 8% of each run, Pallas kernels for 0% -> 16%
where the time goes in v4:
time: 180 us; the launch traced here: 179 us
  Pallas kernels  48.8 us (27%)
  starting transfers between devices  34.6 us (19%)
  waiting for transfers between devices  34.1 us (19%)
  blocking collectives  27.6 us (15%)
  local copies, waits for them, and re-layouts  20.7 us (12%)
  matrix products  6.41 us (4%)
  other arithmetic  5.17 us (3%)
    all_to_all x2, blocking collectives, spread(): return lax.all_to_all(copies, axes, 0, 0, tiled=True)  27.6 us
    pallas_call x2, Pallas kernels, backward(): pl.pallas_call(functools.partial(second_pass, coef, scale, last), grid=(s...  25.9 us
    unnamed x30, local copies, waits for them, and re-layouts  14.2 us
    ppermute x3, waiting for transfers between devices, per_device(): line = line + lax.ppermute(piece, 'x', shift(-k)).astype(F32)  13.8 us
    pallas_call x2, Pallas kernels, forward(): pl.pallas_call(functools.partial(first_pass, coef, carried, last), grid=(...  13 us
    ppermute x3, waiting for transfers between devices, per_device(): nears = [block] + [lax.ppermute(block, 'x', shift(k)) for k in range(1, NX)]  11.3 us
    all_to_all x2, starting transfers between devices, halves(): return lax.all_to_all(t, SEQ, 0, 0, tiled=True).reshape(N_SEQ * slots, half)  8.89 us
    all_to_all x1, waiting for transfers between devices, per_device(): shares = lax.all_to_all(line, PLANE, 0, 0, tiled=True)  5.9 us
  transfers between devices with their start and end apart: 20, of which 10 were waited for; matrix products, arithmetic and copies ran while one was open for 8% of the time, Pallas kernels for 16%

profile of v4, /device:TPU:0, one launch (start us, length us, event | category | flops | bytes accessed | tf_op | source)
XLA Modules:
  0.0 178.9 jit_solution(17984307281676153654)
XLA Ops:
  1.4 17.1 %all_to_all.30 = bf16[16,40,256]{2,1,0:T(8,128)(2,1)S(1)} all-to-all(bf16[16,40,256]{2,1,0:T(8,128)(2,1)S(1)} %broadcast_in_dim.46), channel_id=1, replica_groups=mesh['x'=4,'zh'=2,'c'=2,'y'=4,'zl'=2] {'zh','y','zl'}, dimensions={0} | all-to-all | bytes 655360 | tf_op jit(solution)/shard_map/all_to_all | solution.py:203
  20.8 3.6 %all-to-all-start.1 = ((bf16[8,128,512]{2,1,0:T(8,128)(2,1)}), bf16[8,128,512]{2,1,0:T(8,128)(2,1)S(1)}, u32[]{:S(2)}, u32[]{:S(2)}) async-start(bf16[8,128,512]{2,1,0:T(8,128)(2,1)} %bitcast.10), calls=%async_computation.1 | async-start | bytes 2097152 | tf_op jit(solution)/shard_map/all_to_all | solution.py:234
  26.0 2.7 %collective-permute-start.1 = (bf16[2,320,256]{2,1,0:T(8,128)(2,1)S(1)}, bf16[2,320,256]{2,1,0:T(8,128)(2,1)S(1)}, u32[]{:S(2)}, u32[]{:S(2)}) collective-permute-start(bf16[2,320,256]{2,1,0:T(8,128)(2,1)S(1)} %bitcast.73), channel_id=1, source_target_pairs={{64,0},{96,32},{0,64},{32,96},{65,1},{97,33},{1,65},{33,97},{66,2}... | collective-permute-start | bytes 983048 | tf_op jit(solution)/shard_map/ppermute | solution.py:228
  30.4 5.0 %collective-permute-done.2.refs_3_ = bf16[2,320,256]{2,1,0:T(8,128)(2,1)S(1)} collective-permute-done((bf16[2,320,256]{2,1,0:T(8,128)(2,1)S(1)}, bf16[2,320,256]{2,1,0:T(8,128)(2,1)S(1)}, u32[]{:S(2)}, u32[]{:S(2)}) %collective-permute-start.2) | collective-permute-done | bytes 327712 | tf_op jit(solution)/shard_map/ppermute | solution.py:228
  35.4 6.2 %collective-permute-done.1.refs_2_ = bf16[2,320,256]{2,1,0:T(8,128)(2,1)S(1)} collective-permute-done((bf16[2,320,256]{2,1,0:T(8,128)(2,1)S(1)}, bf16[2,320,256]{2,1,0:T(8,128)(2,1)S(1)}, u32[]{:S(2)}, u32[]{:S(2)}) %collective-permute-start.1) | collective-permute-done | bytes 327712 | tf_op jit(solution)/shard_map/ppermute | solution.py:228
  46.2 5.3 %all-to-all-start.2 = ((bf16[8,128,512]{2,1,0:T(8,128)(2,1)}), bf16[8,128,512]{2,1,0:T(8,128)(2,1)}, u32[]{:S(2)}, u32[]{:S(2)}) async-start(bf16[8,128,512]{2,1,0:T(8,128)(2,1)} %bitcast.77), calls=%async_computation.2 | async-start | bytes 2097152 | tf_op jit(solution)/shard_map/all_to_all | solution.py:234
  53.7 4.0 %copy-done = bf16[1,1024,5120]{2,1,0:T(8,128)(2,1)S(1)} copy-done((bf16[1,1024,5120]{2,1,0:T(8,128)(2,1)S(1)}, bf16[1,1024,5120]{2,1,0:T(8,128)(2,1)}, u32[]{:S(2)}) %copy-start) | copy-done | bytes 10485784
  59.6 4.6 %project.1.kv_ref = bf16[1152,256]{1,0:T(8,128)(2,1)S(1)} custom-call(s32[2]{0:T(128)S(1)} %pad_add_fusion.place_ref, bf16[2,320,256]{2,1,0:T(8,128)(2,1)S(1)} %bitcast.76, bf16[2,320,256]{2,1,0:T(8,128)(2,1)S(1)} %collective-permute-done.refs_1_, bf16[2,320,256]{2,1,0:T(8,128)(2,1)S(1)} %collective-permute-done.1.refs_2_, ...), custom_call_target="tpu_custom_call" | custom-call | flops 3019898880 | bytes 11796480 | tf_op jit(solution)/shard_map/project/pallas_call | solution.py:240
  64.2 2.1 %collective-permute-start.7 = (bf16[1152,256]{1,0:T(8,128)(2,1)S(1)}, bf16[1152,256]{1,0:T(8,128)(2,1)S(1)}, u32[]{:S(2)}, u32[]{:S(2)}) collective-permute-start(bf16[1152,256]{1,0:T(8,128)(2,1)S(1)} %project.1.kv_ref), channel_id=1, source_target_pairs={{0,1},{1,0},{2,3},{3,2},{4,5},{5,4},{6,7},{7,6},{8,9},{9,8},{10,11... | collective-permute-start | bytes 1769480 | tf_op jit(solution)/shard_map/ppermute | solution.py:255
  67.2 6.3 %attend_own.1 = (f32[128,2560]{1,0:T(8,128)S(1)}, f32[3,2560]{1,0:T(4,128)S(1)}) custom-call(s32[1]{0:T(128)S(6)} %sub.45.valid_ref, s32[8,640]{1,0:T(8,128)S(1)} %broadcast_in_dim.89.limit_ref, bf16[640,512]{1,0:T(8,128)(2,1)S(1)} %fusion.4.q_ref, bf16[1152,256]{1,0:T(8,128)(2,1)S(1)} %project.1.kv_ref), custom_call_target="tpu_custom_call" | custom-call | flops 1509949440 | bytes 4194304 | tf_op jit(solution)/shard_map/attend_own/pallas_call | solution.py:288
  75.4 2.2 %fusion.5.refs_2_.g_ref = bf16[640,512]{1,0:T(8,128)(2,1)S(1)} fusion(bf16[1024,512]{1,0:T(8,128)(2,1)} %bitcast.14, s32[640]{0:T(1024)S(1)} %get-tuple-element.57), kind=kOutput, calls=%fused_computation.6 | convolution fusion | flops 672071680 | bytes 1706496 | tf_op jit(solution)/shard_map/dot_general | solution.py:309
  79.3 6.7 %attend_more.1 = (f32[128,2560]{1,0:T(8,128)S(1)}, f32[3,2560]{1,0:T(4,128)S(1)}) custom-call(s32[1]{0:T(128)S(6)} %sub.49.valid_ref, s32[8,640]{1,0:T(8,128)S(1)} %broadcast_in_dim.88.limit_ref, bf16[640,512]{1,0:T(8,128)(2,1)S(1)} %copy-done.10, bf16[1152,256]{1,0:T(8,128)(2,1)S(1)} %collective-permute-done.7.kv_ref, f32[128,2560]{1,0:T(8,128)S(1)} %copy-done.8, ...), custom_call_target="tpu_custom_call" | custom-call | flops 1509949440 | bytes 4194304 | tf_op jit(solution)/shard_map/attend_more/pallas_call | solution.py:288
  86.0 10.5 %all_to_all.31.stat_ref = f32[4,3,2560]{2,1,0:T(4,128)S(1)} all-to-all(f32[4,3,2560]{2,1,0:T(4,128)S(1)} %broadcast_in_dim.90), channel_id=1, replica_groups=mesh['x'=4,'zh'=2,'c'=2,'y'=4,'zl'=2] {'y'}, dimensions={0} | all-to-all | bytes 245760 | tf_op jit(solution)/shard_map/all_to_all | solution.py:203
  96.7 13.2 %grads_other.1 = (f32[640,512]{1,0:T(8,128)S(1)}, bf16[1152,256]{1,0:T(8,128)(2,1)}) custom-call(s32[1]{0:T(128)S(6)} %sub.49.valid_ref, s32[640,128]{1,0:T(8,128)S(1)} %broadcast_in_dim.91.limit_ref, bf16[640,512]{1,0:T(8,128)(2,1)S(1)} %copy-done.10, bf16[640,512]{1,0:T(8,128)(2,1)S(1)} %fusion.5.refs_2_.g_ref, ...), custom_call_target="tpu_custom_call" | custom-call | flops 3774873600 | bytes 8388608 | tf_op jit(solution)/shard_map/grads_other/pallas_call | solution.py:315
  111.4 12.7 %grads_own.1 = (bf16[640,1024]{1,0:T(8,128)(2,1)S(1)}, f32[1152,256]{1,0:T(8,128)S(1)}) custom-call(s32[1]{0:T(128)S(6)} %sub.45.valid_ref, s32[640,128]{1,0:T(8,128)S(1)} %broadcast_in_dim.45.limit_ref, bf16[640,512]{1,0:T(8,128)(2,1)S(1)} %copy-done.10, bf16[640,512]{1,0:T(8,128)(2,1)S(1)} %fusion.5.refs_2_.g_ref, bf16[1152,256]{1,0:T(8,128)(2,1)S(1)} %project.1.kv_ref, ...), custom_call_target="tpu_custom_call" | custom-call | flops 3774873600 | bytes 8388608 | tf_op jit(solution)/shard_map/grads_own/pallas_call | solution.py:315
  124.2 3.3 %fusion.3 = bf16[1024,1024]{1,0:T(8,128)(2,1)} fusion(bf16[640,1024]{1,0:T(8,128)(2,1)S(1)} %get-tuple-element.34, s32[640]{0:T(1024)S(1)} %get-tuple-element.57), kind=kOutput, calls=%fused_computation.4 | convolution fusion | flops 1343881216 | bytes 3410432 | tf_op jit(solution)/shard_map/dot_general | solution.py:344
  127.4 4.3 %all-to-all-start.4 = ((bf16[8,128,1024]{2,1,0:T(8,128)(2,1)}), bf16[8,128,1024]{2,1,0:T(8,128)(2,1)}, u32[]{:S(2)}, u32[]{:S(2)}) async-start(bf16[8,128,1024]{2,1,0:T(8,128)(2,1)} %bitcast.78), calls=%async_computation.4 | async-start | bytes 4194304 | tf_op jit(solution)/shard_map/all_to_all | solution.py:346
  131.8 4.0 %copy-done.1 = bf16[1,1024,5120]{2,1,0:T(8,128)(2,1)S(1)} copy-done((bf16[1,1024,5120]{2,1,0:T(8,128)(2,1)S(1)}, bf16[1,1024,5120]{2,1,0:T(8,128)(2,1)}, u32[]{:S(2)}) %copy-start.1) | copy-done | bytes 10485784
  135.8 5.3 %weight_grad.1 = (bf16[1024,256]{1,0:T(8,128)(2,1)}, f32[4,2,320,256]{3,2,1,0:T(8,128)S(1)}, bf16[4,2,320,256]{3,2,1,0:T(8,128)(2,1)S(1)}) custom-call(s32[2]{0:T(128)S(1)} %pad_add_fusion.place_ref, f32[1152,256]{1,0:T(8,128)S(1)} %get-tuple-element.36.own_ref, bf16[1152,256]{1,0:T(8,128)(2,1)} %collective-permute-done.8.got_ref, ...), custom_call_target="tpu_custom_call" | custom-call | flops 3019898880 | bytes 11796480 | tf_op jit(solution)/shard_map/weight_grad/pallas_call | solution.py:348
  149.0 6.6 %collective-permute-done.11 = bf16[2,320,256]{2,1,0:T(8,128)(2,1)S(1)} collective-permute-done((bf16[2,320,256]{2,1,0:T(8,128)(2,1)S(1)}, bf16[2,320,256]{2,1,0:T(8,128)(2,1)S(1)}, u32[]{:S(2)}, u32[]{:S(2)}) %collective-permute-start.11) | collective-permute-done | bytes 327712 | tf_op jit(solution)/shard_map/ppermute | solution.py:368
  155.5 6.0 %collective-permute-done.15 = bf16[2,320,256]{2,1,0:T(8,128)(2,1)S(1)} collective-permute-done((bf16[2,320,256]{2,1,0:T(8,128)(2,1)S(1)}, bf16[2,320,256]{2,1,0:T(8,128)(2,1)S(1)}, u32[]{:S(2)}, u32[]{:S(2)}) %collective-permute-start.15) | collective-permute-done | bytes 327712 | tf_op jit(solution)/shard_map/ppermute | solution.py:368
  163.7 5.7 %all-to-all-start.5 = ((bf16[16,40,256]{2,1,0:T(8,128)(2,1)}), bf16[16,40,256]{2,1,0:T(8,128)(2,1)S(1)}, u32[]{:S(2)}, u32[]{:S(2)}) async-start(bf16[16,40,256]{2,1,0:T(8,128)(2,1)} %bitcast.26), calls=%async_computation.5 | async-start | bytes 655360 | tf_op jit(solution)/shard_map/all_to_all | solution.py:371
  169.4 2.0 %reduce_sum.31 = bf16[2,128,1024]{2,1,0:T(8,128)(2,1)S(1)} reduce(bf16[4,2,128,1024]{3,2,1,0:T(8,128)(2,1)} %bitcast.28, bf16[]{:T(256)} %constant.35.clone.1), dimensions={0}, to_apply=%region_2.3 | reduce | flops 786432 | bytes 2621442 | tf_op jit(solution)/shard_map/reduce_sum | solution.py:374
  172.3 5.9 %all-to-all-done.5 = bf16[16,40,256]{2,1,0:T(8,128)(2,1)S(1)} async-done(((bf16[16,40,256]{2,1,0:T(8,128)(2,1)}), bf16[16,40,256]{2,1,0:T(8,128)(2,1)S(1)}, u32[]{:S(2)}, u32[]{:S(2)}) %all-to-all-start.5) | async-done | bytes 327712 | tf_op jit(solution)/shard_map/all_to_all | solution.py:371
  (81 shorter events, 31.9 us)
Async XLA Ops:
  19.6 4.7 %copy-start.14 = (s32[1,8]{1,0:T(1,128)S(1)}, s32[1,8]{1,0:T(1,128)}, u32[]{:S(2)}) copy-start(s32[1,8]{1,0:T(1,128)} %param.13) | copy-start | bytes 100
  19.6 23.5 %copy-start.13 = (bf16[1,128,1024]{2,1,0:T(8,128)(2,1)S(1)}, bf16[1,128,1024]{2,1,0:T(8,128)(2,1)}, u32[]{:S(2)}) copy-start(bf16[1,128,1024]{2,1,0:T(8,128)(2,1)} %param.10) | copy-start | bytes 786436
  20.8 21.5 %all-to-all-start.1 = ((bf16[8,128,512]{2,1,0:T(8,128)(2,1)}), bf16[8,128,512]{2,1,0:T(8,128)(2,1)S(1)}, u32[]{:S(2)}, u32[]{:S(2)}) async-start(bf16[8,128,512]{2,1,0:T(8,128)(2,1)} %bitcast.10), calls=%async_computation.1 | async-start | bytes 2097152 | tf_op jit(solution)/shard_map/all_to_all | solution.py:234
  24.5 10.9 %collective-permute-start.2 = (bf16[2,320,256]{2,1,0:T(8,128)(2,1)S(1)}, bf16[2,320,256]{2,1,0:T(8,128)(2,1)S(1)}, u32[]{:S(2)}, u32[]{:S(2)}) collective-permute-start(bf16[2,320,256]{2,1,0:T(8,128)(2,1)S(1)} %bitcast.72), channel_id=1, source_target_pairs={{96,0},{0,32},{32,64},{64,96},{97,1},{1,33},{33,65},{65,97},{98,2}... | collective-permute-start | bytes 983048 | tf_op jit(solution)/shard_map/ppermute | solution.py:228
  26.0 15.6 %collective-permute-start.1 = (bf16[2,320,256]{2,1,0:T(8,128)(2,1)S(1)}, bf16[2,320,256]{2,1,0:T(8,128)(2,1)S(1)}, u32[]{:S(2)}, u32[]{:S(2)}) collective-permute-start(bf16[2,320,256]{2,1,0:T(8,128)(2,1)S(1)} %bitcast.73), channel_id=1, source_target_pairs={{64,0},{96,32},{0,64},{32,96},{65,1},{97,33},{1,65},{33,97},{66,2}... | collective-permute-start | bytes 983048 | tf_op jit(solution)/shard_map/ppermute | solution.py:228
  28.7 12.9 %collective-permute-start = (bf16[2,320,256]{2,1,0:T(8,128)(2,1)S(1)}, bf16[2,320,256]{2,1,0:T(8,128)(2,1)S(1)}, u32[]{:S(2)}, u32[]{:S(2)}) collective-permute-start(bf16[2,320,256]{2,1,0:T(8,128)(2,1)S(1)} %bitcast.74), channel_id=1, source_target_pairs={{32,0},{64,32},{96,64},{0,96},{33,1},{65,33},{97,65},{1,97},{34,2}... | collective-permute-start | bytes 983048 | tf_op jit(solution)/shard_map/ppermute | solution.py:228
  30.3 21.9 %collective-permute-start.3 = (bf16[2,320,256]{2,1,0:T(8,128)(2,1)S(1)}, bf16[2,320,256]{2,1,0:T(8,128)(2,1)S(1)}, u32[]{:S(2)}, u32[]{:S(2)}) collective-permute-start(bf16[2,320,256]{2,1,0:T(8,128)(2,1)S(1)} %bitcast.75), channel_id=1, source_target_pairs={{0,8},{8,0},{1,9},{9,1},{2,10},{10,2},{3,11},{11,3},{4,12},{12,4},... | collective-permute-start | bytes 983048 | tf_op jit(solution)/shard_map/ppermute | solution.py:229
  35.4 17.6 %collective-permute-start.6 = (bf16[2,320,256]{2,1,0:T(8,128)(2,1)S(1)}, bf16[2,320,256]{2,1,0:T(8,128)(2,1)S(1)}, u32[]{:S(2)}, u32[]{:S(2)}) collective-permute-start(bf16[2,320,256]{2,1,0:T(8,128)(2,1)S(1)} %collective-permute-done.2.refs_3_), channel_id=1, source_target_pairs={{0,8},{8,0},{1,9},{9,1},{2,10},{10,2},{3,11},{11,3},{4,12},{12,4},... | collective-permute-start | bytes 983048 | tf_op jit(solution)/shard_map/ppermute | solution.py:229
  41.6 12.1 %collective-permute-start.5 = (bf16[2,320,256]{2,1,0:T(8,128)(2,1)S(1)}, bf16[2,320,256]{2,1,0:T(8,128)(2,1)}, u32[]{:S(2)}, u32[]{:S(2)}) collective-permute-start(bf16[2,320,256]{2,1,0:T(8,128)(2,1)S(1)} %collective-permute-done.1.refs_2_), channel_id=1, source_target_pairs={{0,8},{8,0},{1,9},{9,1},{2,10},{10,2},{3,11},{11,3},{4,12},{12,4},... | collective-permute-start | bytes 983048 | tf_op jit(solution)/shard_map/ppermute | solution.py:229
  41.6 12.1 %collective-permute-start.4 = (bf16[2,320,256]{2,1,0:T(8,128)(2,1)S(1)}, bf16[2,320,256]{2,1,0:T(8,128)(2,1)}, u32[]{:S(2)}, u32[]{:S(2)}) collective-permute-start(bf16[2,320,256]{2,1,0:T(8,128)(2,1)S(1)} %collective-permute-done.refs_1_), channel_id=1, source_target_pairs={{0,8},{8,0},{1,9},{9,1},{2,10},{10,2},{3,11},{11,3},{4,12},{12,4},... | collective-permute-start | bytes 983048 | tf_op jit(solution)/shard_map/ppermute | solution.py:229
  44.1 9.6 %copy-start.2 = (bf16[1,128,5120]{2,1,0:T(8,128)(2,1)S(1)}, bf16[1,128,5120]{2,1,0:T(8,128)(2,1)}, u32[]{:S(2)}) copy-start(bf16[1,128,5120]{2,1,0:T(8,128)(2,1)} %param.8) | copy-start | bytes 3932164
  46.2 29.2 %all-to-all-start.2 = ((bf16[8,128,512]{2,1,0:T(8,128)(2,1)}), bf16[8,128,512]{2,1,0:T(8,128)(2,1)}, u32[]{:S(2)}, u32[]{:S(2)}) async-start(bf16[8,128,512]{2,1,0:T(8,128)(2,1)} %bitcast.77), calls=%async_computation.2 | async-start | bytes 2097152 | tf_op jit(solution)/shard_map/all_to_all | solution.py:234
  59.6 6.7 %copy-start.12 = (bf16[8,128,512]{2,1,0:T(8,128)(2,1)S(1)}, bf16[8,128,512]{2,1,0:T(8,128)(2,1)}, u32[]{:S(2)}) copy-start(bf16[8,128,512]{2,1,0:T(8,128)(2,1)} %copy-done.11) | copy-start | bytes 3145732
  64.2 15.0 %collective-permute-start.7 = (bf16[1152,256]{1,0:T(8,128)(2,1)S(1)}, bf16[1152,256]{1,0:T(8,128)(2,1)S(1)}, u32[]{:S(2)}, u32[]{:S(2)}) collective-permute-start(bf16[1152,256]{1,0:T(8,128)(2,1)S(1)} %project.1.kv_ref), channel_id=1, source_target_pairs={{0,1},{1,0},{2,3},{3,2},{4,5},{5,4},{6,7},{7,6},{8,9},{9,8},{10,11... | collective-permute-start | bytes 1769480 | tf_op jit(solution)/shard_map/ppermute | solution.py:255
  109.8 21.9 %collective-permute-start.8 = (bf16[1152,256]{1,0:T(8,128)(2,1)}, bf16[1152,256]{1,0:T(8,128)(2,1)}, u32[]{:S(2)}, u32[]{:S(2)}) collective-permute-start(bf16[1152,256]{1,0:T(8,128)(2,1)} %get-tuple-element.37), channel_id=1, source_target_pairs={{0,1},{1,0},{2,3},{3,2},{4,5},{5,4},{6,7},{7,6},{8,9},{9,8},{10,11... | collective-permute-start | bytes 1769480 | tf_op jit(solution)/shard_map/ppermute | solution.py:341
  127.4 36.2 %all-to-all-start.4 = ((bf16[8,128,1024]{2,1,0:T(8,128)(2,1)}), bf16[8,128,1024]{2,1,0:T(8,128)(2,1)}, u32[]{:S(2)}, u32[]{:S(2)}) async-start(bf16[8,128,1024]{2,1,0:T(8,128)(2,1)} %bitcast.78), calls=%async_computation.4 | async-start | bytes 4194304 | tf_op jit(solution)/shard_map/all_to_all | solution.py:346
  141.2 1.7 collective-permute-start.14
  141.3 2.1 %collective-permute-start.12 = (bf16[2,320,256]{2,1,0:T(8,128)(2,1)S(1)}, bf16[2,320,256]{2,1,0:T(8,128)(2,1)S(1)}, u32[]{:S(2)}, u32[]{:S(2)}) collective-permute-start(bf16[2,320,256]{2,1,0:T(8,128)(2,1)S(1)} %get-tuple-element.49), channel_id=1, source_target_pairs={{0,8},{8,0},{1,9},{9,1},{2,10},{10,2},{3,11},{11,3},{4,12},{12,4},... | collective-permute-start | bytes 983048 | tf_op jit(solution)/shard_map/ppermute | solution.py:364
  141.8 2.1 %collective-permute-start.10 = (bf16[2,320,256]{2,1,0:T(8,128)(2,1)S(1)}, bf16[2,320,256]{2,1,0:T(8,128)(2,1)S(1)}, u32[]{:S(2)}, u32[]{:S(2)}) collective-permute-start(bf16[2,320,256]{2,1,0:T(8,128)(2,1)S(1)} %get-tuple-element.50), channel_id=1, source_target_pairs={{0,8},{8,0},{1,9},{9,1},{2,10},{10,2},{3,11},{11,3},{4,12},{12,4},... | collective-permute-start | bytes 983048 | tf_op jit(solution)/shard_map/ppermute | solution.py:364
  142.1 6.9 %collective-permute-start.9 = (bf16[2,320,256]{2,1,0:T(8,128)(2,1)S(1)}, bf16[2,320,256]{2,1,0:T(8,128)(2,1)S(1)}, u32[]{:S(2)}, u32[]{:S(2)}) collective-permute-start(bf16[2,320,256]{2,1,0:T(8,128)(2,1)S(1)} %get-tuple-element.47), channel_id=1, source_target_pairs={{0,8},{8,0},{1,9},{9,1},{2,10},{10,2},{3,11},{11,3},{4,12},{12,4},... | collective-permute-start | bytes 983048 | tf_op jit(solution)/shard_map/ppermute | solution.py:364
  144.2 11.3 %collective-permute-start.11 = (bf16[2,320,256]{2,1,0:T(8,128)(2,1)S(1)}, bf16[2,320,256]{2,1,0:T(8,128)(2,1)S(1)}, u32[]{:S(2)}, u32[]{:S(2)}) collective-permute-start(bf16[2,320,256]{2,1,0:T(8,128)(2,1)S(1)} %get-tuple-element.44), channel_id=1, source_target_pairs={{96,0},{0,32},{32,64},{64,96},{97,1},{1,33},{33,65},{65,97},{98,2}... | collective-permute-start | bytes 983048 | tf_op jit(solution)/shard_map/ppermute | solution.py:368
  145.6 15.9 %collective-permute-start.15 = (bf16[2,320,256]{2,1,0:T(8,128)(2,1)S(1)}, bf16[2,320,256]{2,1,0:T(8,128)(2,1)S(1)}, u32[]{:S(2)}, u32[]{:S(2)}) collective-permute-start(bf16[2,320,256]{2,1,0:T(8,128)(2,1)S(1)} %get-tuple-element.45), channel_id=1, source_target_pairs={{32,0},{64,32},{96,64},{0,96},{33,1},{65,33},{97,65},{1,97},{34,2}... | collective-permute-start | bytes 983048 | tf_op jit(solution)/shard_map/ppermute | solution.py:368
  147.5 15.2 %collective-permute-start.13 = (bf16[2,320,256]{2,1,0:T(8,128)(2,1)S(1)}, bf16[2,320,256]{2,1,0:T(8,128)(2,1)S(1)}, u32[]{:S(2)}, u32[]{:S(2)}) collective-permute-start(bf16[2,320,256]{2,1,0:T(8,128)(2,1)S(1)} %get-tuple-element.46), channel_id=1, source_target_pairs={{64,0},{96,32},{0,64},{32,96},{65,1},{97,33},{1,65},{33,97},{66,2}... | collective-permute-start | bytes 983048 | tf_op jit(solution)/shard_map/ppermute | solution.py:368
  163.7 14.5 %all-to-all-start.5 = ((bf16[16,40,256]{2,1,0:T(8,128)(2,1)}), bf16[16,40,256]{2,1,0:T(8,128)(2,1)S(1)}, u32[]{:S(2)}, u32[]{:S(2)}) async-start(bf16[16,40,256]{2,1,0:T(8,128)(2,1)} %bitcast.26), calls=%async_computation.5 | async-start | bytes 655360 | tf_op jit(solution)/shard_map/all_to_all | solution.py:371
  (11 other events, 21.9 us)

commit v5 on v4

--- a/solution.py
+++ b/solution.py
@@ -11,7 +11,6 @@
 AXES = ("x", "zh", "c", "y", "zl")
 GRP = ("x", "zh", "c")
 SEQ = ("y", "zl")
-PLANE = ("zh", "y", "zl")
 N_SEQ = 8
 NX = 4
 NY = 4
@@ -41,31 +40,52 @@
     return jnp.concatenate([ref[:, h * DH : (h + 1) * DH] for h in range(HALF)], 0)
 
 
-def project_kernel(place_ref, *refs):
-    nears, fars = refs[:NX], refs[NX : 2 * NX]
-    prompt_ref, resp_ref, kv_ref, weight, acc = refs[2 * NX :]
+def fetch(steps, x, prompt_ref, resp_ref, buf, sems):
     plen = prompt_ref.shape[0]
-    wide = weight.shape[0] // NX
+    wide = prompt_ref.shape[1] // NX
+    half = wide // 2
+    copies = []
+    for n, k in enumerate(steps):
+        for part in range(2):
+            there = pl.ds(pl.multiple_of(lax.rem(x + k, NX) * wide + part * half, DH), half)
+            here = pl.ds(n * wide + part * half, half)
+            sem = sems.at[n * 2 + part]
+            pair = (
+                pltpu.make_async_copy(prompt_ref.at[:, there], buf.at[:plen, here], sem.at[0]),
+                pltpu.make_async_copy(resp_ref.at[:, there], buf.at[plen:, here], sem.at[1]),
+            )
+            for copy in pair:
+                copy.start()
+            copies.append(pair)
+    return copies
+
+
+def project_kernel(steps, first, last, place_ref, prompt_ref, resp_ref, *refs):
+    refs = list(refs)
+    nears = [refs.pop(0) for _ in steps]
+    fars = [refs.pop(0) for _ in steps]
+    prev_ref = None if first else refs.pop(0)
+    kv_ref, buf, weight, sems = refs
+    wide = prompt_ref.shape[1] // NX
+    half = wide // 2
     part = wide // 4
     x, core = place_ref[0], place_ref[1]
-    for k in range(NX):
+    copies = fetch(steps, x, prompt_ref, resp_ref, buf, sems)
+    for n in range(len(steps)):
         for z in range(2):
-            base = k * wide + z * 2 * part
-            weight[pl.ds(pl.multiple_of(base + core * part, part), part)] = nears[k][z]
-            weight[pl.ds(pl.multiple_of(base + (1 - core) * part, part), part)] = fars[k][z]
-    for k in range(NX):
-        cols = pl.ds(pl.multiple_of(lax.rem(x + k, NX) * wide, DH), wide)
-        w = weight[k * wide : (k + 1) * wide]
-        a = jnp.dot(prompt_ref[:, cols], w, preferred_element_type=F32)
-        b = jnp.dot(resp_ref[:, cols], w, preferred_element_type=F32)
-        if k == 0:
-            acc[:plen], acc[plen:] = a, b
-        elif k < NX - 1:
-            acc[:plen] += a
-            acc[plen:] += b
-        else:
-            kv_ref[:plen] = (acc[:plen] + a).astype(BF16)
-            kv_ref[plen:] = (acc[plen:] + b).astype(BF16)
+            base = n * wide + z * half
+            weight[pl.ds(pl.multiple_of(base + core * part, part), part)] = nears[n][z]
+            weight[pl.ds(pl.multiple_of(base + (1 - core) * part, part), part)] = fars[n][z]
+    total = None
+    for n, pair in enumerate(copies):
+        for copy in pair:
+            copy.wait()
+        cols = slice(n * half, (n + 1) * half)
+        t = jnp.dot(buf[:, cols], weight[cols], preferred_element_type=F32)
+        total = t if total is None else total + t
+    if not first:
+        total = total + prev_ref[...]
+    kv_ref[...] = total.astype(kv_ref.dtype)
 
 
 def first_pass(coef, carried, last, valid_ref, limit_ref, q_ref, kv_ref, *refs):
@@ -112,18 +132,19 @@
         stat_ref[1:2, lanes] = total
 
 
-def second_pass(coef, scale, last, valid_ref, limit_ref, q_ref, g_ref, kv_ref, stat_ref, *refs):
+def second_pass(coef, scale, last, valid_ref, limit_ref, q_ref, g_ref, kv_ref, *refs):
+    stat_refs, refs = refs[:NY], refs[NY:]
     if last:
-        own_stat_ref, out_ref, prev_ref, back_ref, kvgrad_ref, acc, bias = refs
+        out_ref, prev_ref, back_ref, kvgrad_ref, acc, bias = refs
     else:
         back_ref, kvgrad_ref, acc, bias = refs
     step = pl.program_id(0)
     plen = kv_ref.shape[0] - DH
-    tops = stat_ref[:, 0:1]
-    top = jnp.max(tops, 0)
-    share = stat_ref[:, 1:2] * jnp.exp2(tops - top)
-    inv = 1.0 / jnp.sum(share, 0)
-    delta = jnp.sum(share * stat_ref[:, 2:3], 0) * inv
+    tops = [ref[0:1] for ref in stat_refs]
+    top = functools.reduce(jnp.maximum, tops)
+    share = [ref[1:2] * jnp.exp2(t - top) for ref, t in zip(stat_refs, tops)]
+    inv = 1.0 / sum(share)
+    delta = sum(w * ref[2:3] for w, ref in zip(share, stat_refs)) * inv
     row = lax.broadcasted_iota(jnp.int32, (8, ROWS), 0)
     columns = jnp.where(row == 0, top, jnp.where(row == 1, inv, delta))
     columns = jnp.concatenate([columns] * 16, 0).T
@@ -135,7 +156,7 @@
         bias[...] = jnp.where(place < valid_ref[0], 0.0, NEG)
 
     if last:
-        weight = own_stat_ref[1:2] * jnp.exp2(own_stat_ref[0:1] - top) * inv
+        weight = share[0] * inv
         att = (out_ref[...] * weight).T
         for h in range(HALF):
             back_ref[:, h * DH : (h + 1) * DH] = att[h * SLOTS : (h + 1) * SLOTS].astype(BF16)
@@ -177,30 +198,34 @@
         kvgrad_ref[...] = acc[...].T.astype(kvgrad_ref.dtype)
 
 
-def weight_kernel(place_ref, own_ref, got_ref, prompt_ref, resp_ref, kvgrad_ref, keep_ref, give_ref, whole):
+def weight_kernel(steps, first, place_ref, prompt_ref, resp_ref, *refs):
+    refs = list(refs)
     plen = prompt_ref.shape[0]
-    wide = whole.shape[0]
+    wide = prompt_ref.shape[1] // NX
+    half = wide // 2
     part = wide // 4
     x, core = place_ref[0], place_ref[1]
-    grad = (own_ref[...] + got_ref[...].astype(F32)).astype(BF16)
-    kvgrad_ref[...] = grad[:plen]
-    for k in range(NX):
-        cols = pl.ds(pl.multiple_of(lax.rem(x + k, NX) * wide, DH), wide)
-        t = lax.dot_general(prompt_ref[:, cols], grad[:plen], TN, preferred_element_type=F32)
-        whole[...] = t + lax.dot_general(
-            resp_ref[:, cols], grad[plen:], TN, preferred_element_type=F32
-        )
-        for z in range(2):
-            base = z * 2 * part
-            mine = pl.ds(pl.multiple_of(base + core * part, part), part)
-            theirs = pl.ds(pl.multiple_of(base + (1 - core) * part, part), part)
-            keep_ref[k, z] = whole[mine]
-            give_ref[k, z] = whole[theirs].astype(BF16)
-
-
-def spread(block, axes, count):
-    copies = jnp.broadcast_to(block[None], (count,) + block.shape)
-    return lax.all_to_all(copies, axes, 0, 0, tiled=True)
+    if first:
+        own_ref, got_ref, prompt_grad_ref, resp_grad_ref = (refs.pop(i) for i in (0, 0, 0, 0))
+    else:
+        prompt_grad_ref, resp_grad_ref = refs.pop(0), refs.pop(0)
+    keep_ref, give_ref, buf, whole, sems = refs
+    copies = fetch(steps, x, prompt_ref, resp_ref, buf, sems)
+    if first:
+        grad = (own_ref[...] + got_ref[...].astype(F32)).astype(BF16)
+        prompt_grad_ref[...] = grad[:plen]
+        resp_grad_ref[...] = grad[plen:]
+    else:
+        grad = jnp.concatenate([prompt_grad_ref[...], resp_grad_ref[...]], 0)
+    mine = pl.ds(pl.multiple_of(core * part, part), part)
+    theirs = pl.ds(pl.multiple_of((1 - core) * part, part), part)
+    for n, pair in enumerate(copies):
+        for copy in pair:
+            copy.wait()
+        cols = slice(n * half, (n + 1) * half)
+        whole[n] = lax.dot_general(buf[:, cols], grad, TN, preferred_element_type=F32)
+        keep_ref[n // 2, n % 2] = whole[n, mine]
+        give_ref[n // 2, n % 2] = whole[n, theirs].astype(BF16)
 
 
 def per_device(
@@ -223,35 +248,58 @@
     smem = pl.BlockSpec(memory_space=pltpu.SMEM)
     vmem = pl.BlockSpec(memory_space=pltpu.VMEM)
 
-    block = spread(kv_weight, PLANE, 16).reshape(2, 8 * shard, 2 * DH)
-    q_own, g_own, block = lax.optimization_barrier((queries[0], grad_out[0], block))
+    y = lax.axis_index("y")
+    z = lax.axis_index(("zh", "zl"))
+
+    def gather(t, axis, place_of):
+        run = [t] + [lax.ppermute(t, axis, shift(k)) for k in range(1, 4)]
+        run = jnp.stack(run + run[:3], 0)
+        return lax.dynamic_slice_in_dim(run, (4 - place_of) % 4, 4, 0)
+
+    block = gather(kv_weight, "y", y)
+    block = gather(block, ("zh", "zl"), z).reshape(2, 2, NY, shard, 2 * DH)
+    block = block.transpose(0, 2, 1, 3, 4).reshape(2, 8 * shard, 2 * DH)
+
+    def halves(t):
+        return t.reshape(slots, 2, half).transpose(1, 0, 2)
+
+    qg = jnp.concatenate([halves(queries[0]), halves(grad_out[0])], 2)
+    qg = jnp.broadcast_to(qg[None], (NY, 2, slots, 2 * half)).reshape(N_SEQ, slots, 2 * half)
+    qg, block = lax.optimization_barrier((qg, block))
     nears = [block] + [lax.ppermute(block, "x", shift(k)) for k in range(1, NX)]
     fars = [lax.ppermute(piece, "c", SWAP) for piece in nears]
-
-    def halves(t):
-        t = t.reshape(slots, 2, half).transpose(1, 0, 2)[None]
-        t = jnp.broadcast_to(t, (NY, 2, slots, half)).reshape(N_SEQ, slots, half)
-        return lax.all_to_all(t, SEQ, 0, 0, tiled=True).reshape(N_SEQ * slots, half)
-
-    q_all = halves(q_own)
-    g_own, q_all = lax.optimization_barrier((g_own, q_all))
-    g_all = halves(g_own)
-
-    kv = pl.pallas_call(
-        project_kernel,
-        in_specs=[smem] + [vmem] * (2 * NX + 2),
-        out_specs=vmem,
-        out_shape=jax.ShapeDtypeStruct((keys, 2 * DH), BF16),
-        scratch_shapes=[
-            pltpu.VMEM((model, 2 * DH), BF16),
-            pltpu.VMEM((keys, 2 * DH), F32),
-        ],
-        compiler_params=params(32),
-        cost_estimate=pl.CostEstimate(
-            flops=2 * keys * model * 2 * DH, bytes_accessed=2 * keys * model, transcendentals=0
-        ),
-        name="project",
-    )(place, *nears, *fars, prompt_rows, resp_rows)
+    qg, fars[0] = lax.optimization_barrier((qg, fars[0]))
+    qg_all = lax.all_to_all(qg, SEQ, 0, 0, tiled=True).reshape(N_SEQ * slots, 2 * half)
+
+    hbm = pl.BlockSpec(memory_space=pltpu.HBM)
+
+    def project(steps, prev, last):
+        count = len(steps)
+        return pl.pallas_call(
+            functools.partial(project_kernel, steps, prev is None, last),
+            in_specs=[smem, hbm, hbm] + [vmem] * (2 * count + (prev is not None)),
+            out_specs=vmem,
+            out_shape=jax.ShapeDtypeStruct((keys, 2 * DH), BF16 if last else F32),
+            scratch_shapes=[
+                pltpu.VMEM((keys, count * model // NX), BF16),
+                pltpu.VMEM((count * model // NX, 2 * DH), BF16),
+                pltpu.SemaphoreType.DMA((2 * count, 2)),
+            ],
+            compiler_params=params(24),
+            cost_estimate=pl.CostEstimate(
+                flops=2 * keys * model * DH * count // 2,
+                bytes_accessed=keys * model * count // 2,
+                transcendentals=0,
+            ),
+            name="project_last" if last else "project",
+        )(
+            place, prompt_rows, resp_rows, *[nears[k] for k in steps], *[fars[k] for k in steps],
+            *(() if prev is None else (prev,)),
+        )
+
+    kv = project((0,), None, False)
+    kv = project((3,), kv, False)
+    kv = project((1, 2), kv, True)
     kv_other = lax.ppermute(kv, "zl", SWAP)
 
     lengths = response_lengths[0]
@@ -278,19 +326,20 @@
     rows = live_all * HALF
     whole = pl.BlockSpec((keys, 2 * DH), lambda i: (0, 0))
     slot_block = pl.BlockSpec((SLOTS, half), lambda i: (i, 0))
+    g_block = pl.BlockSpec((SLOTS, half), lambda i: (i, 1))
     lane_block = pl.BlockSpec((DH, ROWS), lambda i: (0, i))
     limit_lane = pl.BlockSpec((8, SLOTS), lambda i: (0, i))
     limit_slot = pl.BlockSpec((SLOTS, DH), lambda i: (i, 0))
     stat_block = pl.BlockSpec((3, ROWS), lambda i: (0, i))
 
-    def forward(valid, limit, q, kv, state, g):
-        carried, last = state is not None, g is not None
+    def forward(valid, limit, kv, state):
+        carried = last = state is not None
         return pl.pallas_call(
             functools.partial(first_pass, coef, carried, last),
             grid=(steps,),
             in_specs=[smem, limit_lane, slot_block, whole]
             + [lane_block, stat_block] * carried
-            + [slot_block] * last,
+            + [g_block] * last,
             out_specs=[lane_block, stat_block],
             out_shape=[
                 jax.ShapeDtypeStruct((DH, rows), F32),
@@ -302,13 +351,12 @@
                 flops=4 * rows * keys * DH, bytes_accessed=4 << 20, transcendentals=rows * keys
             ),
             name="attend_more" if carried else "attend_own",
-        )(valid, limit, q, kv, *(state or ()), *([g] if last else []))
-
-    q = jnp.dot(pick, q_all, preferred_element_type=F32).astype(BF16)
-    state = forward(valid, limit_rows, q, kv, None, None)
-    g = jnp.dot(pick, g_all, preferred_element_type=F32).astype(BF16)
-    out, stat = forward(valid_other, limit_rows_other, q, kv_other, state, g)
-    stats = spread(stat, "y", NY)
+        )(valid, limit, qg, kv, *(state or ()), *([qg] if last else []))
+
+    qg = jnp.dot(pick, qg_all, preferred_element_type=F32).astype(BF16)
+    state = forward(valid, limit_rows, kv, None)
+    out, stat = forward(valid_other, limit_rows_other, kv_other, state)
+    stats = [stat] + [lax.ppermute(stat, "y", shift(k)) for k in range(1, NY)]
 
     def backward(valid, limit, kv, more):
         last = bool(more)
@@ -316,9 +364,8 @@
             functools.partial(second_pass, coef, scale, last),
             grid=(steps,),
             in_specs=[
-                smem, limit_slot, slot_block, slot_block, whole,
-                pl.BlockSpec((NY, 3, ROWS), lambda i: (0, 0, i)),
-            ] + [stat_block, lane_block, slot_block] * last,
+                smem, limit_slot, slot_block, g_block, whole,
+            ] + [stat_block] * NY + [lane_block, slot_block] * last,
             out_specs=[
                 pl.BlockSpec((SLOTS, 2 * half), lambda i: (i, 0)) if last else slot_block,
                 whole,
@@ -335,41 +382,67 @@
                 flops=10 * rows * keys * DH, bytes_accessed=8 << 20, transcendentals=rows * keys
             ),
             name="grads_own" if last else "grads_other",
-        )(valid, limit, q, g, kv, stats, *more)
+        )(valid, limit, qg, qg, kv, *stats, *more)
 
     qgrad_part, kvgrad_other = backward(valid_other, limit_cols_other, kv_other, ())
     kvgrad_got = lax.ppermute(kvgrad_other, "zl", SWAP)
-    back, kvgrad_own = backward(valid, limit_cols, kv, (stat, out, qgrad_part))
+    back, kvgrad_own = backward(valid, limit_cols, kv, (out, qgrad_part))
 
     back = lax.dot_general(pick, back, TN, preferred_element_type=F32).astype(BF16)
     back, kvgrad_own = lax.optimization_barrier((back, kvgrad_own))
     back = lax.all_to_all(back.reshape(N_SEQ, slots, 2 * half), SEQ, 0, 0, tiled=True)
 
-    prompt_grad, keep, give = pl.pallas_call(
-        weight_kernel,
-        in_specs=[smem] + [vmem] * 4,
-        out_specs=[vmem] * 3,
-        out_shape=[
-            jax.ShapeDtypeStruct((plen, 2 * DH), BF16),
-            jax.ShapeDtypeStruct((NX, 2, 8 * shard, 2 * DH), F32),
-            jax.ShapeDtypeStruct((NX, 2, 8 * shard, 2 * DH), BF16),
-        ],
-        scratch_shapes=[pltpu.VMEM((model // NX, 2 * DH), F32)],
-        compiler_params=params(32),
-        cost_estimate=pl.CostEstimate(
-            flops=2 * keys * model * 2 * DH, bytes_accessed=2 * keys * model, transcendentals=0
-        ),
-        name="weight_grad",
-    )(place, kvgrad_own, kvgrad_got, prompt_rows, resp_rows)
-    got = [lax.ppermute(give[k], "c", SWAP) for k in range(NX)]
-    line = keep[0] + got[0].astype(F32)
-    for k in range(1, NX):
-        piece = (keep[k] + got[k].astype(F32)).astype(BF16)
+    def weight_part(steps, grads):
+        first = grads is None
+        count = len(steps)
+        pieces = [
+            jax.ShapeDtypeStruct((count, 2, 8 * shard, 2 * DH), F32),
+            jax.ShapeDtypeStruct((count, 2, 8 * shard, 2 * DH), BF16),
+        ]
+        if first:
+            grads = (kvgrad_own, kvgrad_got)
+            pieces = [
+                jax.ShapeDtypeStruct((plen, 2 * DH), BF16),
+                jax.ShapeDtypeStruct((slots, 2 * DH), BF16),
+            ] + pieces
+        return pl.pallas_call(
+            functools.partial(weight_kernel, steps, first),
+            in_specs=[smem, hbm, hbm, vmem, vmem],
+            out_specs=[vmem] * len(pieces),
+            out_shape=pieces,
+            scratch_shapes=[
+                pltpu.VMEM((keys, count * model // NX), BF16),
+                pltpu.VMEM((2 * count, model // NX // 2, 2 * DH), F32),
+                pltpu.SemaphoreType.DMA((2 * count, 2)),
+            ],
+            compiler_params=params(32),
+            cost_estimate=pl.CostEstimate(
+                flops=2 * keys * model * DH * count // 2,
+                bytes_accessed=keys * model * count // 2,
+                transcendentals=0,
+            ),
+            name="weight_near" if first else "weight_far",
+        )(place, prompt_rows, resp_rows, *grads)
+
+    prompt_grad, resp_grad, keep, give = weight_part((1, 3), None)
+    near_sum = [(keep[n], lax.ppermute(give[n], "c", SWAP)) for n in range(2)]
+    keep, give = weight_part((2, 0), (prompt_grad, resp_grad))
+    far_sum = [(keep[n], lax.ppermute(give[n], "c", SWAP)) for n in range(2)]
+    line = far_sum[1][0] + far_sum[1][1].astype(F32)
+    for k, (kept, got) in zip((1, 3, 2), near_sum + far_sum):
+        piece = (kept + got.astype(F32)).astype(BF16)
         line = line + lax.ppermute(piece, "x", shift(-k)).astype(F32)
-    line = line.astype(BF16).reshape(16, shard, 2 * DH)
-    line, back = lax.optimization_barrier((line, back))
-    shares = lax.all_to_all(line, PLANE, 0, 0, tiled=True)
-    weight_grad = jnp.sum(shares.astype(F32), 0)
+
+    def scatter(t, axis, place_of, dtype):
+        t = lax.dynamic_slice_in_dim(jnp.concatenate([t, t[:3]], 0), place_of, 4, 0)
+        total = t[0]
+        for k in range(1, 4):
+            total = total + lax.ppermute(t[k].astype(dtype), axis, shift(-k)).astype(F32)
+        return total
+
+    line = line.reshape(2, NY, 2, shard, 2 * DH).transpose(0, 2, 1, 3, 4)
+    line = scatter(line.reshape(4, NY, shard, 2 * DH), ("zh", "zl"), z, BF16)
+    weight_grad = scatter(line, "y", y, F32)
 
     back = jnp.sum(back.reshape(NY, 2, slots, 2 * half).astype(F32), 0).astype(BF16)
     attended = jnp.concatenate([back[0, :, :half], back[1, :, :half]], 1)

time: 180 us -> 189 us (1.050)
  blocking collectives: 27.6 us -> 0 us
  starting transfers between devices: 34.6 us -> 53.1 us
  waiting for transfers between devices: 34.1 us -> 50.8 us
  Pallas kernels: 48.8 us -> 59.4 us
  local copies, waits for them, and re-layouts: 20.7 us -> 10.6 us
    ppermute x4 -> x19, starting transfers between devices: 1.09 us -> 29.8 us  [the longest x6 11.5 us: scatter(): lax.ppermute(t[k].astype(dtype), axis, shift(-k)).astype(F32)]
    all_to_all x2 -> x0, blocking collectives: 27.6 us -> none  [spread(): return lax.all_to_all(copies, axes, 0, 0, tiled=True)]
    ppermute x4 -> x19, waiting for transfers between devices: 1.55 us -> 24.2 us  [the longest x6 16.4 us: scatter(): lax.ppermute(t[k].astype(dtype), axis, shift(-k)).astype(F32)]
    pallas_call x2 -> x5, Pallas kernels: 9.93 us -> 20.9 us  [the longest x2 11.4 us: weight_part(): pl.pallas_call(functools.partial(weight_kernel, steps, first), in_specs=[...]
    all_to_all x3 -> x1, starting transfers between devices: 14.6 us -> 4.51 us  [per_device(): lax.all_to_all(qg, SEQ, 0, 0, tiled=True).reshape(N_SEQ * slots, 2 * half)]
    unnamed x30 -> x26, local copies, waits for them, and re-layouts: 14.2 us -> 5.95 us
    all_to_all x3 -> x1, waiting for transfers between devices: 5.91 us -> 0.01 us  [per_device(): lax.all_to_all(qg, SEQ, 0, 0, tiled=True).reshape(N_SEQ * slots, 2 * half)]
    ppermute x3, waiting for transfers between devices: 13.8 us -> 8.64 us  [per_device(): line = line + lax.ppermute(piece, 'x', shift(-k)).astype(F32)]
  transfers between devices with their start and end apart: 20 -> 33, of which waited for: 10 -> 17; matrix products, arithmetic and copies ran while one was open for 8% -> 7% of each run, Pallas kernels for 16% -> 18%
where the time goes in v5:
time: 189 us
  Pallas kernels  59.4 us (31%)
  starting transfers between devices  53.1 us (28%)
  waiting for transfers between devices  50.8 us (27%)
  local copies, waits for them, and re-layouts  10.6 us (6%)
  other arithmetic  6.67 us (4%)
  matrix products  6.4 us (3%)
    pallas_call x2, Pallas kernels, backward(): pl.pallas_call(functools.partial(second_pass, coef, scale, last), grid=(s...  25.1 us
    ppermute x6, waiting for transfers between devices, scatter(): lax.ppermute(t[k].astype(dtype), axis, shift(-k)).astype(F32)  16.4 us
    pallas_call x2, Pallas kernels, forward(): pl.pallas_call(functools.partial(first_pass, coef, carried, last), grid=(...  13.4 us
    ppermute x3, waiting for transfers between devices, per_device(): nears = [block] + [lax.ppermute(block, 'x', shift(k)) for k in range(1, NX)]  13 us
    ppermute x6, starting transfers between devices, scatter(): lax.ppermute(t[k].astype(dtype), axis, shift(-k)).astype(F32)  11.5 us
    pallas_call x2, Pallas kernels, weight_part(): pl.pallas_call(functools.partial(weight_kernel, steps, first), in_specs=[...  11.4 us
    ppermute x6, starting transfers between devices, gather(): run = [t] + [lax.ppermute(t, axis, shift(k)) for k in range(1, 4)]  11.4 us
    pallas_call x3, Pallas kernels, project(): pl.pallas_call(functools.partial(project_kernel, steps, prev is None, las...  9.54 us
  transfers between devices with their start and end apart: 33, of which 17 were waited for; matrix products, arithmetic and copies ran while one was open for 7% of the time, Pallas kernels for 18%

profile of v5, /device:TPU:0, one launch (start us, length us, event | category | flops | bytes accessed | tf_op | source)
XLA Modules:
  0.0 188.8 jit_solution(17761613252464479491)
XLA Ops:
  0.6 3.2 %collective-permute-start = (bf16[40,256]{1,0:T(8,128)(2,1)}, bf16[40,256]{1,0:T(8,128)(2,1)S(1)}, u32[]{:S(2)}, u32[]{:S(2)}) collective-permute-start(bf16[40,256]{1,0:T(8,128)(2,1)} %param.11), channel_id=1, source_target_pairs={{2,0},{4,2},{6,4},{0,6},{3,1},{5,3},{7,5},{1,7},{10,8},{12,10},{14... | collective-permute-start | bytes 61448 | tf_op jit(solution)/shard_map/ppermute | solution.py:255
  10.1 4.1 %collective-permute-start.3 = (bf16[4,40,256]{2,1,0:T(8,128)(2,1)S(1)}, bf16[4,40,256]{2,1,0:T(8,128)(2,1)S(1)}, u32[]{:S(2)}, u32[]{:S(2)}) collective-permute-start(bf16[4,40,256]{2,1,0:T(8,128)(2,1)S(1)} %get-tuple-element.47), channel_id=1, source_target_pairs={{1,0},{16,1},{17,16},{0,17},{3,2},{18,3},{19,18},{2,19},{5,4},{20,... | collective-permute-start | bytes 245768 | tf_op jit(solution)/shard_map/ppermute | solution.py:255
  16.7 4.3 %collective-permute-done.4 = bf16[4,40,256]{2,1,0:T(8,128)(2,1)S(1)} collective-permute-done((bf16[4,40,256]{2,1,0:T(8,128)(2,1)S(1)}, bf16[4,40,256]{2,1,0:T(8,128)(2,1)S(1)}, u32[]{:S(2)}, u32[]{:S(2)}) %collective-permute-start.4) | collective-permute-done | bytes 81952 | tf_op jit(solution)/shard_map/ppermute | solution.py:255
  24.7 4.5 %all-to-all-start = ((bf16[8,128,1024]{2,1,0:T(8,128)(2,1)}), bf16[8,128,1024]{2,1,0:T(8,128)(2,1)}, u32[]{:S(2)}, u32[]{:S(2)}) async-start(bf16[8,128,1024]{2,1,0:T(8,128)(2,1)} %bitcast.135), calls=%async_computation | async-start | bytes 4194304 | tf_op jit(solution)/shard_map/all_to_all | solution.py:272
  30.7 2.7 %collective-permute-start.8 = (bf16[2,320,256]{2,1,0:T(8,128)(2,1)S(1)}, bf16[2,320,256]{2,1,0:T(8,128)(2,1)S(1)}, u32[]{:S(2)}, u32[]{:S(2)}) collective-permute-start(bf16[2,320,256]{2,1,0:T(8,128)(2,1)S(1)} %bitcast.131), channel_id=1, source_target_pairs={{64,0},{96,32},{0,64},{32,96},{65,1},{97,33},{1,65},{33,97},{66,2}... | collective-permute-start | bytes 983048 | tf_op jit(solution)/shard_map/ppermute | solution.py:269
  34.9 5.2 %collective-permute-done.11.refs_0_ = bf16[2,320,256]{2,1,0:T(8,128)(2,1)S(1)} collective-permute-done((bf16[2,320,256]{2,1,0:T(8,128)(2,1)S(1)}, bf16[2,320,256]{2,1,0:T(8,128)(2,1)S(1)}, u32[]{:S(2)}, u32[]{:S(2)}) %collective-permute-start.11) | collective-permute-done | bytes 327712 | tf_op jit(solution)/shard_map/ppermute | solution.py:269
  40.3 7.8 %collective-permute-done.8.refs_1_ = bf16[2,320,256]{2,1,0:T(8,128)(2,1)S(1)} collective-permute-done((bf16[2,320,256]{2,1,0:T(8,128)(2,1)S(1)}, bf16[2,320,256]{2,1,0:T(8,128)(2,1)S(1)}, u32[]{:S(2)}, u32[]{:S(2)}) %collective-permute-start.8) | collective-permute-done | bytes 327712 | tf_op jit(solution)/shard_map/ppermute | solution.py:269
  48.8 4.0 %copy-done = bf16[1,1024,5120]{2,1,0:T(8,128)(2,1)S(1)} copy-done((bf16[1,1024,5120]{2,1,0:T(8,128)(2,1)S(1)}, bf16[1,1024,5120]{2,1,0:T(8,128)(2,1)}, u32[]{:S(2)}) %copy-start) | copy-done | bytes 10485784
  57.3 5.1 %project_last.1.kv_ref = bf16[1152,256]{1,0:T(8,128)(2,1)S(1)} custom-call(s32[2]{0:T(128)S(1)} %pad_add_fusion.place_ref, bf16[1024,5120]{1,0:T(8,128)(2,1)S(1)} %bitcast.119, bf16[128,5120]{1,0:T(8,128)(2,1)S(1)} %bitcast.126, bf16[2,320,256]{2,1,0:T(8,128)(2,1)S(1)} %collective-permute-done.7.refs_0_, ...), custom_call_target="tpu_custom_call" | custom-call | flops 1509949440 | bytes 5898240 | tf_op jit(solution)/shard_map/project_last/pallas_call | solution.py:278
  64.8 3.2 %fusion.3.q_ref.refs_2_.g_ref = bf16[640,1024]{1,0:T(8,128)(2,1)S(1)} fusion(bf16[1024,1024]{1,0:T(8,128)(2,1)} %bitcast.18, s32[640]{0:T(1024)S(1)} %get-tuple-element.66), kind=kOutput, calls=%fused_computation.4 | convolution fusion | flops 1343488000 | bytes 3410432 | tf_op jit(solution)/shard_map/dot_general | solution.py:356
  68.0 6.5 %attend_own.1 = (f32[128,2560]{1,0:T(8,128)S(1)}, f32[3,2560]{1,0:T(4,128)S(1)}) custom-call(s32[1]{0:T(128)S(6)} %sub.51.valid_ref, s32[8,640]{1,0:T(8,128)S(1)} %broadcast_in_dim.69.limit_ref, bf16[640,1024]{1,0:T(8,128)(2,1)S(1)} %fusion.3.q_ref.refs_2_.g_ref, bf16[1152,256]{1,0:T(8,128)(2,1)S(1)} %project_last.1.kv_ref), custom_call_target="tpu_custom_call" | custom-call | flops 1509949440 | bytes 4194304 | tf_op jit(solution)/shard_map/attend_own/pallas_call | solution.py:337
  74.5 3.3 %collective-permute-done.13.kv_ref = bf16[1152,256]{1,0:T(8,128)(2,1)S(1)} collective-permute-done((bf16[1152,256]{1,0:T(8,128)(2,1)S(1)}, bf16[1152,256]{1,0:T(8,128)(2,1)S(1)}, u32[]{:S(2)}, u32[]{:S(2)}) %collective-permute-start.13) | collective-permute-done | bytes 589856 | tf_op jit(solution)/shard_map/ppermute | solution.py:303
  77.9 6.9 %attend_more.1 = (f32[128,2560]{1,0:T(8,128)S(1)}, f32[3,2560]{1,0:T(4,128)S(1)}) custom-call(s32[1]{0:T(128)S(6)} %sub.57.valid_ref, s32[8,640]{1,0:T(8,128)S(1)} %broadcast_in_dim.68.limit_ref, bf16[640,1024]{1,0:T(8,128)(2,1)S(1)} %fusion.3.q_ref.refs_2_.g_ref, bf16[1152,256]{1,0:T(8,128)(2,1)S(1)} %collective-permute-done.13.kv_ref, ...), custom_call_target="tpu_custom_call" | custom-call | flops 1509949440 | bytes 4194304 | tf_op jit(solution)/shard_map/attend_more/pallas_call | solution.py:337
  86.6 3.0 %collective-permute-start.15 = (f32[3,2560]{1,0:T(4,128)S(1)}, f32[3,2560]{1,0:T(4,128)S(1)}, u32[]{:S(2)}, u32[]{:S(2)}) collective-permute-start(f32[3,2560]{1,0:T(4,128)S(1)} %get-tuple-element.30.refs_0_), channel_id=1, source_target_pairs={{4,0},{6,2},{0,4},{2,6},{5,1},{7,3},{1,5},{3,7},{12,8},{14,10},{8,... | collective-permute-start | bytes 92168 | tf_op jit(solution)/shard_map/ppermute | solution.py:359
  93.7 12.4 %grads_other.1 = (f32[640,512]{1,0:T(8,128)S(1)}, bf16[1152,256]{1,0:T(8,128)(2,1)S(1)}) custom-call(s32[1]{0:T(128)S(6)} %sub.57.valid_ref, s32[640,128]{1,0:T(8,128)S(1)} %broadcast_in_dim.70.limit_ref, bf16[640,1024]{1,0:T(8,128)(2,1)S(1)} %fusion.3.q_ref.refs_2_.g_ref, bf16[640,1024]{1,0:T(8,128)(2,1)S(1)} %fusion.3.q_ref.refs_2_.g_ref, ...), custom_call_target="tpu_custom_call" | custom-call | flops 3774873600 | bytes 8388608 | tf_op jit(solution)/shard_map/grads_other/pallas_call | solution.py:363
  107.6 12.7 %grads_own.1 = (bf16[640,1024]{1,0:T(8,128)(2,1)S(1)}, f32[1152,256]{1,0:T(8,128)S(1)}) custom-call(s32[1]{0:T(128)S(6)} %sub.51.valid_ref, s32[640,128]{1,0:T(8,128)S(1)} %broadcast_in_dim.66.limit_ref, bf16[640,1024]{1,0:T(8,128)(2,1)S(1)} %fusion.3.q_ref.refs_2_.g_ref, bf16[640,1024]{1,0:T(8,128)(2,1)S(1)} %fusion.3.q_ref.refs_2_.g_ref, ...), custom_call_target="tpu_custom_call" | custom-call | flops 3774873600 | bytes 8388608 | tf_op jit(solution)/shard_map/grads_own/pallas_call | solution.py:363
  120.3 3.3 %fusion.2 = bf16[1024,1024]{1,0:T(8,128)(2,1)} fusion(bf16[640,1024]{1,0:T(8,128)(2,1)S(1)} %get-tuple-element.33, s32[640]{0:T(1024)S(1)} %get-tuple-element.66), kind=kOutput, calls=%fused_computation.3 | convolution fusion | flops 1343881216 | bytes 3410432 | tf_op jit(solution)/shard_map/dot_general | solution.py:391
  123.6 5.7 %weight_near.1 = (bf16[1024,256]{1,0:T(8,128)(2,1)}, bf16[128,256]{1,0:T(8,128)(2,1)S(1)}, f32[2,2,320,256]{3,2,1,0:T(8,128)S(1)}, bf16[2,2,320,256]{3,2,1,0:T(8,128)(2,1)S(1)}) custom-call(s32[2]{0:T(128)S(1)} %pad_add_fusion.place_ref, bf16[1024,5120]{1,0:T(8,128)(2,1)S(1)} %bitcast.122, bf16[128,5120]{1,0:T(8,128)(2,1)S(1)} %bitcast.127, ...), custom_call_target="tpu_custom_call" | custom-call | flops 1509949440 | bytes 5898240 | tf_op jit(solution)/shard_map/weight_near/pallas_call | solution.py:408
  130.4 5.7 %weight_far.1 = (f32[2,2,320,256]{3,2,1,0:T(8,128)S(1)}, bf16[2,2,320,256]{3,2,1,0:T(8,128)(2,1)S(1)}) custom-call(s32[2]{0:T(128)S(1)} %pad_add_fusion.place_ref, bf16[1024,5120]{1,0:T(8,128)(2,1)S(1)} %bitcast.123, bf16[128,5120]{1,0:T(8,128)(2,1)S(1)} %bitcast.128, bf16[1024,256]{1,0:T(8,128)(2,1)S(1)} %copy-done.2, ...), custom_call_target="tpu_custom_call" | custom-call | flops 1509949440 | bytes 5898240 | tf_op jit(solution)/shard_map/weight_far/pallas_call | solution.py:408
  142.7 4.4 %all-to-all-start.1 = ((bf16[8,128,1024]{2,1,0:T(8,128)(2,1)}), bf16[8,128,1024]{2,1,0:T(8,128)(2,1)}, u32[]{:S(2)}, u32[]{:S(2)}) async-start(bf16[8,128,1024]{2,1,0:T(8,128)(2,1)} %bitcast.139), calls=%async_computation.1 | async-start | bytes 4194304 | tf_op jit(solution)/shard_map/all_to_all | solution.py:393
  148.5 6.0 %collective-permute-done.22 = bf16[2,320,256]{2,1,0:T(8,128)(2,1)S(1)} collective-permute-done((bf16[2,320,256]{2,1,0:T(8,128)(2,1)S(1)}, bf16[2,320,256]{2,1,0:T(8,128)(2,1)S(1)}, u32[]{:S(2)}, u32[]{:S(2)}) %collective-permute-start.22) | collective-permute-done | bytes 327712 | tf_op jit(solution)/shard_map/ppermute | solution.py:434
  162.8 8.7 %collective-permute-done.25 = bf16[4,40,256]{2,1,0:T(8,128)(2,1)S(1)} collective-permute-done((bf16[4,40,256]{2,1,0:T(8,128)(2,1)S(1)}, bf16[4,40,256]{2,1,0:T(8,128)(2,1)S(1)}, u32[]{:S(2)}, u32[]{:S(2)}) %collective-permute-start.25) | collective-permute-done | bytes 81952 | tf_op jit(solution)/shard_map/ppermute | solution.py:440
  173.9 3.0 %collective-permute-done.26 = bf16[4,40,256]{2,1,0:T(8,128)(2,1)S(1)} collective-permute-done((bf16[4,40,256]{2,1,0:T(8,128)(2,1)S(1)}, bf16[4,40,256]{2,1,0:T(8,128)(2,1)S(1)}, u32[]{:S(2)}, u32[]{:S(2)}) %collective-permute-start.26) | collective-permute-done | bytes 81952 | tf_op jit(solution)/shard_map/ppermute | solution.py:440
  178.5 2.7 %collective-permute-start.29 = (f32[40,256]{1,0:T(8,128)S(1)}, f32[40,256]{1,0:T(8,128)S(1)}, u32[]{:S(2)}, u32[]{:S(2)}) collective-permute-start(f32[40,256]{1,0:T(8,128)S(1)} %get-tuple-element.62), channel_id=1, source_target_pairs={{4,0},{6,2},{0,4},{2,6},{5,1},{7,3},{1,5},{3,7},{12,8},{14,10},{8,... | collective-permute-start | bytes 122888 | tf_op jit(solution)/shard_map/ppermute | solution.py:440
  (115 shorter events, 58.8 us)
Async XLA Ops:
  0.6 8.5 %collective-permute-start = (bf16[40,256]{1,0:T(8,128)(2,1)}, bf16[40,256]{1,0:T(8,128)(2,1)S(1)}, u32[]{:S(2)}, u32[]{:S(2)}) collective-permute-start(bf16[40,256]{1,0:T(8,128)(2,1)} %param.11), channel_id=1, source_target_pairs={{2,0},{4,2},{6,4},{0,6},{3,1},{5,3},{7,5},{1,7},{10,8},{12,10},{14... | collective-permute-start | bytes 61448 | tf_op jit(solution)/shard_map/ppermute | solution.py:255
  10.1 6.6 %collective-permute-start.3 = (bf16[4,40,256]{2,1,0:T(8,128)(2,1)S(1)}, bf16[4,40,256]{2,1,0:T(8,128)(2,1)S(1)}, u32[]{:S(2)}, u32[]{:S(2)}) collective-permute-start(bf16[4,40,256]{2,1,0:T(8,128)(2,1)S(1)} %get-tuple-element.47), channel_id=1, source_target_pairs={{1,0},{16,1},{17,16},{0,17},{3,2},{18,3},{19,18},{2,19},{5,4},{20,... | collective-permute-start | bytes 245768 | tf_op jit(solution)/shard_map/ppermute | solution.py:255
  14.8 6.6 %collective-permute-start.5 = (bf16[4,40,256]{2,1,0:T(8,128)(2,1)S(1)}, bf16[4,40,256]{2,1,0:T(8,128)(2,1)S(1)}, u32[]{:S(2)}, u32[]{:S(2)}) collective-permute-start(bf16[4,40,256]{2,1,0:T(8,128)(2,1)S(1)} %get-tuple-element.47), channel_id=1, source_target_pairs={{17,0},{0,1},{1,16},{16,17},{19,2},{2,3},{3,18},{18,19},{21,4},{4,... | collective-permute-start | bytes 245768 | tf_op jit(solution)/shard_map/ppermute | solution.py:255
  14.8 6.1 %collective-permute-start.4 = (bf16[4,40,256]{2,1,0:T(8,128)(2,1)S(1)}, bf16[4,40,256]{2,1,0:T(8,128)(2,1)S(1)}, u32[]{:S(2)}, u32[]{:S(2)}) collective-permute-start(bf16[4,40,256]{2,1,0:T(8,128)(2,1)S(1)} %get-tuple-element.47), channel_id=1, source_target_pairs={{16,0},{17,1},{0,16},{1,17},{18,2},{19,3},{2,18},{3,19},{20,4},{21... | collective-permute-start | bytes 245768 | tf_op jit(solution)/shard_map/ppermute | solution.py:255
  24.7 40.1 %all-to-all-start = ((bf16[8,128,1024]{2,1,0:T(8,128)(2,1)}), bf16[8,128,1024]{2,1,0:T(8,128)(2,1)}, u32[]{:S(2)}, u32[]{:S(2)}) async-start(bf16[8,128,1024]{2,1,0:T(8,128)(2,1)} %bitcast.135), calls=%async_computation | async-start | bytes 4194304 | tf_op jit(solution)/shard_map/all_to_all | solution.py:272
  29.2 10.9 %collective-permute-start.11 = (bf16[2,320,256]{2,1,0:T(8,128)(2,1)S(1)}, bf16[2,320,256]{2,1,0:T(8,128)(2,1)S(1)}, u32[]{:S(2)}, u32[]{:S(2)}) collective-permute-start(bf16[2,320,256]{2,1,0:T(8,128)(2,1)S(1)} %bitcast.130), channel_id=1, source_target_pairs={{96,0},{0,32},{32,64},{64,96},{97,1},{1,33},{33,65},{65,97},{98,2}... | collective-permute-start | bytes 983048 | tf_op jit(solution)/shard_map/ppermute | solution.py:269
  30.7 17.4 %collective-permute-start.8 = (bf16[2,320,256]{2,1,0:T(8,128)(2,1)S(1)}, bf16[2,320,256]{2,1,0:T(8,128)(2,1)S(1)}, u32[]{:S(2)}, u32[]{:S(2)}) collective-permute-start(bf16[2,320,256]{2,1,0:T(8,128)(2,1)S(1)} %bitcast.131), channel_id=1, source_target_pairs={{64,0},{96,32},{0,64},{32,96},{65,1},{97,33},{1,65},{33,97},{66,2}... | collective-permute-start | bytes 983048 | tf_op jit(solution)/shard_map/ppermute | solution.py:269
  33.4 14.7 %collective-permute-start.7 = (bf16[2,320,256]{2,1,0:T(8,128)(2,1)S(1)}, bf16[2,320,256]{2,1,0:T(8,128)(2,1)S(1)}, u32[]{:S(2)}, u32[]{:S(2)}) collective-permute-start(bf16[2,320,256]{2,1,0:T(8,128)(2,1)S(1)} %bitcast.132), channel_id=1, source_target_pairs={{32,0},{64,32},{96,64},{0,96},{33,1},{65,33},{97,65},{1,97},{34,2}... | collective-permute-start | bytes 983048 | tf_op jit(solution)/shard_map/ppermute | solution.py:269
  40.1 14.9 %collective-permute-start.12 = (bf16[2,320,256]{2,1,0:T(8,128)(2,1)S(1)}, bf16[2,320,256]{2,1,0:T(8,128)(2,1)S(1)}, u32[]{:S(2)}, u32[]{:S(2)}) collective-permute-start(bf16[2,320,256]{2,1,0:T(8,128)(2,1)S(1)} %collective-permute-done.11.refs_0_), channel_id=1, source_target_pairs={{0,8},{8,0},{1,9},{9,1},{2,10},{10,2},{3,11},{11,3},{4,12},{12,4},... | collective-permute-start | bytes 983048 | tf_op jit(solution)/shard_map/ppermute | solution.py:270
  48.1 9.1 %collective-permute-start.10 = (bf16[2,320,256]{2,1,0:T(8,128)(2,1)S(1)}, bf16[2,320,256]{2,1,0:T(8,128)(2,1)S(1)}, u32[]{:S(2)}, u32[]{:S(2)}) collective-permute-start(bf16[2,320,256]{2,1,0:T(8,128)(2,1)S(1)} %collective-permute-done.8.refs_1_), channel_id=1, source_target_pairs={{0,8},{8,0},{1,9},{9,1},{2,10},{10,2},{3,11},{11,3},{4,12},{12,4},... | collective-permute-start | bytes 983048 | tf_op jit(solution)/shard_map/ppermute | solution.py:270
  48.1 9.1 %collective-permute-start.9 = (bf16[2,320,256]{2,1,0:T(8,128)(2,1)S(1)}, bf16[2,320,256]{2,1,0:T(8,128)(2,1)S(1)}, u32[]{:S(2)}, u32[]{:S(2)}) collective-permute-start(bf16[2,320,256]{2,1,0:T(8,128)(2,1)S(1)} %collective-permute-done.7.refs_0_), channel_id=1, source_target_pairs={{0,8},{8,0},{1,9},{9,1},{2,10},{10,2},{3,11},{11,3},{4,12},{12,4},... | collective-permute-start | bytes 983048 | tf_op jit(solution)/shard_map/ppermute | solution.py:270
  62.4 15.5 %collective-permute-start.13 = (bf16[1152,256]{1,0:T(8,128)(2,1)S(1)}, bf16[1152,256]{1,0:T(8,128)(2,1)S(1)}, u32[]{:S(2)}, u32[]{:S(2)}) collective-permute-start(bf16[1152,256]{1,0:T(8,128)(2,1)S(1)} %project_last.1.kv_ref), channel_id=1, source_target_pairs={{0,1},{1,0},{2,3},{3,2},{4,5},{5,4},{6,7},{7,6},{8,9},{9,8},{10,11... | collective-permute-start | bytes 1769480 | tf_op jit(solution)/shard_map/ppermute | solution.py:303
  106.1 17.5 %collective-permute-start.17 = (bf16[1152,256]{1,0:T(8,128)(2,1)S(1)}, bf16[1152,256]{1,0:T(8,128)(2,1)S(1)}, u32[]{:S(2)}, u32[]{:S(2)}) collective-permute-start(bf16[1152,256]{1,0:T(8,128)(2,1)S(1)} %get-tuple-element.37), channel_id=1, source_target_pairs={{0,1},{1,0},{2,3},{3,2},{4,5},{5,4},{6,7},{7,6},{8,9},{9,8},{10,11... | collective-permute-start | bytes 1769480 | tf_op jit(solution)/shard_map/ppermute | solution.py:388
  129.4 7.3 %collective-permute-start.19 = (bf16[2,320,256]{2,1,0:T(8,128)(2,1)S(1)}, bf16[2,320,256]{2,1,0:T(8,128)(2,1)S(1)}, u32[]{:S(2)}, u32[]{:S(2)}) collective-permute-start(bf16[2,320,256]{2,1,0:T(8,128)(2,1)S(1)} %get-tuple-element.52), channel_id=1, source_target_pairs={{0,8},{8,0},{1,9},{9,1},{2,10},{10,2},{3,11},{11,3},{4,12},{12,4},... | collective-permute-start | bytes 983048 | tf_op jit(solution)/shard_map/ppermute | solution.py:428
  129.5 7.2 %collective-permute-start.21 = (bf16[2,320,256]{2,1,0:T(8,128)(2,1)S(1)}, bf16[2,320,256]{2,1,0:T(8,128)(2,1)S(1)}, u32[]{:S(2)}, u32[]{:S(2)}) collective-permute-start(bf16[2,320,256]{2,1,0:T(8,128)(2,1)S(1)} %get-tuple-element.53), channel_id=1, source_target_pairs={{0,8},{8,0},{1,9},{9,1},{2,10},{10,2},{3,11},{11,3},{4,12},{12,4},... | collective-permute-start | bytes 983048 | tf_op jit(solution)/shard_map/ppermute | solution.py:428
  136.2 10.9 %collective-permute-start.18 = (bf16[2,320,256]{2,1,0:T(8,128)(2,1)S(1)}, bf16[2,320,256]{2,1,0:T(8,128)(2,1)S(1)}, u32[]{:S(2)}, u32[]{:S(2)}) collective-permute-start(bf16[2,320,256]{2,1,0:T(8,128)(2,1)S(1)} %get-tuple-element.50), channel_id=1, source_target_pairs={{0,8},{8,0},{1,9},{9,1},{2,10},{10,2},{3,11},{11,3},{4,12},{12,4},... | collective-permute-start | bytes 983048 | tf_op jit(solution)/shard_map/ppermute | solution.py:430
  136.9 11.6 %collective-permute-start.20 = (bf16[2,320,256]{2,1,0:T(8,128)(2,1)S(1)}, bf16[2,320,256]{2,1,0:T(8,128)(2,1)S(1)}, u32[]{:S(2)}, u32[]{:S(2)}) collective-permute-start(bf16[2,320,256]{2,1,0:T(8,128)(2,1)S(1)} %get-tuple-element.48), channel_id=1, source_target_pairs={{96,0},{0,32},{32,64},{64,96},{97,1},{1,33},{33,65},{65,97},{98,2}... | collective-permute-start | bytes 983048 | tf_op jit(solution)/shard_map/ppermute | solution.py:434
  138.6 15.9 %collective-permute-start.22 = (bf16[2,320,256]{2,1,0:T(8,128)(2,1)S(1)}, bf16[2,320,256]{2,1,0:T(8,128)(2,1)S(1)}, u32[]{:S(2)}, u32[]{:S(2)}) collective-permute-start(bf16[2,320,256]{2,1,0:T(8,128)(2,1)S(1)} %get-tuple-element.49), channel_id=1, source_target_pairs={{32,0},{64,32},{96,64},{0,96},{33,1},{65,33},{97,65},{1,97},{34,2}... | collective-permute-start | bytes 983048 | tf_op jit(solution)/shard_map/ppermute | solution.py:434
  141.3 14.5 %collective-permute-start.24 = (bf16[2,320,256]{2,1,0:T(8,128)(2,1)}, bf16[2,320,256]{2,1,0:T(8,128)(2,1)}, u32[]{:S(2)}, u32[]{:S(2)}) collective-permute-start(bf16[2,320,256]{2,1,0:T(8,128)(2,1)} %fusion.7), channel_id=1, source_target_pairs={{64,0},{96,32},{0,64},{32,96},{65,1},{97,33},{1,65},{33,97},{66,2}... | collective-permute-start | bytes 983048 | tf_op jit(solution)/shard_map/ppermute | solution.py:434
  142.7 43.1 %all-to-all-start.1 = ((bf16[8,128,1024]{2,1,0:T(8,128)(2,1)}), bf16[8,128,1024]{2,1,0:T(8,128)(2,1)}, u32[]{:S(2)}, u32[]{:S(2)}) async-start(bf16[8,128,1024]{2,1,0:T(8,128)(2,1)} %bitcast.139), calls=%async_computation.1 | async-start | bytes 4194304 | tf_op jit(solution)/shard_map/all_to_all | solution.py:393
  157.2 14.4 %collective-permute-start.25 = (bf16[4,40,256]{2,1,0:T(8,128)(2,1)S(1)}, bf16[4,40,256]{2,1,0:T(8,128)(2,1)S(1)}, u32[]{:S(2)}, u32[]{:S(2)}) collective-permute-start(bf16[4,40,256]{2,1,0:T(8,128)(2,1)S(1)} %get-tuple-element.58), channel_id=1, source_target_pairs={{17,0},{0,1},{1,16},{16,17},{19,2},{2,3},{3,18},{18,19},{21,4},{4,... | collective-permute-start | bytes 245768 | tf_op jit(solution)/shard_map/ppermute | solution.py:440
  158.2 15.7 %collective-permute-start.27 = (bf16[4,40,256]{2,1,0:T(8,128)(2,1)S(1)}, bf16[4,40,256]{2,1,0:T(8,128)(2,1)S(1)}, u32[]{:S(2)}, u32[]{:S(2)}) collective-permute-start(bf16[4,40,256]{2,1,0:T(8,128)(2,1)S(1)} %get-tuple-element.59), channel_id=1, source_target_pairs={{1,0},{16,1},{17,16},{0,17},{3,2},{18,3},{19,18},{2,19},{5,4},{20,... | collective-permute-start | bytes 245768 | tf_op jit(solution)/shard_map/ppermute | solution.py:440
  160.5 16.4 %collective-permute-start.26 = (bf16[4,40,256]{2,1,0:T(8,128)(2,1)S(1)}, bf16[4,40,256]{2,1,0:T(8,128)(2,1)S(1)}, u32[]{:S(2)}, u32[]{:S(2)}) collective-permute-start(bf16[4,40,256]{2,1,0:T(8,128)(2,1)S(1)} %get-tuple-element.60), channel_id=1, source_target_pairs={{16,0},{17,1},{0,16},{1,17},{18,2},{19,3},{2,18},{3,19},{20,4},{21... | collective-permute-start | bytes 245768 | tf_op jit(solution)/shard_map/ppermute | solution.py:440
  177.1 5.8 %collective-permute-start.28 = (f32[40,256]{1,0:T(8,128)S(1)}, f32[40,256]{1,0:T(8,128)S(1)}, u32[]{:S(2)}, u32[]{:S(2)}) collective-permute-start(f32[40,256]{1,0:T(8,128)S(1)} %get-tuple-element.61), channel_id=1, source_target_pairs={{6,0},{0,2},{2,4},{4,6},{7,1},{1,3},{3,5},{5,7},{14,8},{8,10},{10,... | collective-permute-start | bytes 122888 | tf_op jit(solution)/shard_map/ppermute | solution.py:440
  (16 other events, 124.8 us)

commit v6 on v5

--- a/solution.py
+++ b/solution.py
@@ -11,6 +11,7 @@
 AXES = ("x", "zh", "c", "y", "zl")
 GRP = ("x", "zh", "c")
 SEQ = ("y", "zl")
+PLANE = ("zh", "y", "zl")
 N_SEQ = 8
 NX = 4
 NY = 4
@@ -248,17 +249,8 @@
     smem = pl.BlockSpec(memory_space=pltpu.SMEM)
     vmem = pl.BlockSpec(memory_space=pltpu.VMEM)
 
-    y = lax.axis_index("y")
-    z = lax.axis_index(("zh", "zl"))
-
-    def gather(t, axis, place_of):
-        run = [t] + [lax.ppermute(t, axis, shift(k)) for k in range(1, 4)]
-        run = jnp.stack(run + run[:3], 0)
-        return lax.dynamic_slice_in_dim(run, (4 - place_of) % 4, 4, 0)
-
-    block = gather(kv_weight, "y", y)
-    block = gather(block, ("zh", "zl"), z).reshape(2, 2, NY, shard, 2 * DH)
-    block = block.transpose(0, 2, 1, 3, 4).reshape(2, 8 * shard, 2 * DH)
+    block = jnp.broadcast_to(kv_weight[None], (16,) + kv_weight.shape)
+    block = lax.all_to_all(block, PLANE, 0, 0, tiled=True).reshape(2, 8 * shard, 2 * DH)
 
     def halves(t):
         return t.reshape(slots, 2, half).transpose(1, 0, 2)
@@ -267,8 +259,7 @@
     qg = jnp.broadcast_to(qg[None], (NY, 2, slots, 2 * half)).reshape(N_SEQ, slots, 2 * half)
     qg, block = lax.optimization_barrier((qg, block))
     nears = [block] + [lax.ppermute(block, "x", shift(k)) for k in range(1, NX)]
-    fars = [lax.ppermute(piece, "c", SWAP) for piece in nears]
-    qg, fars[0] = lax.optimization_barrier((qg, fars[0]))
+    fars = [lax.ppermute(block, "c", SWAP)]
     qg_all = lax.all_to_all(qg, SEQ, 0, 0, tiled=True).reshape(N_SEQ * slots, 2 * half)
 
     hbm = pl.BlockSpec(memory_space=pltpu.HBM)
@@ -285,7 +276,7 @@
                 pltpu.VMEM((count * model // NX, 2 * DH), BF16),
                 pltpu.SemaphoreType.DMA((2 * count, 2)),
             ],
-            compiler_params=params(24),
+            compiler_params=params(54),
             cost_estimate=pl.CostEstimate(
                 flops=2 * keys * model * DH * count // 2,
                 bytes_accessed=keys * model * count // 2,
@@ -298,6 +289,8 @@
         )
 
     kv = project((0,), None, False)
+    nears[3], kv = lax.optimization_barrier((nears[3], kv))
+    fars = fars + [lax.ppermute(piece, "c", SWAP) for piece in nears[1:]]
     kv = project((3,), kv, False)
     kv = project((1, 2), kv, True)
     kv_other = lax.ppermute(kv, "zl", SWAP)
@@ -415,7 +408,7 @@
                 pltpu.VMEM((2 * count, model // NX // 2, 2 * DH), F32),
                 pltpu.SemaphoreType.DMA((2 * count, 2)),
             ],
-            compiler_params=params(32),
+            compiler_params=params(54),
             cost_estimate=pl.CostEstimate(
                 flops=2 * keys * model * DH * count // 2,
                 bytes_accessed=keys * model * count // 2,
@@ -433,16 +426,10 @@
         piece = (kept + got.astype(F32)).astype(BF16)
         line = line + lax.ppermute(piece, "x", shift(-k)).astype(F32)
 
-    def scatter(t, axis, place_of, dtype):
-        t = lax.dynamic_slice_in_dim(jnp.concatenate([t, t[:3]], 0), place_of, 4, 0)
-        total = t[0]
-        for k in range(1, 4):
-            total = total + lax.ppermute(t[k].astype(dtype), axis, shift(-k)).astype(F32)
-        return total
-
-    line = line.reshape(2, NY, 2, shard, 2 * DH).transpose(0, 2, 1, 3, 4)
-    line = scatter(line.reshape(4, NY, shard, 2 * DH), ("zh", "zl"), z, BF16)
-    weight_grad = scatter(line, "y", y, F32)
+    line = line.astype(BF16).reshape(16, shard, 2 * DH)
+    line, back = lax.optimization_barrier((line, back))
+    shares = lax.all_to_all(line, PLANE, 0, 0, tiled=True)
+    weight_grad = jnp.sum(shares.astype(F32), 0)
 
     back = jnp.sum(back.reshape(NY, 2, slots, 2 * half).astype(F32), 0).astype(BF16)
     attended = jnp.concatenate([back[0, :, :half], back[1, :, :half]], 1)

time: 189 us -> 182 us (0.963)
  Pallas kernels: 59.4 us -> 72.6 us
  starting transfers between devices: 53.1 us -> 43.7 us
  waiting for transfers between devices: 50.8 us -> 43.8 us
  other arithmetic: 6.67 us -> 4.4 us
    ppermute x16 -> x4, waiting for transfers between devices: 22.9 us -> 0.01 us  [the longest x3 0.01 us: per_device(): fars = fars + [lax.ppermute(piece, 'c', SWAP) for piece in nears[1:]]]
    ppermute x16 -> x4, starting transfers between devices: 23.4 us -> 0.67 us  [the longest x3 0.58 us: per_device(): fars = fars + [lax.ppermute(piece, 'c', SWAP) for piece in nears[1:]]]
    all_to_all x0 -> x2, waiting for transfers between devices: none -> 14.7 us  [the longest x1 7.5 us: per_device(): shares = lax.all_to_all(line, PLANE, 0, 0, tiled=True)]
    all_to_all x0 -> x2, starting transfers between devices: none -> 13.9 us  [the longest x1 8.13 us: per_device(): lax.all_to_all(block, PLANE, 0, 0, tiled=True).reshape(2, 8 * shard, 2 * DH)]
    pallas_call x3, Pallas kernels: 9.54 us -> 18.2 us  [project(): pl.pallas_call(functools.partial(project_kernel, steps, prev is None, las...]
    ppermute x3, waiting for transfers between devices: 13 us -> 7.73 us  [per_device(): nears = [block] + [lax.ppermute(block, 'x', shift(k)) for k in range(1, NX)]]
    ppermute x3, waiting for transfers between devices: 8.64 us -> 13.6 us  [per_device(): line = line + lax.ppermute(piece, 'x', shift(-k)).astype(F32)]
    pallas_call x2, Pallas kernels: 11.4 us -> 16.3 us  [weight_part(): pl.pallas_call(functools.partial(weight_kernel, steps, first), in_specs=[...]
  transfers between devices with their start and end apart: 33 -> 23, of which waited for: 17 -> 9; matrix products, arithmetic and copies ran while one was open for 7% -> 7% of each run, Pallas kernels for 18% -> 29%
where the time goes in v6:
time: 182 us; the launch traced here: 181 us
  Pallas kernels  72.6 us (40%)
  waiting for transfers between devices  43.8 us (24%)
  starting transfers between devices  43.7 us (24%)
  local copies, waits for them, and re-layouts  10.3 us (6%)
  matrix products  4.83 us (3%)
  other arithmetic  4.4 us (2%)
    pallas_call x2, Pallas kernels, backward(): pl.pallas_call(functools.partial(second_pass, coef, scale, last), grid=(s...  25 us
    pallas_call x3, Pallas kernels, project(): pl.pallas_call(functools.partial(project_kernel, steps, prev is None, las...  18.2 us
    pallas_call x2, Pallas kernels, weight_part(): pl.pallas_call(functools.partial(weight_kernel, steps, first), in_specs=[...  16.3 us
    ppermute x3, waiting for transfers between devices, per_device(): line = line + lax.ppermute(piece, 'x', shift(-k)).astype(F32)  13.6 us
    pallas_call x2, Pallas kernels, forward(): pl.pallas_call(functools.partial(first_pass, coef, carried, last), grid=(...  13.1 us
    all_to_all x1, starting transfers between devices, per_device(): lax.all_to_all(block, PLANE, 0, 0, tiled=True).reshape(2, 8 * shard, 2 * DH)  8.13 us
    ppermute x3, waiting for transfers between devices, per_device(): nears = [block] + [lax.ppermute(block, 'x', shift(k)) for k in range(1, NX)]  7.73 us
    all_to_all x1, waiting for transfers between devices, per_device(): shares = lax.all_to_all(line, PLANE, 0, 0, tiled=True)  7.5 us
  transfers between devices with their start and end apart: 23, of which 9 were waited for; matrix products, arithmetic and copies ran while one was open for 7% of the time, Pallas kernels for 29%

profile of v6, /device:TPU:0, one launch (start us, length us, event | category | flops | bytes accessed | tf_op | source)
XLA Modules:
  0.0 181.3 jit_solution(15638104984314294062)
XLA Ops:
  2.2 8.1 %all-to-all-start = ((bf16[16,40,256]{2,1,0:T(8,128)(2,1)}), bf16[16,40,256]{2,1,0:T(8,128)(2,1)S(1)}, u32[]{:S(2)}, u32[]{:S(2)}) async-start(bf16[16,40,256]{2,1,0:T(8,128)(2,1)} %broadcast_in_dim.74), calls=%async_computation | async-start | bytes 655360 | tf_op jit(solution)/shard_map/all_to_all | solution.py:253
  12.2 7.2 %all-to-all-done = bf16[16,40,256]{2,1,0:T(8,128)(2,1)S(1)} async-done(((bf16[16,40,256]{2,1,0:T(8,128)(2,1)}), bf16[16,40,256]{2,1,0:T(8,128)(2,1)S(1)}, u32[]{:S(2)}, u32[]{:S(2)}) %all-to-all-start) | async-done | bytes 327712 | tf_op jit(solution)/shard_map/all_to_all | solution.py:253
  21.1 3.7 %all-to-all-start.1 = ((bf16[8,128,1024]{2,1,0:T(8,128)(2,1)}), bf16[8,128,1024]{2,1,0:T(8,128)(2,1)S(1)}, u32[]{:S(2)}, u32[]{:S(2)}) async-start(bf16[8,128,1024]{2,1,0:T(8,128)(2,1)} %bitcast.10), calls=%async_computation.1 | async-start | bytes 4194304 | tf_op jit(solution)/shard_map/all_to_all | solution.py:263
  26.5 2.7 %collective-permute-start.1 = (bf16[2,320,256]{2,1,0:T(8,128)(2,1)S(1)}, bf16[2,320,256]{2,1,0:T(8,128)(2,1)S(1)}, u32[]{:S(2)}, u32[]{:S(2)}) collective-permute-start(bf16[2,320,256]{2,1,0:T(8,128)(2,1)S(1)} %bitcast.78), channel_id=1, source_target_pairs={{64,0},{96,32},{0,64},{32,96},{65,1},{97,33},{1,65},{33,97},{66,2}... | collective-permute-start | bytes 983048 | tf_op jit(solution)/shard_map/ppermute | solution.py:261
  31.4 5.0 %project.2.refs_2_ = f32[1152,256]{1,0:T(8,128)} custom-call(s32[2]{0:T(128)} %pad_add_fusion.place_ref, bf16[1024,5120]{1,0:T(8,128)(2,1)} %bitcast.63, bf16[128,5120]{1,0:T(8,128)(2,1)} %bitcast.68, bf16[2,320,256]{2,1,0:T(8,128)(2,1)} %bitcast.80, bf16[2,320,256]{2,1,0:T(8,128)(2,1)} %collective-permute-done.5.refs_1_), custom_call_target="tpu_custom_call" | custom-call | flops 754974720 | bytes 2949120 | tf_op jit(solution)/shard_map/project/pallas_call | solution.py:269
  36.5 7.7 %collective-permute-done.1.refs_1_ = bf16[2,320,256]{2,1,0:T(8,128)(2,1)S(1)} collective-permute-done((bf16[2,320,256]{2,1,0:T(8,128)(2,1)S(1)}, bf16[2,320,256]{2,1,0:T(8,128)(2,1)S(1)}, u32[]{:S(2)}, u32[]{:S(2)}) %collective-permute-start.1) | collective-permute-done | bytes 327712 | tf_op jit(solution)/shard_map/ppermute | solution.py:261
  45.6 5.4 %project.3.refs_4_ = f32[1152,256]{1,0:T(8,128)} custom-call(s32[2]{0:T(128)} %pad_add_fusion.place_ref, bf16[1024,5120]{1,0:T(8,128)(2,1)} %bitcast.64, bf16[128,5120]{1,0:T(8,128)(2,1)} %bitcast.69, bf16[2,320,256]{2,1,0:T(8,128)(2,1)} %copy-done.8, bf16[2,320,256]{2,1,0:T(8,128)(2,1)} %copy-done.10, f32[1152,256]{1,0:T(8,128)} %project.2.refs_2_), custom_call_target="tpu_custom_call" | custom-call | flops 754974720 | bytes 2949120 | tf_op jit(solution)/shard_map/project/pallas_call | solution.py:269
  52.6 7.8 %project_last.1.kv_ref = bf16[1152,256]{1,0:T(8,128)(2,1)} custom-call(s32[2]{0:T(128)} %pad_add_fusion.place_ref, bf16[1024,5120]{1,0:T(8,128)(2,1)} %bitcast.65, bf16[128,5120]{1,0:T(8,128)(2,1)} %bitcast.70, bf16[2,320,256]{2,1,0:T(8,128)(2,1)} %copy-done.7, bf16[2,320,256]{2,1,0:T(8,128)(2,1)} %copy-done.6, bf16[2,320,256]{2,1,0:T(8,128)(2,1)} %copy-done.11, ...), custom_call_target="tpu_custom_call" | custom-call | flops 1509949440 | bytes 5898240 | tf_op jit(solution)/shard_map/project_last/pallas_call | solution.py:269
  60.4 2.1 %collective-permute-start.7 = (bf16[1152,256]{1,0:T(8,128)(2,1)}, bf16[1152,256]{1,0:T(8,128)(2,1)S(1)}, u32[]{:S(2)}, u32[]{:S(2)}) collective-permute-start(bf16[1152,256]{1,0:T(8,128)(2,1)} %project_last.1.kv_ref), channel_id=1, source_target_pairs={{0,1},{1,0},{2,3},{3,2},{4,5},{5,4},{6,7},{7,6},{8,9},{9,8},{10,11... | collective-permute-start | bytes 1769480 | tf_op jit(solution)/shard_map/ppermute | solution.py:296
  64.7 6.3 %attend_own.1 = (f32[128,2560]{1,0:T(8,128)S(1)}, f32[3,2560]{1,0:T(4,128)S(1)}) custom-call(s32[1]{0:T(128)S(6)} %sub.45.valid_ref, s32[8,640]{1,0:T(8,128)S(1)} %broadcast_in_dim.76.limit_ref, bf16[640,1024]{1,0:T(8,128)(2,1)S(1)} %fusion.3.q_ref.refs_2_.g_ref, bf16[1152,256]{1,0:T(8,128)(2,1)S(1)} %copy-done.1), custom_call_target="tpu_custom_call" | custom-call | flops 1509949440 | bytes 4194304 | tf_op jit(solution)/shard_map/attend_own/pallas_call | solution.py:330
  71.1 5.2 %collective-permute-done.7.kv_ref = bf16[1152,256]{1,0:T(8,128)(2,1)S(1)} collective-permute-done((bf16[1152,256]{1,0:T(8,128)(2,1)}, bf16[1152,256]{1,0:T(8,128)(2,1)S(1)}, u32[]{:S(2)}, u32[]{:S(2)}) %collective-permute-start.7) | collective-permute-done | bytes 589856 | tf_op jit(solution)/shard_map/ppermute | solution.py:296
  76.2 6.8 %attend_more.1 = (f32[128,2560]{1,0:T(8,128)S(1)}, f32[3,2560]{1,0:T(4,128)S(1)}) custom-call(s32[1]{0:T(128)S(6)} %sub.49.valid_ref, s32[8,640]{1,0:T(8,128)S(1)} %broadcast_in_dim.75.limit_ref, bf16[640,1024]{1,0:T(8,128)(2,1)S(1)} %fusion.3.q_ref.refs_2_.g_ref, bf16[1152,256]{1,0:T(8,128)(2,1)S(1)} %collective-permute-done.7.kv_ref, ...), custom_call_target="tpu_custom_call" | custom-call | flops 1509949440 | bytes 4194304 | tf_op jit(solution)/shard_map/attend_more/pallas_call | solution.py:330
  84.8 2.7 %collective-permute-start.9 = (f32[3,2560]{1,0:T(4,128)S(1)}, f32[3,2560]{1,0:T(4,128)S(1)}, u32[]{:S(2)}, u32[]{:S(2)}) collective-permute-start(f32[3,2560]{1,0:T(4,128)S(1)} %get-tuple-element.32.refs_0_), channel_id=1, source_target_pairs={{4,0},{6,2},{0,4},{2,6},{5,1},{7,3},{1,5},{3,7},{12,8},{14,10},{8,... | collective-permute-start | bytes 92168 | tf_op jit(solution)/shard_map/ppermute | solution.py:352
  91.7 12.4 %grads_other.1 = (f32[640,512]{1,0:T(8,128)S(1)}, bf16[1152,256]{1,0:T(8,128)(2,1)S(1)}) custom-call(s32[1]{0:T(128)S(6)} %sub.49.valid_ref, s32[640,128]{1,0:T(8,128)S(1)} %broadcast_in_dim.77.limit_ref, bf16[640,1024]{1,0:T(8,128)(2,1)S(1)} %fusion.3.q_ref.refs_2_.g_ref, bf16[640,1024]{1,0:T(8,128)(2,1)S(1)} %fusion.3.q_ref.refs_2_.g_ref, ...), custom_call_target="tpu_custom_call" | custom-call | flops 3774873600 | bytes 8388608 | tf_op jit(solution)/shard_map/grads_other/pallas_call | solution.py:356
  106.0 12.6 %grads_own.1 = (bf16[640,1024]{1,0:T(8,128)(2,1)S(1)}, f32[1152,256]{1,0:T(8,128)S(1)}) custom-call(s32[1]{0:T(128)S(6)} %sub.45.valid_ref, s32[640,128]{1,0:T(8,128)S(1)} %broadcast_in_dim.72.limit_ref, bf16[640,1024]{1,0:T(8,128)(2,1)S(1)} %fusion.3.q_ref.refs_2_.g_ref, bf16[640,1024]{1,0:T(8,128)(2,1)S(1)} %fusion.3.q_ref.refs_2_.g_ref, ...), custom_call_target="tpu_custom_call" | custom-call | flops 3774873600 | bytes 8388608 | tf_op jit(solution)/shard_map/grads_own/pallas_call | solution.py:356
  118.6 3.3 %fusion.2 = bf16[1024,1024]{1,0:T(8,128)(2,1)} fusion(bf16[640,1024]{1,0:T(8,128)(2,1)S(1)} %get-tuple-element.35, s32[640]{0:T(1024)S(1)} %get-tuple-element.60), kind=kOutput, calls=%fused_computation.3 | convolution fusion | flops 1343881216 | bytes 3410432 | tf_op jit(solution)/shard_map/dot_general | solution.py:384
  121.9 3.9 %all-to-all-start.2 = ((bf16[8,128,1024]{2,1,0:T(8,128)(2,1)}), bf16[8,128,1024]{2,1,0:T(8,128)(2,1)S(1)}, u32[]{:S(2)}, u32[]{:S(2)}) async-start(bf16[8,128,1024]{2,1,0:T(8,128)(2,1)} %bitcast.75), calls=%async_computation.2 | async-start | bytes 4194304 | tf_op jit(solution)/shard_map/all_to_all | solution.py:386
  126.7 8.3 %weight_near.1 = (bf16[1024,256]{1,0:T(8,128)(2,1)}, bf16[128,256]{1,0:T(8,128)(2,1)}, f32[2,2,320,256]{3,2,1,0:T(8,128)}, bf16[2,2,320,256]{3,2,1,0:T(8,128)(2,1)}) custom-call(s32[2]{0:T(128)} %pad_add_fusion.place_ref, bf16[1024,5120]{1,0:T(8,128)(2,1)} %bitcast.66, bf16[128,5120]{1,0:T(8,128)(2,1)} %bitcast.71, f32[1152,256]{1,0:T(8,128)} %copy-done, ...), custom_call_target="tpu_custom_call" | custom-call | flops 1509949440 | bytes 5898240 | tf_op jit(solution)/shard_map/weight_near/pallas_call | solution.py:401
  136.7 8.0 %weight_far.1 = (f32[2,2,320,256]{3,2,1,0:T(8,128)}, bf16[2,2,320,256]{3,2,1,0:T(8,128)(2,1)}) custom-call(s32[2]{0:T(128)} %pad_add_fusion.place_ref, bf16[1024,5120]{1,0:T(8,128)(2,1)} %bitcast.67, bf16[128,5120]{1,0:T(8,128)(2,1)} %bitcast.72, bf16[1024,256]{1,0:T(8,128)(2,1)} %get-tuple-element.39.refs_0_, bf16[128,256]{1,0:T(8,128)(2,1)} %get-tuple-element.40.refs_1_), custom_call_target="tpu_custom_call" | custom-call | flops 1509949440 | bytes 5898240 | tf_op jit(solution)/shard_map/weight_far/pallas_call | solution.py:401
  148.0 2.0 %collective-permute-start.16 = (bf16[2,320,256]{2,1,0:T(8,128)(2,1)S(1)}, bf16[2,320,256]{2,1,0:T(8,128)(2,1)S(1)}, u32[]{:S(2)}, u32[]{:S(2)}) collective-permute-start(bf16[2,320,256]{2,1,0:T(8,128)(2,1)S(1)} %get-tuple-element.49), channel_id=1, source_target_pairs={{32,0},{64,32},{96,64},{0,96},{33,1},{65,33},{97,65},{1,97},{34,2}... | collective-permute-start | bytes 983048 | tf_op jit(solution)/shard_map/ppermute | solution.py:427
  151.5 6.6 %collective-permute-done.14 = bf16[2,320,256]{2,1,0:T(8,128)(2,1)S(1)} collective-permute-done((bf16[2,320,256]{2,1,0:T(8,128)(2,1)S(1)}, bf16[2,320,256]{2,1,0:T(8,128)(2,1)S(1)}, u32[]{:S(2)}, u32[]{:S(2)}) %collective-permute-start.14) | collective-permute-done | bytes 327712 | tf_op jit(solution)/shard_map/ppermute | solution.py:427
  158.1 5.9 %collective-permute-done.16 = bf16[2,320,256]{2,1,0:T(8,128)(2,1)S(1)} collective-permute-done((bf16[2,320,256]{2,1,0:T(8,128)(2,1)S(1)}, bf16[2,320,256]{2,1,0:T(8,128)(2,1)S(1)}, u32[]{:S(2)}, u32[]{:S(2)}) %collective-permute-start.16) | collective-permute-done | bytes 327712 | tf_op jit(solution)/shard_map/ppermute | solution.py:427
  166.0 5.8 %all-to-all-start.3 = ((bf16[16,40,256]{2,1,0:T(8,128)(2,1)}), bf16[16,40,256]{2,1,0:T(8,128)(2,1)S(1)}, u32[]{:S(2)}, u32[]{:S(2)}) async-start(bf16[16,40,256]{2,1,0:T(8,128)(2,1)} %bitcast.22), calls=%async_computation.3 | async-start | bytes 655360 | tf_op jit(solution)/shard_map/all_to_all | solution.py:431
  173.1 7.5 %all-to-all-done.3 = bf16[16,40,256]{2,1,0:T(8,128)(2,1)S(1)} async-done(((bf16[16,40,256]{2,1,0:T(8,128)(2,1)}), bf16[16,40,256]{2,1,0:T(8,128)(2,1)S(1)}, u32[]{:S(2)}, u32[]{:S(2)}) %all-to-all-start.3) | async-done | bytes 327712 | tf_op jit(solution)/shard_map/all_to_all | solution.py:431
  (85 shorter events, 32.5 us)
Async XLA Ops:
  0.6 10.8 %copy-start.12 = (bf16[1,128,1024]{2,1,0:T(8,128)(2,1)S(1)}, bf16[1,128,1024]{2,1,0:T(8,128)(2,1)}, u32[]{:S(2)}) copy-start(bf16[1,128,1024]{2,1,0:T(8,128)(2,1)} %param.10) | copy-start | bytes 786436
  2.2 17.3 %all-to-all-start = ((bf16[16,40,256]{2,1,0:T(8,128)(2,1)}), bf16[16,40,256]{2,1,0:T(8,128)(2,1)S(1)}, u32[]{:S(2)}, u32[]{:S(2)}) async-start(bf16[16,40,256]{2,1,0:T(8,128)(2,1)} %broadcast_in_dim.74), calls=%async_computation | async-start | bytes 655360 | tf_op jit(solution)/shard_map/all_to_all | solution.py:253
  21.1 42.0 %all-to-all-start.1 = ((bf16[8,128,1024]{2,1,0:T(8,128)(2,1)}), bf16[8,128,1024]{2,1,0:T(8,128)(2,1)S(1)}, u32[]{:S(2)}, u32[]{:S(2)}) async-start(bf16[8,128,1024]{2,1,0:T(8,128)(2,1)} %bitcast.10), calls=%async_computation.1 | async-start | bytes 4194304 | tf_op jit(solution)/shard_map/all_to_all | solution.py:263
  24.8 6.6 %collective-permute-start.5 = (bf16[2,320,256]{2,1,0:T(8,128)(2,1)S(1)}, bf16[2,320,256]{2,1,0:T(8,128)(2,1)}, u32[]{:S(2)}, u32[]{:S(2)}) collective-permute-start(bf16[2,320,256]{2,1,0:T(8,128)(2,1)S(1)} %bitcast.76), channel_id=1, source_target_pairs={{0,8},{8,0},{1,9},{9,1},{2,10},{10,2},{3,11},{11,3},{4,12},{12,4},... | collective-permute-start | bytes 983048 | tf_op jit(solution)/shard_map/ppermute | solution.py:262
  24.9 11.5 %collective-permute-start.4 = (bf16[2,320,256]{2,1,0:T(8,128)(2,1)S(1)}, bf16[2,320,256]{2,1,0:T(8,128)(2,1)S(1)}, u32[]{:S(2)}, u32[]{:S(2)}) collective-permute-start(bf16[2,320,256]{2,1,0:T(8,128)(2,1)S(1)} %bitcast.77), channel_id=1, source_target_pairs={{96,0},{0,32},{32,64},{64,96},{97,1},{1,33},{33,65},{65,97},{98,2}... | collective-permute-start | bytes 983048 | tf_op jit(solution)/shard_map/ppermute | solution.py:261
  26.5 17.8 %collective-permute-start.1 = (bf16[2,320,256]{2,1,0:T(8,128)(2,1)S(1)}, bf16[2,320,256]{2,1,0:T(8,128)(2,1)S(1)}, u32[]{:S(2)}, u32[]{:S(2)}) collective-permute-start(bf16[2,320,256]{2,1,0:T(8,128)(2,1)S(1)} %bitcast.78), channel_id=1, source_target_pairs={{64,0},{96,32},{0,64},{32,96},{65,1},{97,33},{1,65},{33,97},{66,2}... | collective-permute-start | bytes 983048 | tf_op jit(solution)/shard_map/ppermute | solution.py:261
  29.2 15.1 %collective-permute-start = (bf16[2,320,256]{2,1,0:T(8,128)(2,1)S(1)}, bf16[2,320,256]{2,1,0:T(8,128)(2,1)S(1)}, u32[]{:S(2)}, u32[]{:S(2)}) collective-permute-start(bf16[2,320,256]{2,1,0:T(8,128)(2,1)S(1)} %bitcast.79), channel_id=1, source_target_pairs={{32,0},{64,32},{96,64},{0,96},{33,1},{65,33},{97,65},{1,97},{34,2}... | collective-permute-start | bytes 983048 | tf_op jit(solution)/shard_map/ppermute | solution.py:261
  36.4 8.4 %collective-permute-start.6 = (bf16[2,320,256]{2,1,0:T(8,128)(2,1)S(1)}, bf16[2,320,256]{2,1,0:T(8,128)(2,1)S(1)}, u32[]{:S(2)}, u32[]{:S(2)}) collective-permute-start(bf16[2,320,256]{2,1,0:T(8,128)(2,1)S(1)} %collective-permute-done.4.refs_0_), channel_id=1, source_target_pairs={{0,8},{8,0},{1,9},{9,1},{2,10},{10,2},{3,11},{11,3},{4,12},{12,4},... | collective-permute-start | bytes 983048 | tf_op jit(solution)/shard_map/ppermute | solution.py:293
  44.3 6.8 %collective-permute-start.3 = (bf16[2,320,256]{2,1,0:T(8,128)(2,1)S(1)}, bf16[2,320,256]{2,1,0:T(8,128)(2,1)S(1)}, u32[]{:S(2)}, u32[]{:S(2)}) collective-permute-start(bf16[2,320,256]{2,1,0:T(8,128)(2,1)S(1)} %collective-permute-done.1.refs_1_), channel_id=1, source_target_pairs={{0,8},{8,0},{1,9},{9,1},{2,10},{10,2},{3,11},{11,3},{4,12},{12,4},... | collective-permute-start | bytes 983048 | tf_op jit(solution)/shard_map/ppermute | solution.py:293
  44.3 6.8 %collective-permute-start.2 = (bf16[2,320,256]{2,1,0:T(8,128)(2,1)S(1)}, bf16[2,320,256]{2,1,0:T(8,128)(2,1)S(1)}, u32[]{:S(2)}, u32[]{:S(2)}) collective-permute-start(bf16[2,320,256]{2,1,0:T(8,128)(2,1)S(1)} %collective-permute-done.refs_0_), channel_id=1, source_target_pairs={{0,8},{8,0},{1,9},{9,1},{2,10},{10,2},{3,11},{11,3},{4,12},{12,4},... | collective-permute-start | bytes 983048 | tf_op jit(solution)/shard_map/ppermute | solution.py:293
  60.4 15.9 %collective-permute-start.7 = (bf16[1152,256]{1,0:T(8,128)(2,1)}, bf16[1152,256]{1,0:T(8,128)(2,1)S(1)}, u32[]{:S(2)}, u32[]{:S(2)}) collective-permute-start(bf16[1152,256]{1,0:T(8,128)(2,1)} %project_last.1.kv_ref), channel_id=1, source_target_pairs={{0,1},{1,0},{2,3},{3,2},{4,5},{5,4},{6,7},{7,6},{8,9},{9,8},{10,11... | collective-permute-start | bytes 1769480 | tf_op jit(solution)/shard_map/ppermute | solution.py:296
  83.0 6.0 %collective-permute-start.10 = (f32[3,2560]{1,0:T(4,128)S(1)}, f32[3,2560]{1,0:T(4,128)S(1)}, u32[]{:S(2)}, u32[]{:S(2)}) collective-permute-start(f32[3,2560]{1,0:T(4,128)S(1)} %get-tuple-element.32.refs_0_), channel_id=1, source_target_pairs={{6,0},{0,2},{2,4},{4,6},{7,1},{1,3},{3,5},{5,7},{14,8},{8,10},{10,... | collective-permute-start | bytes 92168 | tf_op jit(solution)/shard_map/ppermute | solution.py:352
  84.8 5.5 %collective-permute-start.9 = (f32[3,2560]{1,0:T(4,128)S(1)}, f32[3,2560]{1,0:T(4,128)S(1)}, u32[]{:S(2)}, u32[]{:S(2)}) collective-permute-start(f32[3,2560]{1,0:T(4,128)S(1)} %get-tuple-element.32.refs_0_), channel_id=1, source_target_pairs={{4,0},{6,2},{0,4},{2,6},{5,1},{7,3},{1,5},{3,7},{12,8},{14,10},{8,... | collective-permute-start | bytes 92168 | tf_op jit(solution)/shard_map/ppermute | solution.py:352
  87.5 4.0 %collective-permute-start.8 = (f32[3,2560]{1,0:T(4,128)S(1)}, f32[3,2560]{1,0:T(4,128)S(1)}, u32[]{:S(2)}, u32[]{:S(2)}) collective-permute-start(f32[3,2560]{1,0:T(4,128)S(1)} %get-tuple-element.32.refs_0_), channel_id=1, source_target_pairs={{2,0},{4,2},{6,4},{0,6},{3,1},{5,3},{7,5},{1,7},{10,8},{12,10},{14... | collective-permute-start | bytes 92168 | tf_op jit(solution)/shard_map/ppermute | solution.py:352
  104.1 21.8 %collective-permute-start.11 = (bf16[1152,256]{1,0:T(8,128)(2,1)S(1)}, bf16[1152,256]{1,0:T(8,128)(2,1)S(1)}, u32[]{:S(2)}, u32[]{:S(2)}) collective-permute-start(bf16[1152,256]{1,0:T(8,128)(2,1)S(1)} %get-tuple-element.38), channel_id=1, source_target_pairs={{0,1},{1,0},{2,3},{3,2},{4,5},{5,4},{6,7},{7,6},{8,9},{9,8},{10,11... | collective-permute-start | bytes 1769480 | tf_op jit(solution)/shard_map/ppermute | solution.py:381
  121.9 44.1 %all-to-all-start.2 = ((bf16[8,128,1024]{2,1,0:T(8,128)(2,1)}), bf16[8,128,1024]{2,1,0:T(8,128)(2,1)S(1)}, u32[]{:S(2)}, u32[]{:S(2)}) async-start(bf16[8,128,1024]{2,1,0:T(8,128)(2,1)} %bitcast.75), calls=%async_computation.2 | async-start | bytes 4194304 | tf_op jit(solution)/shard_map/all_to_all | solution.py:386
  136.1 10.4 %collective-permute-start.13 = (bf16[2,320,256]{2,1,0:T(8,128)(2,1)S(1)}, bf16[2,320,256]{2,1,0:T(8,128)(2,1)S(1)}, u32[]{:S(2)}, u32[]{:S(2)}) collective-permute-start(bf16[2,320,256]{2,1,0:T(8,128)(2,1)S(1)} %get-tuple-element.52), channel_id=1, source_target_pairs={{0,8},{8,0},{1,9},{9,1},{2,10},{10,2},{3,11},{11,3},{4,12},{12,4},... | collective-permute-start | bytes 983048 | tf_op jit(solution)/shard_map/ppermute | solution.py:421
  136.2 10.3 %collective-permute-start.15 = (bf16[2,320,256]{2,1,0:T(8,128)(2,1)S(1)}, bf16[2,320,256]{2,1,0:T(8,128)(2,1)S(1)}, u32[]{:S(2)}, u32[]{:S(2)}) collective-permute-start(bf16[2,320,256]{2,1,0:T(8,128)(2,1)S(1)} %get-tuple-element.53), channel_id=1, source_target_pairs={{0,8},{8,0},{1,9},{9,1},{2,10},{10,2},{3,11},{11,3},{4,12},{12,4},... | collective-permute-start | bytes 983048 | tf_op jit(solution)/shard_map/ppermute | solution.py:421
  145.9 4.1 %collective-permute-start.17 = (bf16[2,320,256]{2,1,0:T(8,128)(2,1)S(1)}, bf16[2,320,256]{2,1,0:T(8,128)(2,1)S(1)}, u32[]{:S(2)}, u32[]{:S(2)}) collective-permute-start(bf16[2,320,256]{2,1,0:T(8,128)(2,1)S(1)} %get-tuple-element.51), channel_id=1, source_target_pairs={{0,8},{8,0},{1,9},{9,1},{2,10},{10,2},{3,11},{11,3},{4,12},{12,4},... | collective-permute-start | bytes 983048 | tf_op jit(solution)/shard_map/ppermute | solution.py:423
  146.1 5.4 %collective-permute-start.12 = (bf16[2,320,256]{2,1,0:T(8,128)(2,1)S(1)}, bf16[2,320,256]{2,1,0:T(8,128)(2,1)S(1)}, u32[]{:S(2)}, u32[]{:S(2)}) collective-permute-start(bf16[2,320,256]{2,1,0:T(8,128)(2,1)S(1)} %get-tuple-element.50), channel_id=1, source_target_pairs={{0,8},{8,0},{1,9},{9,1},{2,10},{10,2},{3,11},{11,3},{4,12},{12,4},... | collective-permute-start | bytes 983048 | tf_op jit(solution)/shard_map/ppermute | solution.py:423
  146.7 11.4 %collective-permute-start.14 = (bf16[2,320,256]{2,1,0:T(8,128)(2,1)S(1)}, bf16[2,320,256]{2,1,0:T(8,128)(2,1)S(1)}, u32[]{:S(2)}, u32[]{:S(2)}) collective-permute-start(bf16[2,320,256]{2,1,0:T(8,128)(2,1)S(1)} %get-tuple-element.48), channel_id=1, source_target_pairs={{96,0},{0,32},{32,64},{64,96},{97,1},{1,33},{33,65},{65,97},{98,2}... | collective-permute-start | bytes 983048 | tf_op jit(solution)/shard_map/ppermute | solution.py:427
  148.0 16.0 %collective-permute-start.16 = (bf16[2,320,256]{2,1,0:T(8,128)(2,1)S(1)}, bf16[2,320,256]{2,1,0:T(8,128)(2,1)S(1)}, u32[]{:S(2)}, u32[]{:S(2)}) collective-permute-start(bf16[2,320,256]{2,1,0:T(8,128)(2,1)S(1)} %get-tuple-element.49), channel_id=1, source_target_pairs={{32,0},{64,32},{96,64},{0,96},{33,1},{65,33},{97,65},{1,97},{34,2}... | collective-permute-start | bytes 983048 | tf_op jit(solution)/shard_map/ppermute | solution.py:427
  150.1 15.0 %collective-permute-start.18 = (bf16[2,320,256]{2,1,0:T(8,128)(2,1)S(1)}, bf16[2,320,256]{2,1,0:T(8,128)(2,1)S(1)}, u32[]{:S(2)}, u32[]{:S(2)}) collective-permute-start(bf16[2,320,256]{2,1,0:T(8,128)(2,1)S(1)} %fusion.6), channel_id=1, source_target_pairs={{64,0},{96,32},{0,64},{32,96},{65,1},{97,33},{1,65},{33,97},{66,2}... | collective-permute-start | bytes 983048 | tf_op jit(solution)/shard_map/ppermute | solution.py:427
  166.0 14.6 %all-to-all-start.3 = ((bf16[16,40,256]{2,1,0:T(8,128)(2,1)}), bf16[16,40,256]{2,1,0:T(8,128)(2,1)S(1)}, u32[]{:S(2)}, u32[]{:S(2)}) async-start(bf16[16,40,256]{2,1,0:T(8,128)(2,1)} %bitcast.22), calls=%async_computation.3 | async-start | bytes 655360 | tf_op jit(solution)/shard_map/all_to_all | solution.py:431
  (13 other events, 54.5 us)

commit v7 on v6

v7 whole, which is shorter than its diff:
```python
import functools

import jax
import jax.numpy as jnp
from jax import lax
from jax.experimental import pallas as pl
from jax.experimental.pallas import tpu as pltpu
from jax.sharding import Mesh
from jax.sharding import PartitionSpec as P

AXES = ("x", "zh", "c", "y", "zl")
GRP = ("x", "zh", "c")
SEQ = ("y", "zl")
PLANE = ("zh", "y", "zl")
N_SEQ = 8
NX = 4
NY = 4
HEADS = 8
HALF = 4
DH = 128
SLOTS = 128
ROWS = HALF * SLOTS
NEG = -1e30
LOG2E = 1.4426950408889634
NT = (((1,), (1,)), ((), ()))
TN = (((0,), (0,)), ((), ()))
F32 = jnp.float32
BF16 = jnp.bfloat16
SWAP = [(0, 1), (1, 0)]


def params(mib):
    return pltpu.CompilerParams(vmem_limit_bytes=mib << 20)


def shift(k):
    return [((i + k) % 4, i) for i in range(4)]


def stack_heads(ref):
    return jnp.concatenate([ref[:, h * DH : (h + 1) * DH] for h in range(HALF)], 0)


def project_kernel(steps, first, last, place_ref, prompt_ref, resp_ref, *refs):
    refs = list(refs)
    nears = [refs.pop(0) for _ in steps]
    fars = [refs.pop(0) for _ in steps]
    prev_ref = None if first else refs.pop(0)
    kv_ref, weight = refs
    plen = prompt_ref.shape[0]
    wide = prompt_ref.shape[1] // NX
    half = wide // 2
    part = wide // 4
    x, core = place_ref[0], place_ref[1]
    tops, ends = [], []
    for n, k in enumerate(steps):
        for z in range(2):
            base = n * wide + z * half
            weight[pl.ds(pl.multiple_of(base + core * part, part), part)] = nears[n][z]
            weight[pl.ds(pl.multiple_of(base + (1 - core) * part, part), part)] = fars[n][z]
        cols = pl.ds(pl.multiple_of(lax.rem(x + k, NX) * wide, DH), wide)
        w = weight[n * wide : (n + 1) * wide]
        tops.append(jnp.dot(prompt_ref[:, cols], w, preferred_element_type=F32))
        ends.append(jnp.dot(resp_ref[:, cols], w, preferred_element_type=F32))
    top, end = sum(tops[1:], tops[0]), sum(ends[1:], ends[0])
    if not first:
        top, end = top + prev_ref[:plen], end + prev_ref[plen:]
    kv_ref[:plen] = top.astype(kv_ref.dtype)
    kv_ref[plen:] = end.astype(kv_ref.dtype)


def crossing(start_ref, r, block):
    start, end = start_ref[r], start_ref[r + 1]
    base = block * SLOTS
    meets = (start < base + SLOTS) & (end > base)

    def onehot(row_axis):
        row = lax.broadcasted_iota(jnp.int32, (SLOTS, SLOTS), row_axis) + base
        slot = lax.broadcasted_iota(jnp.int32, (SLOTS, SLOTS), 1 - row_axis) + start
        return jnp.where((row == slot) & (row < end), 1.0, 0.0).astype(BF16)

    return meets, onehot


def first_pass(coef, last, valid_ref, limit_ref, *refs):
    if last:
        q_ref, kv_ref, g_ref, prev_out_ref, prev_stat_ref, out_ref, stat_ref, bias, values = refs
    else:
        q_ref, kv_ref, out_ref, stat_ref, bias, values = refs
    plen = kv_ref.shape[0] - DH

    @pl.when(pl.program_id(0) == 0)
    def _():
        place = lax.broadcasted_iota(jnp.int32, (plen, DH), 0)
        bias[...] = jnp.where(place < valid_ref[0], 0.0, NEG)
        values[...] = kv_ref[:, DH:].T

    causal = jnp.where(
        lax.broadcasted_iota(jnp.int32, (DH, SLOTS), 0) <= limit_ref[0:1], 0.0, NEG
    )
    bias_all = jnp.concatenate([bias[...], causal], 0)
    bias_all = jnp.concatenate([bias_all] * 2, 1)
    keys = kv_ref[:, :DH]

    def scores(i):
        q = jnp.concatenate([q_ref[:, h * DH : (h + 1) * DH] for h in (2 * i, 2 * i + 1)], 0)
        return lax.dot_general(keys, q, NT, preferred_element_type=F32)

    following = scores(0)
    for i in range(HALF // 2):
        s = following * coef + bias_all
        if i + 1 < HALF // 2:
            following = scores(i + 1)
        lanes = slice(2 * i * SLOTS, 2 * (i + 1) * SLOTS)
        top = jnp.max(s, 0, keepdims=True)
        if last:
            before = prev_stat_ref[0:1, lanes]
            top = jnp.maximum(top, before)
        p = jnp.exp2(s - top)
        total = jnp.sum(p, 0, keepdims=True)
        o = jnp.dot(values[...], p.astype(BF16), preferred_element_type=F32)
        if last:
            alpha = jnp.exp2(before - top)
            total = total + prev_stat_ref[1:2, lanes] * alpha
            o = (o + prev_out_ref[:, lanes] * alpha) / total
            for j in range(2):
                h = 2 * i + j
                cols = slice(h * DH, (h + 1) * DH)
                part = o[:, j * SLOTS : (j + 1) * SLOTS]
                d = jnp.sum(part * g_ref[:, cols].astype(F32).T, 0, keepdims=True)
                stat_ref[2:3, h * SLOTS : (h + 1) * SLOTS] = d
                out_ref[:, cols] = part.T.astype(BF16)
        else:
            out_ref[:, lanes] = o
        stat_ref[0:1, lanes] = top
        stat_ref[1:2, lanes] = total


def second_pass(coef, scale, last, valid_ref, limit_ref, q_ref, g_ref, kv_ref, *refs):
    stat_refs, refs = refs[:NY], refs[NY:]
    if last:
        start_ref, out_ref, prev_ref, back_ref, kvgrad_ref, acc, bias = refs
    else:
        back_ref, kvgrad_ref, acc, bias = refs
    step = pl.program_id(0)
    plen = kv_ref.shape[0] - DH
    tops = [ref[0:1] for ref in stat_refs]
    top = functools.reduce(jnp.maximum, tops)
    share = [ref[1:2] * jnp.exp2(t - top) for ref, t in zip(stat_refs, tops)]
    inv = 1.0 / sum(share)
    delta = sum(w * ref[2:3] for w, ref in zip(share, stat_refs)) * inv
    row = lax.broadcasted_iota(jnp.int32, (8, ROWS), 0)
    weight = share[0] * inv
    columns = jnp.where(row == 0, top, jnp.where(row == 1, inv, jnp.where(row == 2, delta, weight)))
    columns = jnp.concatenate([columns] * 16, 0).T

    @pl.when(step == 0)
    def _():
        acc[...] = jnp.zeros_like(acc)
        place = lax.broadcasted_iota(jnp.int32, (8, plen), 1)
        bias[...] = jnp.where(place < valid_ref[0], 0.0, NEG)

    c_top, c_inv, c_delta = columns[:, 0:1], columns[:, 1:2], columns[:, 2:3]
    q = stack_heads(q_ref)
    g = stack_heads(g_ref)
    qt = q.T
    gt = g.T
    lane = lax.broadcasted_iota(jnp.int32, (SLOTS, DH), 1)
    causal = jnp.concatenate([jnp.where(lane <= limit_ref[...], 0.0, NEG)] * HALF, 0)
    chunk = 256
    cuts = [slice(i, i + chunk) for i in range(0, plen, chunk)] + [slice(plen, plen + DH)]

    def products(keys):
        s = lax.dot_general(q, kv_ref[keys, :DH], NT, preferred_element_type=F32)
        return s, lax.dot_general(g, kv_ref[keys, DH:], NT, preferred_element_type=F32)

    def weights(keys, s, dp):
        hidden = bias[0:1, keys] if keys.start < plen else causal
        p = jnp.exp2(s * coef - c_top + hidden) * c_inv
        return p.astype(BF16), (p * (dp - c_delta) * scale).astype(BF16)

    def gradients(keys, p, ds):
        acc[:DH, keys] += jnp.dot(qt, ds, preferred_element_type=F32)
        acc[DH:, keys] += jnp.dot(gt, p, preferred_element_type=F32)
        return jnp.dot(ds, kv_ref[keys, :DH], preferred_element_type=F32)

    dq = jnp.zeros((ROWS, DH), F32)
    following = products(cuts[0])
    for i, keys in enumerate(cuts):
        current = following
        if i + 1 < len(cuts):
            following = products(cuts[i + 1])
        if i:
            dq = dq + gradients(cuts[i - 1], *ready)
        ready = weights(keys, *current)
    dq = dq + gradients(cuts[-1], *ready)
    parts = [slice(h * SLOTS, (h + 1) * SLOTS) for h in range(HALF)]
    if last:
        att = [out_ref[:, r].astype(F32) * columns[r, 3:4] for r in parts]
        grad = [dq[r] + prev_ref[:, r] for r in parts]
        back = jnp.concatenate(att + grad, 1).astype(BF16)

        @pl.when(step == 0)
        def _():
            back_ref[...] = jnp.zeros_like(back_ref)

        for r in range(N_SEQ):
            meets, onehot = crossing(start_ref, r, step)

            @pl.when(meets)
            def _():
                rows = slice(r * SLOTS, (r + 1) * SLOTS)
                back_ref[rows] += jnp.dot(onehot(1), back, preferred_element_type=F32).astype(BF16)
    else:
        for r in parts:
            back_ref[:, r] = dq[r]

    @pl.when(step == pl.num_programs(0) - 1)
    def _():
        kvgrad_ref[...] = acc[...].T.astype(kvgrad_ref.dtype)


def weight_kernel(cuts, place_ref, own_ref, got_ref, prompt_ref, resp_ref, *refs):
    keeps, gives = refs[:NX], refs[NX : 2 * NX]
    prompt_grad_ref, buf, grad, whole, sems = refs[2 * NX :]
    plen = prompt_ref.shape[0]
    wide = prompt_ref.shape[1] // NX
    part = wide // 4
    copies = [
        pltpu.make_async_copy(prompt_ref.at[lo:hi], buf.at[lo:hi], sems.at[n])
        for n, (lo, hi) in enumerate(cuts)
    ]
    copies.append(pltpu.make_async_copy(resp_ref, buf.at[plen:], sems.at[len(cuts)]))
    for copy in copies:
        copy.start()
    x, core = place_ref[0], place_ref[1]
    grad[...] = (own_ref[...] + got_ref[...].astype(F32)).astype(BF16)
    prompt_grad_ref[...] = grad[:plen]
    spans = list(cuts[:-1]) + [(cuts[-1][0], buf.shape[0])]
    for n, (lo, hi) in enumerate(spans):
        copies[n].wait()
        if n + 1 == len(spans):
            copies[n + 1].wait()
        for k in range(NX):
            cols = pl.ds(pl.multiple_of(lax.rem(x + k, NX) * wide, DH), wide)
            t = lax.dot_general(buf[lo:hi, cols], grad[lo:hi], TN, preferred_element_type=F32)
            if n:
                t = t + whole[k]
            whole[k] = t
            if n + 1 == len(spans):
                for z in range(2):
                    base = z * 2 * part
                    mine = pl.ds(pl.multiple_of(base + core * part, part), part)
                    theirs = pl.ds(pl.multiple_of(base + (1 - core) * part, part), part)
                    keeps[k][z] = whole[k, mine]
                    gives[k][z] = whole[k, theirs].astype(BF16)


def finish_kernel(back_ref, attended_ref, query_grad_ref):
    width = back_ref.shape[2] // 2
    for side in range(2):
        total = sum(back_ref[2 * k + side].astype(F32) for k in range(NY)).astype(BF16)
        there = slice(side * width, (side + 1) * width)
        attended_ref[:, there] = total[:, :width]
        query_grad_ref[:, there] = total[:, width:]


def per_device(
    prompt_hidden, resp_hidden, queries, grad_out, kv_weight, prompt_lengths, response_lengths
):
    rank = lax.axis_index(SEQ)
    x = lax.axis_index("x")
    place = jnp.stack([x, lax.axis_index("c")]).astype(jnp.int32)
    slots = resp_hidden.shape[1]
    plen = prompt_hidden.shape[1]
    model = prompt_hidden.shape[2]
    width = queries.shape[2]
    half = width // 2
    scale = DH ** (-0.5)
    coef = scale * LOG2E
    prompt_rows = prompt_hidden[0]
    resp_rows = resp_hidden[0]
    keys = plen + slots
    shard = kv_weight.shape[0]
    smem = pl.BlockSpec(memory_space=pltpu.SMEM)
    vmem = pl.BlockSpec(memory_space=pltpu.VMEM)

    block = jnp.broadcast_to(kv_weight[None], (16,) + kv_weight.shape)
    block = lax.all_to_all(block, PLANE, 0, 0, tiled=True).reshape(2, 8 * shard, 2 * DH)

    def halves(t):
        return t.reshape(slots, 2, half).transpose(1, 0, 2)

    qg = jnp.concatenate([halves(queries[0]), halves(grad_out[0])], 2)
    qg = jnp.broadcast_to(qg[None], (NY, 2, slots, 2 * half)).reshape(N_SEQ, slots, 2 * half)
    qg, block = lax.optimization_barrier((qg, block))
    nears = [block] + [lax.ppermute(block, "x", shift(k)) for k in range(1, NX)]
    fars = [lax.ppermute(block, "c", SWAP)]
    qg_all = lax.all_to_all(qg, SEQ, 0, 0, tiled=True).reshape(N_SEQ * slots, 2 * half)

    def project(steps, prev, last):
        count = len(steps)
        return pl.pallas_call(
            functools.partial(project_kernel, steps, prev is None, last),
            in_specs=[smem] + [vmem] * (2 + 2 * count + (prev is not None)),
            out_specs=vmem,
            out_shape=jax.ShapeDtypeStruct((keys, 2 * DH), BF16 if last else F32),
            scratch_shapes=[pltpu.VMEM((count * model // NX, 2 * DH), BF16)],
            compiler_params=params(20),
            cost_estimate=pl.CostEstimate(
                flops=2 * keys * model * DH * count // 2,
                bytes_accessed=keys * model * count // 2,
                transcendentals=0,
            ),
            name="project_last" if last else "project",
        )(
            place, prompt_rows, resp_rows, *[nears[k] for k in steps], *[fars[k] for k in steps],
            *(() if prev is None else (prev,)),
        )

    kv = project((0,), None, False)
    nears[3], kv = lax.optimization_barrier((nears[3], kv))
    fars = fars + [lax.ppermute(piece, "c", SWAP) for piece in nears[1:]]
    kv = project((3,), kv, False)
    kv = project((1, 2), kv, True)
    kv_other = lax.ppermute(kv, "zl", SWAP)

    lengths = response_lengths[0]
    live_all = slots * N_SEQ * 5 // 8
    ends = jnp.cumsum(lengths)
    packed = jnp.arange(live_all)
    past = packed[:, None] >= ends[None, :]
    source = packed + jnp.sum(jnp.where(past, slots - lengths[None, :], 0), 1)
    starts = jnp.concatenate([jnp.zeros((1,), jnp.int32), ends.astype(jnp.int32)])

    def masks(owner):
        offset = source - owner * slots
        limit = jnp.where((offset >= 0) & (offset < slots), offset, -1).astype(jnp.int32)
        return (
            (prompt_lengths - plen * owner).astype(jnp.int32),
            jnp.broadcast_to(limit[None, :], (8, live_all)),
            jnp.broadcast_to(limit[:, None], (live_all, DH)),
        )

    valid, limit_rows, limit_cols = masks(rank)
    valid_other, limit_rows_other, limit_cols_other = masks(rank ^ 1)

    steps = live_all // SLOTS
    rows = live_all * HALF
    whole = pl.BlockSpec((keys, 2 * DH), lambda i: (0, 0))
    slot_block = pl.BlockSpec((SLOTS, half), lambda i: (i, 0))
    g_block = pl.BlockSpec((SLOTS, half), lambda i: (i, 1))
    lane_block = pl.BlockSpec((DH, ROWS), lambda i: (0, i))
    limit_lane = pl.BlockSpec((8, SLOTS), lambda i: (0, i))
    limit_slot = pl.BlockSpec((SLOTS, DH), lambda i: (i, 0))
    stat_block = pl.BlockSpec((3, ROWS), lambda i: (0, i))

    every = pl.BlockSpec((N_SEQ * slots, 2 * half), lambda i: (0, 0))

    def forward(valid, limit, kv, more):
        last = bool(more)
        return pl.pallas_call(
            functools.partial(first_pass, coef, last),
            grid=(steps,),
            in_specs=[smem, limit_lane, slot_block, whole]
            + [g_block, lane_block, stat_block] * last,
            out_specs=[slot_block if last else lane_block, stat_block],
            out_shape=[
                jax.ShapeDtypeStruct((live_all, half), BF16)
                if last
                else jax.ShapeDtypeStruct((DH, rows), F32),
                jax.ShapeDtypeStruct((3, rows), F32),
            ],
            scratch_shapes=[pltpu.VMEM((plen, DH), F32), pltpu.VMEM((DH, keys), BF16)],
            compiler_params=params(20),
            cost_estimate=pl.CostEstimate(
                flops=4 * rows * keys * DH, bytes_accessed=4 << 20, transcendentals=rows * keys
            ),
            name="attend_more" if last else "attend_own",
        )(valid, limit, qg, kv, *more)

    pick = (source[:, None] == jnp.arange(N_SEQ * slots)[None, :]).astype(BF16)
    qg = jnp.dot(pick, qg_all, preferred_element_type=F32).astype(BF16)
    state = forward(valid, limit_rows, kv, ())
    out, stat = forward(valid_other, limit_rows_other, kv_other, (qg, *state))
    stats = [stat] + [lax.ppermute(stat, "y", shift(k)) for k in range(1, NY)]

    def backward(valid, limit, kv, more):
        last = bool(more)
        return pl.pallas_call(
            functools.partial(second_pass, coef, scale, last),
            grid=(steps,),
            in_specs=[
                smem, limit_slot, slot_block, g_block, whole,
            ] + [stat_block] * NY + [smem, slot_block, slot_block] * last,
            out_specs=[
                every if last else slot_block,
                whole,
            ],
            out_shape=[
                jax.ShapeDtypeStruct((N_SEQ * slots, 2 * half), BF16)
                if last
                else jax.ShapeDtypeStruct((live_all, half), F32),
                jax.ShapeDtypeStruct((keys, 2 * DH), F32 if last else BF16),
            ],
            scratch_shapes=[pltpu.VMEM((2 * DH, keys), F32), pltpu.VMEM((8, plen), F32)],
            compiler_params=params(20),
            cost_estimate=pl.CostEstimate(
                flops=10 * rows * keys * DH, bytes_accessed=8 << 20, transcendentals=rows * keys
            ),
            name="grads_own" if last else "grads_other",
        )(valid, limit, qg, qg, kv, *stats, *more)

    qgrad_part, kvgrad_other = backward(valid_other, limit_cols_other, kv_other, ())
    kvgrad_got = lax.ppermute(kvgrad_other, "zl", SWAP)
    back, kvgrad_own = backward(valid, limit_cols, kv, (starts, out, qgrad_part))

    back, kvgrad_own = lax.optimization_barrier((back, kvgrad_own))
    back = lax.all_to_all(back.reshape(N_SEQ, slots, 2 * half), SEQ, 0, 0, tiled=True)

    cuts = ((0, plen // 4), (plen // 4, 3 * plen // 4), (3 * plen // 4, plen))
    piece = (2, 8 * shard, 2 * DH)
    *pieces, prompt_grad = pl.pallas_call(
        functools.partial(weight_kernel, cuts),
        in_specs=[smem] + [vmem] * 2 + [pl.BlockSpec(memory_space=pltpu.HBM)] * 2,
        out_specs=[vmem] * (2 * NX + 1),
        out_shape=[jax.ShapeDtypeStruct(piece, F32)] * NX
        + [jax.ShapeDtypeStruct(piece, BF16)] * NX
        + [jax.ShapeDtypeStruct((plen, 2 * DH), BF16)],
        scratch_shapes=[
            pltpu.VMEM((keys, model), BF16),
            pltpu.VMEM((keys, 2 * DH), BF16),
            pltpu.VMEM((NX, model // NX, 2 * DH), F32),
            pltpu.SemaphoreType.DMA((len(cuts) + 1,)),
        ],
        compiler_params=params(50),
        cost_estimate=pl.CostEstimate(
            flops=4 * keys * model * DH, bytes_accessed=2 * keys * model, transcendentals=0
        ),
        name="weight_grad",
    )(place, kvgrad_own, kvgrad_got, prompt_rows, resp_rows)
    keeps, gives = pieces[:NX], pieces[NX:]
    got = [lax.ppermute(give, "c", SWAP) for give in gives]
    line = keeps[0] + got[0].astype(F32)
    for k in range(1, NX):
        piece = (keeps[k] + got[k].astype(F32)).astype(BF16)
        line = line + lax.ppermute(piece, "x", shift(-k)).astype(F32)
    line = line.astype(BF16).reshape(16, shard, 2 * DH)
    line, back = lax.optimization_barrier((line, back))
    shares = lax.all_to_all(line, PLANE, 0, 0, tiled=True)
    weight_grad = jnp.sum(shares.astype(F32), 0)

    attended, query_grad = pl.pallas_call(
        finish_kernel,
        in_specs=[vmem],
        out_specs=[vmem] * 2,
        out_shape=[jax.ShapeDtypeStruct((slots, width), BF16)] * 2,
        compiler_params=params(16),
        name="finish",
    )(back)
    return attended[None], query_grad[None], prompt_grad[None], weight_grad


def solution(mesh):
    fine = Mesh(mesh.devices.reshape(4, 2, 2, 4, 2), AXES)
    return jax.shard_map(
        per_device,
        mesh=fine,
        in_specs=(
            P(GRP, SEQ, None),
            P(GRP, SEQ, None),
            P(GRP, SEQ, None),
            P(GRP, SEQ, None),
            P(AXES, None),
            P(GRP),
            P(GRP, None),
        ),
        out_specs=(
            P(GRP, SEQ, None),
            P(GRP, SEQ, None),
            P(GRP, SEQ, None),
            P(AXES, None),
        ),
        check_vma=False,
    )
```

time: 182 us -> 160 us (0.88)
  Pallas kernels: 72.6 us -> 52 us
    pallas_call x3, Pallas kernels: 18.2 us -> 5.43 us  [project(): pl.pallas_call(functools.partial(project_kernel, steps, prev is None, las...]
    pallas_call x4, Pallas kernels: 29.4 us -> 22.8 us  [the longest x2 12.4 us: forward(): pl.pallas_call(functools.partial(first_pass, coef, last), grid=(steps,),...]
    ppermute x1, waiting for transfers between devices: 5.17 us -> 1.45 us  [per_device(): kv_other = lax.ppermute(kv, 'zl', SWAP)]
    unnamed x28 -> x12, local copies, waits for them, and re-layouts: 3.04 us -> 6.36 us
    dot_general x1 -> x0, matrix products: 3.27 us -> none  [per_device(): lax.dot_general(pick, back, TN, preferred_element_type=F32).astype(BF16)]
    all_to_all x1, waiting for transfers between devices: 0.01 us -> 2.42 us  [per_device(): lax.all_to_all(qg, SEQ, 0, 0, tiled=True).reshape(N_SEQ * slots, 2 * half)]
    squeeze x3 -> x0, local copies, waits for them, and re-layouts: 2.37 us -> none  [the longest x1 1.22 us: per_device(): far_sum = [(keep[n], lax.ppermute(give[n], 'c', SWAP)) for n in range(2)]]
  transfers between devices with their start and end apart: 23 -> 23, of which waited for: 9 -> 11; matrix products, arithmetic and copies ran while one was open for 7% -> 5% of each run, Pallas kernels for 29% -> 22%
where the time goes in v7:
time: 160 us; the launch traced here: 158 us
  Pallas kernels  52 us (32%)
  starting transfers between devices  44.6 us (28%)
  waiting for transfers between devices  42.2 us (26%)
  local copies, waits for them, and re-layouts  12.1 us (8%)
  matrix products  3.15 us (2%)
  other arithmetic  2.65 us (2%)
    pallas_call x2, Pallas kernels, backward(): pl.pallas_call(functools.partial(second_pass, coef, scale, last), grid=(s...  23.7 us
    ppermute x3, waiting for transfers between devices, per_device(): line = line + lax.ppermute(piece, 'x', shift(-k)).astype(F32)  13.3 us
    pallas_call x2, Pallas kernels, forward(): pl.pallas_call(functools.partial(first_pass, coef, last), grid=(steps,),...  12.4 us
    pallas_call x1, Pallas kernels, per_device(): pl.pallas_call(functools.partial(weight_kernel, cuts), in_specs=[smem] +...  9.5 us
    all_to_all x1, starting transfers between devices, per_device(): lax.all_to_all(block, PLANE, 0, 0, tiled=True).reshape(2, 8 * shard, 2 * DH)  8.13 us
    all_to_all x1, waiting for transfers between devices, per_device(): shares = lax.all_to_all(line, PLANE, 0, 0, tiled=True)  7.84 us
    ppermute x3, waiting for transfers between devices, per_device(): nears = [block] + [lax.ppermute(block, 'x', shift(k)) for k in range(1, NX)]  7.74 us
    unnamed x12, local copies, waits for them, and re-layouts  6.36 us
  transfers between devices with their start and end apart: 23, of which 11 were waited for; matrix products, arithmetic and copies ran while one was open for 5% of the time, Pallas kernels for 22%

profile of v7, /device:TPU:0, one launch (start us, length us, event | category | flops | bytes accessed | tf_op | source)
XLA Modules:
  0.0 158.1 jit_solution(4238636362673871285)
XLA Ops:
  2.1 8.1 %all-to-all-start = ((bf16[16,40,256]{2,1,0:T(8,128)(2,1)}), bf16[16,40,256]{2,1,0:T(8,128)(2,1)S(1)}, u32[]{:S(2)}, u32[]{:S(2)}) async-start(bf16[16,40,256]{2,1,0:T(8,128)(2,1)} %broadcast_in_dim.74), calls=%async_computation | async-start | bytes 655360 | tf_op jit(solution)/shard_map/all_to_all | solution.py:289
  13.1 6.3 %all-to-all-done = bf16[16,40,256]{2,1,0:T(8,128)(2,1)S(1)} async-done(((bf16[16,40,256]{2,1,0:T(8,128)(2,1)}), bf16[16,40,256]{2,1,0:T(8,128)(2,1)S(1)}, u32[]{:S(2)}, u32[]{:S(2)}) %all-to-all-start) | async-done | bytes 327712 | tf_op jit(solution)/shard_map/all_to_all | solution.py:289
  19.4 1.6 broadcast_in_dim.73
  21.0 4.5 %all-to-all-start.1 = ((bf16[8,128,1024]{2,1,0:T(8,128)(2,1)}), bf16[8,128,1024]{2,1,0:T(8,128)(2,1)}, u32[]{:S(2)}, u32[]{:S(2)}) async-start(bf16[8,128,1024]{2,1,0:T(8,128)(2,1)} %bitcast.35), calls=%async_computation.1 | async-start | bytes 4194304 | tf_op jit(solution)/shard_map/all_to_all | solution.py:299
  27.1 2.7 %collective-permute-start.1 = (bf16[2,320,256]{2,1,0:T(8,128)(2,1)S(1)}, bf16[2,320,256]{2,1,0:T(8,128)(2,1)S(1)}, u32[]{:S(2)}, u32[]{:S(2)}) collective-permute-start(bf16[2,320,256]{2,1,0:T(8,128)(2,1)S(1)} %bitcast.32), channel_id=1, source_target_pairs={{64,0},{96,32},{0,64},{32,96},{65,1},{97,33},{1,65},{33,97},{66,2}... | collective-permute-start | bytes 983048 | tf_op jit(solution)/shard_map/ppermute | solution.py:297
  31.6 4.0 %copy-done = bf16[1,1024,5120]{2,1,0:T(8,128)(2,1)S(1)} copy-done((bf16[1,1024,5120]{2,1,0:T(8,128)(2,1)S(1)}, bf16[1,1024,5120]{2,1,0:T(8,128)(2,1)}, u32[]{:S(2)}) %copy-start) | copy-done | bytes 10485784
  37.2 7.7 %collective-permute-done.1.refs_1_ = bf16[2,320,256]{2,1,0:T(8,128)(2,1)S(1)} collective-permute-done((bf16[2,320,256]{2,1,0:T(8,128)(2,1)S(1)}, bf16[2,320,256]{2,1,0:T(8,128)(2,1)S(1)}, u32[]{:S(2)}, u32[]{:S(2)}) %collective-permute-start.1) | collective-permute-done | bytes 327712 | tf_op jit(solution)/shard_map/ppermute | solution.py:297
  47.1 2.4 %project_last.1.refs_1_.kv_ref = bf16[1152,256]{1,0:T(8,128)(2,1)S(1)} custom-call(s32[2]{0:T(128)S(1)} %pad_add_fusion.place_ref, bf16[1024,5120]{1,0:T(8,128)(2,1)S(1)} %bitcast.24, bf16[128,5120]{1,0:T(8,128)(2,1)S(1)} %bitcast.28, bf16[2,320,256]{2,1,0:T(8,128)(2,1)S(1)} %collective-permute-done.refs_0_, ...), custom_call_target="tpu_custom_call" | custom-call | flops 1509949440 | bytes 5898240 | tf_op jit(solution)/shard_map/project_last/pallas_call | solution.py:303
  49.5 1.9 %collective-permute-start.7 = (bf16[1152,256]{1,0:T(8,128)(2,1)S(1)}, bf16[1152,256]{1,0:T(8,128)(2,1)S(1)}, u32[]{:S(2)}, u32[]{:S(2)}) collective-permute-start(bf16[1152,256]{1,0:T(8,128)(2,1)S(1)} %project_last.1.refs_1_.kv_ref), channel_id=1, source_target_pairs={{0,1},{1,0},{2,3},{3,2},{4,5},{5,4},{6,7},{7,6},{8,9},{9,8},{10,11... | collective-permute-start | bytes 1769480 | tf_op jit(solution)/shard_map/ppermute | solution.py:326
  52.0 2.4 %all-to-all-done.1 = bf16[8,128,1024]{2,1,0:T(8,128)(2,1)} async-done(((bf16[8,128,1024]{2,1,0:T(8,128)(2,1)}), bf16[8,128,1024]{2,1,0:T(8,128)(2,1)}, u32[]{:S(2)}, u32[]{:S(2)}) %all-to-all-start.1) | async-done | bytes 2097184 | tf_op jit(solution)/shard_map/all_to_all | solution.py:299
  54.4 3.2 %fusion.1.refs_0_.refs_2_.q_ref.g_ref = bf16[640,1024]{1,0:T(8,128)(2,1)S(1)} fusion(bf16[1024,1024]{1,0:T(8,128)(2,1)} %bitcast.10, s32[640]{0:T(1024)S(1)} %get-tuple-element.56), kind=kOutput, calls=%fused_computation.2 | convolution fusion | flops 1343488000 | bytes 3410432 | tf_op jit(solution)/shard_map/dot_general | solution.py:383
  57.6 5.8 %attend_own.1 = (f32[128,2560]{1,0:T(8,128)S(1)}, f32[3,2560]{1,0:T(4,128)S(1)}) custom-call(s32[1]{0:T(128)S(6)} %sub.44.valid_ref, s32[8,640]{1,0:T(8,128)S(1)} %broadcast_in_dim.76.limit_ref, bf16[640,1024]{1,0:T(8,128)(2,1)S(1)} %fusion.1.refs_0_.refs_2_.q_ref.g_ref, bf16[1152,256]{1,0:T(8,128)(2,1)S(1)} %project_last.1.refs_1_.kv_ref), custom_call_target="tpu_custom_call" | custom-call | flops 1509949440 | bytes 4194304 | tf_op jit(solution)/shard_map/attend_own/pallas_call | solution.py:362
  64.9 6.5 %attend_more.1 = (bf16[640,512]{1,0:T(8,128)(2,1)S(1)}, f32[3,2560]{1,0:T(4,128)S(1)}) custom-call(s32[1]{0:T(128)S(6)} %sub.49.valid_ref, s32[8,640]{1,0:T(8,128)S(1)} %broadcast_in_dim.75.limit_ref, bf16[640,1024]{1,0:T(8,128)(2,1)S(1)} %fusion.1.refs_0_.refs_2_.q_ref.g_ref, bf16[1152,256]{1,0:T(8,128)(2,1)S(1)} %collective-permute-done.7.refs_1_.kv_ref, ...), custom_call_target="tpu_custom_call" | custom-call | flops 1509949440 | bytes 4194304 | tf_op jit(solution)/shard_map/attend_more/pallas_call | solution.py:362
  71.4 1.8 %collective-permute-start.10 = (f32[3,2560]{1,0:T(4,128)S(1)}, f32[3,2560]{1,0:T(4,128)S(1)}, u32[]{:S(2)}, u32[]{:S(2)}) collective-permute-start(f32[3,2560]{1,0:T(4,128)S(1)} %get-tuple-element.35.refs_0_), channel_id=1, source_target_pairs={{6,0},{0,2},{2,4},{4,6},{7,1},{1,3},{3,5},{5,7},{14,8},{8,10},{10,... | collective-permute-start | bytes 92168 | tf_op jit(solution)/shard_map/ppermute | solution.py:386
  73.2 2.7 %collective-permute-start.9 = (f32[3,2560]{1,0:T(4,128)S(1)}, f32[3,2560]{1,0:T(4,128)S(1)}, u32[]{:S(2)}, u32[]{:S(2)}) collective-permute-start(f32[3,2560]{1,0:T(4,128)S(1)} %get-tuple-element.35.refs_0_), channel_id=1, source_target_pairs={{4,0},{6,2},{0,4},{2,6},{5,1},{7,3},{1,5},{3,7},{12,8},{14,10},{8,... | collective-permute-start | bytes 92168 | tf_op jit(solution)/shard_map/ppermute | solution.py:386
  80.1 10.4 %grads_other.1 = (f32[640,512]{1,0:T(8,128)S(1)}, bf16[1152,256]{1,0:T(8,128)(2,1)}) custom-call(s32[1]{0:T(128)S(6)} %sub.49.valid_ref, s32[640,128]{1,0:T(8,128)S(1)} %broadcast_in_dim.77.limit_ref, bf16[640,1024]{1,0:T(8,128)(2,1)S(1)} %fusion.1.refs_0_.refs_2_.q_ref.g_ref, bf16[640,1024]{1,0:T(8,128)(2,1)S(1)} %fusion.1.refs_0_.refs_2_.q_ref.g_ref, ...), custom_call_target="tpu_custom_call" | custom-call | flops 3774873600 | bytes 8388608 | tf_op jit(solution)/shard_map/grads_other/pallas_call | solution.py:390
  92.2 13.3 %grads_own.1 = (bf16[1024,1024]{1,0:T(8,128)(2,1)S(1)}, f32[1152,256]{1,0:T(8,128)S(1)}) custom-call(s32[1]{0:T(128)S(6)} %sub.44.valid_ref, s32[640,128]{1,0:T(8,128)S(1)} %broadcast_in_dim.72.limit_ref, bf16[640,1024]{1,0:T(8,128)(2,1)S(1)} %fusion.1.refs_0_.refs_2_.q_ref.g_ref, bf16[640,1024]{1,0:T(8,128)(2,1)S(1)} %fusion.1.refs_0_.refs_2_.q_ref.g_ref, ...), custom_call_target="tpu_custom_call" | custom-call | flops 3774873600 | bytes 8388608 | tf_op jit(solution)/shard_map/grads_own/pallas_call | solution.py:390
  107.9 3.9 %all-to-all-start.2 = ((bf16[8,128,1024]{2,1,0:T(8,128)(2,1)}), bf16[8,128,1024]{2,1,0:T(8,128)(2,1)S(1)}, u32[]{:S(2)}, u32[]{:S(2)}) async-start(bf16[8,128,1024]{2,1,0:T(8,128)(2,1)} %bitcast.29), calls=%async_computation.2 | async-start | bytes 4194304 | tf_op jit(solution)/shard_map/all_to_all | solution.py:419
  111.8 9.5 %weight_grad.1 = (f32[2,320,256]{2,1,0:T(8,128)S(1)}, f32[2,320,256]{2,1,0:T(8,128)S(1)}, f32[2,320,256]{2,1,0:T(8,128)S(1)}, f32[2,320,256]{2,1,0:T(8,128)}, bf...) custom-call(s32[2]{0:T(128)S(1)} %pad_add_fusion.place_ref, ...), custom_call_target="tpu_custom_call" | custom-call | flops 3019898880 | bytes 11796480 | tf_op jit(solution)/shard_map/weight_grad/pallas_call | solution.py:423
  124.3 2.7 %collective-permute-start.16 = (bf16[2,320,256]{2,1,0:T(8,128)(2,1)S(1)}, bf16[2,320,256]{2,1,0:T(8,128)(2,1)S(1)}, u32[]{:S(2)}, u32[]{:S(2)}) collective-permute-start(bf16[2,320,256]{2,1,0:T(8,128)(2,1)S(1)} %add_convert_fusion.2), channel_id=1, source_target_pairs={{64,0},{96,32},{0,64},{32,96},{65,1},{97,33},{1,65},{33,97},{66,2}... | collective-permute-start | bytes 983048 | tf_op jit(solution)/shard_map/ppermute | solution.py:447
  128.7 5.8 %collective-permute-done.14 = bf16[2,320,256]{2,1,0:T(8,128)(2,1)S(1)} collective-permute-done((bf16[2,320,256]{2,1,0:T(8,128)(2,1)S(1)}, bf16[2,320,256]{2,1,0:T(8,128)(2,1)S(1)}, u32[]{:S(2)}, u32[]{:S(2)}) %collective-permute-start.14) | collective-permute-done | bytes 327712 | tf_op jit(solution)/shard_map/ppermute | solution.py:447
  134.5 7.1 %collective-permute-done.16 = bf16[2,320,256]{2,1,0:T(8,128)(2,1)S(1)} collective-permute-done((bf16[2,320,256]{2,1,0:T(8,128)(2,1)S(1)}, bf16[2,320,256]{2,1,0:T(8,128)(2,1)S(1)}, u32[]{:S(2)}, u32[]{:S(2)}) %collective-permute-start.16) | collective-permute-done | bytes 327712 | tf_op jit(solution)/shard_map/ppermute | solution.py:447
  142.8 5.8 %all-to-all-start.3 = ((bf16[16,40,256]{2,1,0:T(8,128)(2,1)}), bf16[16,40,256]{2,1,0:T(8,128)(2,1)S(1)}, u32[]{:S(2)}, u32[]{:S(2)}) async-start(bf16[16,40,256]{2,1,0:T(8,128)(2,1)} %bitcast.14), calls=%async_computation.3 | async-start | bytes 655360 | tf_op jit(solution)/shard_map/all_to_all | solution.py:450
  149.6 7.8 %all-to-all-done.3 = bf16[16,40,256]{2,1,0:T(8,128)(2,1)S(1)} async-done(((bf16[16,40,256]{2,1,0:T(8,128)(2,1)}), bf16[16,40,256]{2,1,0:T(8,128)(2,1)S(1)}, u32[]{:S(2)}, u32[]{:S(2)}) %all-to-all-start.3) | async-done | bytes 327712 | tf_op jit(solution)/shard_map/all_to_all | solution.py:450
  (65 shorter events, 28.6 us)
Async XLA Ops:
  2.1 17.3 %all-to-all-start = ((bf16[16,40,256]{2,1,0:T(8,128)(2,1)}), bf16[16,40,256]{2,1,0:T(8,128)(2,1)S(1)}, u32[]{:S(2)}, u32[]{:S(2)}) async-start(bf16[16,40,256]{2,1,0:T(8,128)(2,1)} %broadcast_in_dim.74), calls=%async_computation | async-start | bytes 655360 | tf_op jit(solution)/shard_map/all_to_all | solution.py:289
  21.0 10.6 %copy-start.1 = (bf16[1,128,5120]{2,1,0:T(8,128)(2,1)S(1)}, bf16[1,128,5120]{2,1,0:T(8,128)(2,1)}, u32[]{:S(2)}) copy-start(bf16[1,128,5120]{2,1,0:T(8,128)(2,1)} %param.8) | copy-start | bytes 3932164
  21.0 33.4 %all-to-all-start.1 = ((bf16[8,128,1024]{2,1,0:T(8,128)(2,1)}), bf16[8,128,1024]{2,1,0:T(8,128)(2,1)}, u32[]{:S(2)}, u32[]{:S(2)}) async-start(bf16[8,128,1024]{2,1,0:T(8,128)(2,1)} %bitcast.35), calls=%async_computation.1 | async-start | bytes 4194304 | tf_op jit(solution)/shard_map/all_to_all | solution.py:299
  25.5 6.1 %collective-permute-start.5 = (bf16[2,320,256]{2,1,0:T(8,128)(2,1)S(1)}, bf16[2,320,256]{2,1,0:T(8,128)(2,1)S(1)}, u32[]{:S(2)}, u32[]{:S(2)}) collective-permute-start(bf16[2,320,256]{2,1,0:T(8,128)(2,1)S(1)} %bitcast.30), channel_id=1, source_target_pairs={{0,8},{8,0},{1,9},{9,1},{2,10},{10,2},{3,11},{11,3},{4,12},{12,4},... | collective-permute-start | bytes 983048 | tf_op jit(solution)/shard_map/ppermute | solution.py:298
  25.6 11.5 %collective-permute-start.4 = (bf16[2,320,256]{2,1,0:T(8,128)(2,1)S(1)}, bf16[2,320,256]{2,1,0:T(8,128)(2,1)S(1)}, u32[]{:S(2)}, u32[]{:S(2)}) collective-permute-start(bf16[2,320,256]{2,1,0:T(8,128)(2,1)S(1)} %bitcast.31), channel_id=1, source_target_pairs={{96,0},{0,32},{32,64},{64,96},{97,1},{1,33},{33,65},{65,97},{98,2}... | collective-permute-start | bytes 983048 | tf_op jit(solution)/shard_map/ppermute | solution.py:297
  27.1 17.8 %collective-permute-start.1 = (bf16[2,320,256]{2,1,0:T(8,128)(2,1)S(1)}, bf16[2,320,256]{2,1,0:T(8,128)(2,1)S(1)}, u32[]{:S(2)}, u32[]{:S(2)}) collective-permute-start(bf16[2,320,256]{2,1,0:T(8,128)(2,1)S(1)} %bitcast.32), channel_id=1, source_target_pairs={{64,0},{96,32},{0,64},{32,96},{65,1},{97,33},{1,65},{33,97},{66,2}... | collective-permute-start | bytes 983048 | tf_op jit(solution)/shard_map/ppermute | solution.py:297
  29.9 15.1 %collective-permute-start = (bf16[2,320,256]{2,1,0:T(8,128)(2,1)S(1)}, bf16[2,320,256]{2,1,0:T(8,128)(2,1)S(1)}, u32[]{:S(2)}, u32[]{:S(2)}) collective-permute-start(bf16[2,320,256]{2,1,0:T(8,128)(2,1)S(1)} %bitcast.33), channel_id=1, source_target_pairs={{32,0},{64,32},{96,64},{0,96},{33,1},{65,33},{97,65},{1,97},{34,2}... | collective-permute-start | bytes 983048 | tf_op jit(solution)/shard_map/ppermute | solution.py:297
  37.1 8.4 %collective-permute-start.6 = (bf16[2,320,256]{2,1,0:T(8,128)(2,1)S(1)}, bf16[2,320,256]{2,1,0:T(8,128)(2,1)S(1)}, u32[]{:S(2)}, u32[]{:S(2)}) collective-permute-start(bf16[2,320,256]{2,1,0:T(8,128)(2,1)S(1)} %collective-permute-done.4.refs_0_), channel_id=1, source_target_pairs={{0,8},{8,0},{1,9},{9,1},{2,10},{10,2},{3,11},{11,3},{4,12},{12,4},... | collective-permute-start | bytes 983048 | tf_op jit(solution)/shard_map/ppermute | solution.py:323
  44.9 2.2 %collective-permute-start.3 = (bf16[2,320,256]{2,1,0:T(8,128)(2,1)S(1)}, bf16[2,320,256]{2,1,0:T(8,128)(2,1)S(1)}, u32[]{:S(2)}, u32[]{:S(2)}) collective-permute-start(bf16[2,320,256]{2,1,0:T(8,128)(2,1)S(1)} %collective-permute-done.1.refs_1_), channel_id=1, source_target_pairs={{0,8},{8,0},{1,9},{9,1},{2,10},{10,2},{3,11},{11,3},{4,12},{12,4},... | collective-permute-start | bytes 983048 | tf_op jit(solution)/shard_map/ppermute | solution.py:323
  44.9 2.2 %collective-permute-start.2 = (bf16[2,320,256]{2,1,0:T(8,128)(2,1)S(1)}, bf16[2,320,256]{2,1,0:T(8,128)(2,1)S(1)}, u32[]{:S(2)}, u32[]{:S(2)}) collective-permute-start(bf16[2,320,256]{2,1,0:T(8,128)(2,1)S(1)} %collective-permute-done.refs_0_), channel_id=1, source_target_pairs={{0,8},{8,0},{1,9},{9,1},{2,10},{10,2},{3,11},{11,3},{4,12},{12,4},... | collective-permute-start | bytes 983048 | tf_op jit(solution)/shard_map/ppermute | solution.py:323
  49.5 15.4 %collective-permute-start.7 = (bf16[1152,256]{1,0:T(8,128)(2,1)S(1)}, bf16[1152,256]{1,0:T(8,128)(2,1)S(1)}, u32[]{:S(2)}, u32[]{:S(2)}) collective-permute-start(bf16[1152,256]{1,0:T(8,128)(2,1)S(1)} %project_last.1.refs_1_.kv_ref), channel_id=1, source_target_pairs={{0,1},{1,0},{2,3},{3,2},{4,5},{5,4},{6,7},{7,6},{8,9},{9,8},{10,11... | collective-permute-start | bytes 1769480 | tf_op jit(solution)/shard_map/ppermute | solution.py:326
  71.4 6.0 %collective-permute-start.10 = (f32[3,2560]{1,0:T(4,128)S(1)}, f32[3,2560]{1,0:T(4,128)S(1)}, u32[]{:S(2)}, u32[]{:S(2)}) collective-permute-start(f32[3,2560]{1,0:T(4,128)S(1)} %get-tuple-element.35.refs_0_), channel_id=1, source_target_pairs={{6,0},{0,2},{2,4},{4,6},{7,1},{1,3},{3,5},{5,7},{14,8},{8,10},{10,... | collective-permute-start | bytes 92168 | tf_op jit(solution)/shard_map/ppermute | solution.py:386
  73.2 5.5 %collective-permute-start.9 = (f32[3,2560]{1,0:T(4,128)S(1)}, f32[3,2560]{1,0:T(4,128)S(1)}, u32[]{:S(2)}, u32[]{:S(2)}) collective-permute-start(f32[3,2560]{1,0:T(4,128)S(1)} %get-tuple-element.35.refs_0_), channel_id=1, source_target_pairs={{4,0},{6,2},{0,4},{2,6},{5,1},{7,3},{1,5},{3,7},{12,8},{14,10},{8,... | collective-permute-start | bytes 92168 | tf_op jit(solution)/shard_map/ppermute | solution.py:386
  75.9 4.0 %collective-permute-start.8 = (f32[3,2560]{1,0:T(4,128)S(1)}, f32[3,2560]{1,0:T(4,128)S(1)}, u32[]{:S(2)}, u32[]{:S(2)}) collective-permute-start(f32[3,2560]{1,0:T(4,128)S(1)} %get-tuple-element.35.refs_0_), channel_id=1, source_target_pairs={{2,0},{4,2},{6,4},{0,6},{3,1},{5,3},{7,5},{1,7},{10,8},{12,10},{14... | collective-permute-start | bytes 92168 | tf_op jit(solution)/shard_map/ppermute | solution.py:386
  90.5 21.3 %collective-permute-start.11 = (bf16[1152,256]{1,0:T(8,128)(2,1)}, bf16[1152,256]{1,0:T(8,128)(2,1)S(1)}, u32[]{:S(2)}, u32[]{:S(2)}) collective-permute-start(bf16[1152,256]{1,0:T(8,128)(2,1)} %get-tuple-element.39), channel_id=1, source_target_pairs={{0,1},{1,0},{2,3},{3,2},{4,5},{5,4},{6,7},{7,6},{8,9},{9,8},{10,11... | collective-permute-start | bytes 1769480 | tf_op jit(solution)/shard_map/ppermute | solution.py:415
  107.9 35.0 %all-to-all-start.2 = ((bf16[8,128,1024]{2,1,0:T(8,128)(2,1)}), bf16[8,128,1024]{2,1,0:T(8,128)(2,1)S(1)}, u32[]{:S(2)}, u32[]{:S(2)}) async-start(bf16[8,128,1024]{2,1,0:T(8,128)(2,1)} %bitcast.29), calls=%async_computation.2 | async-start | bytes 4194304 | tf_op jit(solution)/shard_map/all_to_all | solution.py:419
  121.3 1.7 %collective-permute-start.13 = (bf16[2,320,256]{2,1,0:T(8,128)(2,1)S(1)}, bf16[2,320,256]{2,1,0:T(8,128)(2,1)S(1)}, u32[]{:S(2)}, u32[]{:S(2)}) collective-permute-start(bf16[2,320,256]{2,1,0:T(8,128)(2,1)S(1)} %get-tuple-element.43), channel_id=1, source_target_pairs={{0,8},{8,0},{1,9},{9,1},{2,10},{10,2},{3,11},{11,3},{4,12},{12,4},... | collective-permute-start | bytes 983048 | tf_op jit(solution)/shard_map/ppermute | solution.py:443
  121.4 2.8 %collective-permute-start.15 = (bf16[2,320,256]{2,1,0:T(8,128)(2,1)S(1)}, bf16[2,320,256]{2,1,0:T(8,128)(2,1)S(1)}, u32[]{:S(2)}, u32[]{:S(2)}) collective-permute-start(bf16[2,320,256]{2,1,0:T(8,128)(2,1)S(1)} %get-tuple-element.45), channel_id=1, source_target_pairs={{0,8},{8,0},{1,9},{9,1},{2,10},{10,2},{3,11},{11,3},{4,12},{12,4},... | collective-permute-start | bytes 983048 | tf_op jit(solution)/shard_map/ppermute | solution.py:443
  121.9 6.8 %collective-permute-start.12 = (bf16[2,320,256]{2,1,0:T(8,128)(2,1)S(1)}, bf16[2,320,256]{2,1,0:T(8,128)(2,1)S(1)}, u32[]{:S(2)}, u32[]{:S(2)}) collective-permute-start(bf16[2,320,256]{2,1,0:T(8,128)(2,1)S(1)} %get-tuple-element.41), channel_id=1, source_target_pairs={{0,8},{8,0},{1,9},{9,1},{2,10},{10,2},{3,11},{11,3},{4,12},{12,4},... | collective-permute-start | bytes 983048 | tf_op jit(solution)/shard_map/ppermute | solution.py:443
  122.0 5.0 %collective-permute-start.17 = (bf16[2,320,256]{2,1,0:T(8,128)(2,1)S(1)}, bf16[2,320,256]{2,1,0:T(8,128)(2,1)S(1)}, u32[]{:S(2)}, u32[]{:S(2)}) collective-permute-start(bf16[2,320,256]{2,1,0:T(8,128)(2,1)S(1)} %get-tuple-element.47), channel_id=1, source_target_pairs={{0,8},{8,0},{1,9},{9,1},{2,10},{10,2},{3,11},{11,3},{4,12},{12,4},... | collective-permute-start | bytes 983048 | tf_op jit(solution)/shard_map/ppermute | solution.py:443
  123.1 11.4 %collective-permute-start.14 = (bf16[2,320,256]{2,1,0:T(8,128)(2,1)S(1)}, bf16[2,320,256]{2,1,0:T(8,128)(2,1)S(1)}, u32[]{:S(2)}, u32[]{:S(2)}) collective-permute-start(bf16[2,320,256]{2,1,0:T(8,128)(2,1)S(1)} %add_convert_fusion.3), channel_id=1, source_target_pairs={{96,0},{0,32},{32,64},{64,96},{97,1},{1,33},{33,65},{65,97},{98,2}... | collective-permute-start | bytes 983048 | tf_op jit(solution)/shard_map/ppermute | solution.py:447
  124.3 17.3 %collective-permute-start.16 = (bf16[2,320,256]{2,1,0:T(8,128)(2,1)S(1)}, bf16[2,320,256]{2,1,0:T(8,128)(2,1)S(1)}, u32[]{:S(2)}, u32[]{:S(2)}) collective-permute-start(bf16[2,320,256]{2,1,0:T(8,128)(2,1)S(1)} %add_convert_fusion.2), channel_id=1, source_target_pairs={{64,0},{96,32},{0,64},{32,96},{65,1},{97,33},{1,65},{33,97},{66,2}... | collective-permute-start | bytes 983048 | tf_op jit(solution)/shard_map/ppermute | solution.py:447
  127.1 14.8 %collective-permute-start.18 = (bf16[2,320,256]{2,1,0:T(8,128)(2,1)S(1)}, bf16[2,320,256]{2,1,0:T(8,128)(2,1)S(1)}, u32[]{:S(2)}, u32[]{:S(2)}) collective-permute-start(bf16[2,320,256]{2,1,0:T(8,128)(2,1)S(1)} %add_convert_fusion.1), channel_id=1, source_target_pairs={{32,0},{64,32},{96,64},{0,96},{33,1},{65,33},{97,65},{1,97},{34,2}... | collective-permute-start | bytes 983048 | tf_op jit(solution)/shard_map/ppermute | solution.py:447
  142.8 14.6 %all-to-all-start.3 = ((bf16[16,40,256]{2,1,0:T(8,128)(2,1)}), bf16[16,40,256]{2,1,0:T(8,128)(2,1)S(1)}, u32[]{:S(2)}, u32[]{:S(2)}) async-start(bf16[16,40,256]{2,1,0:T(8,128)(2,1)} %bitcast.14), calls=%async_computation.3 | async-start | bytes 655360 | tf_op jit(solution)/shard_map/all_to_all | solution.py:450
  (5 other events, 22.4 us)

commit v8 on v7

--- a/solution.py
+++ b/solution.py
@@ -39,6 +39,26 @@
 
 def stack_heads(ref):
     return jnp.concatenate([ref[:, h * DH : (h + 1) * DH] for h in range(HALF)], 0)
+
+
+def copies_kernel(block_ref, out_ref):
+    for i in range(out_ref.shape[0]):
+        out_ref[i] = block_ref[...]
+
+
+def halves_kernel(q_ref, g_ref, out_ref, buf, sems):
+    half = q_ref.shape[1] // 2
+    for side in range(2):
+        cols = slice(side * half, (side + 1) * half)
+        buf[side, :, :half] = q_ref[:, cols]
+        buf[side, :, half:] = g_ref[:, cols]
+    copies = [
+        pltpu.make_async_copy(buf, out_ref.at[2 * k : 2 * k + 2], sems.at[k]) for k in range(NY)
+    ]
+    for copy in copies:
+        copy.start()
+    for copy in copies:
+        copy.wait()
 
 
 def project_kernel(steps, first, last, place_ref, prompt_ref, resp_ref, *refs):
@@ -69,20 +89,19 @@
     kv_ref[plen:] = end.astype(kv_ref.dtype)
 
 
-def crossing(start_ref, r, block):
-    start, end = start_ref[r], start_ref[r + 1]
-    base = block * SLOTS
-    meets = (start < base + SLOTS) & (end > base)
-
-    def onehot(row_axis):
-        row = lax.broadcasted_iota(jnp.int32, (SLOTS, SLOTS), row_axis) + base
-        slot = lax.broadcasted_iota(jnp.int32, (SLOTS, SLOTS), 1 - row_axis) + start
-        return jnp.where((row == slot) & (row < end), 1.0, 0.0).astype(BF16)
-
-    return meets, onehot
-
-
-def first_pass(coef, last, valid_ref, limit_ref, *refs):
+def one_hot(start_ref, r, block):
+    row = lax.broadcasted_iota(jnp.int32, (SLOTS, SLOTS), 1) + block * SLOTS
+    slot = lax.broadcasted_iota(jnp.int32, (SLOTS, SLOTS), 0) + start_ref[r]
+    return jnp.where((row == slot) & (row < start_ref[r + 1]), 1.0, 0.0).astype(BF16)
+
+
+def visible(start_ref, r, block, row_axis):
+    row = lax.broadcasted_iota(jnp.int32, (SLOTS, SLOTS), row_axis) + block * SLOTS
+    slot = lax.broadcasted_iota(jnp.int32, (SLOTS, SLOTS), 1 - row_axis) + start_ref[r]
+    return (slot <= row) & (row < start_ref[r + 1])
+
+
+def first_pass(coef, last, info_ref, start_ref, *refs):
     if last:
         q_ref, kv_ref, g_ref, prev_out_ref, prev_stat_ref, out_ref, stat_ref, bias, values = refs
     else:
@@ -92,12 +111,10 @@
     @pl.when(pl.program_id(0) == 0)
     def _():
         place = lax.broadcasted_iota(jnp.int32, (plen, DH), 0)
-        bias[...] = jnp.where(place < valid_ref[0], 0.0, NEG)
+        bias[...] = jnp.where(place < info_ref[0], 0.0, NEG)
         values[...] = kv_ref[:, DH:].T
 
-    causal = jnp.where(
-        lax.broadcasted_iota(jnp.int32, (DH, SLOTS), 0) <= limit_ref[0:1], 0.0, NEG
-    )
+    causal = jnp.where(visible(start_ref, info_ref[1], pl.program_id(0), 1), 0.0, NEG)
     bias_all = jnp.concatenate([bias[...], causal], 0)
     bias_all = jnp.concatenate([bias_all] * 2, 1)
     keys = kv_ref[:, :DH]
@@ -136,10 +153,10 @@
         stat_ref[1:2, lanes] = total
 
 
-def second_pass(coef, scale, last, valid_ref, limit_ref, q_ref, g_ref, kv_ref, *refs):
+def second_pass(coef, scale, last, info_ref, start_ref, q_ref, g_ref, kv_ref, *refs):
     stat_refs, refs = refs[:NY], refs[NY:]
     if last:
-        start_ref, out_ref, prev_ref, back_ref, kvgrad_ref, acc, bias = refs
+        span_ref, out_ref, prev_ref, back_ref, kvgrad_ref, acc, bias = refs
     else:
         back_ref, kvgrad_ref, acc, bias = refs
     step = pl.program_id(0)
@@ -158,15 +175,15 @@
     def _():
         acc[...] = jnp.zeros_like(acc)
         place = lax.broadcasted_iota(jnp.int32, (8, plen), 1)
-        bias[...] = jnp.where(place < valid_ref[0], 0.0, NEG)
+        bias[...] = jnp.where(place < info_ref[0], 0.0, NEG)
 
     c_top, c_inv, c_delta = columns[:, 0:1], columns[:, 1:2], columns[:, 2:3]
     q = stack_heads(q_ref)
     g = stack_heads(g_ref)
     qt = q.T
     gt = g.T
-    lane = lax.broadcasted_iota(jnp.int32, (SLOTS, DH), 1)
-    causal = jnp.concatenate([jnp.where(lane <= limit_ref[...], 0.0, NEG)] * HALF, 0)
+    seen = visible(start_ref, info_ref[1], step, 0)
+    causal = jnp.concatenate([jnp.where(seen, 0.0, NEG)] * HALF, 0)
     chunk = 256
     cuts = [slice(i, i + chunk) for i in range(0, plen, chunk)] + [slice(plen, plen + DH)]
 
@@ -204,13 +221,13 @@
         def _():
             back_ref[...] = jnp.zeros_like(back_ref)
 
-        for r in range(N_SEQ):
-            meets, onehot = crossing(start_ref, r, step)
-
-            @pl.when(meets)
-            def _():
-                rows = slice(r * SLOTS, (r + 1) * SLOTS)
-                back_ref[rows] += jnp.dot(onehot(1), back, preferred_element_type=F32).astype(BF16)
+        def place(r, _):
+            slots = pl.ds(pl.multiple_of(r * SLOTS, SLOTS), SLOTS)
+            onehot = one_hot(start_ref, r, step)
+            back_ref[slots] += jnp.dot(onehot, back, preferred_element_type=F32).astype(BF16)
+            return 0
+
+        lax.fori_loop(span_ref[2 * step], span_ref[2 * step + 1], place, 0)
     else:
         for r in parts:
             back_ref[:, r] = dq[r]
@@ -222,7 +239,7 @@
 
 def weight_kernel(cuts, place_ref, own_ref, got_ref, prompt_ref, resp_ref, *refs):
     keeps, gives = refs[:NX], refs[NX : 2 * NX]
-    prompt_grad_ref, buf, grad, whole, sems = refs[2 * NX :]
+    prompt_grad_ref, buf, whole, sems = refs[2 * NX :]
     plen = prompt_ref.shape[0]
     wide = prompt_ref.shape[1] // NX
     part = wide // 4
@@ -234,8 +251,9 @@
     for copy in copies:
         copy.start()
     x, core = place_ref[0], place_ref[1]
-    grad[...] = (own_ref[...] + got_ref[...].astype(F32)).astype(BF16)
+    grad = (own_ref[...] + got_ref[...].astype(F32)).astype(BF16)
     prompt_grad_ref[...] = grad[:plen]
+    grad = grad.T
     spans = list(cuts[:-1]) + [(cuts[-1][0], buf.shape[0])]
     for n, (lo, hi) in enumerate(spans):
         copies[n].wait()
@@ -243,7 +261,7 @@
             copies[n + 1].wait()
         for k in range(NX):
             cols = pl.ds(pl.multiple_of(lax.rem(x + k, NX) * wide, DH), wide)
-            t = lax.dot_general(buf[lo:hi, cols], grad[lo:hi], TN, preferred_element_type=F32)
+            t = jnp.dot(grad[:, lo:hi], buf[lo:hi, cols], preferred_element_type=F32).T
             if n:
                 t = t + whole[k]
             whole[k] = t
@@ -285,15 +303,46 @@
     smem = pl.BlockSpec(memory_space=pltpu.SMEM)
     vmem = pl.BlockSpec(memory_space=pltpu.VMEM)
 
-    block = jnp.broadcast_to(kv_weight[None], (16,) + kv_weight.shape)
+    lengths = response_lengths[0]
+    live_all = slots * N_SEQ * 5 // 8
+    ends = jnp.cumsum(lengths)
+    packed = jnp.arange(live_all)
+    past = packed[:, None] >= ends[None, :]
+    source = packed + jnp.sum(jnp.where(past, slots - lengths[None, :], 0), 1)
+    starts = jnp.concatenate([jnp.zeros((1,), jnp.int32), ends.astype(jnp.int32)])
+    lows = jnp.arange(live_all // SLOTS)[:, None] * SLOTS
+    first = jnp.sum(ends[None, :] <= lows, 1)
+    behind = jnp.sum((ends - lengths)[None, :] < lows + SLOTS, 1)
+    spans = jnp.stack([first, behind], 1).astype(jnp.int32).reshape(-1)
+
+    def info(owner):
+        return jnp.stack([prompt_lengths[0] - plen * owner, owner]).astype(jnp.int32)
+
+    mine, others = info(rank), info(rank ^ 1)
+
+    block = pl.pallas_call(
+        copies_kernel,
+        in_specs=[vmem],
+        out_specs=vmem,
+        out_shape=jax.ShapeDtypeStruct((16,) + kv_weight.shape, BF16),
+        compiler_params=params(16),
+        name="weight_copies",
+    )(kv_weight)
     block = lax.all_to_all(block, PLANE, 0, 0, tiled=True).reshape(2, 8 * shard, 2 * DH)
 
-    def halves(t):
-        return t.reshape(slots, 2, half).transpose(1, 0, 2)
-
-    qg = jnp.concatenate([halves(queries[0]), halves(grad_out[0])], 2)
-    qg = jnp.broadcast_to(qg[None], (NY, 2, slots, 2 * half)).reshape(N_SEQ, slots, 2 * half)
-    qg, block = lax.optimization_barrier((qg, block))
+    qg = pl.pallas_call(
+        halves_kernel,
+        in_specs=[vmem] * 2,
+        out_specs=pl.BlockSpec(memory_space=pl.ANY),
+        out_shape=jax.ShapeDtypeStruct((N_SEQ, slots, 2 * half), BF16),
+        scratch_shapes=[pltpu.VMEM((2, slots, 2 * half), BF16), pltpu.SemaphoreType.DMA((NY,))],
+        compiler_params=params(16),
+        cost_estimate=pl.CostEstimate(flops=0, bytes_accessed=8 << 20, transcendentals=0),
+        name="query_halves",
+    )(queries[0], grad_out[0])
+    small = (place, source, starts, spans, mine, others)
+    qg, block, small = lax.optimization_barrier((qg, block, small))
+    place, source, starts, spans, mine, others = small
     nears = [block] + [lax.ppermute(block, "x", shift(k)) for k in range(1, NX)]
     fars = [lax.ppermute(block, "c", SWAP)]
     qg_all = lax.all_to_all(qg, SEQ, 0, 0, tiled=True).reshape(N_SEQ * slots, 2 * half)
@@ -325,44 +374,22 @@
     kv = project((1, 2), kv, True)
     kv_other = lax.ppermute(kv, "zl", SWAP)
 
-    lengths = response_lengths[0]
-    live_all = slots * N_SEQ * 5 // 8
-    ends = jnp.cumsum(lengths)
-    packed = jnp.arange(live_all)
-    past = packed[:, None] >= ends[None, :]
-    source = packed + jnp.sum(jnp.where(past, slots - lengths[None, :], 0), 1)
-    starts = jnp.concatenate([jnp.zeros((1,), jnp.int32), ends.astype(jnp.int32)])
-
-    def masks(owner):
-        offset = source - owner * slots
-        limit = jnp.where((offset >= 0) & (offset < slots), offset, -1).astype(jnp.int32)
-        return (
-            (prompt_lengths - plen * owner).astype(jnp.int32),
-            jnp.broadcast_to(limit[None, :], (8, live_all)),
-            jnp.broadcast_to(limit[:, None], (live_all, DH)),
-        )
-
-    valid, limit_rows, limit_cols = masks(rank)
-    valid_other, limit_rows_other, limit_cols_other = masks(rank ^ 1)
-
     steps = live_all // SLOTS
     rows = live_all * HALF
     whole = pl.BlockSpec((keys, 2 * DH), lambda i: (0, 0))
     slot_block = pl.BlockSpec((SLOTS, half), lambda i: (i, 0))
     g_block = pl.BlockSpec((SLOTS, half), lambda i: (i, 1))
     lane_block = pl.BlockSpec((DH, ROWS), lambda i: (0, i))
-    limit_lane = pl.BlockSpec((8, SLOTS), lambda i: (0, i))
-    limit_slot = pl.BlockSpec((SLOTS, DH), lambda i: (i, 0))
     stat_block = pl.BlockSpec((3, ROWS), lambda i: (0, i))
 
     every = pl.BlockSpec((N_SEQ * slots, 2 * half), lambda i: (0, 0))
 
-    def forward(valid, limit, kv, more):
+    def forward(owner, kv, more):
         last = bool(more)
         return pl.pallas_call(
             functools.partial(first_pass, coef, last),
             grid=(steps,),
-            in_specs=[smem, limit_lane, slot_block, whole]
+            in_specs=[smem, smem, slot_block, whole]
             + [g_block, lane_block, stat_block] * last,
             out_specs=[slot_block if last else lane_block, stat_block],
             out_shape=[
@@ -377,21 +404,21 @@
                 flops=4 * rows * keys * DH, bytes_accessed=4 << 20, transcendentals=rows * keys
             ),
             name="attend_more" if last else "attend_own",
-        )(valid, limit, qg, kv, *more)
+        )(owner, starts, qg, kv, *more)
 
     pick = (source[:, None] == jnp.arange(N_SEQ * slots)[None, :]).astype(BF16)
     qg = jnp.dot(pick, qg_all, preferred_element_type=F32).astype(BF16)
-    state = forward(valid, limit_rows, kv, ())
-    out, stat = forward(valid_other, limit_rows_other, kv_other, (qg, *state))
+    state = forward(mine, kv, ())
+    out, stat = forward(others, kv_other, (qg, *state))
     stats = [stat] + [lax.ppermute(stat, "y", shift(k)) for k in range(1, NY)]
 
-    def backward(valid, limit, kv, more):
+    def backward(owner, kv, more):
         last = bool(more)
         return pl.pallas_call(
             functools.partial(second_pass, coef, scale, last),
             grid=(steps,),
             in_specs=[
-                smem, limit_slot, slot_block, g_block, whole,
+                smem, smem, slot_block, g_block, whole,
             ] + [stat_block] * NY + [smem, slot_block, slot_block] * last,
             out_specs=[
                 every if last else slot_block,
@@ -409,16 +436,16 @@
                 flops=10 * rows * keys * DH, bytes_accessed=8 << 20, transcendentals=rows * keys
             ),
             name="grads_own" if last else "grads_other",
-        )(valid, limit, qg, qg, kv, *stats, *more)
-
-    qgrad_part, kvgrad_other = backward(valid_other, limit_cols_other, kv_other, ())
+        )(owner, starts, qg, qg, kv, *stats, *more)
+
+    qgrad_part, kvgrad_other = backward(others, kv_other, ())
     kvgrad_got = lax.ppermute(kvgrad_other, "zl", SWAP)
-    back, kvgrad_own = backward(valid, limit_cols, kv, (starts, out, qgrad_part))
+    back, kvgrad_own = backward(mine, kv, (spans, out, qgrad_part))
 
     back, kvgrad_own = lax.optimization_barrier((back, kvgrad_own))
     back = lax.all_to_all(back.reshape(N_SEQ, slots, 2 * half), SEQ, 0, 0, tiled=True)
 
-    cuts = ((0, plen // 4), (plen // 4, 3 * plen // 4), (3 * plen // 4, plen))
+    cuts = ((0, plen // 2), (plen // 2, plen))
     piece = (2, 8 * shard, 2 * DH)
     *pieces, prompt_grad = pl.pallas_call(
         functools.partial(weight_kernel, cuts),
@@ -429,7 +456,6 @@
         + [jax.ShapeDtypeStruct((plen, 2 * DH), BF16)],
         scratch_shapes=[
             pltpu.VMEM((keys, model), BF16),
-            pltpu.VMEM((keys, 2 * DH), BF16),
             pltpu.VMEM((NX, model // NX, 2 * DH), F32),
             pltpu.SemaphoreType.DMA((len(cuts) + 1,)),
         ],

time: 160 us -> 157 us (0.981)
  local copies, waits for them, and re-layouts: 12.1 us -> 9.14 us
  waiting for transfers between devices: 42.2 us -> 39.4 us
  Pallas kernels: 52 us -> 54.2 us
    all_to_all x1, waiting for transfers between devices: 6.28 us -> 2.79 us  [per_device(): lax.all_to_all(block, PLANE, 0, 0, tiled=True).reshape(2, 8 * shard, 2 * DH)]
    broadcast_in_dim x6 -> x0, local copies, waits for them, and re-layouts: 3.33 us -> none  [the longest x1 1.57 us: per_device(): jnp.broadcast_to(qg[None], (NY, 2, slots, 2 * half))]
    unnamed x12 -> x16, local copies, waits for them, and re-layouts: 6.36 us -> 8.96 us
    another operation x2 -> x1, local copies, waits for them, and re-layouts: 2.3 us -> 0.1 us  [per_device(): spans = jnp.stack([first, behind], 1).astype(jnp.int32).reshape(-1)]
    pallas_call x0 -> x2, Pallas kernels: none -> 2.16 us  [the longest x1 1.41 us: per_device(): pl.pallas_call(halves_kernel, in_specs=[vmem] * 2, out_specs=pl.BlockSpec...]
  transfers between devices with their start and end apart: 23 -> 23, of which waited for: 11 -> 12; matrix products, arithmetic and copies ran while one was open for 5% -> 4% of each run, Pallas kernels for 22% -> 23%
where the time goes in v8:
time: 157 us; the launch traced here: 156 us
  Pallas kernels  54.2 us (35%)
  starting transfers between devices  44.5 us (28%)
  waiting for transfers between devices  39.4 us (25%)
  local copies, waits for them, and re-layouts  9.14 us (6%)
  other arithmetic  3.98 us (3%)
  matrix products  3.15 us (2%)
    pallas_call x2, Pallas kernels, backward(): pl.pallas_call(functools.partial(second_pass, coef, scale, last), grid=(s...  22.9 us
    pallas_call x2, Pallas kernels, forward(): pl.pallas_call(functools.partial(first_pass, coef, last), grid=(steps,),...  13.5 us
    ppermute x3, waiting for transfers between devices, per_device(): line = line + lax.ppermute(piece, 'x', shift(-k)).astype(F32)  13.4 us
    pallas_call x1, Pallas kernels, per_device(): pl.pallas_call(functools.partial(weight_kernel, cuts), in_specs=[smem] +...  9.21 us
    unnamed x16, local copies, waits for them, and re-layouts  8.96 us
    all_to_all x1, starting transfers between devices, per_device(): lax.all_to_all(block, PLANE, 0, 0, tiled=True).reshape(2, 8 * shard, 2 * DH)  8.13 us
    ppermute x3, waiting for transfers between devices, per_device(): nears = [block] + [lax.ppermute(block, 'x', shift(k)) for k in range(1, NX)]  8.11 us
    all_to_all x1, waiting for transfers between devices, per_device(): shares = lax.all_to_all(line, PLANE, 0, 0, tiled=True)  7.84 us
  transfers between devices with their start and end apart: 23, of which 12 were waited for; matrix products, arithmetic and copies ran while one was open for 4% of the time, Pallas kernels for 23%

profile of v8, /device:TPU:0, one launch (start us, length us, event | category | flops | bytes accessed | tf_op | source)
XLA Modules:
  0.0 155.8 jit_solution(429120470469627342)
XLA Ops:
  2.1 8.1 %all-to-all-start = ((bf16[16,40,256]{2,1,0:T(8,128)(2,1)}), bf16[16,40,256]{2,1,0:T(8,128)(2,1)S(1)}, u32[]{:S(2)}, u32[]{:S(2)}) async-start(bf16[16,40,256]{2,1,0:T(8,128)(2,1)} %weight_copies.1), calls=%async_computation | async-start | bytes 655360 | tf_op jit(solution)/shard_map/all_to_all | solution.py:331
  16.6 2.8 %all-to-all-done = bf16[16,40,256]{2,1,0:T(8,128)(2,1)S(1)} async-done(((bf16[16,40,256]{2,1,0:T(8,128)(2,1)}), bf16[16,40,256]{2,1,0:T(8,128)(2,1)S(1)}, u32[]{:S(2)}, u32[]{:S(2)}) %all-to-all-start) | async-done | bytes 327712 | tf_op jit(solution)/shard_map/all_to_all | solution.py:331
  19.4 4.5 %all-to-all-start.1 = ((bf16[8,128,1024]{2,1,0:T(8,128)(2,1)}), bf16[8,128,1024]{2,1,0:T(8,128)(2,1)}, u32[]{:S(2)}, u32[]{:S(2)}) async-start(bf16[8,128,1024]{2,1,0:T(8,128)(2,1)} %query_halves.1), calls=%async_computation.1 | async-start | bytes 4194304 | tf_op jit(solution)/shard_map/all_to_all | solution.py:348
  24.0 1.6 %collective-permute-start.4 = (bf16[2,320,256]{2,1,0:T(8,128)(2,1)S(1)}, bf16[2,320,256]{2,1,0:T(8,128)(2,1)S(1)}, u32[]{:S(2)}, u32[]{:S(2)}) collective-permute-start(bf16[2,320,256]{2,1,0:T(8,128)(2,1)S(1)} %bitcast.43), channel_id=1, source_target_pairs={{96,0},{0,32},{32,64},{64,96},{97,1},{1,33},{33,65},{65,97},{98,2}... | collective-permute-start | bytes 983048 | tf_op jit(solution)/shard_map/ppermute | solution.py:346
  25.6 2.7 %collective-permute-start.1 = (bf16[2,320,256]{2,1,0:T(8,128)(2,1)S(1)}, bf16[2,320,256]{2,1,0:T(8,128)(2,1)S(1)}, u32[]{:S(2)}, u32[]{:S(2)}) collective-permute-start(bf16[2,320,256]{2,1,0:T(8,128)(2,1)S(1)} %bitcast.44), channel_id=1, source_target_pairs={{64,0},{96,32},{0,64},{32,96},{65,1},{97,33},{1,65},{33,97},{66,2}... | collective-permute-start | bytes 983048 | tf_op jit(solution)/shard_map/ppermute | solution.py:346
  29.7 4.0 %copy-done = bf16[1,1024,5120]{2,1,0:T(8,128)(2,1)S(1)} copy-done((bf16[1,1024,5120]{2,1,0:T(8,128)(2,1)S(1)}, bf16[1,1024,5120]{2,1,0:T(8,128)(2,1)}, u32[]{:S(2)}) %copy-start) | copy-done | bytes 10485784
  35.3 8.0 %collective-permute-done.1.refs_1_ = bf16[2,320,256]{2,1,0:T(8,128)(2,1)S(1)} collective-permute-done((bf16[2,320,256]{2,1,0:T(8,128)(2,1)S(1)}, bf16[2,320,256]{2,1,0:T(8,128)(2,1)S(1)}, u32[]{:S(2)}, u32[]{:S(2)}) %collective-permute-start.1) | collective-permute-done | bytes 327712 | tf_op jit(solution)/shard_map/ppermute | solution.py:346
  45.4 2.4 %project_last.1.refs_1_.kv_ref = bf16[1152,256]{1,0:T(8,128)(2,1)S(1)} custom-call(s32[2]{0:T(128)S(1)} %get-tuple-element.35.place_ref, bf16[1024,5120]{1,0:T(8,128)(2,1)S(1)} %bitcast.36, bf16[128,5120]{1,0:T(8,128)(2,1)S(1)} %bitcast.40, bf16[2,320,256]{2,1,0:T(8,128)(2,1)S(1)} %collective-permute-done.refs_0_, ...), custom_call_target="tpu_custom_call" | custom-call | flops 1509949440 | bytes 5898240 | tf_op jit(solution)/shard_map/project_last/pallas_call | solution.py:352
  47.8 1.9 %collective-permute-start.7 = (bf16[1152,256]{1,0:T(8,128)(2,1)S(1)}, bf16[1152,256]{1,0:T(8,128)(2,1)S(1)}, u32[]{:S(2)}, u32[]{:S(2)}) collective-permute-start(bf16[1152,256]{1,0:T(8,128)(2,1)S(1)} %project_last.1.refs_1_.kv_ref), channel_id=1, source_target_pairs={{0,1},{1,0},{2,3},{3,2},{4,5},{5,4},{6,7},{7,6},{8,9},{9,8},{10,11... | collective-permute-start | bytes 1769480 | tf_op jit(solution)/shard_map/ppermute | solution.py:375
  49.7 3.2 %all-to-all-done.1 = bf16[8,128,1024]{2,1,0:T(8,128)(2,1)} async-done(((bf16[8,128,1024]{2,1,0:T(8,128)(2,1)}), bf16[8,128,1024]{2,1,0:T(8,128)(2,1)}, u32[]{:S(2)}, u32[]{:S(2)}) %all-to-all-start.1) | async-done | bytes 2097184 | tf_op jit(solution)/shard_map/all_to_all | solution.py:348
  52.9 3.1 %fusion.1.refs_0_.refs_2_.q_ref.g_ref = bf16[640,1024]{1,0:T(8,128)(2,1)S(1)} fusion(bf16[1024,1024]{1,0:T(8,128)(2,1)} %bitcast.17, s32[640]{0:T(1024)S(1)} %iota_add_fusion), kind=kOutput, calls=%fused_computation.2 | convolution fusion | flops 1343488000 | bytes 3410432 | tf_op jit(solution)/shard_map/dot_general | solution.py:410
  56.0 6.4 %attend_own.1 = (f32[128,2560]{1,0:T(8,128)S(1)}, f32[3,2560]{1,0:T(4,128)S(1)}) custom-call(s32[2]{0:T(128)S(1)} %get-tuple-element.36.info_ref, s32[9]{0:T(128)S(1)} %pad_add_fusion.2.start_ref, bf16[640,1024]{1,0:T(8,128)(2,1)S(1)} %fusion.1.refs_0_.refs_2_.q_ref.g_ref, bf16[1152,256]{1,0:T(8,128)(2,1)S(1)} %project_last.1.refs_1_.kv_ref), custom_call_target="tpu_custom_call" | custom-call | flops 1509949440 | bytes 4194304 | tf_op jit(solution)/shard_map/attend_own/pallas_call | solution.py:389
  63.3 7.1 %attend_more.1 = (bf16[640,512]{1,0:T(8,128)(2,1)S(1)}, f32[3,2560]{1,0:T(4,128)S(1)}) custom-call(s32[2]{0:T(128)S(1)} %pad_add_fusion.4.info_ref, s32[9]{0:T(128)S(1)} %pad_add_fusion.2.start_ref, bf16[640,1024]{1,0:T(8,128)(2,1)S(1)} %fusion.1.refs_0_.refs_2_.q_ref.g_ref, bf16[1152,256]{1,0:T(8,128)(2,1)S(1)} %collective-permute-done.7.refs_1_.kv_ref, ...), custom_call_target="tpu_custom_call" | custom-call | flops 1509949440 | bytes 4194304 | tf_op jit(solution)/shard_map/attend_more/pallas_call | solution.py:389
  70.4 1.8 %collective-permute-start.10 = (f32[3,2560]{1,0:T(4,128)S(1)}, f32[3,2560]{1,0:T(4,128)S(1)}, u32[]{:S(2)}, u32[]{:S(2)}) collective-permute-start(f32[3,2560]{1,0:T(4,128)S(1)} %get-tuple-element.46.refs_0_), channel_id=1, source_target_pairs={{6,0},{0,2},{2,4},{4,6},{7,1},{1,3},{3,5},{5,7},{14,8},{8,10},{10,... | collective-permute-start | bytes 92168 | tf_op jit(solution)/shard_map/ppermute | solution.py:413
  72.2 2.7 %collective-permute-start.9 = (f32[3,2560]{1,0:T(4,128)S(1)}, f32[3,2560]{1,0:T(4,128)S(1)}, u32[]{:S(2)}, u32[]{:S(2)}) collective-permute-start(f32[3,2560]{1,0:T(4,128)S(1)} %get-tuple-element.46.refs_0_), channel_id=1, source_target_pairs={{4,0},{6,2},{0,4},{2,6},{5,1},{7,3},{1,5},{3,7},{12,8},{14,10},{8,... | collective-permute-start | bytes 92168 | tf_op jit(solution)/shard_map/ppermute | solution.py:413
  78.9 10.2 %grads_other.1 = (f32[640,512]{1,0:T(8,128)S(1)}, bf16[1152,256]{1,0:T(8,128)(2,1)S(1)}) custom-call(s32[2]{0:T(128)S(1)} %pad_add_fusion.4.info_ref, s32[9]{0:T(128)S(1)} %pad_add_fusion.2.start_ref, bf16[640,1024]{1,0:T(8,128)(2,1)S(1)} %fusion.1.refs_0_.refs_2_.q_ref.g_ref, bf16[640,1024]{1,0:T(8,128)(2,1)S(1)} %fusion.1.refs_0_.refs_2_.q_ref.g_ref, ...), custom_call_target="tpu_custom_call" | custom-call | flops 3774873600 | bytes 8388608 | tf_op jit(solution)/shard_map/grads_other/pallas_call | solution.py:417
  90.7 12.7 %grads_own.1 = (bf16[1024,1024]{1,0:T(8,128)(2,1)S(1)}, f32[1152,256]{1,0:T(8,128)S(1)}) custom-call(s32[2]{0:T(128)S(1)} %get-tuple-element.36.info_ref, s32[9]{0:T(128)S(1)} %pad_add_fusion.2.start_ref, bf16[640,1024]{1,0:T(8,128)(2,1)S(1)} %fusion.1.refs_0_.refs_2_.q_ref.g_ref, bf16[640,1024]{1,0:T(8,128)(2,1)S(1)} %fusion.1.refs_0_.refs_2_.q_ref.g_ref, ...), custom_call_target="tpu_custom_call" | custom-call | flops 3774873600 | bytes 8388608 | tf_op jit(solution)/shard_map/grads_own/pallas_call | solution.py:417
  105.8 4.0 %all-to-all-start.2 = ((bf16[8,128,1024]{2,1,0:T(8,128)(2,1)}), bf16[8,128,1024]{2,1,0:T(8,128)(2,1)S(1)}, u32[]{:S(2)}, u32[]{:S(2)}) async-start(bf16[8,128,1024]{2,1,0:T(8,128)(2,1)} %bitcast.41), calls=%async_computation.2 | async-start | bytes 4194304 | tf_op jit(solution)/shard_map/all_to_all | solution.py:446
  109.7 9.2 %weight_grad.1 = (f32[2,320,256]{2,1,0:T(8,128)S(1)}, f32[2,320,256]{2,1,0:T(8,128)S(1)}, f32[2,320,256]{2,1,0:T(8,128)S(1)}, f32[2,320,256]{2,1,0:T(8,128)}, bf...) custom-call(s32[2]{0:T(128)S(1)} %get-tuple-element.35.place_ref, ...), custom_call_target="tpu_custom_call" | custom-call | flops 3019898880 | bytes 11796480 | tf_op jit(solution)/shard_map/weight_grad/pallas_call | solution.py:450
  122.1 2.7 %collective-permute-start.16 = (bf16[2,320,256]{2,1,0:T(8,128)(2,1)S(1)}, bf16[2,320,256]{2,1,0:T(8,128)(2,1)S(1)}, u32[]{:S(2)}, u32[]{:S(2)}) collective-permute-start(bf16[2,320,256]{2,1,0:T(8,128)(2,1)S(1)} %add_convert_fusion.2), channel_id=1, source_target_pairs={{64,0},{96,32},{0,64},{32,96},{65,1},{97,33},{1,65},{33,97},{66,2}... | collective-permute-start | bytes 983048 | tf_op jit(solution)/shard_map/ppermute | solution.py:473
  126.2 5.8 %collective-permute-done.14 = bf16[2,320,256]{2,1,0:T(8,128)(2,1)S(1)} collective-permute-done((bf16[2,320,256]{2,1,0:T(8,128)(2,1)S(1)}, bf16[2,320,256]{2,1,0:T(8,128)(2,1)S(1)}, u32[]{:S(2)}, u32[]{:S(2)}) %collective-permute-start.14) | collective-permute-done | bytes 327712 | tf_op jit(solution)/shard_map/ppermute | solution.py:473
  132.0 7.3 %collective-permute-done.16 = bf16[2,320,256]{2,1,0:T(8,128)(2,1)S(1)} collective-permute-done((bf16[2,320,256]{2,1,0:T(8,128)(2,1)S(1)}, bf16[2,320,256]{2,1,0:T(8,128)(2,1)S(1)}, u32[]{:S(2)}, u32[]{:S(2)}) %collective-permute-start.16) | collective-permute-done | bytes 327712 | tf_op jit(solution)/shard_map/ppermute | solution.py:473
  140.5 5.8 %all-to-all-start.3 = ((bf16[16,40,256]{2,1,0:T(8,128)(2,1)}), bf16[16,40,256]{2,1,0:T(8,128)(2,1)S(1)}, u32[]{:S(2)}, u32[]{:S(2)}) async-start(bf16[16,40,256]{2,1,0:T(8,128)(2,1)} %bitcast.20), calls=%async_computation.3 | async-start | bytes 655360 | tf_op jit(solution)/shard_map/all_to_all | solution.py:476
  147.3 7.8 %all-to-all-done.3 = bf16[16,40,256]{2,1,0:T(8,128)(2,1)S(1)} async-done(((bf16[16,40,256]{2,1,0:T(8,128)(2,1)}), bf16[16,40,256]{2,1,0:T(8,128)(2,1)S(1)}, u32[]{:S(2)}, u32[]{:S(2)}) %all-to-all-start.3) | async-done | bytes 327712 | tf_op jit(solution)/shard_map/all_to_all | solution.py:476
  (69 shorter events, 28.5 us)
Async XLA Ops:
  2.1 17.3 %all-to-all-start = ((bf16[16,40,256]{2,1,0:T(8,128)(2,1)}), bf16[16,40,256]{2,1,0:T(8,128)(2,1)S(1)}, u32[]{:S(2)}, u32[]{:S(2)}) async-start(bf16[16,40,256]{2,1,0:T(8,128)(2,1)} %weight_copies.1), calls=%async_computation | async-start | bytes 655360 | tf_op jit(solution)/shard_map/all_to_all | solution.py:331
  19.4 10.3 %copy-start.1 = (bf16[1,128,5120]{2,1,0:T(8,128)(2,1)S(1)}, bf16[1,128,5120]{2,1,0:T(8,128)(2,1)}, u32[]{:S(2)}) copy-start(bf16[1,128,5120]{2,1,0:T(8,128)(2,1)} %param.8) | copy-start | bytes 3932164
  19.4 33.4 %all-to-all-start.1 = ((bf16[8,128,1024]{2,1,0:T(8,128)(2,1)}), bf16[8,128,1024]{2,1,0:T(8,128)(2,1)}, u32[]{:S(2)}, u32[]{:S(2)}) async-start(bf16[8,128,1024]{2,1,0:T(8,128)(2,1)} %query_halves.1), calls=%async_computation.1 | async-start | bytes 4194304 | tf_op jit(solution)/shard_map/all_to_all | solution.py:348
  23.9 5.8 %collective-permute-start.5 = (bf16[2,320,256]{2,1,0:T(8,128)(2,1)S(1)}, bf16[2,320,256]{2,1,0:T(8,128)(2,1)S(1)}, u32[]{:S(2)}, u32[]{:S(2)}) collective-permute-start(bf16[2,320,256]{2,1,0:T(8,128)(2,1)S(1)} %bitcast.42), channel_id=1, source_target_pairs={{0,8},{8,0},{1,9},{9,1},{2,10},{10,2},{3,11},{11,3},{4,12},{12,4},... | collective-permute-start | bytes 983048 | tf_op jit(solution)/shard_map/ppermute | solution.py:347
  24.0 11.3 %collective-permute-start.4 = (bf16[2,320,256]{2,1,0:T(8,128)(2,1)S(1)}, bf16[2,320,256]{2,1,0:T(8,128)(2,1)S(1)}, u32[]{:S(2)}, u32[]{:S(2)}) collective-permute-start(bf16[2,320,256]{2,1,0:T(8,128)(2,1)S(1)} %bitcast.43), channel_id=1, source_target_pairs={{96,0},{0,32},{32,64},{64,96},{97,1},{1,33},{33,65},{65,97},{98,2}... | collective-permute-start | bytes 983048 | tf_op jit(solution)/shard_map/ppermute | solution.py:346
  25.6 17.8 %collective-permute-start.1 = (bf16[2,320,256]{2,1,0:T(8,128)(2,1)S(1)}, bf16[2,320,256]{2,1,0:T(8,128)(2,1)S(1)}, u32[]{:S(2)}, u32[]{:S(2)}) collective-permute-start(bf16[2,320,256]{2,1,0:T(8,128)(2,1)S(1)} %bitcast.44), channel_id=1, source_target_pairs={{64,0},{96,32},{0,64},{32,96},{65,1},{97,33},{1,65},{33,97},{66,2}... | collective-permute-start | bytes 983048 | tf_op jit(solution)/shard_map/ppermute | solution.py:346
  28.3 15.1 %collective-permute-start = (bf16[2,320,256]{2,1,0:T(8,128)(2,1)S(1)}, bf16[2,320,256]{2,1,0:T(8,128)(2,1)S(1)}, u32[]{:S(2)}, u32[]{:S(2)}) collective-permute-start(bf16[2,320,256]{2,1,0:T(8,128)(2,1)S(1)} %bitcast.45), channel_id=1, source_target_pairs={{32,0},{64,32},{96,64},{0,96},{33,1},{65,33},{97,65},{1,97},{34,2}... | collective-permute-start | bytes 983048 | tf_op jit(solution)/shard_map/ppermute | solution.py:346
  35.3 8.5 %collective-permute-start.6 = (bf16[2,320,256]{2,1,0:T(8,128)(2,1)S(1)}, bf16[2,320,256]{2,1,0:T(8,128)(2,1)S(1)}, u32[]{:S(2)}, u32[]{:S(2)}) collective-permute-start(bf16[2,320,256]{2,1,0:T(8,128)(2,1)S(1)} %collective-permute-done.4.refs_0_), channel_id=1, source_target_pairs={{0,8},{8,0},{1,9},{9,1},{2,10},{10,2},{3,11},{11,3},{4,12},{12,4},... | collective-permute-start | bytes 983048 | tf_op jit(solution)/shard_map/ppermute | solution.py:372
  43.3 2.1 %collective-permute-start.3 = (bf16[2,320,256]{2,1,0:T(8,128)(2,1)S(1)}, bf16[2,320,256]{2,1,0:T(8,128)(2,1)S(1)}, u32[]{:S(2)}, u32[]{:S(2)}) collective-permute-start(bf16[2,320,256]{2,1,0:T(8,128)(2,1)S(1)} %collective-permute-done.1.refs_1_), channel_id=1, source_target_pairs={{0,8},{8,0},{1,9},{9,1},{2,10},{10,2},{3,11},{11,3},{4,12},{12,4},... | collective-permute-start | bytes 983048 | tf_op jit(solution)/shard_map/ppermute | solution.py:372
  43.3 2.1 %collective-permute-start.2 = (bf16[2,320,256]{2,1,0:T(8,128)(2,1)S(1)}, bf16[2,320,256]{2,1,0:T(8,128)(2,1)S(1)}, u32[]{:S(2)}, u32[]{:S(2)}) collective-permute-start(bf16[2,320,256]{2,1,0:T(8,128)(2,1)S(1)} %collective-permute-done.refs_0_), channel_id=1, source_target_pairs={{0,8},{8,0},{1,9},{9,1},{2,10},{10,2},{3,11},{11,3},{4,12},{12,4},... | collective-permute-start | bytes 983048 | tf_op jit(solution)/shard_map/ppermute | solution.py:372
  47.8 15.5 %collective-permute-start.7 = (bf16[1152,256]{1,0:T(8,128)(2,1)S(1)}, bf16[1152,256]{1,0:T(8,128)(2,1)S(1)}, u32[]{:S(2)}, u32[]{:S(2)}) collective-permute-start(bf16[1152,256]{1,0:T(8,128)(2,1)S(1)} %project_last.1.refs_1_.kv_ref), channel_id=1, source_target_pairs={{0,1},{1,0},{2,3},{3,2},{4,5},{5,4},{6,7},{7,6},{8,9},{9,8},{10,11... | collective-permute-start | bytes 1769480 | tf_op jit(solution)/shard_map/ppermute | solution.py:375
  70.4 6.0 %collective-permute-start.10 = (f32[3,2560]{1,0:T(4,128)S(1)}, f32[3,2560]{1,0:T(4,128)S(1)}, u32[]{:S(2)}, u32[]{:S(2)}) collective-permute-start(f32[3,2560]{1,0:T(4,128)S(1)} %get-tuple-element.46.refs_0_), channel_id=1, source_target_pairs={{6,0},{0,2},{2,4},{4,6},{7,1},{1,3},{3,5},{5,7},{14,8},{8,10},{10,... | collective-permute-start | bytes 92168 | tf_op jit(solution)/shard_map/ppermute | solution.py:413
  72.2 5.5 %collective-permute-start.9 = (f32[3,2560]{1,0:T(4,128)S(1)}, f32[3,2560]{1,0:T(4,128)S(1)}, u32[]{:S(2)}, u32[]{:S(2)}) collective-permute-start(f32[3,2560]{1,0:T(4,128)S(1)} %get-tuple-element.46.refs_0_), channel_id=1, source_target_pairs={{4,0},{6,2},{0,4},{2,6},{5,1},{7,3},{1,5},{3,7},{12,8},{14,10},{8,... | collective-permute-start | bytes 92168 | tf_op jit(solution)/shard_map/ppermute | solution.py:413
  74.9 4.0 %collective-permute-start.8 = (f32[3,2560]{1,0:T(4,128)S(1)}, f32[3,2560]{1,0:T(4,128)S(1)}, u32[]{:S(2)}, u32[]{:S(2)}) collective-permute-start(f32[3,2560]{1,0:T(4,128)S(1)} %get-tuple-element.46.refs_0_), channel_id=1, source_target_pairs={{2,0},{4,2},{6,4},{0,6},{3,1},{5,3},{7,5},{1,7},{10,8},{12,10},{14... | collective-permute-start | bytes 92168 | tf_op jit(solution)/shard_map/ppermute | solution.py:413
  89.2 20.6 %collective-permute-start.11 = (bf16[1152,256]{1,0:T(8,128)(2,1)S(1)}, bf16[1152,256]{1,0:T(8,128)(2,1)S(1)}, u32[]{:S(2)}, u32[]{:S(2)}) collective-permute-start(bf16[1152,256]{1,0:T(8,128)(2,1)S(1)} %get-tuple-element.51), channel_id=1, source_target_pairs={{0,1},{1,0},{2,3},{3,2},{4,5},{5,4},{6,7},{7,6},{8,9},{9,8},{10,11... | collective-permute-start | bytes 1769480 | tf_op jit(solution)/shard_map/ppermute | solution.py:442
  105.8 34.7 %all-to-all-start.2 = ((bf16[8,128,1024]{2,1,0:T(8,128)(2,1)}), bf16[8,128,1024]{2,1,0:T(8,128)(2,1)S(1)}, u32[]{:S(2)}, u32[]{:S(2)}) async-start(bf16[8,128,1024]{2,1,0:T(8,128)(2,1)} %bitcast.41), calls=%async_computation.2 | async-start | bytes 4194304 | tf_op jit(solution)/shard_map/all_to_all | solution.py:446
  119.0 1.7 %collective-permute-start.13 = (bf16[2,320,256]{2,1,0:T(8,128)(2,1)S(1)}, bf16[2,320,256]{2,1,0:T(8,128)(2,1)S(1)}, u32[]{:S(2)}, u32[]{:S(2)}) collective-permute-start(bf16[2,320,256]{2,1,0:T(8,128)(2,1)S(1)} %get-tuple-element.55), channel_id=1, source_target_pairs={{0,8},{8,0},{1,9},{9,1},{2,10},{10,2},{3,11},{11,3},{4,12},{12,4},... | collective-permute-start | bytes 983048 | tf_op jit(solution)/shard_map/ppermute | solution.py:469
  119.0 2.9 %collective-permute-start.15 = (bf16[2,320,256]{2,1,0:T(8,128)(2,1)S(1)}, bf16[2,320,256]{2,1,0:T(8,128)(2,1)S(1)}, u32[]{:S(2)}, u32[]{:S(2)}) collective-permute-start(bf16[2,320,256]{2,1,0:T(8,128)(2,1)S(1)} %get-tuple-element.57), channel_id=1, source_target_pairs={{0,8},{8,0},{1,9},{9,1},{2,10},{10,2},{3,11},{11,3},{4,12},{12,4},... | collective-permute-start | bytes 983048 | tf_op jit(solution)/shard_map/ppermute | solution.py:469
  119.5 6.7 %collective-permute-start.12 = (bf16[2,320,256]{2,1,0:T(8,128)(2,1)S(1)}, bf16[2,320,256]{2,1,0:T(8,128)(2,1)S(1)}, u32[]{:S(2)}, u32[]{:S(2)}) collective-permute-start(bf16[2,320,256]{2,1,0:T(8,128)(2,1)S(1)} %get-tuple-element.53), channel_id=1, source_target_pairs={{0,8},{8,0},{1,9},{9,1},{2,10},{10,2},{3,11},{11,3},{4,12},{12,4},... | collective-permute-start | bytes 983048 | tf_op jit(solution)/shard_map/ppermute | solution.py:469
  119.6 5.1 %collective-permute-start.17 = (bf16[2,320,256]{2,1,0:T(8,128)(2,1)S(1)}, bf16[2,320,256]{2,1,0:T(8,128)(2,1)S(1)}, u32[]{:S(2)}, u32[]{:S(2)}) collective-permute-start(bf16[2,320,256]{2,1,0:T(8,128)(2,1)S(1)} %get-tuple-element.59), channel_id=1, source_target_pairs={{0,8},{8,0},{1,9},{9,1},{2,10},{10,2},{3,11},{11,3},{4,12},{12,4},... | collective-permute-start | bytes 983048 | tf_op jit(solution)/shard_map/ppermute | solution.py:469
  120.7 11.3 %collective-permute-start.14 = (bf16[2,320,256]{2,1,0:T(8,128)(2,1)S(1)}, bf16[2,320,256]{2,1,0:T(8,128)(2,1)S(1)}, u32[]{:S(2)}, u32[]{:S(2)}) collective-permute-start(bf16[2,320,256]{2,1,0:T(8,128)(2,1)S(1)} %add_convert_fusion.3), channel_id=1, source_target_pairs={{96,0},{0,32},{32,64},{64,96},{97,1},{1,33},{33,65},{65,97},{98,2}... | collective-permute-start | bytes 983048 | tf_op jit(solution)/shard_map/ppermute | solution.py:473
  122.1 17.3 %collective-permute-start.16 = (bf16[2,320,256]{2,1,0:T(8,128)(2,1)S(1)}, bf16[2,320,256]{2,1,0:T(8,128)(2,1)S(1)}, u32[]{:S(2)}, u32[]{:S(2)}) collective-permute-start(bf16[2,320,256]{2,1,0:T(8,128)(2,1)S(1)} %add_convert_fusion.2), channel_id=1, source_target_pairs={{64,0},{96,32},{0,64},{32,96},{65,1},{97,33},{1,65},{33,97},{66,2}... | collective-permute-start | bytes 983048 | tf_op jit(solution)/shard_map/ppermute | solution.py:473
  124.8 14.8 %collective-permute-start.18 = (bf16[2,320,256]{2,1,0:T(8,128)(2,1)S(1)}, bf16[2,320,256]{2,1,0:T(8,128)(2,1)S(1)}, u32[]{:S(2)}, u32[]{:S(2)}) collective-permute-start(bf16[2,320,256]{2,1,0:T(8,128)(2,1)S(1)} %add_convert_fusion.1), channel_id=1, source_target_pairs={{32,0},{64,32},{96,64},{0,96},{33,1},{65,33},{97,65},{1,97},{34,2}... | collective-permute-start | bytes 983048 | tf_op jit(solution)/shard_map/ppermute | solution.py:473
  140.5 14.6 %all-to-all-start.3 = ((bf16[16,40,256]{2,1,0:T(8,128)(2,1)}), bf16[16,40,256]{2,1,0:T(8,128)(2,1)S(1)}, u32[]{:S(2)}, u32[]{:S(2)}) async-start(bf16[16,40,256]{2,1,0:T(8,128)(2,1)} %bitcast.20), calls=%async_computation.3 | async-start | bytes 655360 | tf_op jit(solution)/shard_map/all_to_all | solution.py:476
  (7 other events, 14.8 us)

commit v9 on v8

--- a/solution.py
+++ b/solution.py
@@ -95,13 +95,7 @@
     return jnp.where((row == slot) & (row < start_ref[r + 1]), 1.0, 0.0).astype(BF16)
 
 
-def visible(start_ref, r, block, row_axis):
-    row = lax.broadcasted_iota(jnp.int32, (SLOTS, SLOTS), row_axis) + block * SLOTS
-    slot = lax.broadcasted_iota(jnp.int32, (SLOTS, SLOTS), 1 - row_axis) + start_ref[r]
-    return (slot <= row) & (row < start_ref[r + 1])
-
-
-def first_pass(coef, last, info_ref, start_ref, *refs):
+def first_pass(coef, last, bound_ref, *refs):
     if last:
         q_ref, kv_ref, g_ref, prev_out_ref, prev_stat_ref, out_ref, stat_ref, bias, values = refs
     else:
@@ -111,10 +105,11 @@
     @pl.when(pl.program_id(0) == 0)
     def _():
         place = lax.broadcasted_iota(jnp.int32, (plen, DH), 0)
-        bias[...] = jnp.where(place < info_ref[0], 0.0, NEG)
+        bias[...] = jnp.where(place < bound_ref[8:9], 0.0, NEG)
         values[...] = kv_ref[:, DH:].T
 
-    causal = jnp.where(visible(start_ref, info_ref[1], pl.program_id(0), 1), 0.0, NEG)
+    slot = lax.broadcasted_iota(jnp.int32, (DH, SLOTS), 0)
+    causal = jnp.where(slot <= bound_ref[0:1], 0.0, NEG)
     bias_all = jnp.concatenate([bias[...], causal], 0)
     bias_all = jnp.concatenate([bias_all] * 2, 1)
     keys = kv_ref[:, :DH]
@@ -153,10 +148,10 @@
         stat_ref[1:2, lanes] = total
 
 
-def second_pass(coef, scale, last, info_ref, start_ref, q_ref, g_ref, kv_ref, *refs):
+def second_pass(coef, scale, last, bound_ref, q_ref, g_ref, kv_ref, *refs):
     stat_refs, refs = refs[:NY], refs[NY:]
     if last:
-        span_ref, out_ref, prev_ref, back_ref, kvgrad_ref, acc, bias = refs
+        layout_ref, out_ref, prev_ref, back_hbm, kvgrad_hbm, acc, bias, back_ref, total_ref, sems = refs
     else:
         back_ref, kvgrad_ref, acc, bias = refs
     step = pl.program_id(0)
@@ -175,15 +170,16 @@
     def _():
         acc[...] = jnp.zeros_like(acc)
         place = lax.broadcasted_iota(jnp.int32, (8, plen), 1)
-        bias[...] = jnp.where(place < info_ref[0], 0.0, NEG)
+        bias[...] = jnp.where(place < bound_ref[8:16, 0:1], 0.0, NEG)
 
     c_top, c_inv, c_delta = columns[:, 0:1], columns[:, 1:2], columns[:, 2:3]
     q = stack_heads(q_ref)
     g = stack_heads(g_ref)
     qt = q.T
     gt = g.T
-    seen = visible(start_ref, info_ref[1], step, 0)
-    causal = jnp.concatenate([jnp.where(seen, 0.0, NEG)] * HALF, 0)
+    slot = lax.broadcasted_iota(jnp.int32, (DH, SLOTS), 0)
+    hidden_slots = jnp.where(slot <= bound_ref[0:1], 0.0, NEG).T
+    causal = jnp.concatenate([hidden_slots] * HALF, 0)
     chunk = 256
     cuts = [slice(i, i + chunk) for i in range(0, plen, chunk)] + [slice(plen, plen + DH)]
 
@@ -221,20 +217,38 @@
         def _():
             back_ref[...] = jnp.zeros_like(back_ref)
 
+        def leave(r):
+            slots = pl.ds(pl.multiple_of(r * SLOTS, SLOTS), SLOTS)
+            return pltpu.make_async_copy(back_ref.at[slots], back_hbm.at[slots], sems.at[r])
+
         def place(r, _):
             slots = pl.ds(pl.multiple_of(r * SLOTS, SLOTS), SLOTS)
-            onehot = one_hot(start_ref, r, step)
+            onehot = one_hot(layout_ref, r, step)
             back_ref[slots] += jnp.dot(onehot, back, preferred_element_type=F32).astype(BF16)
+
+            @pl.when(layout_ref[r + 1] <= (step + 1) * SLOTS)
+            def _():
+                leave(r).start()
+
             return 0
 
-        lax.fori_loop(span_ref[2 * step], span_ref[2 * step + 1], place, 0)
+        base = N_SEQ + 1 + 2 * step
+        lax.fori_loop(layout_ref[base], layout_ref[base + 1], place, 0)
     else:
         for r in parts:
             back_ref[:, r] = dq[r]
 
     @pl.when(step == pl.num_programs(0) - 1)
     def _():
-        kvgrad_ref[...] = acc[...].T.astype(kvgrad_ref.dtype)
+        if last:
+            total_ref[...] = acc[...].T
+            copy = pltpu.make_async_copy(total_ref, kvgrad_hbm, sems.at[N_SEQ])
+            copy.start()
+            for r in range(N_SEQ):
+                leave(r).wait()
+            copy.wait()
+        else:
+            kvgrad_ref[...] = acc[...].T.astype(BF16)
 
 
 def weight_kernel(cuts, place_ref, own_ref, got_ref, prompt_ref, resp_ref, *refs):
@@ -255,23 +269,25 @@
     prompt_grad_ref[...] = grad[:plen]
     grad = grad.T
     spans = list(cuts[:-1]) + [(cuts[-1][0], buf.shape[0])]
+    swapped = core == 1
     for n, (lo, hi) in enumerate(spans):
         copies[n].wait()
         if n + 1 == len(spans):
             copies[n + 1].wait()
         for k in range(NX):
             cols = pl.ds(pl.multiple_of(lax.rem(x + k, NX) * wide, DH), wide)
-            t = jnp.dot(grad[:, lo:hi], buf[lo:hi, cols], preferred_element_type=F32).T
+            t = jnp.dot(grad[:, lo:hi], buf[lo:hi, cols], preferred_element_type=F32)
             if n:
                 t = t + whole[k]
-            whole[k] = t
-            if n + 1 == len(spans):
-                for z in range(2):
-                    base = z * 2 * part
-                    mine = pl.ds(pl.multiple_of(base + core * part, part), part)
-                    theirs = pl.ds(pl.multiple_of(base + (1 - core) * part, part), part)
-                    keeps[k][z] = whole[k, mine]
-                    gives[k][z] = whole[k, theirs].astype(BF16)
+            if n + 1 < len(spans):
+                whole[k] = t
+                continue
+            t = t.T
+            for z in range(2):
+                low = t[2 * z * part : (2 * z + 1) * part]
+                high = t[(2 * z + 1) * part : (2 * z + 2) * part]
+                keeps[k][z] = jnp.where(swapped, high, low)
+                gives[k][z] = jnp.where(swapped, low, high).astype(BF16)
 
 
 def finish_kernel(back_ref, attended_ref, query_grad_ref):
@@ -302,6 +318,7 @@
     shard = kv_weight.shape[0]
     smem = pl.BlockSpec(memory_space=pltpu.SMEM)
     vmem = pl.BlockSpec(memory_space=pltpu.VMEM)
+    hbm = pl.BlockSpec(memory_space=pltpu.HBM)
 
     lengths = response_lengths[0]
     live_all = slots * N_SEQ * 5 // 8
@@ -314,11 +331,15 @@
     first = jnp.sum(ends[None, :] <= lows, 1)
     behind = jnp.sum((ends - lengths)[None, :] < lows + SLOTS, 1)
     spans = jnp.stack([first, behind], 1).astype(jnp.int32).reshape(-1)
-
-    def info(owner):
-        return jnp.stack([prompt_lengths[0] - plen * owner, owner]).astype(jnp.int32)
-
-    mine, others = info(rank), info(rank ^ 1)
+    layout = jnp.concatenate([starts, spans])
+
+    def bounds(owner):
+        offset = source - owner * slots
+        limit = jnp.where((offset >= 0) & (offset < slots), offset, -1)
+        live = jnp.broadcast_to(prompt_lengths[0] - plen * owner, (8, live_all))
+        return jnp.concatenate([jnp.broadcast_to(limit[None, :], (8, live_all)), live], 0).astype(jnp.int32)
+
+    mine, others = bounds(rank), bounds(rank ^ 1)
 
     block = pl.pallas_call(
         copies_kernel,
@@ -340,9 +361,9 @@
         cost_estimate=pl.CostEstimate(flops=0, bytes_accessed=8 << 20, transcendentals=0),
         name="query_halves",
     )(queries[0], grad_out[0])
-    small = (place, source, starts, spans, mine, others)
+    small = (place, source, layout, mine, others)
     qg, block, small = lax.optimization_barrier((qg, block, small))
-    place, source, starts, spans, mine, others = small
+    place, source, layout, mine, others = small
     nears = [block] + [lax.ppermute(block, "x", shift(k)) for k in range(1, NX)]
     fars = [lax.ppermute(block, "c", SWAP)]
     qg_all = lax.all_to_all(qg, SEQ, 0, 0, tiled=True).reshape(N_SEQ * slots, 2 * half)
@@ -382,14 +403,13 @@
     lane_block = pl.BlockSpec((DH, ROWS), lambda i: (0, i))
     stat_block = pl.BlockSpec((3, ROWS), lambda i: (0, i))
 
-    every = pl.BlockSpec((N_SEQ * slots, 2 * half), lambda i: (0, 0))
 
     def forward(owner, kv, more):
         last = bool(more)
         return pl.pallas_call(
             functools.partial(first_pass, coef, last),
             grid=(steps,),
-            in_specs=[smem, smem, slot_block, whole]
+            in_specs=[pl.BlockSpec((16, SLOTS), lambda i: (0, i)), slot_block, whole]
             + [g_block, lane_block, stat_block] * last,
             out_specs=[slot_block if last else lane_block, stat_block],
             out_shape=[
@@ -404,7 +424,7 @@
                 flops=4 * rows * keys * DH, bytes_accessed=4 << 20, transcendentals=rows * keys
             ),
             name="attend_more" if last else "attend_own",
-        )(owner, starts, qg, kv, *more)
+        )(owner, qg, kv, *more)
 
     pick = (source[:, None] == jnp.arange(N_SEQ * slots)[None, :]).astype(BF16)
     qg = jnp.dot(pick, qg_all, preferred_element_type=F32).astype(BF16)
@@ -418,29 +438,35 @@
             functools.partial(second_pass, coef, scale, last),
             grid=(steps,),
             in_specs=[
-                smem, smem, slot_block, g_block, whole,
+                pl.BlockSpec((16, SLOTS), lambda i: (0, i)), slot_block, g_block, whole,
             ] + [stat_block] * NY + [smem, slot_block, slot_block] * last,
-            out_specs=[
-                every if last else slot_block,
-                whole,
+            out_specs=[hbm, hbm] if last else [slot_block, whole],
+            out_shape=[
+                pltpu.HBM((N_SEQ * slots, 2 * half), BF16),
+                pltpu.HBM((keys, 2 * DH), F32),
+            ]
+            if last
+            else [
+                jax.ShapeDtypeStruct((live_all, half), F32),
+                jax.ShapeDtypeStruct((keys, 2 * DH), BF16),
             ],
-            out_shape=[
-                jax.ShapeDtypeStruct((N_SEQ * slots, 2 * half), BF16)
-                if last
-                else jax.ShapeDtypeStruct((live_all, half), F32),
-                jax.ShapeDtypeStruct((keys, 2 * DH), F32 if last else BF16),
-            ],
-            scratch_shapes=[pltpu.VMEM((2 * DH, keys), F32), pltpu.VMEM((8, plen), F32)],
+            scratch_shapes=[pltpu.VMEM((2 * DH, keys), F32), pltpu.VMEM((8, plen), F32)]
+            + [
+                pltpu.VMEM((N_SEQ * slots, 2 * half), BF16),
+                pltpu.VMEM((keys, 2 * DH), F32),
+                pltpu.SemaphoreType.DMA((N_SEQ + 1,)),
+            ]
+            * last,
             compiler_params=params(20),
             cost_estimate=pl.CostEstimate(
                 flops=10 * rows * keys * DH, bytes_accessed=8 << 20, transcendentals=rows * keys
             ),
             name="grads_own" if last else "grads_other",
-        )(owner, starts, qg, qg, kv, *stats, *more)
+        )(owner, qg, qg, kv, *stats, *more)
 
     qgrad_part, kvgrad_other = backward(others, kv_other, ())
     kvgrad_got = lax.ppermute(kvgrad_other, "zl", SWAP)
-    back, kvgrad_own = backward(mine, kv, (spans, out, qgrad_part))
+    back, kvgrad_own = backward(mine, kv, (layout, out, qgrad_part))
 
     back, kvgrad_own = lax.optimization_barrier((back, kvgrad_own))
     back = lax.all_to_all(back.reshape(N_SEQ, slots, 2 * half), SEQ, 0, 0, tiled=True)
@@ -456,7 +482,7 @@
         + [jax.ShapeDtypeStruct((plen, 2 * DH), BF16)],
         scratch_shapes=[
             pltpu.VMEM((keys, model), BF16),
-            pltpu.VMEM((NX, model // NX, 2 * DH), F32),
+            pltpu.VMEM((NX, 2 * DH, model // NX), F32),
             pltpu.SemaphoreType.DMA((len(cuts) + 1,)),
         ],
         compiler_params=params(50),

time: 157 us -> 155 us (0.987)
  local copies, waits for them, and re-layouts: 9.14 us -> 6.79 us
    unnamed x16 -> x12, local copies, waits for them, and re-layouts: 8.96 us -> 6.6 us
  transfers between devices with their start and end apart: 23 -> 23, of which waited for: 12 -> 12; matrix products, arithmetic and copies ran while one was open for 4% -> 4% of each run, Pallas kernels for 23% -> 24%
where the time goes in v9:
time: 155 us; the launch traced here: 154 us
  Pallas kernels  53.7 us (35%)
  starting transfers between devices  44.2 us (29%)
  waiting for transfers between devices  40.2 us (26%)
  local copies, waits for them, and re-layouts  6.79 us (4%)
  other arithmetic  3.92 us (3%)
  matrix products  3.15 us (2%)
    pallas_call x2, Pallas kernels, backward(): pl.pallas_call(functools.partial(second_pass, coef, scale, last), grid=(s...  23.8 us
    ppermute x3, waiting for transfers between devices, per_device(): line = line + lax.ppermute(piece, 'x', shift(-k)).astype(F32)  13.6 us
    pallas_call x2, Pallas kernels, forward(): pl.pallas_call(functools.partial(first_pass, coef, last), grid=(steps,),...  12.4 us
    pallas_call x1, Pallas kernels, per_device(): pl.pallas_call(functools.partial(weight_kernel, cuts), in_specs=[smem] +...  8.95 us
    all_to_all x1, starting transfers between devices, per_device(): lax.all_to_all(block, PLANE, 0, 0, tiled=True).reshape(2, 8 * shard, 2 * DH)  8.13 us
    ppermute x3, waiting for transfers between devices, per_device(): nears = [block] + [lax.ppermute(block, 'x', shift(k)) for k in range(1, NX)]  8.1 us
    all_to_all x1, waiting for transfers between devices, per_device(): shares = lax.all_to_all(line, PLANE, 0, 0, tiled=True)  7.84 us
    unnamed x12, local copies, waits for them, and re-layouts  6.6 us
  transfers between devices with their start and end apart: 23, of which 12 were waited for; matrix products, arithmetic and copies ran while one was open for 4% of the time, Pallas kernels for 24%

profile of v9, /device:TPU:0, one launch (start us, length us, event | category | flops | bytes accessed | tf_op | source)
XLA Modules:
  0.0 153.6 jit_solution(5487333201462765488)
XLA Ops:
  2.1 8.1 %all-to-all-start = ((bf16[16,40,256]{2,1,0:T(8,128)(2,1)}), bf16[16,40,256]{2,1,0:T(8,128)(2,1)S(1)}, u32[]{:S(2)}, u32[]{:S(2)}) async-start(bf16[16,40,256]{2,1,0:T(8,128)(2,1)} %weight_copies.1), calls=%async_computation | async-start | bytes 655360 | tf_op jit(solution)/shard_map/all_to_all | solution.py:352
  16.5 2.9 %all-to-all-done = bf16[16,40,256]{2,1,0:T(8,128)(2,1)S(1)} async-done(((bf16[16,40,256]{2,1,0:T(8,128)(2,1)}), bf16[16,40,256]{2,1,0:T(8,128)(2,1)S(1)}, u32[]{:S(2)}, u32[]{:S(2)}) %all-to-all-start) | async-done | bytes 327712 | tf_op jit(solution)/shard_map/all_to_all | solution.py:352
  19.4 4.5 %all-to-all-start.1 = ((bf16[8,128,1024]{2,1,0:T(8,128)(2,1)}), bf16[8,128,1024]{2,1,0:T(8,128)(2,1)}, u32[]{:S(2)}, u32[]{:S(2)}) async-start(bf16[8,128,1024]{2,1,0:T(8,128)(2,1)} %query_halves.1), calls=%async_computation.1 | async-start | bytes 4194304 | tf_op jit(solution)/shard_map/all_to_all | solution.py:369
  24.0 1.6 %collective-permute-start.4 = (bf16[2,320,256]{2,1,0:T(8,128)(2,1)S(1)}, bf16[2,320,256]{2,1,0:T(8,128)(2,1)S(1)}, u32[]{:S(2)}, u32[]{:S(2)}) collective-permute-start(bf16[2,320,256]{2,1,0:T(8,128)(2,1)S(1)} %bitcast.38), channel_id=1, source_target_pairs={{96,0},{0,32},{32,64},{64,96},{97,1},{1,33},{33,65},{65,97},{98,2}... | collective-permute-start | bytes 983048 | tf_op jit(solution)/shard_map/ppermute | solution.py:367
  25.6 2.7 %collective-permute-start.1 = (bf16[2,320,256]{2,1,0:T(8,128)(2,1)S(1)}, bf16[2,320,256]{2,1,0:T(8,128)(2,1)S(1)}, u32[]{:S(2)}, u32[]{:S(2)}) collective-permute-start(bf16[2,320,256]{2,1,0:T(8,128)(2,1)S(1)} %bitcast.39), channel_id=1, source_target_pairs={{64,0},{96,32},{0,64},{32,96},{65,1},{97,33},{1,65},{33,97},{66,2}... | collective-permute-start | bytes 983048 | tf_op jit(solution)/shard_map/ppermute | solution.py:367
  29.7 4.0 %copy-done = bf16[1,1024,5120]{2,1,0:T(8,128)(2,1)S(1)} copy-done((bf16[1,1024,5120]{2,1,0:T(8,128)(2,1)S(1)}, bf16[1,1024,5120]{2,1,0:T(8,128)(2,1)}, u32[]{:S(2)}) %copy-start) | copy-done | bytes 10485784
  35.3 8.0 %collective-permute-done.1.refs_1_ = bf16[2,320,256]{2,1,0:T(8,128)(2,1)S(1)} collective-permute-done((bf16[2,320,256]{2,1,0:T(8,128)(2,1)S(1)}, bf16[2,320,256]{2,1,0:T(8,128)(2,1)S(1)}, u32[]{:S(2)}, u32[]{:S(2)}) %collective-permute-start.1) | collective-permute-done | bytes 327712 | tf_op jit(solution)/shard_map/ppermute | solution.py:367
  45.4 2.4 %project_last.1.refs_1_.kv_ref = bf16[1152,256]{1,0:T(8,128)(2,1)S(1)} custom-call(s32[2]{0:T(128)S(1)} %pad_add_fusion.1.place_ref, bf16[1024,5120]{1,0:T(8,128)(2,1)S(1)} %bitcast.32, bf16[128,5120]{1,0:T(8,128)(2,1)S(1)} %bitcast.36, bf16[2,320,256]{2,1,0:T(8,128)(2,1)S(1)} %collective-permute-done.refs_0_, ...), custom_call_target="tpu_custom_call" | custom-call | flops 1509949440 | bytes 5898240 | tf_op jit(solution)/shard_map/project_last/pallas_call | solution.py:373
  47.9 1.9 %collective-permute-start.7 = (bf16[1152,256]{1,0:T(8,128)(2,1)S(1)}, bf16[1152,256]{1,0:T(8,128)(2,1)S(1)}, u32[]{:S(2)}, u32[]{:S(2)}) collective-permute-start(bf16[1152,256]{1,0:T(8,128)(2,1)S(1)} %project_last.1.refs_1_.kv_ref), channel_id=1, source_target_pairs={{0,1},{1,0},{2,3},{3,2},{4,5},{5,4},{6,7},{7,6},{8,9},{9,8},{10,11... | collective-permute-start | bytes 1769480 | tf_op jit(solution)/shard_map/ppermute | solution.py:396
  49.7 3.1 %all-to-all-done.1 = bf16[8,128,1024]{2,1,0:T(8,128)(2,1)} async-done(((bf16[8,128,1024]{2,1,0:T(8,128)(2,1)}), bf16[8,128,1024]{2,1,0:T(8,128)(2,1)}, u32[]{:S(2)}, u32[]{:S(2)}) %all-to-all-start.1) | async-done | bytes 2097184 | tf_op jit(solution)/shard_map/all_to_all | solution.py:369
  52.9 3.1 %fusion.1.refs_0_.refs_2_.q_ref.g_ref = bf16[640,1024]{1,0:T(8,128)(2,1)S(1)} fusion(bf16[1024,1024]{1,0:T(8,128)(2,1)} %bitcast.13, s32[640]{0:T(1024)S(1)} %get-tuple-element.36), kind=kOutput, calls=%fused_computation.2 | convolution fusion | flops 1343488000 | bytes 3410432 | tf_op jit(solution)/shard_map/dot_general | solution.py:430
  56.0 5.8 %attend_own.1 = (f32[128,2560]{1,0:T(8,128)S(1)}, f32[3,2560]{1,0:T(4,128)S(1)}) custom-call(s32[16,640]{1,0:T(8,128)S(1)} %concatenate.10.bound_ref, bf16[640,1024]{1,0:T(8,128)(2,1)S(1)} %fusion.1.refs_0_.refs_2_.q_ref.g_ref, bf16[1152,256]{1,0:T(8,128)(2,1)S(1)} %project_last.1.refs_1_.kv_ref), custom_call_target="tpu_custom_call" | custom-call | flops 1509949440 | bytes 4194304 | tf_op jit(solution)/shard_map/attend_own/pallas_call | solution.py:409
  63.4 6.5 %attend_more.1 = (bf16[640,512]{1,0:T(8,128)(2,1)S(1)}, f32[3,2560]{1,0:T(4,128)S(1)}) custom-call(s32[16,640]{1,0:T(8,128)S(1)} %concatenate.11.bound_ref, bf16[640,1024]{1,0:T(8,128)(2,1)S(1)} %fusion.1.refs_0_.refs_2_.q_ref.g_ref, bf16[1152,256]{1,0:T(8,128)(2,1)S(1)} %collective-permute-done.7.refs_1_.kv_ref, ...), custom_call_target="tpu_custom_call" | custom-call | flops 1509949440 | bytes 4194304 | tf_op jit(solution)/shard_map/attend_more/pallas_call | solution.py:409
  69.9 1.8 %collective-permute-start.10 = (f32[3,2560]{1,0:T(4,128)S(1)}, f32[3,2560]{1,0:T(4,128)S(1)}, u32[]{:S(2)}, u32[]{:S(2)}) collective-permute-start(f32[3,2560]{1,0:T(4,128)S(1)} %get-tuple-element.44.refs_0_), channel_id=1, source_target_pairs={{6,0},{0,2},{2,4},{4,6},{7,1},{1,3},{3,5},{5,7},{14,8},{8,10},{10,... | collective-permute-start | bytes 92168 | tf_op jit(solution)/shard_map/ppermute | solution.py:433
  71.7 2.7 %collective-permute-start.9 = (f32[3,2560]{1,0:T(4,128)S(1)}, f32[3,2560]{1,0:T(4,128)S(1)}, u32[]{:S(2)}, u32[]{:S(2)}) collective-permute-start(f32[3,2560]{1,0:T(4,128)S(1)} %get-tuple-element.44.refs_0_), channel_id=1, source_target_pairs={{4,0},{6,2},{0,4},{2,6},{5,1},{7,3},{1,5},{3,7},{12,8},{14,10},{8,... | collective-permute-start | bytes 92168 | tf_op jit(solution)/shard_map/ppermute | solution.py:433
  78.4 9.7 %grads_other.1 = (f32[640,512]{1,0:T(8,128)S(1)}, bf16[1152,256]{1,0:T(8,128)(2,1)S(1)}) custom-call(s32[16,640]{1,0:T(8,128)S(1)} %concatenate.11.bound_ref, bf16[640,1024]{1,0:T(8,128)(2,1)S(1)} %fusion.1.refs_0_.refs_2_.q_ref.g_ref, bf16[640,1024]{1,0:T(8,128)(2,1)S(1)} %fusion.1.refs_0_.refs_2_.q_ref.g_ref, ...), custom_call_target="tpu_custom_call" | custom-call | flops 3774873600 | bytes 8388608 | tf_op jit(solution)/shard_map/grads_other/pallas_call | solution.py:437
  89.6 14.2 %grads_own.1 = (bf16[1024,1024]{1,0:T(8,128)(2,1)}, f32[1152,256]{1,0:T(8,128)}) custom-call(s32[16,640]{1,0:T(8,128)S(1)} %concatenate.10.bound_ref, bf16[640,1024]{1,0:T(8,128)(2,1)S(1)} %fusion.1.refs_0_.refs_2_.q_ref.g_ref, bf16[640,1024]{1,0:T(8,128)(2,1)S(1)} %fusion.1.refs_0_.refs_2_.q_ref.g_ref, bf16[1152,256]{1,0:T(8,128)(2,1)S(1)} %project_last.1.refs_1_.kv_ref, ...), custom_call_target="tpu_custom_call" | custom-call | flops 3774873600 | bytes 8388608 | tf_op jit(solution)/shard_map/grads_own/pallas_call | solution.py:437
  103.8 4.0 %all-to-all-start.2 = ((bf16[8,128,1024]{2,1,0:T(8,128)(2,1)}), bf16[8,128,1024]{2,1,0:T(8,128)(2,1)S(1)}, u32[]{:S(2)}, u32[]{:S(2)}) async-start(bf16[8,128,1024]{2,1,0:T(8,128)(2,1)} %bitcast.44), calls=%async_computation.2 | async-start | bytes 4194304 | tf_op jit(solution)/shard_map/all_to_all | solution.py:472
  107.8 9.0 %weight_grad.1 = (f32[2,320,256]{2,1,0:T(8,128)S(1)}, f32[2,320,256]{2,1,0:T(8,128)S(1)}, f32[2,320,256]{2,1,0:T(8,128)S(1)}, f32[2,320,256]{2,1,0:T(8,128)}, bf...) custom-call(s32[2]{0:T(128)S(1)} %pad_add_fusion.1.place_ref, ...), custom_call_target="tpu_custom_call" | custom-call | flops 3019898880 | bytes 11796480 | tf_op jit(solution)/shard_map/weight_grad/pallas_call | solution.py:476
  119.8 2.5 %collective-permute-start.16 = (bf16[2,320,256]{2,1,0:T(8,128)(2,1)S(1)}, bf16[2,320,256]{2,1,0:T(8,128)(2,1)S(1)}, u32[]{:S(2)}, u32[]{:S(2)}) collective-permute-start(bf16[2,320,256]{2,1,0:T(8,128)(2,1)S(1)} %add_convert_fusion.2), channel_id=1, source_target_pairs={{64,0},{96,32},{0,64},{32,96},{65,1},{97,33},{1,65},{33,97},{66,2}... | collective-permute-start | bytes 983048 | tf_op jit(solution)/shard_map/ppermute | solution.py:499
  123.8 6.2 %collective-permute-done.14 = bf16[2,320,256]{2,1,0:T(8,128)(2,1)S(1)} collective-permute-done((bf16[2,320,256]{2,1,0:T(8,128)(2,1)S(1)}, bf16[2,320,256]{2,1,0:T(8,128)(2,1)S(1)}, u32[]{:S(2)}, u32[]{:S(2)}) %collective-permute-start.14) | collective-permute-done | bytes 327712 | tf_op jit(solution)/shard_map/ppermute | solution.py:499
  130.1 6.9 %collective-permute-done.16 = bf16[2,320,256]{2,1,0:T(8,128)(2,1)S(1)} collective-permute-done((bf16[2,320,256]{2,1,0:T(8,128)(2,1)S(1)}, bf16[2,320,256]{2,1,0:T(8,128)(2,1)S(1)}, u32[]{:S(2)}, u32[]{:S(2)}) %collective-permute-start.16) | collective-permute-done | bytes 327712 | tf_op jit(solution)/shard_map/ppermute | solution.py:499
  138.3 5.8 %all-to-all-start.3 = ((bf16[16,40,256]{2,1,0:T(8,128)(2,1)}), bf16[16,40,256]{2,1,0:T(8,128)(2,1)S(1)}, u32[]{:S(2)}, u32[]{:S(2)}) async-start(bf16[16,40,256]{2,1,0:T(8,128)(2,1)} %bitcast.16), calls=%async_computation.3 | async-start | bytes 655360 | tf_op jit(solution)/shard_map/all_to_all | solution.py:502
  145.1 7.8 %all-to-all-done.3 = bf16[16,40,256]{2,1,0:T(8,128)(2,1)S(1)} async-done(((bf16[16,40,256]{2,1,0:T(8,128)(2,1)}), bf16[16,40,256]{2,1,0:T(8,128)(2,1)S(1)}, u32[]{:S(2)}, u32[]{:S(2)}) %all-to-all-start.3) | async-done | bytes 327712 | tf_op jit(solution)/shard_map/all_to_all | solution.py:502
  (68 shorter events, 26.9 us)
Async XLA Ops:
  2.1 17.3 %all-to-all-start = ((bf16[16,40,256]{2,1,0:T(8,128)(2,1)}), bf16[16,40,256]{2,1,0:T(8,128)(2,1)S(1)}, u32[]{:S(2)}, u32[]{:S(2)}) async-start(bf16[16,40,256]{2,1,0:T(8,128)(2,1)} %weight_copies.1), calls=%async_computation | async-start | bytes 655360 | tf_op jit(solution)/shard_map/all_to_all | solution.py:352
  19.4 10.3 %copy-start.1 = (bf16[1,128,5120]{2,1,0:T(8,128)(2,1)S(1)}, bf16[1,128,5120]{2,1,0:T(8,128)(2,1)}, u32[]{:S(2)}) copy-start(bf16[1,128,5120]{2,1,0:T(8,128)(2,1)} %param.8) | copy-start | bytes 3932164
  19.4 33.4 %all-to-all-start.1 = ((bf16[8,128,1024]{2,1,0:T(8,128)(2,1)}), bf16[8,128,1024]{2,1,0:T(8,128)(2,1)}, u32[]{:S(2)}, u32[]{:S(2)}) async-start(bf16[8,128,1024]{2,1,0:T(8,128)(2,1)} %query_halves.1), calls=%async_computation.1 | async-start | bytes 4194304 | tf_op jit(solution)/shard_map/all_to_all | solution.py:369
  23.9 5.8 %collective-permute-start.5 = (bf16[2,320,256]{2,1,0:T(8,128)(2,1)S(1)}, bf16[2,320,256]{2,1,0:T(8,128)(2,1)S(1)}, u32[]{:S(2)}, u32[]{:S(2)}) collective-permute-start(bf16[2,320,256]{2,1,0:T(8,128)(2,1)S(1)} %bitcast.37), channel_id=1, source_target_pairs={{0,8},{8,0},{1,9},{9,1},{2,10},{10,2},{3,11},{11,3},{4,12},{12,4},... | collective-permute-start | bytes 983048 | tf_op jit(solution)/shard_map/ppermute | solution.py:368
  24.0 11.3 %collective-permute-start.4 = (bf16[2,320,256]{2,1,0:T(8,128)(2,1)S(1)}, bf16[2,320,256]{2,1,0:T(8,128)(2,1)S(1)}, u32[]{:S(2)}, u32[]{:S(2)}) collective-permute-start(bf16[2,320,256]{2,1,0:T(8,128)(2,1)S(1)} %bitcast.38), channel_id=1, source_target_pairs={{96,0},{0,32},{32,64},{64,96},{97,1},{1,33},{33,65},{65,97},{98,2}... | collective-permute-start | bytes 983048 | tf_op jit(solution)/shard_map/ppermute | solution.py:367
  25.6 17.8 %collective-permute-start.1 = (bf16[2,320,256]{2,1,0:T(8,128)(2,1)S(1)}, bf16[2,320,256]{2,1,0:T(8,128)(2,1)S(1)}, u32[]{:S(2)}, u32[]{:S(2)}) collective-permute-start(bf16[2,320,256]{2,1,0:T(8,128)(2,1)S(1)} %bitcast.39), channel_id=1, source_target_pairs={{64,0},{96,32},{0,64},{32,96},{65,1},{97,33},{1,65},{33,97},{66,2}... | collective-permute-start | bytes 983048 | tf_op jit(solution)/shard_map/ppermute | solution.py:367
  28.3 15.1 %collective-permute-start = (bf16[2,320,256]{2,1,0:T(8,128)(2,1)S(1)}, bf16[2,320,256]{2,1,0:T(8,128)(2,1)S(1)}, u32[]{:S(2)}, u32[]{:S(2)}) collective-permute-start(bf16[2,320,256]{2,1,0:T(8,128)(2,1)S(1)} %bitcast.40), channel_id=1, source_target_pairs={{32,0},{64,32},{96,64},{0,96},{33,1},{65,33},{97,65},{1,97},{34,2}... | collective-permute-start | bytes 983048 | tf_op jit(solution)/shard_map/ppermute | solution.py:367
  35.3 8.5 %collective-permute-start.6 = (bf16[2,320,256]{2,1,0:T(8,128)(2,1)S(1)}, bf16[2,320,256]{2,1,0:T(8,128)(2,1)S(1)}, u32[]{:S(2)}, u32[]{:S(2)}) collective-permute-start(bf16[2,320,256]{2,1,0:T(8,128)(2,1)S(1)} %collective-permute-done.4.refs_0_), channel_id=1, source_target_pairs={{0,8},{8,0},{1,9},{9,1},{2,10},{10,2},{3,11},{11,3},{4,12},{12,4},... | collective-permute-start | bytes 983048 | tf_op jit(solution)/shard_map/ppermute | solution.py:393
  43.3 2.1 %collective-permute-start.3 = (bf16[2,320,256]{2,1,0:T(8,128)(2,1)S(1)}, bf16[2,320,256]{2,1,0:T(8,128)(2,1)S(1)}, u32[]{:S(2)}, u32[]{:S(2)}) collective-permute-start(bf16[2,320,256]{2,1,0:T(8,128)(2,1)S(1)} %collective-permute-done.1.refs_1_), channel_id=1, source_target_pairs={{0,8},{8,0},{1,9},{9,1},{2,10},{10,2},{3,11},{11,3},{4,12},{12,4},... | collective-permute-start | bytes 983048 | tf_op jit(solution)/shard_map/ppermute | solution.py:393
  43.3 2.1 %collective-permute-start.2 = (bf16[2,320,256]{2,1,0:T(8,128)(2,1)S(1)}, bf16[2,320,256]{2,1,0:T(8,128)(2,1)S(1)}, u32[]{:S(2)}, u32[]{:S(2)}) collective-permute-start(bf16[2,320,256]{2,1,0:T(8,128)(2,1)S(1)} %collective-permute-done.refs_0_), channel_id=1, source_target_pairs={{0,8},{8,0},{1,9},{9,1},{2,10},{10,2},{3,11},{11,3},{4,12},{12,4},... | collective-permute-start | bytes 983048 | tf_op jit(solution)/shard_map/ppermute | solution.py:393
  47.9 15.5 %collective-permute-start.7 = (bf16[1152,256]{1,0:T(8,128)(2,1)S(1)}, bf16[1152,256]{1,0:T(8,128)(2,1)S(1)}, u32[]{:S(2)}, u32[]{:S(2)}) collective-permute-start(bf16[1152,256]{1,0:T(8,128)(2,1)S(1)} %project_last.1.refs_1_.kv_ref), channel_id=1, source_target_pairs={{0,1},{1,0},{2,3},{3,2},{4,5},{5,4},{6,7},{7,6},{8,9},{9,8},{10,11... | collective-permute-start | bytes 1769480 | tf_op jit(solution)/shard_map/ppermute | solution.py:396
  69.9 6.0 %collective-permute-start.10 = (f32[3,2560]{1,0:T(4,128)S(1)}, f32[3,2560]{1,0:T(4,128)S(1)}, u32[]{:S(2)}, u32[]{:S(2)}) collective-permute-start(f32[3,2560]{1,0:T(4,128)S(1)} %get-tuple-element.44.refs_0_), channel_id=1, source_target_pairs={{6,0},{0,2},{2,4},{4,6},{7,1},{1,3},{3,5},{5,7},{14,8},{8,10},{10,... | collective-permute-start | bytes 92168 | tf_op jit(solution)/shard_map/ppermute | solution.py:433
  71.7 5.5 %collective-permute-start.9 = (f32[3,2560]{1,0:T(4,128)S(1)}, f32[3,2560]{1,0:T(4,128)S(1)}, u32[]{:S(2)}, u32[]{:S(2)}) collective-permute-start(f32[3,2560]{1,0:T(4,128)S(1)} %get-tuple-element.44.refs_0_), channel_id=1, source_target_pairs={{4,0},{6,2},{0,4},{2,6},{5,1},{7,3},{1,5},{3,7},{12,8},{14,10},{8,... | collective-permute-start | bytes 92168 | tf_op jit(solution)/shard_map/ppermute | solution.py:433
  74.4 4.0 %collective-permute-start.8 = (f32[3,2560]{1,0:T(4,128)S(1)}, f32[3,2560]{1,0:T(4,128)S(1)}, u32[]{:S(2)}, u32[]{:S(2)}) collective-permute-start(f32[3,2560]{1,0:T(4,128)S(1)} %get-tuple-element.44.refs_0_), channel_id=1, source_target_pairs={{2,0},{4,2},{6,4},{0,6},{3,1},{5,3},{7,5},{1,7},{10,8},{12,10},{14... | collective-permute-start | bytes 92168 | tf_op jit(solution)/shard_map/ppermute | solution.py:433
  88.1 19.7 %collective-permute-start.11 = (bf16[1152,256]{1,0:T(8,128)(2,1)S(1)}, bf16[1152,256]{1,0:T(8,128)(2,1)S(1)}, u32[]{:S(2)}, u32[]{:S(2)}) collective-permute-start(bf16[1152,256]{1,0:T(8,128)(2,1)S(1)} %get-tuple-element.49), channel_id=1, source_target_pairs={{0,1},{1,0},{2,3},{3,2},{4,5},{5,4},{6,7},{7,6},{8,9},{9,8},{10,11... | collective-permute-start | bytes 1769480 | tf_op jit(solution)/shard_map/ppermute | solution.py:468
  103.8 34.5 %all-to-all-start.2 = ((bf16[8,128,1024]{2,1,0:T(8,128)(2,1)}), bf16[8,128,1024]{2,1,0:T(8,128)(2,1)S(1)}, u32[]{:S(2)}, u32[]{:S(2)}) async-start(bf16[8,128,1024]{2,1,0:T(8,128)(2,1)} %bitcast.44), calls=%async_computation.2 | async-start | bytes 4194304 | tf_op jit(solution)/shard_map/all_to_all | solution.py:472
  116.8 1.7 %collective-permute-start.13 = (bf16[2,320,256]{2,1,0:T(8,128)(2,1)S(1)}, bf16[2,320,256]{2,1,0:T(8,128)(2,1)S(1)}, u32[]{:S(2)}, u32[]{:S(2)}) collective-permute-start(bf16[2,320,256]{2,1,0:T(8,128)(2,1)S(1)} %get-tuple-element.53), channel_id=1, source_target_pairs={{0,8},{8,0},{1,9},{9,1},{2,10},{10,2},{3,11},{11,3},{4,12},{12,4},... | collective-permute-start | bytes 983048 | tf_op jit(solution)/shard_map/ppermute | solution.py:495
  116.8 2.9 %collective-permute-start.15 = (bf16[2,320,256]{2,1,0:T(8,128)(2,1)S(1)}, bf16[2,320,256]{2,1,0:T(8,128)(2,1)S(1)}, u32[]{:S(2)}, u32[]{:S(2)}) collective-permute-start(bf16[2,320,256]{2,1,0:T(8,128)(2,1)S(1)} %get-tuple-element.55), channel_id=1, source_target_pairs={{0,8},{8,0},{1,9},{9,1},{2,10},{10,2},{3,11},{11,3},{4,12},{12,4},... | collective-permute-start | bytes 983048 | tf_op jit(solution)/shard_map/ppermute | solution.py:495
  117.3 6.5 %collective-permute-start.12 = (bf16[2,320,256]{2,1,0:T(8,128)(2,1)S(1)}, bf16[2,320,256]{2,1,0:T(8,128)(2,1)S(1)}, u32[]{:S(2)}, u32[]{:S(2)}) collective-permute-start(bf16[2,320,256]{2,1,0:T(8,128)(2,1)S(1)} %get-tuple-element.51), channel_id=1, source_target_pairs={{0,8},{8,0},{1,9},{9,1},{2,10},{10,2},{3,11},{11,3},{4,12},{12,4},... | collective-permute-start | bytes 983048 | tf_op jit(solution)/shard_map/ppermute | solution.py:495
  117.4 4.9 %collective-permute-start.17 = (bf16[2,320,256]{2,1,0:T(8,128)(2,1)S(1)}, bf16[2,320,256]{2,1,0:T(8,128)(2,1)S(1)}, u32[]{:S(2)}, u32[]{:S(2)}) collective-permute-start(bf16[2,320,256]{2,1,0:T(8,128)(2,1)S(1)} %get-tuple-element.57), channel_id=1, source_target_pairs={{0,8},{8,0},{1,9},{9,1},{2,10},{10,2},{3,11},{11,3},{4,12},{12,4},... | collective-permute-start | bytes 983048 | tf_op jit(solution)/shard_map/ppermute | solution.py:495
  118.5 11.5 %collective-permute-start.14 = (bf16[2,320,256]{2,1,0:T(8,128)(2,1)S(1)}, bf16[2,320,256]{2,1,0:T(8,128)(2,1)S(1)}, u32[]{:S(2)}, u32[]{:S(2)}) collective-permute-start(bf16[2,320,256]{2,1,0:T(8,128)(2,1)S(1)} %add_convert_fusion.3), channel_id=1, source_target_pairs={{96,0},{0,32},{32,64},{64,96},{97,1},{1,33},{33,65},{65,97},{98,2}... | collective-permute-start | bytes 983048 | tf_op jit(solution)/shard_map/ppermute | solution.py:499
  119.8 17.1 %collective-permute-start.16 = (bf16[2,320,256]{2,1,0:T(8,128)(2,1)S(1)}, bf16[2,320,256]{2,1,0:T(8,128)(2,1)S(1)}, u32[]{:S(2)}, u32[]{:S(2)}) collective-permute-start(bf16[2,320,256]{2,1,0:T(8,128)(2,1)S(1)} %add_convert_fusion.2), channel_id=1, source_target_pairs={{64,0},{96,32},{0,64},{32,96},{65,1},{97,33},{1,65},{33,97},{66,2}... | collective-permute-start | bytes 983048 | tf_op jit(solution)/shard_map/ppermute | solution.py:499
  122.4 15.0 %collective-permute-start.18 = (bf16[2,320,256]{2,1,0:T(8,128)(2,1)S(1)}, bf16[2,320,256]{2,1,0:T(8,128)(2,1)S(1)}, u32[]{:S(2)}, u32[]{:S(2)}) collective-permute-start(bf16[2,320,256]{2,1,0:T(8,128)(2,1)S(1)} %add_convert_fusion.1), channel_id=1, source_target_pairs={{32,0},{64,32},{96,64},{0,96},{33,1},{65,33},{97,65},{1,97},{34,2}... | collective-permute-start | bytes 983048 | tf_op jit(solution)/shard_map/ppermute | solution.py:499
  138.3 14.6 %all-to-all-start.3 = ((bf16[16,40,256]{2,1,0:T(8,128)(2,1)}), bf16[16,40,256]{2,1,0:T(8,128)(2,1)S(1)}, u32[]{:S(2)}, u32[]{:S(2)}) async-start(bf16[16,40,256]{2,1,0:T(8,128)(2,1)} %bitcast.16), calls=%async_computation.3 | async-start | bytes 655360 | tf_op jit(solution)/shard_map/all_to_all | solution.py:502
  (5 other events, 12.2 us)

commit v10 on v9

--- a/solution.py
+++ b/solution.py
@@ -61,7 +61,7 @@
         copy.wait()
 
 
-def project_kernel(steps, first, last, place_ref, prompt_ref, resp_ref, *refs):
+def project_kernel(steps, first, last, prompt_ref, resp_ref, *refs):
     refs = list(refs)
     nears = [refs.pop(0) for _ in steps]
     fars = [refs.pop(0) for _ in steps]
@@ -71,7 +71,7 @@
     wide = prompt_ref.shape[1] // NX
     half = wide // 2
     part = wide // 4
-    x, core = place_ref[0], place_ref[1]
+    x, core = lax.axis_index("x"), lax.axis_index("c")
     tops, ends = [], []
     for n, k in enumerate(steps):
         for z in range(2):
@@ -151,7 +151,9 @@
 def second_pass(coef, scale, last, bound_ref, q_ref, g_ref, kv_ref, *refs):
     stat_refs, refs = refs[:NY], refs[NY:]
     if last:
-        layout_ref, out_ref, prev_ref, back_hbm, kvgrad_hbm, acc, bias, back_ref, total_ref, sems = refs
+        layout_hbm, out_ref, prev_ref, back_hbm, kvgrad_hbm = refs[:5]
+        acc, bias, back_ref, total_ref, layout_ref, sems = refs[5:]
+        bring = pltpu.make_async_copy(layout_hbm, layout_ref, sems.at[N_SEQ + 1])
     else:
         back_ref, kvgrad_ref, acc, bias = refs
     step = pl.program_id(0)
@@ -168,6 +170,8 @@
 
     @pl.when(step == 0)
     def _():
+        if last:
+            bring.start()
         acc[...] = jnp.zeros_like(acc)
         place = lax.broadcasted_iota(jnp.int32, (8, plen), 1)
         bias[...] = jnp.where(place < bound_ref[8:16, 0:1], 0.0, NEG)
@@ -215,6 +219,7 @@
 
         @pl.when(step == 0)
         def _():
+            bring.wait()
             back_ref[...] = jnp.zeros_like(back_ref)
 
         def leave(r):
@@ -251,7 +256,7 @@
             kvgrad_ref[...] = acc[...].T.astype(BF16)
 
 
-def weight_kernel(cuts, place_ref, own_ref, got_ref, prompt_ref, resp_ref, *refs):
+def weight_kernel(cuts, own_ref, got_ref, prompt_ref, resp_ref, *refs):
     keeps, gives = refs[:NX], refs[NX : 2 * NX]
     prompt_grad_ref, buf, whole, sems = refs[2 * NX :]
     plen = prompt_ref.shape[0]
@@ -264,7 +269,7 @@
     copies.append(pltpu.make_async_copy(resp_ref, buf.at[plen:], sems.at[len(cuts)]))
     for copy in copies:
         copy.start()
-    x, core = place_ref[0], place_ref[1]
+    x, core = lax.axis_index("x"), lax.axis_index("c")
     grad = (own_ref[...] + got_ref[...].astype(F32)).astype(BF16)
     prompt_grad_ref[...] = grad[:plen]
     grad = grad.T
@@ -304,7 +309,6 @@
 ):
     rank = lax.axis_index(SEQ)
     x = lax.axis_index("x")
-    place = jnp.stack([x, lax.axis_index("c")]).astype(jnp.int32)
     slots = resp_hidden.shape[1]
     plen = prompt_hidden.shape[1]
     model = prompt_hidden.shape[2]
@@ -316,7 +320,6 @@
     resp_rows = resp_hidden[0]
     keys = plen + slots
     shard = kv_weight.shape[0]
-    smem = pl.BlockSpec(memory_space=pltpu.SMEM)
     vmem = pl.BlockSpec(memory_space=pltpu.VMEM)
     hbm = pl.BlockSpec(memory_space=pltpu.HBM)
 
@@ -332,6 +335,7 @@
     behind = jnp.sum((ends - lengths)[None, :] < lows + SLOTS, 1)
     spans = jnp.stack([first, behind], 1).astype(jnp.int32).reshape(-1)
     layout = jnp.concatenate([starts, spans])
+    layout = jnp.pad(layout, (0, 3 * N_SEQ - layout.shape[0]))
 
     def bounds(owner):
         offset = source - owner * slots
@@ -361,9 +365,9 @@
         cost_estimate=pl.CostEstimate(flops=0, bytes_accessed=8 << 20, transcendentals=0),
         name="query_halves",
     )(queries[0], grad_out[0])
-    small = (place, source, layout, mine, others)
+    small = (source, layout, mine, others)
     qg, block, small = lax.optimization_barrier((qg, block, small))
-    place, source, layout, mine, others = small
+    source, layout, mine, others = small
     nears = [block] + [lax.ppermute(block, "x", shift(k)) for k in range(1, NX)]
     fars = [lax.ppermute(block, "c", SWAP)]
     qg_all = lax.all_to_all(qg, SEQ, 0, 0, tiled=True).reshape(N_SEQ * slots, 2 * half)
@@ -372,7 +376,7 @@
         count = len(steps)
         return pl.pallas_call(
             functools.partial(project_kernel, steps, prev is None, last),
-            in_specs=[smem] + [vmem] * (2 + 2 * count + (prev is not None)),
+            in_specs=[vmem] * (2 + 2 * count + (prev is not None)),
             out_specs=vmem,
             out_shape=jax.ShapeDtypeStruct((keys, 2 * DH), BF16 if last else F32),
             scratch_shapes=[pltpu.VMEM((count * model // NX, 2 * DH), BF16)],
@@ -384,7 +388,7 @@
             ),
             name="project_last" if last else "project",
         )(
-            place, prompt_rows, resp_rows, *[nears[k] for k in steps], *[fars[k] for k in steps],
+            prompt_rows, resp_rows, *[nears[k] for k in steps], *[fars[k] for k in steps],
             *(() if prev is None else (prev,)),
         )
 
@@ -439,7 +443,7 @@
             grid=(steps,),
             in_specs=[
                 pl.BlockSpec((16, SLOTS), lambda i: (0, i)), slot_block, g_block, whole,
-            ] + [stat_block] * NY + [smem, slot_block, slot_block] * last,
+            ] + [stat_block] * NY + [hbm, slot_block, slot_block] * last,
             out_specs=[hbm, hbm] if last else [slot_block, whole],
             out_shape=[
                 pltpu.HBM((N_SEQ * slots, 2 * half), BF16),
@@ -454,7 +458,8 @@
             + [
                 pltpu.VMEM((N_SEQ * slots, 2 * half), BF16),
                 pltpu.VMEM((keys, 2 * DH), F32),
-                pltpu.SemaphoreType.DMA((N_SEQ + 1,)),
+                pltpu.SMEM((3 * N_SEQ,), jnp.int32),
+                pltpu.SemaphoreType.DMA((N_SEQ + 2,)),
             ]
             * last,
             compiler_params=params(20),
@@ -475,7 +480,7 @@
     piece = (2, 8 * shard, 2 * DH)
     *pieces, prompt_grad = pl.pallas_call(
         functools.partial(weight_kernel, cuts),
-        in_specs=[smem] + [vmem] * 2 + [pl.BlockSpec(memory_space=pltpu.HBM)] * 2,
+        in_specs=[vmem] * 2 + [pl.BlockSpec(memory_space=pltpu.HBM)] * 2,
         out_specs=[vmem] * (2 * NX + 1),
         out_shape=[jax.ShapeDtypeStruct(piece, F32)] * NX
         + [jax.ShapeDtypeStruct(piece, BF16)] * NX
@@ -490,7 +495,7 @@
             flops=4 * keys * model * DH, bytes_accessed=2 * keys * model, transcendentals=0
         ),
         name="weight_grad",
-    )(place, kvgrad_own, kvgrad_got, prompt_rows, resp_rows)
+    )(kvgrad_own, kvgrad_got, prompt_rows, resp_rows)
     keeps, gives = pieces[:NX], pieces[NX:]
     got = [lax.ppermute(give, "c", SWAP) for give in gives]
     line = keeps[0] + got[0].astype(F32)

time: 155 us -> 154 us (level)
  Pallas kernels: 53.7 us -> 51.8 us
    pallas_call x3, Pallas kernels: 5.48 us -> 3.88 us  [project(): pl.pallas_call(functools.partial(project_kernel, steps, prev is None, las...]
  transfers between devices with their start and end apart: 23 -> 23, of which waited for: 12 -> 13; matrix products, arithmetic and copies ran while one was open for 4% -> 4% of each run, Pallas kernels for 24% -> 23%
where the time goes in v10:
time: 154 us; the launch traced here: 153 us
  Pallas kernels  51.8 us (34%)
  starting transfers between devices  43.9 us (29%)
  waiting for transfers between devices  41.6 us (27%)
  local copies, waits for them, and re-layouts  6.81 us (4%)
  other arithmetic  3.83 us (2%)
  matrix products  3.15 us (2%)
    pallas_call x2, Pallas kernels, backward(): pl.pallas_call(functools.partial(second_pass, coef, scale, last), grid=(s...  23.5 us
    ppermute x3, waiting for transfers between devices, per_device(): line = line + lax.ppermute(piece, 'x', shift(-k)).astype(F32)  13.9 us
    pallas_call x2, Pallas kernels, forward(): pl.pallas_call(functools.partial(first_pass, coef, last), grid=(steps,),...  12.4 us
    pallas_call x1, Pallas kernels, per_device(): pl.pallas_call(functools.partial(weight_kernel, cuts), in_specs=[vmem] *...  8.95 us
    ppermute x3, waiting for transfers between devices, per_device(): nears = [block] + [lax.ppermute(block, 'x', shift(k)) for k in range(1, NX)]  8.63 us
    all_to_all x1, starting transfers between devices, per_device(): lax.all_to_all(block, PLANE, 0, 0, tiled=True).reshape(2, 8 * shard, 2 * DH)  8.13 us
    all_to_all x1, waiting for transfers between devices, per_device(): shares = lax.all_to_all(line, PLANE, 0, 0, tiled=True)  7.84 us
    unnamed x12, local copies, waits for them, and re-layouts  6.6 us
  transfers between devices with their start and end apart: 23, of which 13 were waited for; matrix products, arithmetic and copies ran while one was open for 4% of the time, Pallas kernels for 23%

profile of v10, /device:TPU:0, one launch (start us, length us, event | category | flops | bytes accessed | tf_op | source)
XLA Modules:
  0.0 152.7 jit_solution(10476136923911468272)
XLA Ops:
  2.1 8.1 %all-to-all-start = ((bf16[16,40,256]{2,1,0:T(8,128)(2,1)}), bf16[16,40,256]{2,1,0:T(8,128)(2,1)S(1)}, u32[]{:S(2)}, u32[]{:S(2)}) async-start(bf16[16,40,256]{2,1,0:T(8,128)(2,1)} %weight_copies.1), calls=%async_computation | async-start | bytes 655360 | tf_op jit(solution)/shard_map/all_to_all | solution.py:356
  16.5 2.9 %all-to-all-done = bf16[16,40,256]{2,1,0:T(8,128)(2,1)S(1)} async-done(((bf16[16,40,256]{2,1,0:T(8,128)(2,1)}), bf16[16,40,256]{2,1,0:T(8,128)(2,1)S(1)}, u32[]{:S(2)}, u32[]{:S(2)}) %all-to-all-start) | async-done | bytes 327712 | tf_op jit(solution)/shard_map/all_to_all | solution.py:356
  19.4 4.5 %all-to-all-start.1 = ((bf16[8,128,1024]{2,1,0:T(8,128)(2,1)}), bf16[8,128,1024]{2,1,0:T(8,128)(2,1)}, u32[]{:S(2)}, u32[]{:S(2)}) async-start(bf16[8,128,1024]{2,1,0:T(8,128)(2,1)} %query_halves.1), calls=%async_computation.1 | async-start | bytes 4194304 | tf_op jit(solution)/shard_map/all_to_all | solution.py:373
  24.0 1.6 %collective-permute-start.4 = (bf16[2,320,256]{2,1,0:T(8,128)(2,1)S(1)}, bf16[2,320,256]{2,1,0:T(8,128)(2,1)S(1)}, u32[]{:S(2)}, u32[]{:S(2)}) collective-permute-start(bf16[2,320,256]{2,1,0:T(8,128)(2,1)S(1)} %bitcast.36), channel_id=1, source_target_pairs={{96,0},{0,32},{32,64},{64,96},{97,1},{1,33},{33,65},{65,97},{98,2}... | collective-permute-start | bytes 983048 | tf_op jit(solution)/shard_map/ppermute | solution.py:371
  25.6 2.7 %collective-permute-start.1 = (bf16[2,320,256]{2,1,0:T(8,128)(2,1)S(1)}, bf16[2,320,256]{2,1,0:T(8,128)(2,1)S(1)}, u32[]{:S(2)}, u32[]{:S(2)}) collective-permute-start(bf16[2,320,256]{2,1,0:T(8,128)(2,1)S(1)} %bitcast.37), channel_id=1, source_target_pairs={{64,0},{96,32},{0,64},{32,96},{65,1},{97,33},{1,65},{33,97},{66,2}... | collective-permute-start | bytes 983048 | tf_op jit(solution)/shard_map/ppermute | solution.py:371
  29.7 4.0 %copy-done = bf16[1,1024,5120]{2,1,0:T(8,128)(2,1)S(1)} copy-done((bf16[1,1024,5120]{2,1,0:T(8,128)(2,1)S(1)}, bf16[1,1024,5120]{2,1,0:T(8,128)(2,1)}, u32[]{:S(2)}) %copy-start) | copy-done | bytes 10485784
  35.3 8.0 %collective-permute-done.1.refs_1_ = bf16[2,320,256]{2,1,0:T(8,128)(2,1)S(1)} collective-permute-done((bf16[2,320,256]{2,1,0:T(8,128)(2,1)S(1)}, bf16[2,320,256]{2,1,0:T(8,128)(2,1)S(1)}, u32[]{:S(2)}, u32[]{:S(2)}) %collective-permute-start.1) | collective-permute-done | bytes 327712 | tf_op jit(solution)/shard_map/ppermute | solution.py:371
  45.4 1.9 %project_last.1.refs_1_.kv_ref = bf16[1152,256]{1,0:T(8,128)(2,1)S(1)} custom-call(bf16[1024,5120]{1,0:T(8,128)(2,1)S(1)} %bitcast.30, bf16[128,5120]{1,0:T(8,128)(2,1)S(1)} %bitcast.34, bf16[2,320,256]{2,1,0:T(8,128)(2,1)S(1)} %collective-permute-done.refs_0_, bf16[2,320,256]{2,1,0:T(8,128)(2,1)S(1)} %collective-permute-done.1.refs_1_, ...), custom_call_target="tpu_custom_call" | custom-call | flops 1509949440 | bytes 5898240 | tf_op jit(solution)/shard_map/project_last/pallas_call | solution.py:377
  47.3 1.9 %collective-permute-start.7 = (bf16[1152,256]{1,0:T(8,128)(2,1)S(1)}, bf16[1152,256]{1,0:T(8,128)(2,1)S(1)}, u32[]{:S(2)}, u32[]{:S(2)}) collective-permute-start(bf16[1152,256]{1,0:T(8,128)(2,1)S(1)} %project_last.1.refs_1_.kv_ref), channel_id=1, source_target_pairs={{0,1},{1,0},{2,3},{3,2},{4,5},{5,4},{6,7},{7,6},{8,9},{9,8},{10,11... | collective-permute-start | bytes 1769480 | tf_op jit(solution)/shard_map/ppermute | solution.py:400
  49.2 3.7 %all-to-all-done.1 = bf16[8,128,1024]{2,1,0:T(8,128)(2,1)} async-done(((bf16[8,128,1024]{2,1,0:T(8,128)(2,1)}), bf16[8,128,1024]{2,1,0:T(8,128)(2,1)}, u32[]{:S(2)}, u32[]{:S(2)}) %all-to-all-start.1) | async-done | bytes 2097184 | tf_op jit(solution)/shard_map/all_to_all | solution.py:373
  52.9 3.1 %fusion.1.refs_0_.refs_2_.q_ref.g_ref = bf16[640,1024]{1,0:T(8,128)(2,1)S(1)} fusion(bf16[1024,1024]{1,0:T(8,128)(2,1)} %bitcast.11, s32[640]{0:T(1024)S(1)} %get-tuple-element.34), kind=kOutput, calls=%fused_computation.2 | convolution fusion | flops 1343488000 | bytes 3410432 | tf_op jit(solution)/shard_map/dot_general | solution.py:434
  56.0 5.8 %attend_own.1 = (f32[128,2560]{1,0:T(8,128)S(1)}, f32[3,2560]{1,0:T(4,128)S(1)}) custom-call(s32[16,640]{1,0:T(8,128)S(1)} %concatenate.10.bound_ref, bf16[640,1024]{1,0:T(8,128)(2,1)S(1)} %fusion.1.refs_0_.refs_2_.q_ref.g_ref, bf16[1152,256]{1,0:T(8,128)(2,1)S(1)} %project_last.1.refs_1_.kv_ref), custom_call_target="tpu_custom_call" | custom-call | flops 1509949440 | bytes 4194304 | tf_op jit(solution)/shard_map/attend_own/pallas_call | solution.py:413
  62.8 6.5 %attend_more.1 = (bf16[640,512]{1,0:T(8,128)(2,1)S(1)}, f32[3,2560]{1,0:T(4,128)S(1)}) custom-call(s32[16,640]{1,0:T(8,128)S(1)} %concatenate.11.bound_ref, bf16[640,1024]{1,0:T(8,128)(2,1)S(1)} %fusion.1.refs_0_.refs_2_.q_ref.g_ref, bf16[1152,256]{1,0:T(8,128)(2,1)S(1)} %collective-permute-done.7.refs_1_.kv_ref, ...), custom_call_target="tpu_custom_call" | custom-call | flops 1509949440 | bytes 4194304 | tf_op jit(solution)/shard_map/attend_more/pallas_call | solution.py:413
  69.4 1.8 %collective-permute-start.10 = (f32[3,2560]{1,0:T(4,128)S(1)}, f32[3,2560]{1,0:T(4,128)S(1)}, u32[]{:S(2)}, u32[]{:S(2)}) collective-permute-start(f32[3,2560]{1,0:T(4,128)S(1)} %get-tuple-element.42.refs_0_), channel_id=1, source_target_pairs={{6,0},{0,2},{2,4},{4,6},{7,1},{1,3},{3,5},{5,7},{14,8},{8,10},{10,... | collective-permute-start | bytes 92168 | tf_op jit(solution)/shard_map/ppermute | solution.py:437
  71.2 2.7 %collective-permute-start.9 = (f32[3,2560]{1,0:T(4,128)S(1)}, f32[3,2560]{1,0:T(4,128)S(1)}, u32[]{:S(2)}, u32[]{:S(2)}) collective-permute-start(f32[3,2560]{1,0:T(4,128)S(1)} %get-tuple-element.42.refs_0_), channel_id=1, source_target_pairs={{4,0},{6,2},{0,4},{2,6},{5,1},{7,3},{1,5},{3,7},{12,8},{14,10},{8,... | collective-permute-start | bytes 92168 | tf_op jit(solution)/shard_map/ppermute | solution.py:437
  77.9 9.7 %grads_other.1 = (f32[640,512]{1,0:T(8,128)S(1)}, bf16[1152,256]{1,0:T(8,128)(2,1)S(1)}) custom-call(s32[16,640]{1,0:T(8,128)S(1)} %concatenate.11.bound_ref, bf16[640,1024]{1,0:T(8,128)(2,1)S(1)} %fusion.1.refs_0_.refs_2_.q_ref.g_ref, bf16[640,1024]{1,0:T(8,128)(2,1)S(1)} %fusion.1.refs_0_.refs_2_.q_ref.g_ref, ...), custom_call_target="tpu_custom_call" | custom-call | flops 3774873600 | bytes 8388608 | tf_op jit(solution)/shard_map/grads_other/pallas_call | solution.py:441
  89.1 13.8 %grads_own.1 = (bf16[1024,1024]{1,0:T(8,128)(2,1)}, f32[1152,256]{1,0:T(8,128)}) custom-call(s32[16,640]{1,0:T(8,128)S(1)} %concatenate.10.bound_ref, bf16[640,1024]{1,0:T(8,128)(2,1)S(1)} %fusion.1.refs_0_.refs_2_.q_ref.g_ref, bf16[640,1024]{1,0:T(8,128)(2,1)S(1)} %fusion.1.refs_0_.refs_2_.q_ref.g_ref, bf16[1152,256]{1,0:T(8,128)(2,1)S(1)} %project_last.1.refs_1_.kv_ref, ...), custom_call_target="tpu_custom_call" | custom-call | flops 3774873600 | bytes 8388608 | tf_op jit(solution)/shard_map/grads_own/pallas_call | solution.py:441
  102.9 4.0 %all-to-all-start.2 = ((bf16[8,128,1024]{2,1,0:T(8,128)(2,1)}), bf16[8,128,1024]{2,1,0:T(8,128)(2,1)S(1)}, u32[]{:S(2)}, u32[]{:S(2)}) async-start(bf16[8,128,1024]{2,1,0:T(8,128)(2,1)} %bitcast.42), calls=%async_computation.2 | async-start | bytes 4194304 | tf_op jit(solution)/shard_map/all_to_all | solution.py:477
  106.9 9.0 %weight_grad.1 = (f32[2,320,256]{2,1,0:T(8,128)S(1)}, f32[2,320,256]{2,1,0:T(8,128)S(1)}, f32[2,320,256]{2,1,0:T(8,128)S(1)}, f32[2,320,256]{2,1,0:T(8,128)}, bf...) custom-call(f32[1152,256]{1,0:T(8,128)} %get-tuple-element.46.own_re, ...), custom_call_target="tpu_custom_call" | custom-call | flops 3019898880 | bytes 11796480 | tf_op jit(solution)/shard_map/weight_grad/pallas_call | solution.py:481
  118.2 2.7 %collective-permute-start.16 = (bf16[2,320,256]{2,1,0:T(8,128)(2,1)S(1)}, bf16[2,320,256]{2,1,0:T(8,128)(2,1)S(1)}, u32[]{:S(2)}, u32[]{:S(2)}) collective-permute-start(bf16[2,320,256]{2,1,0:T(8,128)(2,1)S(1)} %add_convert_fusion.2), channel_id=1, source_target_pairs={{64,0},{96,32},{0,64},{32,96},{65,1},{97,33},{1,65},{33,97},{66,2}... | collective-permute-start | bytes 983048 | tf_op jit(solution)/shard_map/ppermute | solution.py:504
  120.9 1.6 %collective-permute-start.18 = (bf16[2,320,256]{2,1,0:T(8,128)(2,1)S(1)}, bf16[2,320,256]{2,1,0:T(8,128)(2,1)S(1)}, u32[]{:S(2)}, u32[]{:S(2)}) collective-permute-start(bf16[2,320,256]{2,1,0:T(8,128)(2,1)S(1)} %add_convert_fusion.1), channel_id=1, source_target_pairs={{32,0},{64,32},{96,64},{0,96},{33,1},{65,33},{97,65},{1,97},{34,2}... | collective-permute-start | bytes 983048 | tf_op jit(solution)/shard_map/ppermute | solution.py:504
  122.6 13.1 %collective-permute-done.14 = bf16[2,320,256]{2,1,0:T(8,128)(2,1)S(1)} collective-permute-done((bf16[2,320,256]{2,1,0:T(8,128)(2,1)S(1)}, bf16[2,320,256]{2,1,0:T(8,128)(2,1)S(1)}, u32[]{:S(2)}, u32[]{:S(2)}) %collective-permute-start.14) | collective-permute-done | bytes 327712 | tf_op jit(solution)/shard_map/ppermute | solution.py:504
  137.4 5.8 %all-to-all-start.3 = ((bf16[16,40,256]{2,1,0:T(8,128)(2,1)}), bf16[16,40,256]{2,1,0:T(8,128)(2,1)S(1)}, u32[]{:S(2)}, u32[]{:S(2)}) async-start(bf16[16,40,256]{2,1,0:T(8,128)(2,1)} %bitcast.14), calls=%async_computation.3 | async-start | bytes 655360 | tf_op jit(solution)/shard_map/all_to_all | solution.py:507
  144.2 7.8 %all-to-all-done.3 = bf16[16,40,256]{2,1,0:T(8,128)(2,1)S(1)} async-done(((bf16[16,40,256]{2,1,0:T(8,128)(2,1)}), bf16[16,40,256]{2,1,0:T(8,128)(2,1)S(1)}, u32[]{:S(2)}, u32[]{:S(2)}) %all-to-all-start.3) | async-done | bytes 327712 | tf_op jit(solution)/shard_map/all_to_all | solution.py:507
  (68 shorter events, 24.4 us)
Async XLA Ops:
  2.1 17.3 %all-to-all-start = ((bf16[16,40,256]{2,1,0:T(8,128)(2,1)}), bf16[16,40,256]{2,1,0:T(8,128)(2,1)S(1)}, u32[]{:S(2)}, u32[]{:S(2)}) async-start(bf16[16,40,256]{2,1,0:T(8,128)(2,1)} %weight_copies.1), calls=%async_computation | async-start | bytes 655360 | tf_op jit(solution)/shard_map/all_to_all | solution.py:356
  19.4 10.3 %copy-start.1 = (bf16[1,128,5120]{2,1,0:T(8,128)(2,1)S(1)}, bf16[1,128,5120]{2,1,0:T(8,128)(2,1)}, u32[]{:S(2)}) copy-start(bf16[1,128,5120]{2,1,0:T(8,128)(2,1)} %param.8) | copy-start | bytes 3932164
  19.4 33.4 %all-to-all-start.1 = ((bf16[8,128,1024]{2,1,0:T(8,128)(2,1)}), bf16[8,128,1024]{2,1,0:T(8,128)(2,1)}, u32[]{:S(2)}, u32[]{:S(2)}) async-start(bf16[8,128,1024]{2,1,0:T(8,128)(2,1)} %query_halves.1), calls=%async_computation.1 | async-start | bytes 4194304 | tf_op jit(solution)/shard_map/all_to_all | solution.py:373
  23.9 5.8 %collective-permute-start.5 = (bf16[2,320,256]{2,1,0:T(8,128)(2,1)S(1)}, bf16[2,320,256]{2,1,0:T(8,128)(2,1)S(1)}, u32[]{:S(2)}, u32[]{:S(2)}) collective-permute-start(bf16[2,320,256]{2,1,0:T(8,128)(2,1)S(1)} %bitcast.35), channel_id=1, source_target_pairs={{0,8},{8,0},{1,9},{9,1},{2,10},{10,2},{3,11},{11,3},{4,12},{12,4},... | collective-permute-start | bytes 983048 | tf_op jit(solution)/shard_map/ppermute | solution.py:372
  24.0 11.3 %collective-permute-start.4 = (bf16[2,320,256]{2,1,0:T(8,128)(2,1)S(1)}, bf16[2,320,256]{2,1,0:T(8,128)(2,1)S(1)}, u32[]{:S(2)}, u32[]{:S(2)}) collective-permute-start(bf16[2,320,256]{2,1,0:T(8,128)(2,1)S(1)} %bitcast.36), channel_id=1, source_target_pairs={{96,0},{0,32},{32,64},{64,96},{97,1},{1,33},{33,65},{65,97},{98,2}... | collective-permute-start | bytes 983048 | tf_op jit(solution)/shard_map/ppermute | solution.py:371
  25.6 17.8 %collective-permute-start.1 = (bf16[2,320,256]{2,1,0:T(8,128)(2,1)S(1)}, bf16[2,320,256]{2,1,0:T(8,128)(2,1)S(1)}, u32[]{:S(2)}, u32[]{:S(2)}) collective-permute-start(bf16[2,320,256]{2,1,0:T(8,128)(2,1)S(1)} %bitcast.37), channel_id=1, source_target_pairs={{64,0},{96,32},{0,64},{32,96},{65,1},{97,33},{1,65},{33,97},{66,2}... | collective-permute-start | bytes 983048 | tf_op jit(solution)/shard_map/ppermute | solution.py:371
  28.3 15.1 %collective-permute-start = (bf16[2,320,256]{2,1,0:T(8,128)(2,1)S(1)}, bf16[2,320,256]{2,1,0:T(8,128)(2,1)S(1)}, u32[]{:S(2)}, u32[]{:S(2)}) collective-permute-start(bf16[2,320,256]{2,1,0:T(8,128)(2,1)S(1)} %bitcast.38), channel_id=1, source_target_pairs={{32,0},{64,32},{96,64},{0,96},{33,1},{65,33},{97,65},{1,97},{34,2}... | collective-permute-start | bytes 983048 | tf_op jit(solution)/shard_map/ppermute | solution.py:371
  35.3 8.5 %collective-permute-start.6 = (bf16[2,320,256]{2,1,0:T(8,128)(2,1)S(1)}, bf16[2,320,256]{2,1,0:T(8,128)(2,1)S(1)}, u32[]{:S(2)}, u32[]{:S(2)}) collective-permute-start(bf16[2,320,256]{2,1,0:T(8,128)(2,1)S(1)} %collective-permute-done.4.refs_0_), channel_id=1, source_target_pairs={{0,8},{8,0},{1,9},{9,1},{2,10},{10,2},{3,11},{11,3},{4,12},{12,4},... | collective-permute-start | bytes 983048 | tf_op jit(solution)/shard_map/ppermute | solution.py:397
  43.3 1.6 %collective-permute-start.3 = (bf16[2,320,256]{2,1,0:T(8,128)(2,1)S(1)}, bf16[2,320,256]{2,1,0:T(8,128)(2,1)S(1)}, u32[]{:S(2)}, u32[]{:S(2)}) collective-permute-start(bf16[2,320,256]{2,1,0:T(8,128)(2,1)S(1)} %collective-permute-done.1.refs_1_), channel_id=1, source_target_pairs={{0,8},{8,0},{1,9},{9,1},{2,10},{10,2},{3,11},{11,3},{4,12},{12,4},... | collective-permute-start | bytes 983048 | tf_op jit(solution)/shard_map/ppermute | solution.py:397
  43.3 2.1 %collective-permute-start.2 = (bf16[2,320,256]{2,1,0:T(8,128)(2,1)S(1)}, bf16[2,320,256]{2,1,0:T(8,128)(2,1)S(1)}, u32[]{:S(2)}, u32[]{:S(2)}) collective-permute-start(bf16[2,320,256]{2,1,0:T(8,128)(2,1)S(1)} %collective-permute-done.refs_0_), channel_id=1, source_target_pairs={{0,8},{8,0},{1,9},{9,1},{2,10},{10,2},{3,11},{11,3},{4,12},{12,4},... | collective-permute-start | bytes 983048 | tf_op jit(solution)/shard_map/ppermute | solution.py:397
  47.3 15.5 %collective-permute-start.7 = (bf16[1152,256]{1,0:T(8,128)(2,1)S(1)}, bf16[1152,256]{1,0:T(8,128)(2,1)S(1)}, u32[]{:S(2)}, u32[]{:S(2)}) collective-permute-start(bf16[1152,256]{1,0:T(8,128)(2,1)S(1)} %project_last.1.refs_1_.kv_ref), channel_id=1, source_target_pairs={{0,1},{1,0},{2,3},{3,2},{4,5},{5,4},{6,7},{7,6},{8,9},{9,8},{10,11... | collective-permute-start | bytes 1769480 | tf_op jit(solution)/shard_map/ppermute | solution.py:400
  69.4 6.0 %collective-permute-start.10 = (f32[3,2560]{1,0:T(4,128)S(1)}, f32[3,2560]{1,0:T(4,128)S(1)}, u32[]{:S(2)}, u32[]{:S(2)}) collective-permute-start(f32[3,2560]{1,0:T(4,128)S(1)} %get-tuple-element.42.refs_0_), channel_id=1, source_target_pairs={{6,0},{0,2},{2,4},{4,6},{7,1},{1,3},{3,5},{5,7},{14,8},{8,10},{10,... | collective-permute-start | bytes 92168 | tf_op jit(solution)/shard_map/ppermute | solution.py:437
  71.2 5.5 %collective-permute-start.9 = (f32[3,2560]{1,0:T(4,128)S(1)}, f32[3,2560]{1,0:T(4,128)S(1)}, u32[]{:S(2)}, u32[]{:S(2)}) collective-permute-start(f32[3,2560]{1,0:T(4,128)S(1)} %get-tuple-element.42.refs_0_), channel_id=1, source_target_pairs={{4,0},{6,2},{0,4},{2,6},{5,1},{7,3},{1,5},{3,7},{12,8},{14,10},{8,... | collective-permute-start | bytes 92168 | tf_op jit(solution)/shard_map/ppermute | solution.py:437
  73.9 4.0 %collective-permute-start.8 = (f32[3,2560]{1,0:T(4,128)S(1)}, f32[3,2560]{1,0:T(4,128)S(1)}, u32[]{:S(2)}, u32[]{:S(2)}) collective-permute-start(f32[3,2560]{1,0:T(4,128)S(1)} %get-tuple-element.42.refs_0_), channel_id=1, source_target_pairs={{2,0},{4,2},{6,4},{0,6},{3,1},{5,3},{7,5},{1,7},{10,8},{12,10},{14... | collective-permute-start | bytes 92168 | tf_op jit(solution)/shard_map/ppermute | solution.py:437
  87.6 19.3 %collective-permute-start.11 = (bf16[1152,256]{1,0:T(8,128)(2,1)S(1)}, bf16[1152,256]{1,0:T(8,128)(2,1)S(1)}, u32[]{:S(2)}, u32[]{:S(2)}) collective-permute-start(bf16[1152,256]{1,0:T(8,128)(2,1)S(1)} %get-tuple-element.47), channel_id=1, source_target_pairs={{0,1},{1,0},{2,3},{3,2},{4,5},{5,4},{6,7},{7,6},{8,9},{9,8},{10,11... | collective-permute-start | bytes 1769480 | tf_op jit(solution)/shard_map/ppermute | solution.py:473
  102.9 34.5 %all-to-all-start.2 = ((bf16[8,128,1024]{2,1,0:T(8,128)(2,1)}), bf16[8,128,1024]{2,1,0:T(8,128)(2,1)S(1)}, u32[]{:S(2)}, u32[]{:S(2)}) async-start(bf16[8,128,1024]{2,1,0:T(8,128)(2,1)} %bitcast.42), calls=%async_computation.2 | async-start | bytes 4194304 | tf_op jit(solution)/shard_map/all_to_all | solution.py:477
  115.8 1.7 %collective-permute-start.13 = (bf16[2,320,256]{2,1,0:T(8,128)(2,1)S(1)}, bf16[2,320,256]{2,1,0:T(8,128)(2,1)S(1)}, u32[]{:S(2)}, u32[]{:S(2)}) collective-permute-start(bf16[2,320,256]{2,1,0:T(8,128)(2,1)S(1)} %get-tuple-element.51), channel_id=1, source_target_pairs={{0,8},{8,0},{1,9},{9,1},{2,10},{10,2},{3,11},{11,3},{4,12},{12,4},... | collective-permute-start | bytes 983048 | tf_op jit(solution)/shard_map/ppermute | solution.py:500
  115.9 2.2 %collective-permute-start.15 = (bf16[2,320,256]{2,1,0:T(8,128)(2,1)S(1)}, bf16[2,320,256]{2,1,0:T(8,128)(2,1)S(1)}, u32[]{:S(2)}, u32[]{:S(2)}) collective-permute-start(bf16[2,320,256]{2,1,0:T(8,128)(2,1)S(1)} %get-tuple-element.53), channel_id=1, source_target_pairs={{0,8},{8,0},{1,9},{9,1},{2,10},{10,2},{3,11},{11,3},{4,12},{12,4},... | collective-permute-start | bytes 983048 | tf_op jit(solution)/shard_map/ppermute | solution.py:500
  116.4 6.1 %collective-permute-start.12 = (bf16[2,320,256]{2,1,0:T(8,128)(2,1)S(1)}, bf16[2,320,256]{2,1,0:T(8,128)(2,1)S(1)}, u32[]{:S(2)}, u32[]{:S(2)}) collective-permute-start(bf16[2,320,256]{2,1,0:T(8,128)(2,1)S(1)} %get-tuple-element.49), channel_id=1, source_target_pairs={{0,8},{8,0},{1,9},{9,1},{2,10},{10,2},{3,11},{11,3},{4,12},{12,4},... | collective-permute-start | bytes 983048 | tf_op jit(solution)/shard_map/ppermute | solution.py:500
  116.5 4.3 %collective-permute-start.17 = (bf16[2,320,256]{2,1,0:T(8,128)(2,1)S(1)}, bf16[2,320,256]{2,1,0:T(8,128)(2,1)S(1)}, u32[]{:S(2)}, u32[]{:S(2)}) collective-permute-start(bf16[2,320,256]{2,1,0:T(8,128)(2,1)S(1)} %get-tuple-element.55), channel_id=1, source_target_pairs={{0,8},{8,0},{1,9},{9,1},{2,10},{10,2},{3,11},{11,3},{4,12},{12,4},... | collective-permute-start | bytes 983048 | tf_op jit(solution)/shard_map/ppermute | solution.py:500
  117.6 18.1 %collective-permute-start.14 = (bf16[2,320,256]{2,1,0:T(8,128)(2,1)S(1)}, bf16[2,320,256]{2,1,0:T(8,128)(2,1)S(1)}, u32[]{:S(2)}, u32[]{:S(2)}) collective-permute-start(bf16[2,320,256]{2,1,0:T(8,128)(2,1)S(1)} %add_convert_fusion.3), channel_id=1, source_target_pairs={{96,0},{0,32},{32,64},{64,96},{97,1},{1,33},{33,65},{65,97},{98,2}... | collective-permute-start | bytes 983048 | tf_op jit(solution)/shard_map/ppermute | solution.py:504
  118.2 17.5 %collective-permute-start.16 = (bf16[2,320,256]{2,1,0:T(8,128)(2,1)S(1)}, bf16[2,320,256]{2,1,0:T(8,128)(2,1)S(1)}, u32[]{:S(2)}, u32[]{:S(2)}) collective-permute-start(bf16[2,320,256]{2,1,0:T(8,128)(2,1)S(1)} %add_convert_fusion.2), channel_id=1, source_target_pairs={{64,0},{96,32},{0,64},{32,96},{65,1},{97,33},{1,65},{33,97},{66,2}... | collective-permute-start | bytes 983048 | tf_op jit(solution)/shard_map/ppermute | solution.py:504
  120.9 15.5 %collective-permute-start.18 = (bf16[2,320,256]{2,1,0:T(8,128)(2,1)S(1)}, bf16[2,320,256]{2,1,0:T(8,128)(2,1)S(1)}, u32[]{:S(2)}, u32[]{:S(2)}) collective-permute-start(bf16[2,320,256]{2,1,0:T(8,128)(2,1)S(1)} %add_convert_fusion.1), channel_id=1, source_target_pairs={{32,0},{64,32},{96,64},{0,96},{33,1},{65,33},{97,65},{1,97},{34,2}... | collective-permute-start | bytes 983048 | tf_op jit(solution)/shard_map/ppermute | solution.py:504
  137.4 14.6 %all-to-all-start.3 = ((bf16[16,40,256]{2,1,0:T(8,128)(2,1)}), bf16[16,40,256]{2,1,0:T(8,128)(2,1)S(1)}, u32[]{:S(2)}, u32[]{:S(2)}) async-start(bf16[16,40,256]{2,1,0:T(8,128)(2,1)} %bitcast.14), calls=%async_computation.3 | async-start | bytes 655360 | tf_op jit(solution)/shard_map/all_to_all | solution.py:507
  (5 other events, 11.6 us)

commit v11 on v10

--- a/solution.py
+++ b/solution.py
@@ -152,7 +152,7 @@
     stat_refs, refs = refs[:NY], refs[NY:]
     if last:
         layout_hbm, out_ref, prev_ref, back_hbm, kvgrad_hbm = refs[:5]
-        acc, bias, back_ref, total_ref, layout_ref, sems = refs[5:]
+        acc, bias, back_ref, layout_ref, sems = refs[5:]
         bring = pltpu.make_async_copy(layout_hbm, layout_ref, sems.at[N_SEQ + 1])
     else:
         back_ref, kvgrad_ref, acc, bias = refs
@@ -246,14 +246,13 @@
     @pl.when(step == pl.num_programs(0) - 1)
     def _():
         if last:
-            total_ref[...] = acc[...].T
-            copy = pltpu.make_async_copy(total_ref, kvgrad_hbm, sems.at[N_SEQ])
+            copy = pltpu.make_async_copy(acc, kvgrad_hbm, sems.at[N_SEQ])
             copy.start()
             for r in range(N_SEQ):
                 leave(r).wait()
             copy.wait()
         else:
-            kvgrad_ref[...] = acc[...].T.astype(BF16)
+            kvgrad_ref[...] = acc[...].astype(BF16)
 
 
 def weight_kernel(cuts, own_ref, got_ref, prompt_ref, resp_ref, *refs):
@@ -271,8 +270,7 @@
         copy.start()
     x, core = lax.axis_index("x"), lax.axis_index("c")
     grad = (own_ref[...] + got_ref[...].astype(F32)).astype(BF16)
-    prompt_grad_ref[...] = grad[:plen]
-    grad = grad.T
+    prompt_grad_ref[...] = grad[:, :plen].T
     spans = list(cuts[:-1]) + [(cuts[-1][0], buf.shape[0])]
     swapped = core == 1
     for n, (lo, hi) in enumerate(spans):
@@ -444,20 +442,21 @@
             in_specs=[
                 pl.BlockSpec((16, SLOTS), lambda i: (0, i)), slot_block, g_block, whole,
             ] + [stat_block] * NY + [hbm, slot_block, slot_block] * last,
-            out_specs=[hbm, hbm] if last else [slot_block, whole],
+            out_specs=[hbm, hbm]
+            if last
+            else [slot_block, pl.BlockSpec((2 * DH, keys), lambda i: (0, 0))],
             out_shape=[
                 pltpu.HBM((N_SEQ * slots, 2 * half), BF16),
-                pltpu.HBM((keys, 2 * DH), F32),
+                pltpu.HBM((2 * DH, keys), F32),
             ]
             if last
             else [
                 jax.ShapeDtypeStruct((live_all, half), F32),
-                jax.ShapeDtypeStruct((keys, 2 * DH), BF16),
+                jax.ShapeDtypeStruct((2 * DH, keys), BF16),
             ],
             scratch_shapes=[pltpu.VMEM((2 * DH, keys), F32), pltpu.VMEM((8, plen), F32)]
             + [
                 pltpu.VMEM((N_SEQ * slots, 2 * half), BF16),
-                pltpu.VMEM((keys, 2 * DH), F32),
                 pltpu.SMEM((3 * N_SEQ,), jnp.int32),
                 pltpu.SemaphoreType.DMA((N_SEQ + 2,)),
             ]

time: 154 us -> 153 us (level)
  no operation moved by 1% of the time
where the time goes in v11:
time: 153 us; the launch traced here: 152 us
  Pallas kernels  51.3 us (34%)
  starting transfers between devices  44.1 us (29%)
  waiting for transfers between devices  41.4 us (27%)
  local copies, waits for them, and re-layouts  6.81 us (4%)
  other arithmetic  3.83 us (3%)
  matrix products  3.15 us (2%)
  between operations  1.53 us (1%)
    pallas_call x2, Pallas kernels, backward(): pl.pallas_call(functools.partial(second_pass, coef, scale, last), grid=(s...  23 us
    ppermute x3, waiting for transfers between devices, per_device(): line = line + lax.ppermute(piece, 'x', shift(-k)).astype(F32)  13.7 us
    pallas_call x2, Pallas kernels, forward(): pl.pallas_call(functools.partial(first_pass, coef, last), grid=(steps,),...  12.4 us
    pallas_call x1, Pallas kernels, per_device(): pl.pallas_call(functools.partial(weight_kernel, cuts), in_specs=[vmem] *...  8.96 us
    ppermute x3, waiting for transfers between devices, per_device(): nears = [block] + [lax.ppermute(block, 'x', shift(k)) for k in range(1, NX)]  8.63 us
    all_to_all x1, starting transfers between devices, per_device(): lax.all_to_all(block, PLANE, 0, 0, tiled=True).reshape(2, 8 * shard, 2 * DH)  8.13 us
    all_to_all x1, waiting for transfers between devices, per_device(): shares = lax.all_to_all(line, PLANE, 0, 0, tiled=True)  7.84 us
    unnamed x12, local copies, waits for them, and re-layouts  6.6 us
  transfers between devices with their start and end apart: 23, of which 13 were waited for; matrix products, arithmetic and copies ran while one was open for 4% of the time, Pallas kernels for 23%

profile of v11, /device:TPU:0, one launch (start us, length us, event | category | flops | bytes accessed | tf_op | source)
XLA Modules:
  0.0 152.2 jit_solution(16768890284901603220)
XLA Ops:
  2.1 8.1 %all-to-all-start = ((bf16[16,40,256]{2,1,0:T(8,128)(2,1)}), bf16[16,40,256]{2,1,0:T(8,128)(2,1)S(1)}, u32[]{:S(2)}, u32[]{:S(2)}) async-start(bf16[16,40,256]{2,1,0:T(8,128)(2,1)} %weight_copies.1), calls=%async_computation | async-start | bytes 655360 | tf_op jit(solution)/shard_map/all_to_all | solution.py:354
  16.5 2.9 %all-to-all-done = bf16[16,40,256]{2,1,0:T(8,128)(2,1)S(1)} async-done(((bf16[16,40,256]{2,1,0:T(8,128)(2,1)}), bf16[16,40,256]{2,1,0:T(8,128)(2,1)S(1)}, u32[]{:S(2)}, u32[]{:S(2)}) %all-to-all-start) | async-done | bytes 327712 | tf_op jit(solution)/shard_map/all_to_all | solution.py:354
  19.4 4.5 %all-to-all-start.1 = ((bf16[8,128,1024]{2,1,0:T(8,128)(2,1)}), bf16[8,128,1024]{2,1,0:T(8,128)(2,1)}, u32[]{:S(2)}, u32[]{:S(2)}) async-start(bf16[8,128,1024]{2,1,0:T(8,128)(2,1)} %query_halves.1), calls=%async_computation.1 | async-start | bytes 4194304 | tf_op jit(solution)/shard_map/all_to_all | solution.py:371
  24.0 1.6 %collective-permute-start.4 = (bf16[2,320,256]{2,1,0:T(8,128)(2,1)S(1)}, bf16[2,320,256]{2,1,0:T(8,128)(2,1)S(1)}, u32[]{:S(2)}, u32[]{:S(2)}) collective-permute-start(bf16[2,320,256]{2,1,0:T(8,128)(2,1)S(1)} %bitcast.36), channel_id=1, source_target_pairs={{96,0},{0,32},{32,64},{64,96},{97,1},{1,33},{33,65},{65,97},{98,2}... | collective-permute-start | bytes 983048 | tf_op jit(solution)/shard_map/ppermute | solution.py:369
  25.6 2.7 %collective-permute-start.1 = (bf16[2,320,256]{2,1,0:T(8,128)(2,1)S(1)}, bf16[2,320,256]{2,1,0:T(8,128)(2,1)S(1)}, u32[]{:S(2)}, u32[]{:S(2)}) collective-permute-start(bf16[2,320,256]{2,1,0:T(8,128)(2,1)S(1)} %bitcast.37), channel_id=1, source_target_pairs={{64,0},{96,32},{0,64},{32,96},{65,1},{97,33},{1,65},{33,97},{66,2}... | collective-permute-start | bytes 983048 | tf_op jit(solution)/shard_map/ppermute | solution.py:369
  29.7 4.0 %copy-done = bf16[1,1024,5120]{2,1,0:T(8,128)(2,1)S(1)} copy-done((bf16[1,1024,5120]{2,1,0:T(8,128)(2,1)S(1)}, bf16[1,1024,5120]{2,1,0:T(8,128)(2,1)}, u32[]{:S(2)}) %copy-start) | copy-done | bytes 10485784
  35.3 8.0 %collective-permute-done.1.refs_1_ = bf16[2,320,256]{2,1,0:T(8,128)(2,1)S(1)} collective-permute-done((bf16[2,320,256]{2,1,0:T(8,128)(2,1)S(1)}, bf16[2,320,256]{2,1,0:T(8,128)(2,1)S(1)}, u32[]{:S(2)}, u32[]{:S(2)}) %collective-permute-start.1) | collective-permute-done | bytes 327712 | tf_op jit(solution)/shard_map/ppermute | solution.py:369
  45.4 1.9 %project_last.1.refs_1_.kv_ref = bf16[1152,256]{1,0:T(8,128)(2,1)S(1)} custom-call(bf16[1024,5120]{1,0:T(8,128)(2,1)S(1)} %bitcast.30, bf16[128,5120]{1,0:T(8,128)(2,1)S(1)} %bitcast.34, bf16[2,320,256]{2,1,0:T(8,128)(2,1)S(1)} %collective-permute-done.refs_0_, bf16[2,320,256]{2,1,0:T(8,128)(2,1)S(1)} %collective-permute-done.1.refs_1_, ...), custom_call_target="tpu_custom_call" | custom-call | flops 1509949440 | bytes 5898240 | tf_op jit(solution)/shard_map/project_last/pallas_call | solution.py:375
  47.3 1.9 %collective-permute-start.7 = (bf16[1152,256]{1,0:T(8,128)(2,1)S(1)}, bf16[1152,256]{1,0:T(8,128)(2,1)S(1)}, u32[]{:S(2)}, u32[]{:S(2)}) collective-permute-start(bf16[1152,256]{1,0:T(8,128)(2,1)S(1)} %project_last.1.refs_1_.kv_ref), channel_id=1, source_target_pairs={{0,1},{1,0},{2,3},{3,2},{4,5},{5,4},{6,7},{7,6},{8,9},{9,8},{10,11... | collective-permute-start | bytes 1769480 | tf_op jit(solution)/shard_map/ppermute | solution.py:398
  49.2 3.7 %all-to-all-done.1 = bf16[8,128,1024]{2,1,0:T(8,128)(2,1)} async-done(((bf16[8,128,1024]{2,1,0:T(8,128)(2,1)}), bf16[8,128,1024]{2,1,0:T(8,128)(2,1)}, u32[]{:S(2)}, u32[]{:S(2)}) %all-to-all-start.1) | async-done | bytes 2097184 | tf_op jit(solution)/shard_map/all_to_all | solution.py:371
  52.9 3.1 %fusion.1.refs_0_.refs_2_.q_ref.g_ref = bf16[640,1024]{1,0:T(8,128)(2,1)S(1)} fusion(bf16[1024,1024]{1,0:T(8,128)(2,1)} %bitcast.11, s32[640]{0:T(1024)S(1)} %get-tuple-element.34), kind=kOutput, calls=%fused_computation.2 | convolution fusion | flops 1343488000 | bytes 3410432 | tf_op jit(solution)/shard_map/dot_general | solution.py:432
  56.0 5.8 %attend_own.1 = (f32[128,2560]{1,0:T(8,128)S(1)}, f32[3,2560]{1,0:T(4,128)S(1)}) custom-call(s32[16,640]{1,0:T(8,128)S(1)} %concatenate.10.bound_ref, bf16[640,1024]{1,0:T(8,128)(2,1)S(1)} %fusion.1.refs_0_.refs_2_.q_ref.g_ref, bf16[1152,256]{1,0:T(8,128)(2,1)S(1)} %project_last.1.refs_1_.kv_ref), custom_call_target="tpu_custom_call" | custom-call | flops 1509949440 | bytes 4194304 | tf_op jit(solution)/shard_map/attend_own/pallas_call | solution.py:411
  62.8 6.5 %attend_more.1 = (bf16[640,512]{1,0:T(8,128)(2,1)S(1)}, f32[3,2560]{1,0:T(4,128)S(1)}) custom-call(s32[16,640]{1,0:T(8,128)S(1)} %concatenate.11.bound_ref, bf16[640,1024]{1,0:T(8,128)(2,1)S(1)} %fusion.1.refs_0_.refs_2_.q_ref.g_ref, bf16[1152,256]{1,0:T(8,128)(2,1)S(1)} %collective-permute-done.7.refs_1_.kv_ref, ...), custom_call_target="tpu_custom_call" | custom-call | flops 1509949440 | bytes 4194304 | tf_op jit(solution)/shard_map/attend_more/pallas_call | solution.py:411
  69.4 1.8 %collective-permute-start.10 = (f32[3,2560]{1,0:T(4,128)S(1)}, f32[3,2560]{1,0:T(4,128)S(1)}, u32[]{:S(2)}, u32[]{:S(2)}) collective-permute-start(f32[3,2560]{1,0:T(4,128)S(1)} %get-tuple-element.42.refs_0_), channel_id=1, source_target_pairs={{6,0},{0,2},{2,4},{4,6},{7,1},{1,3},{3,5},{5,7},{14,8},{8,10},{10,... | collective-permute-start | bytes 92168 | tf_op jit(solution)/shard_map/ppermute | solution.py:435
  71.2 2.7 %collective-permute-start.9 = (f32[3,2560]{1,0:T(4,128)S(1)}, f32[3,2560]{1,0:T(4,128)S(1)}, u32[]{:S(2)}, u32[]{:S(2)}) collective-permute-start(f32[3,2560]{1,0:T(4,128)S(1)} %get-tuple-element.42.refs_0_), channel_id=1, source_target_pairs={{4,0},{6,2},{0,4},{2,6},{5,1},{7,3},{1,5},{3,7},{12,8},{14,10},{8,... | collective-permute-start | bytes 92168 | tf_op jit(solution)/shard_map/ppermute | solution.py:435
  77.9 9.5 %grads_other.1 = (f32[640,512]{1,0:T(8,128)S(1)}, bf16[256,1152]{1,0:T(8,128)(2,1)S(1)}) custom-call(s32[16,640]{1,0:T(8,128)S(1)} %concatenate.11.bound_ref, bf16[640,1024]{1,0:T(8,128)(2,1)S(1)} %fusion.1.refs_0_.refs_2_.q_ref.g_ref, bf16[640,1024]{1,0:T(8,128)(2,1)S(1)} %fusion.1.refs_0_.refs_2_.q_ref.g_ref, ...), custom_call_target="tpu_custom_call" | custom-call | flops 3774873600 | bytes 8388608 | tf_op jit(solution)/shard_map/grads_other/pallas_call | solution.py:439
  88.9 13.5 %grads_own.1 = (bf16[1024,1024]{1,0:T(8,128)(2,1)}, f32[256,1152]{1,0:T(8,128)}) custom-call(s32[16,640]{1,0:T(8,128)S(1)} %concatenate.10.bound_ref, bf16[640,1024]{1,0:T(8,128)(2,1)S(1)} %fusion.1.refs_0_.refs_2_.q_ref.g_ref, bf16[640,1024]{1,0:T(8,128)(2,1)S(1)} %fusion.1.refs_0_.refs_2_.q_ref.g_ref, bf16[1152,256]{1,0:T(8,128)(2,1)S(1)} %project_last.1.refs_1_.kv_ref, ...), custom_call_target="tpu_custom_call" | custom-call | flops 3774873600 | bytes 8388608 | tf_op jit(solution)/shard_map/grads_own/pallas_call | solution.py:439
  102.5 4.0 %all-to-all-start.2 = ((bf16[8,128,1024]{2,1,0:T(8,128)(2,1)}), bf16[8,128,1024]{2,1,0:T(8,128)(2,1)S(1)}, u32[]{:S(2)}, u32[]{:S(2)}) async-start(bf16[8,128,1024]{2,1,0:T(8,128)(2,1)} %bitcast.42), calls=%async_computation.2 | async-start | bytes 4194304 | tf_op jit(solution)/shard_map/all_to_all | solution.py:476
  106.4 9.0 %weight_grad.1 = (f32[2,320,256]{2,1,0:T(8,128)S(1)}, f32[2,320,256]{2,1,0:T(8,128)S(1)}, f32[2,320,256]{2,1,0:T(8,128)S(1)}, f32[2,320,256]{2,1,0:T(8,128)}, bf...) custom-call(f32[256,1152]{1,0:T(8,128)} %get-tuple-element.46.own_re, ...), custom_call_target="tpu_custom_call" | custom-call | flops 3019898880 | bytes 11796480 | tf_op jit(solution)/shard_map/weight_grad/pallas_call | solution.py:480
  117.9 2.5 %collective-permute-start.16 = (bf16[2,320,256]{2,1,0:T(8,128)(2,1)S(1)}, bf16[2,320,256]{2,1,0:T(8,128)(2,1)S(1)}, u32[]{:S(2)}, u32[]{:S(2)}) collective-permute-start(bf16[2,320,256]{2,1,0:T(8,128)(2,1)S(1)} %add_convert_fusion.2), channel_id=1, source_target_pairs={{64,0},{96,32},{0,64},{32,96},{65,1},{97,33},{1,65},{33,97},{66,2}... | collective-permute-start | bytes 983048 | tf_op jit(solution)/shard_map/ppermute | solution.py:503
  120.5 1.8 %collective-permute-start.18 = (bf16[2,320,256]{2,1,0:T(8,128)(2,1)S(1)}, bf16[2,320,256]{2,1,0:T(8,128)(2,1)S(1)}, u32[]{:S(2)}, u32[]{:S(2)}) collective-permute-start(bf16[2,320,256]{2,1,0:T(8,128)(2,1)S(1)} %add_convert_fusion.1), channel_id=1, source_target_pairs={{32,0},{64,32},{96,64},{0,96},{33,1},{65,33},{97,65},{1,97},{34,2}... | collective-permute-start | bytes 983048 | tf_op jit(solution)/shard_map/ppermute | solution.py:503
  122.3 12.9 %collective-permute-done.14 = bf16[2,320,256]{2,1,0:T(8,128)(2,1)S(1)} collective-permute-done((bf16[2,320,256]{2,1,0:T(8,128)(2,1)S(1)}, bf16[2,320,256]{2,1,0:T(8,128)(2,1)S(1)}, u32[]{:S(2)}, u32[]{:S(2)}) %collective-permute-start.14) | collective-permute-done | bytes 327712 | tf_op jit(solution)/shard_map/ppermute | solution.py:503
  136.9 5.8 %all-to-all-start.3 = ((bf16[16,40,256]{2,1,0:T(8,128)(2,1)}), bf16[16,40,256]{2,1,0:T(8,128)(2,1)S(1)}, u32[]{:S(2)}, u32[]{:S(2)}) async-start(bf16[16,40,256]{2,1,0:T(8,128)(2,1)} %bitcast.14), calls=%async_computation.3 | async-start | bytes 655360 | tf_op jit(solution)/shard_map/all_to_all | solution.py:506
  143.7 7.8 %all-to-all-done.3 = bf16[16,40,256]{2,1,0:T(8,128)(2,1)S(1)} async-done(((bf16[16,40,256]{2,1,0:T(8,128)(2,1)}), bf16[16,40,256]{2,1,0:T(8,128)(2,1)S(1)}, u32[]{:S(2)}, u32[]{:S(2)}) %all-to-all-start.3) | async-done | bytes 327712 | tf_op jit(solution)/shard_map/all_to_all | solution.py:506
  (68 shorter events, 24.6 us)
Async XLA Ops:
  2.1 17.3 %all-to-all-start = ((bf16[16,40,256]{2,1,0:T(8,128)(2,1)}), bf16[16,40,256]{2,1,0:T(8,128)(2,1)S(1)}, u32[]{:S(2)}, u32[]{:S(2)}) async-start(bf16[16,40,256]{2,1,0:T(8,128)(2,1)} %weight_copies.1), calls=%async_computation | async-start | bytes 655360 | tf_op jit(solution)/shard_map/all_to_all | solution.py:354
  19.4 10.3 %copy-start.1 = (bf16[1,128,5120]{2,1,0:T(8,128)(2,1)S(1)}, bf16[1,128,5120]{2,1,0:T(8,128)(2,1)}, u32[]{:S(2)}) copy-start(bf16[1,128,5120]{2,1,0:T(8,128)(2,1)} %param.8) | copy-start | bytes 3932164
  19.4 33.4 %all-to-all-start.1 = ((bf16[8,128,1024]{2,1,0:T(8,128)(2,1)}), bf16[8,128,1024]{2,1,0:T(8,128)(2,1)}, u32[]{:S(2)}, u32[]{:S(2)}) async-start(bf16[8,128,1024]{2,1,0:T(8,128)(2,1)} %query_halves.1), calls=%async_computation.1 | async-start | bytes 4194304 | tf_op jit(solution)/shard_map/all_to_all | solution.py:371
  23.9 5.8 %collective-permute-start.5 = (bf16[2,320,256]{2,1,0:T(8,128)(2,1)S(1)}, bf16[2,320,256]{2,1,0:T(8,128)(2,1)S(1)}, u32[]{:S(2)}, u32[]{:S(2)}) collective-permute-start(bf16[2,320,256]{2,1,0:T(8,128)(2,1)S(1)} %bitcast.35), channel_id=1, source_target_pairs={{0,8},{8,0},{1,9},{9,1},{2,10},{10,2},{3,11},{11,3},{4,12},{12,4},... | collective-permute-start | bytes 983048 | tf_op jit(solution)/shard_map/ppermute | solution.py:370
  24.0 11.3 %collective-permute-start.4 = (bf16[2,320,256]{2,1,0:T(8,128)(2,1)S(1)}, bf16[2,320,256]{2,1,0:T(8,128)(2,1)S(1)}, u32[]{:S(2)}, u32[]{:S(2)}) collective-permute-start(bf16[2,320,256]{2,1,0:T(8,128)(2,1)S(1)} %bitcast.36), channel_id=1, source_target_pairs={{96,0},{0,32},{32,64},{64,96},{97,1},{1,33},{33,65},{65,97},{98,2}... | collective-permute-start | bytes 983048 | tf_op jit(solution)/shard_map/ppermute | solution.py:369
  25.6 17.8 %collective-permute-start.1 = (bf16[2,320,256]{2,1,0:T(8,128)(2,1)S(1)}, bf16[2,320,256]{2,1,0:T(8,128)(2,1)S(1)}, u32[]{:S(2)}, u32[]{:S(2)}) collective-permute-start(bf16[2,320,256]{2,1,0:T(8,128)(2,1)S(1)} %bitcast.37), channel_id=1, source_target_pairs={{64,0},{96,32},{0,64},{32,96},{65,1},{97,33},{1,65},{33,97},{66,2}... | collective-permute-start | bytes 983048 | tf_op jit(solution)/shard_map/ppermute | solution.py:369
  28.3 15.1 %collective-permute-start = (bf16[2,320,256]{2,1,0:T(8,128)(2,1)S(1)}, bf16[2,320,256]{2,1,0:T(8,128)(2,1)S(1)}, u32[]{:S(2)}, u32[]{:S(2)}) collective-permute-start(bf16[2,320,256]{2,1,0:T(8,128)(2,1)S(1)} %bitcast.38), channel_id=1, source_target_pairs={{32,0},{64,32},{96,64},{0,96},{33,1},{65,33},{97,65},{1,97},{34,2}... | collective-permute-start | bytes 983048 | tf_op jit(solution)/shard_map/ppermute | solution.py:369
  35.3 8.5 %collective-permute-start.6 = (bf16[2,320,256]{2,1,0:T(8,128)(2,1)S(1)}, bf16[2,320,256]{2,1,0:T(8,128)(2,1)S(1)}, u32[]{:S(2)}, u32[]{:S(2)}) collective-permute-start(bf16[2,320,256]{2,1,0:T(8,128)(2,1)S(1)} %collective-permute-done.4.refs_0_), channel_id=1, source_target_pairs={{0,8},{8,0},{1,9},{9,1},{2,10},{10,2},{3,11},{11,3},{4,12},{12,4},... | collective-permute-start | bytes 983048 | tf_op jit(solution)/shard_map/ppermute | solution.py:395
  43.3 1.6 %collective-permute-start.3 = (bf16[2,320,256]{2,1,0:T(8,128)(2,1)S(1)}, bf16[2,320,256]{2,1,0:T(8,128)(2,1)S(1)}, u32[]{:S(2)}, u32[]{:S(2)}) collective-permute-start(bf16[2,320,256]{2,1,0:T(8,128)(2,1)S(1)} %collective-permute-done.1.refs_1_), channel_id=1, source_target_pairs={{0,8},{8,0},{1,9},{9,1},{2,10},{10,2},{3,11},{11,3},{4,12},{12,4},... | collective-permute-start | bytes 983048 | tf_op jit(solution)/shard_map/ppermute | solution.py:395
  43.3 2.1 %collective-permute-start.2 = (bf16[2,320,256]{2,1,0:T(8,128)(2,1)S(1)}, bf16[2,320,256]{2,1,0:T(8,128)(2,1)S(1)}, u32[]{:S(2)}, u32[]{:S(2)}) collective-permute-start(bf16[2,320,256]{2,1,0:T(8,128)(2,1)S(1)} %collective-permute-done.refs_0_), channel_id=1, source_target_pairs={{0,8},{8,0},{1,9},{9,1},{2,10},{10,2},{3,11},{11,3},{4,12},{12,4},... | collective-permute-start | bytes 983048 | tf_op jit(solution)/shard_map/ppermute | solution.py:395
  47.3 15.5 %collective-permute-start.7 = (bf16[1152,256]{1,0:T(8,128)(2,1)S(1)}, bf16[1152,256]{1,0:T(8,128)(2,1)S(1)}, u32[]{:S(2)}, u32[]{:S(2)}) collective-permute-start(bf16[1152,256]{1,0:T(8,128)(2,1)S(1)} %project_last.1.refs_1_.kv_ref), channel_id=1, source_target_pairs={{0,1},{1,0},{2,3},{3,2},{4,5},{5,4},{6,7},{7,6},{8,9},{9,8},{10,11... | collective-permute-start | bytes 1769480 | tf_op jit(solution)/shard_map/ppermute | solution.py:398
  69.4 6.0 %collective-permute-start.10 = (f32[3,2560]{1,0:T(4,128)S(1)}, f32[3,2560]{1,0:T(4,128)S(1)}, u32[]{:S(2)}, u32[]{:S(2)}) collective-permute-start(f32[3,2560]{1,0:T(4,128)S(1)} %get-tuple-element.42.refs_0_), channel_id=1, source_target_pairs={{6,0},{0,2},{2,4},{4,6},{7,1},{1,3},{3,5},{5,7},{14,8},{8,10},{10,... | collective-permute-start | bytes 92168 | tf_op jit(solution)/shard_map/ppermute | solution.py:435
  71.2 5.5 %collective-permute-start.9 = (f32[3,2560]{1,0:T(4,128)S(1)}, f32[3,2560]{1,0:T(4,128)S(1)}, u32[]{:S(2)}, u32[]{:S(2)}) collective-permute-start(f32[3,2560]{1,0:T(4,128)S(1)} %get-tuple-element.42.refs_0_), channel_id=1, source_target_pairs={{4,0},{6,2},{0,4},{2,6},{5,1},{7,3},{1,5},{3,7},{12,8},{14,10},{8,... | collective-permute-start | bytes 92168 | tf_op jit(solution)/shard_map/ppermute | solution.py:435
  73.9 4.0 %collective-permute-start.8 = (f32[3,2560]{1,0:T(4,128)S(1)}, f32[3,2560]{1,0:T(4,128)S(1)}, u32[]{:S(2)}, u32[]{:S(2)}) collective-permute-start(f32[3,2560]{1,0:T(4,128)S(1)} %get-tuple-element.42.refs_0_), channel_id=1, source_target_pairs={{2,0},{4,2},{6,4},{0,6},{3,1},{5,3},{7,5},{1,7},{10,8},{12,10},{14... | collective-permute-start | bytes 92168 | tf_op jit(solution)/shard_map/ppermute | solution.py:435
  87.4 19.0 %collective-permute-start.11 = (bf16[256,1152]{1,0:T(8,128)(2,1)S(1)}, bf16[256,1152]{1,0:T(8,128)(2,1)S(1)}, u32[]{:S(2)}, u32[]{:S(2)}) collective-permute-start(bf16[256,1152]{1,0:T(8,128)(2,1)S(1)} %get-tuple-element.47), channel_id=1, source_target_pairs={{0,1},{1,0},{2,3},{3,2},{4,5},{5,4},{6,7},{7,6},{8,9},{9,8},{10,11... | collective-permute-start | bytes 1769480 | tf_op jit(solution)/shard_map/ppermute | solution.py:472
  102.5 34.5 %all-to-all-start.2 = ((bf16[8,128,1024]{2,1,0:T(8,128)(2,1)}), bf16[8,128,1024]{2,1,0:T(8,128)(2,1)S(1)}, u32[]{:S(2)}, u32[]{:S(2)}) async-start(bf16[8,128,1024]{2,1,0:T(8,128)(2,1)} %bitcast.42), calls=%async_computation.2 | async-start | bytes 4194304 | tf_op jit(solution)/shard_map/all_to_all | solution.py:476
  115.4 1.7 %collective-permute-start.13 = (bf16[2,320,256]{2,1,0:T(8,128)(2,1)S(1)}, bf16[2,320,256]{2,1,0:T(8,128)(2,1)S(1)}, u32[]{:S(2)}, u32[]{:S(2)}) collective-permute-start(bf16[2,320,256]{2,1,0:T(8,128)(2,1)S(1)} %get-tuple-element.51), channel_id=1, source_target_pairs={{0,8},{8,0},{1,9},{9,1},{2,10},{10,2},{3,11},{11,3},{4,12},{12,4},... | collective-permute-start | bytes 983048 | tf_op jit(solution)/shard_map/ppermute | solution.py:499
  115.5 2.4 %collective-permute-start.15 = (bf16[2,320,256]{2,1,0:T(8,128)(2,1)S(1)}, bf16[2,320,256]{2,1,0:T(8,128)(2,1)S(1)}, u32[]{:S(2)}, u32[]{:S(2)}) collective-permute-start(bf16[2,320,256]{2,1,0:T(8,128)(2,1)S(1)} %get-tuple-element.53), channel_id=1, source_target_pairs={{0,8},{8,0},{1,9},{9,1},{2,10},{10,2},{3,11},{11,3},{4,12},{12,4},... | collective-permute-start | bytes 983048 | tf_op jit(solution)/shard_map/ppermute | solution.py:499
  116.0 6.3 %collective-permute-start.12 = (bf16[2,320,256]{2,1,0:T(8,128)(2,1)S(1)}, bf16[2,320,256]{2,1,0:T(8,128)(2,1)S(1)}, u32[]{:S(2)}, u32[]{:S(2)}) collective-permute-start(bf16[2,320,256]{2,1,0:T(8,128)(2,1)S(1)} %get-tuple-element.49), channel_id=1, source_target_pairs={{0,8},{8,0},{1,9},{9,1},{2,10},{10,2},{3,11},{11,3},{4,12},{12,4},... | collective-permute-start | bytes 983048 | tf_op jit(solution)/shard_map/ppermute | solution.py:499
  116.1 4.3 %collective-permute-start.17 = (bf16[2,320,256]{2,1,0:T(8,128)(2,1)S(1)}, bf16[2,320,256]{2,1,0:T(8,128)(2,1)S(1)}, u32[]{:S(2)}, u32[]{:S(2)}) collective-permute-start(bf16[2,320,256]{2,1,0:T(8,128)(2,1)S(1)} %get-tuple-element.55), channel_id=1, source_target_pairs={{0,8},{8,0},{1,9},{9,1},{2,10},{10,2},{3,11},{11,3},{4,12},{12,4},... | collective-permute-start | bytes 983048 | tf_op jit(solution)/shard_map/ppermute | solution.py:499
  117.2 18.1 %collective-permute-start.14 = (bf16[2,320,256]{2,1,0:T(8,128)(2,1)S(1)}, bf16[2,320,256]{2,1,0:T(8,128)(2,1)S(1)}, u32[]{:S(2)}, u32[]{:S(2)}) collective-permute-start(bf16[2,320,256]{2,1,0:T(8,128)(2,1)S(1)} %add_convert_fusion.3), channel_id=1, source_target_pairs={{96,0},{0,32},{32,64},{64,96},{97,1},{1,33},{33,65},{65,97},{98,2}... | collective-permute-start | bytes 983048 | tf_op jit(solution)/shard_map/ppermute | solution.py:503
  117.9 17.3 %collective-permute-start.16 = (bf16[2,320,256]{2,1,0:T(8,128)(2,1)S(1)}, bf16[2,320,256]{2,1,0:T(8,128)(2,1)S(1)}, u32[]{:S(2)}, u32[]{:S(2)}) collective-permute-start(bf16[2,320,256]{2,1,0:T(8,128)(2,1)S(1)} %add_convert_fusion.2), channel_id=1, source_target_pairs={{64,0},{96,32},{0,64},{32,96},{65,1},{97,33},{1,65},{33,97},{66,2}... | collective-permute-start | bytes 983048 | tf_op jit(solution)/shard_map/ppermute | solution.py:503
  120.5 15.5 %collective-permute-start.18 = (bf16[2,320,256]{2,1,0:T(8,128)(2,1)S(1)}, bf16[2,320,256]{2,1,0:T(8,128)(2,1)S(1)}, u32[]{:S(2)}, u32[]{:S(2)}) collective-permute-start(bf16[2,320,256]{2,1,0:T(8,128)(2,1)S(1)} %add_convert_fusion.1), channel_id=1, source_target_pairs={{32,0},{64,32},{96,64},{0,96},{33,1},{65,33},{97,65},{1,97},{34,2}... | collective-permute-start | bytes 983048 | tf_op jit(solution)/shard_map/ppermute | solution.py:503
  136.9 14.6 %all-to-all-start.3 = ((bf16[16,40,256]{2,1,0:T(8,128)(2,1)}), bf16[16,40,256]{2,1,0:T(8,128)(2,1)S(1)}, u32[]{:S(2)}, u32[]{:S(2)}) async-start(bf16[16,40,256]{2,1,0:T(8,128)(2,1)} %bitcast.14), calls=%async_computation.3 | async-start | bytes 655360 | tf_op jit(solution)/shard_map/all_to_all | solution.py:506
  (5 other events, 11.6 us)

commit v12 on v11

--- a/solution.py
+++ b/solution.py
@@ -366,7 +366,8 @@
     small = (source, layout, mine, others)
     qg, block, small = lax.optimization_barrier((qg, block, small))
     source, layout, mine, others = small
-    nears = [block] + [lax.ppermute(block, "x", shift(k)) for k in range(1, NX)]
+    opposite = lax.ppermute(block, "x", shift(2))
+    nears = [block, lax.ppermute(block, "x", shift(1)), opposite, lax.ppermute(block, "x", shift(3))]
     fars = [lax.ppermute(block, "c", SWAP)]
     qg_all = lax.all_to_all(qg, SEQ, 0, 0, tiled=True).reshape(N_SEQ * slots, 2 * half)
 
@@ -496,11 +497,13 @@
         name="weight_grad",
     )(kvgrad_own, kvgrad_got, prompt_rows, resp_rows)
     keeps, gives = pieces[:NX], pieces[NX:]
-    got = [lax.ppermute(give, "c", SWAP) for give in gives]
+    got = {k: lax.ppermute(gives[k], "c", SWAP) for k in (2, 1, 3, 0)}
+    moved = []
+    for k in (2, 1, 3):
+        piece = (keeps[k] + got[k].astype(F32)).astype(BF16)
+        moved.append(lax.ppermute(piece, "x", shift(-k)))
     line = keeps[0] + got[0].astype(F32)
-    for k in range(1, NX):
-        piece = (keeps[k] + got[k].astype(F32)).astype(BF16)
-        line = line + lax.ppermute(piece, "x", shift(-k)).astype(F32)
+    line = line + moved[0].astype(F32) + moved[1].astype(F32) + moved[2].astype(F32)
     line = line.astype(BF16).reshape(16, shard, 2 * DH)
     line, back = lax.optimization_barrier((line, back))
     shares = lax.all_to_all(line, PLANE, 0, 0, tiled=True)

time: 153 us -> 153 us (level)
  no operation moved by 1% of the time
where the time goes in v12:
time: 153 us; the launch traced here: 152 us
  Pallas kernels  51.3 us (34%)
  starting transfers between devices  44.5 us (29%)
  waiting for transfers between devices  41.1 us (27%)
  local copies, waits for them, and re-layouts  6.81 us (4%)
  other arithmetic  3.83 us (3%)
  matrix products  3.15 us (2%)
  between operations  1.53 us (1%)
    pallas_call x2, Pallas kernels, backward(): pl.pallas_call(functools.partial(second_pass, coef, scale, last), grid=(s...  23 us
    ppermute x3, waiting for transfers between devices, per_device(): moved.append(lax.ppermute(piece, 'x', shift(-k)))  12.8 us
    pallas_call x2, Pallas kernels, forward(): pl.pallas_call(functools.partial(first_pass, coef, last), grid=(steps,),...  12.4 us
    pallas_call x1, Pallas kernels, per_device(): pl.pallas_call(functools.partial(weight_kernel, cuts), in_specs=[vmem] *...  8.96 us
    all_to_all x1, waiting for transfers between devices, per_device(): shares = lax.all_to_all(line, PLANE, 0, 0, tiled=True)  8.36 us
    all_to_all x1, starting transfers between devices, per_device(): lax.all_to_all(block, PLANE, 0, 0, tiled=True).reshape(2, 8 * shard, 2 * DH)  8.13 us
    ppermute x1, waiting for transfers between devices, per_device(): opposite = lax.ppermute(block, 'x', shift(2))  8 us
    unnamed x12, local copies, waits for them, and re-layouts  6.6 us
  transfers between devices with their start and end apart: 23, of which 13 were waited for; matrix products, arithmetic and copies ran while one was open for 4% of the time, Pallas kernels for 23%

profile of v12, /device:TPU:0, one launch (start us, length us, event | category | flops | bytes accessed | tf_op | source)
XLA Modules:
  0.0 152.3 jit_solution(13914566275008455542)
XLA Ops:
  2.1 8.1 %all-to-all-start = ((bf16[16,40,256]{2,1,0:T(8,128)(2,1)}), bf16[16,40,256]{2,1,0:T(8,128)(2,1)S(1)}, u32[]{:S(2)}, u32[]{:S(2)}) async-start(bf16[16,40,256]{2,1,0:T(8,128)(2,1)} %weight_copies.1), calls=%async_computation | async-start | bytes 655360 | tf_op jit(solution)/shard_map/all_to_all | solution.py:354
  16.5 2.9 %all-to-all-done = bf16[16,40,256]{2,1,0:T(8,128)(2,1)S(1)} async-done(((bf16[16,40,256]{2,1,0:T(8,128)(2,1)}), bf16[16,40,256]{2,1,0:T(8,128)(2,1)S(1)}, u32[]{:S(2)}, u32[]{:S(2)}) %all-to-all-start) | async-done | bytes 327712 | tf_op jit(solution)/shard_map/all_to_all | solution.py:354
  19.4 4.5 %all-to-all-start.1 = ((bf16[8,128,1024]{2,1,0:T(8,128)(2,1)}), bf16[8,128,1024]{2,1,0:T(8,128)(2,1)}, u32[]{:S(2)}, u32[]{:S(2)}) async-start(bf16[8,128,1024]{2,1,0:T(8,128)(2,1)} %query_halves.1), calls=%async_computation.1 | async-start | bytes 4194304 | tf_op jit(solution)/shard_map/all_to_all | solution.py:372
  25.6 2.7 %collective-permute-start.1 = (bf16[2,320,256]{2,1,0:T(8,128)(2,1)S(1)}, bf16[2,320,256]{2,1,0:T(8,128)(2,1)S(1)}, u32[]{:S(2)}, u32[]{:S(2)}) collective-permute-start(bf16[2,320,256]{2,1,0:T(8,128)(2,1)S(1)} %bitcast.37), channel_id=1, source_target_pairs={{64,0},{96,32},{0,64},{32,96},{65,1},{97,33},{1,65},{33,97},{66,2}... | collective-permute-start | bytes 983048 | tf_op jit(solution)/shard_map/ppermute | solution.py:369
  29.7 4.0 %copy-done = bf16[1,1024,5120]{2,1,0:T(8,128)(2,1)S(1)} copy-done((bf16[1,1024,5120]{2,1,0:T(8,128)(2,1)S(1)}, bf16[1,1024,5120]{2,1,0:T(8,128)(2,1)}, u32[]{:S(2)}) %copy-start) | copy-done | bytes 10485784
  35.3 8.0 %collective-permute-done.1.refs_1_ = bf16[2,320,256]{2,1,0:T(8,128)(2,1)S(1)} collective-permute-done((bf16[2,320,256]{2,1,0:T(8,128)(2,1)S(1)}, bf16[2,320,256]{2,1,0:T(8,128)(2,1)S(1)}, u32[]{:S(2)}, u32[]{:S(2)}) %collective-permute-start.1) | collective-permute-done | bytes 327712 | tf_op jit(solution)/shard_map/ppermute | solution.py:369
  45.4 1.9 %project_last.1.refs_1_.kv_ref = bf16[1152,256]{1,0:T(8,128)(2,1)S(1)} custom-call(bf16[1024,5120]{1,0:T(8,128)(2,1)S(1)} %bitcast.30, bf16[128,5120]{1,0:T(8,128)(2,1)S(1)} %bitcast.34, bf16[2,320,256]{2,1,0:T(8,128)(2,1)S(1)} %collective-permute-done.refs_0_, bf16[2,320,256]{2,1,0:T(8,128)(2,1)S(1)} %collective-permute-done.1.refs_1_, ...), custom_call_target="tpu_custom_call" | custom-call | flops 1509949440 | bytes 5898240 | tf_op jit(solution)/shard_map/project_last/pallas_call | solution.py:376
  47.3 1.9 %collective-permute-start.7 = (bf16[1152,256]{1,0:T(8,128)(2,1)S(1)}, bf16[1152,256]{1,0:T(8,128)(2,1)S(1)}, u32[]{:S(2)}, u32[]{:S(2)}) collective-permute-start(bf16[1152,256]{1,0:T(8,128)(2,1)S(1)} %project_last.1.refs_1_.kv_ref), channel_id=1, source_target_pairs={{0,1},{1,0},{2,3},{3,2},{4,5},{5,4},{6,7},{7,6},{8,9},{9,8},{10,11... | collective-permute-start | bytes 1769480 | tf_op jit(solution)/shard_map/ppermute | solution.py:399
  49.2 3.7 %all-to-all-done.1 = bf16[8,128,1024]{2,1,0:T(8,128)(2,1)} async-done(((bf16[8,128,1024]{2,1,0:T(8,128)(2,1)}), bf16[8,128,1024]{2,1,0:T(8,128)(2,1)}, u32[]{:S(2)}, u32[]{:S(2)}) %all-to-all-start.1) | async-done | bytes 2097184 | tf_op jit(solution)/shard_map/all_to_all | solution.py:372
  52.9 3.1 %fusion.1.refs_0_.refs_2_.q_ref.g_ref = bf16[640,1024]{1,0:T(8,128)(2,1)S(1)} fusion(bf16[1024,1024]{1,0:T(8,128)(2,1)} %bitcast.11, s32[640]{0:T(1024)S(1)} %get-tuple-element.34), kind=kOutput, calls=%fused_computation.2 | convolution fusion | flops 1343488000 | bytes 3410432 | tf_op jit(solution)/shard_map/dot_general | solution.py:433
  56.0 5.8 %attend_own.1 = (f32[128,2560]{1,0:T(8,128)S(1)}, f32[3,2560]{1,0:T(4,128)S(1)}) custom-call(s32[16,640]{1,0:T(8,128)S(1)} %concatenate.10.bound_ref, bf16[640,1024]{1,0:T(8,128)(2,1)S(1)} %fusion.1.refs_0_.refs_2_.q_ref.g_ref, bf16[1152,256]{1,0:T(8,128)(2,1)S(1)} %project_last.1.refs_1_.kv_ref), custom_call_target="tpu_custom_call" | custom-call | flops 1509949440 | bytes 4194304 | tf_op jit(solution)/shard_map/attend_own/pallas_call | solution.py:412
  62.8 6.5 %attend_more.1 = (bf16[640,512]{1,0:T(8,128)(2,1)S(1)}, f32[3,2560]{1,0:T(4,128)S(1)}) custom-call(s32[16,640]{1,0:T(8,128)S(1)} %concatenate.11.bound_ref, bf16[640,1024]{1,0:T(8,128)(2,1)S(1)} %fusion.1.refs_0_.refs_2_.q_ref.g_ref, bf16[1152,256]{1,0:T(8,128)(2,1)S(1)} %collective-permute-done.7.refs_1_.kv_ref, ...), custom_call_target="tpu_custom_call" | custom-call | flops 1509949440 | bytes 4194304 | tf_op jit(solution)/shard_map/attend_more/pallas_call | solution.py:412
  69.4 1.8 %collective-permute-start.10 = (f32[3,2560]{1,0:T(4,128)S(1)}, f32[3,2560]{1,0:T(4,128)S(1)}, u32[]{:S(2)}, u32[]{:S(2)}) collective-permute-start(f32[3,2560]{1,0:T(4,128)S(1)} %get-tuple-element.42.refs_0_), channel_id=1, source_target_pairs={{6,0},{0,2},{2,4},{4,6},{7,1},{1,3},{3,5},{5,7},{14,8},{8,10},{10,... | collective-permute-start | bytes 92168 | tf_op jit(solution)/shard_map/ppermute | solution.py:436
  71.2 2.7 %collective-permute-start.9 = (f32[3,2560]{1,0:T(4,128)S(1)}, f32[3,2560]{1,0:T(4,128)S(1)}, u32[]{:S(2)}, u32[]{:S(2)}) collective-permute-start(f32[3,2560]{1,0:T(4,128)S(1)} %get-tuple-element.42.refs_0_), channel_id=1, source_target_pairs={{4,0},{6,2},{0,4},{2,6},{5,1},{7,3},{1,5},{3,7},{12,8},{14,10},{8,... | collective-permute-start | bytes 92168 | tf_op jit(solution)/shard_map/ppermute | solution.py:436
  77.9 9.5 %grads_other.1 = (f32[640,512]{1,0:T(8,128)S(1)}, bf16[256,1152]{1,0:T(8,128)(2,1)S(1)}) custom-call(s32[16,640]{1,0:T(8,128)S(1)} %concatenate.11.bound_ref, bf16[640,1024]{1,0:T(8,128)(2,1)S(1)} %fusion.1.refs_0_.refs_2_.q_ref.g_ref, bf16[640,1024]{1,0:T(8,128)(2,1)S(1)} %fusion.1.refs_0_.refs_2_.q_ref.g_ref, ...), custom_call_target="tpu_custom_call" | custom-call | flops 3774873600 | bytes 8388608 | tf_op jit(solution)/shard_map/grads_other/pallas_call | solution.py:440
  88.9 13.5 %grads_own.1 = (bf16[1024,1024]{1,0:T(8,128)(2,1)}, f32[256,1152]{1,0:T(8,128)}) custom-call(s32[16,640]{1,0:T(8,128)S(1)} %concatenate.10.bound_ref, bf16[640,1024]{1,0:T(8,128)(2,1)S(1)} %fusion.1.refs_0_.refs_2_.q_ref.g_ref, bf16[640,1024]{1,0:T(8,128)(2,1)S(1)} %fusion.1.refs_0_.refs_2_.q_ref.g_ref, bf16[1152,256]{1,0:T(8,128)(2,1)S(1)} %project_last.1.refs_1_.kv_ref, ...), custom_call_target="tpu_custom_call" | custom-call | flops 3774873600 | bytes 8388608 | tf_op jit(solution)/shard_map/grads_own/pallas_call | solution.py:440
  102.5 4.0 %all-to-all-start.2 = ((bf16[8,128,1024]{2,1,0:T(8,128)(2,1)}), bf16[8,128,1024]{2,1,0:T(8,128)(2,1)S(1)}, u32[]{:S(2)}, u32[]{:S(2)}) async-start(bf16[8,128,1024]{2,1,0:T(8,128)(2,1)} %bitcast.42), calls=%async_computation.2 | async-start | bytes 4194304 | tf_op jit(solution)/shard_map/all_to_all | solution.py:477
  106.4 9.0 %weight_grad.1 = (f32[2,320,256]{2,1,0:T(8,128)S(1)}, f32[2,320,256]{2,1,0:T(8,128)S(1)}, f32[2,320,256]{2,1,0:T(8,128)S(1)}, f32[2,320,256]{2,1,0:T(8,128)}, bf...) custom-call(f32[256,1152]{1,0:T(8,128)} %get-tuple-element.46.own_re, ...), custom_call_target="tpu_custom_call" | custom-call | flops 3019898880 | bytes 11796480 | tf_op jit(solution)/shard_map/weight_grad/pallas_call | solution.py:481
  117.2 2.0 %collective-permute-start.14 = (bf16[2,320,256]{2,1,0:T(8,128)(2,1)S(1)}, bf16[2,320,256]{2,1,0:T(8,128)(2,1)S(1)}, u32[]{:S(2)}, u32[]{:S(2)}) collective-permute-start(bf16[2,320,256]{2,1,0:T(8,128)(2,1)S(1)} %add_convert_fusion.3), channel_id=1, source_target_pairs={{64,0},{96,32},{0,64},{32,96},{65,1},{97,33},{1,65},{33,97},{66,2}... | collective-permute-start | bytes 983048 | tf_op jit(solution)/shard_map/ppermute | solution.py:504
  120.1 2.6 %collective-permute-start.18 = (bf16[2,320,256]{2,1,0:T(8,128)(2,1)S(1)}, bf16[2,320,256]{2,1,0:T(8,128)(2,1)S(1)}, u32[]{:S(2)}, u32[]{:S(2)}) collective-permute-start(bf16[2,320,256]{2,1,0:T(8,128)(2,1)S(1)} %add_convert_fusion.1), channel_id=1, source_target_pairs={{32,0},{64,32},{96,64},{0,96},{33,1},{65,33},{97,65},{1,97},{34,2}... | collective-permute-start | bytes 983048 | tf_op jit(solution)/shard_map/ppermute | solution.py:504
  122.7 6.7 %collective-permute-done.14 = bf16[2,320,256]{2,1,0:T(8,128)(2,1)S(1)} collective-permute-done((bf16[2,320,256]{2,1,0:T(8,128)(2,1)S(1)}, bf16[2,320,256]{2,1,0:T(8,128)(2,1)S(1)}, u32[]{:S(2)}, u32[]{:S(2)}) %collective-permute-start.14) | collective-permute-done | bytes 327712 | tf_op jit(solution)/shard_map/ppermute | solution.py:504
  129.4 6.2 %collective-permute-done.16 = bf16[2,320,256]{2,1,0:T(8,128)(2,1)S(1)} collective-permute-done((bf16[2,320,256]{2,1,0:T(8,128)(2,1)S(1)}, bf16[2,320,256]{2,1,0:T(8,128)(2,1)S(1)}, u32[]{:S(2)}, u32[]{:S(2)}) %collective-permute-start.16) | collective-permute-done | bytes 327712 | tf_op jit(solution)/shard_map/ppermute | solution.py:504
  136.5 5.8 %all-to-all-start.3 = ((bf16[16,40,256]{2,1,0:T(8,128)(2,1)}), bf16[16,40,256]{2,1,0:T(8,128)(2,1)S(1)}, u32[]{:S(2)}, u32[]{:S(2)}) async-start(bf16[16,40,256]{2,1,0:T(8,128)(2,1)} %bitcast.14), calls=%async_computation.3 | async-start | bytes 655360 | tf_op jit(solution)/shard_map/all_to_all | solution.py:509
  143.2 8.4 %all-to-all-done.3 = bf16[16,40,256]{2,1,0:T(8,128)(2,1)S(1)} async-done(((bf16[16,40,256]{2,1,0:T(8,128)(2,1)}), bf16[16,40,256]{2,1,0:T(8,128)(2,1)S(1)}, u32[]{:S(2)}, u32[]{:S(2)}) %all-to-all-start.3) | async-done | bytes 327712 | tf_op jit(solution)/shard_map/all_to_all | solution.py:509
  (68 shorter events, 25.5 us)
Async XLA Ops:
  2.1 17.3 %all-to-all-start = ((bf16[16,40,256]{2,1,0:T(8,128)(2,1)}), bf16[16,40,256]{2,1,0:T(8,128)(2,1)S(1)}, u32[]{:S(2)}, u32[]{:S(2)}) async-start(bf16[16,40,256]{2,1,0:T(8,128)(2,1)} %weight_copies.1), calls=%async_computation | async-start | bytes 655360 | tf_op jit(solution)/shard_map/all_to_all | solution.py:354
  19.4 10.3 %copy-start.1 = (bf16[1,128,5120]{2,1,0:T(8,128)(2,1)S(1)}, bf16[1,128,5120]{2,1,0:T(8,128)(2,1)}, u32[]{:S(2)}) copy-start(bf16[1,128,5120]{2,1,0:T(8,128)(2,1)} %param.8) | copy-start | bytes 3932164
  19.4 33.4 %all-to-all-start.1 = ((bf16[8,128,1024]{2,1,0:T(8,128)(2,1)}), bf16[8,128,1024]{2,1,0:T(8,128)(2,1)}, u32[]{:S(2)}, u32[]{:S(2)}) async-start(bf16[8,128,1024]{2,1,0:T(8,128)(2,1)} %query_halves.1), calls=%async_computation.1 | async-start | bytes 4194304 | tf_op jit(solution)/shard_map/all_to_all | solution.py:372
  23.9 5.8 %collective-permute-start.5 = (bf16[2,320,256]{2,1,0:T(8,128)(2,1)S(1)}, bf16[2,320,256]{2,1,0:T(8,128)(2,1)S(1)}, u32[]{:S(2)}, u32[]{:S(2)}) collective-permute-start(bf16[2,320,256]{2,1,0:T(8,128)(2,1)S(1)} %bitcast.35), channel_id=1, source_target_pairs={{0,8},{8,0},{1,9},{9,1},{2,10},{10,2},{3,11},{11,3},{4,12},{12,4},... | collective-permute-start | bytes 983048 | tf_op jit(solution)/shard_map/ppermute | solution.py:371
  24.0 11.3 %collective-permute-start.4 = (bf16[2,320,256]{2,1,0:T(8,128)(2,1)S(1)}, bf16[2,320,256]{2,1,0:T(8,128)(2,1)S(1)}, u32[]{:S(2)}, u32[]{:S(2)}) collective-permute-start(bf16[2,320,256]{2,1,0:T(8,128)(2,1)S(1)} %bitcast.36), channel_id=1, source_target_pairs={{96,0},{0,32},{32,64},{64,96},{97,1},{1,33},{33,65},{65,97},{98,2}... | collective-permute-start | bytes 983048 | tf_op jit(solution)/shard_map/ppermute | solution.py:370
  25.6 17.8 %collective-permute-start.1 = (bf16[2,320,256]{2,1,0:T(8,128)(2,1)S(1)}, bf16[2,320,256]{2,1,0:T(8,128)(2,1)S(1)}, u32[]{:S(2)}, u32[]{:S(2)}) collective-permute-start(bf16[2,320,256]{2,1,0:T(8,128)(2,1)S(1)} %bitcast.37), channel_id=1, source_target_pairs={{64,0},{96,32},{0,64},{32,96},{65,1},{97,33},{1,65},{33,97},{66,2}... | collective-permute-start | bytes 983048 | tf_op jit(solution)/shard_map/ppermute | solution.py:369
  28.3 15.1 %collective-permute-start = (bf16[2,320,256]{2,1,0:T(8,128)(2,1)S(1)}, bf16[2,320,256]{2,1,0:T(8,128)(2,1)S(1)}, u32[]{:S(2)}, u32[]{:S(2)}) collective-permute-start(bf16[2,320,256]{2,1,0:T(8,128)(2,1)S(1)} %bitcast.38), channel_id=1, source_target_pairs={{32,0},{64,32},{96,64},{0,96},{33,1},{65,33},{97,65},{1,97},{34,2}... | collective-permute-start | bytes 983048 | tf_op jit(solution)/shard_map/ppermute | solution.py:370
  35.3 8.5 %collective-permute-start.6 = (bf16[2,320,256]{2,1,0:T(8,128)(2,1)S(1)}, bf16[2,320,256]{2,1,0:T(8,128)(2,1)S(1)}, u32[]{:S(2)}, u32[]{:S(2)}) collective-permute-start(bf16[2,320,256]{2,1,0:T(8,128)(2,1)S(1)} %collective-permute-done.4.refs_0_), channel_id=1, source_target_pairs={{0,8},{8,0},{1,9},{9,1},{2,10},{10,2},{3,11},{11,3},{4,12},{12,4},... | collective-permute-start | bytes 983048 | tf_op jit(solution)/shard_map/ppermute | solution.py:396
  43.3 1.6 %collective-permute-start.3 = (bf16[2,320,256]{2,1,0:T(8,128)(2,1)S(1)}, bf16[2,320,256]{2,1,0:T(8,128)(2,1)S(1)}, u32[]{:S(2)}, u32[]{:S(2)}) collective-permute-start(bf16[2,320,256]{2,1,0:T(8,128)(2,1)S(1)} %collective-permute-done.1.refs_1_), channel_id=1, source_target_pairs={{0,8},{8,0},{1,9},{9,1},{2,10},{10,2},{3,11},{11,3},{4,12},{12,4},... | collective-permute-start | bytes 983048 | tf_op jit(solution)/shard_map/ppermute | solution.py:396
  43.3 2.1 %collective-permute-start.2 = (bf16[2,320,256]{2,1,0:T(8,128)(2,1)S(1)}, bf16[2,320,256]{2,1,0:T(8,128)(2,1)S(1)}, u32[]{:S(2)}, u32[]{:S(2)}) collective-permute-start(bf16[2,320,256]{2,1,0:T(8,128)(2,1)S(1)} %collective-permute-done.refs_0_), channel_id=1, source_target_pairs={{0,8},{8,0},{1,9},{9,1},{2,10},{10,2},{3,11},{11,3},{4,12},{12,4},... | collective-permute-start | bytes 983048 | tf_op jit(solution)/shard_map/ppermute | solution.py:396
  47.3 15.5 %collective-permute-start.7 = (bf16[1152,256]{1,0:T(8,128)(2,1)S(1)}, bf16[1152,256]{1,0:T(8,128)(2,1)S(1)}, u32[]{:S(2)}, u32[]{:S(2)}) collective-permute-start(bf16[1152,256]{1,0:T(8,128)(2,1)S(1)} %project_last.1.refs_1_.kv_ref), channel_id=1, source_target_pairs={{0,1},{1,0},{2,3},{3,2},{4,5},{5,4},{6,7},{7,6},{8,9},{9,8},{10,11... | collective-permute-start | bytes 1769480 | tf_op jit(solution)/shard_map/ppermute | solution.py:399
  69.4 6.0 %collective-permute-start.10 = (f32[3,2560]{1,0:T(4,128)S(1)}, f32[3,2560]{1,0:T(4,128)S(1)}, u32[]{:S(2)}, u32[]{:S(2)}) collective-permute-start(f32[3,2560]{1,0:T(4,128)S(1)} %get-tuple-element.42.refs_0_), channel_id=1, source_target_pairs={{6,0},{0,2},{2,4},{4,6},{7,1},{1,3},{3,5},{5,7},{14,8},{8,10},{10,... | collective-permute-start | bytes 92168 | tf_op jit(solution)/shard_map/ppermute | solution.py:436
  71.2 5.5 %collective-permute-start.9 = (f32[3,2560]{1,0:T(4,128)S(1)}, f32[3,2560]{1,0:T(4,128)S(1)}, u32[]{:S(2)}, u32[]{:S(2)}) collective-permute-start(f32[3,2560]{1,0:T(4,128)S(1)} %get-tuple-element.42.refs_0_), channel_id=1, source_target_pairs={{4,0},{6,2},{0,4},{2,6},{5,1},{7,3},{1,5},{3,7},{12,8},{14,10},{8,... | collective-permute-start | bytes 92168 | tf_op jit(solution)/shard_map/ppermute | solution.py:436
  73.9 4.0 %collective-permute-start.8 = (f32[3,2560]{1,0:T(4,128)S(1)}, f32[3,2560]{1,0:T(4,128)S(1)}, u32[]{:S(2)}, u32[]{:S(2)}) collective-permute-start(f32[3,2560]{1,0:T(4,128)S(1)} %get-tuple-element.42.refs_0_), channel_id=1, source_target_pairs={{2,0},{4,2},{6,4},{0,6},{3,1},{5,3},{7,5},{1,7},{10,8},{12,10},{14... | collective-permute-start | bytes 92168 | tf_op jit(solution)/shard_map/ppermute | solution.py:436
  87.4 19.0 %collective-permute-start.11 = (bf16[256,1152]{1,0:T(8,128)(2,1)S(1)}, bf16[256,1152]{1,0:T(8,128)(2,1)S(1)}, u32[]{:S(2)}, u32[]{:S(2)}) collective-permute-start(bf16[256,1152]{1,0:T(8,128)(2,1)S(1)} %get-tuple-element.47), channel_id=1, source_target_pairs={{0,1},{1,0},{2,3},{3,2},{4,5},{5,4},{6,7},{7,6},{8,9},{9,8},{10,11... | collective-permute-start | bytes 1769480 | tf_op jit(solution)/shard_map/ppermute | solution.py:473
  102.5 34.0 %all-to-all-start.2 = ((bf16[8,128,1024]{2,1,0:T(8,128)(2,1)}), bf16[8,128,1024]{2,1,0:T(8,128)(2,1)S(1)}, u32[]{:S(2)}, u32[]{:S(2)}) async-start(bf16[8,128,1024]{2,1,0:T(8,128)(2,1)} %bitcast.42), calls=%async_computation.2 | async-start | bytes 4194304 | tf_op jit(solution)/shard_map/all_to_all | solution.py:477
  115.4 1.7 %collective-permute-start.13 = (bf16[2,320,256]{2,1,0:T(8,128)(2,1)S(1)}, bf16[2,320,256]{2,1,0:T(8,128)(2,1)S(1)}, u32[]{:S(2)}, u32[]{:S(2)}) collective-permute-start(bf16[2,320,256]{2,1,0:T(8,128)(2,1)S(1)} %get-tuple-element.51), channel_id=1, source_target_pairs={{0,8},{8,0},{1,9},{9,1},{2,10},{10,2},{3,11},{11,3},{4,12},{12,4},... | collective-permute-start | bytes 983048 | tf_op jit(solution)/shard_map/ppermute | solution.py:500
  115.5 3.7 %collective-permute-start.15 = (bf16[2,320,256]{2,1,0:T(8,128)(2,1)S(1)}, bf16[2,320,256]{2,1,0:T(8,128)(2,1)S(1)}, u32[]{:S(2)}, u32[]{:S(2)}) collective-permute-start(bf16[2,320,256]{2,1,0:T(8,128)(2,1)S(1)} %get-tuple-element.53), channel_id=1, source_target_pairs={{0,8},{8,0},{1,9},{9,1},{2,10},{10,2},{3,11},{11,3},{4,12},{12,4},... | collective-permute-start | bytes 983048 | tf_op jit(solution)/shard_map/ppermute | solution.py:500
  116.0 6.7 %collective-permute-start.12 = (bf16[2,320,256]{2,1,0:T(8,128)(2,1)S(1)}, bf16[2,320,256]{2,1,0:T(8,128)(2,1)S(1)}, u32[]{:S(2)}, u32[]{:S(2)}) collective-permute-start(bf16[2,320,256]{2,1,0:T(8,128)(2,1)S(1)} %get-tuple-element.49), channel_id=1, source_target_pairs={{0,8},{8,0},{1,9},{9,1},{2,10},{10,2},{3,11},{11,3},{4,12},{12,4},... | collective-permute-start | bytes 983048 | tf_op jit(solution)/shard_map/ppermute | solution.py:500
  116.1 3.9 %collective-permute-start.17 = (bf16[2,320,256]{2,1,0:T(8,128)(2,1)S(1)}, bf16[2,320,256]{2,1,0:T(8,128)(2,1)S(1)}, u32[]{:S(2)}, u32[]{:S(2)}) collective-permute-start(bf16[2,320,256]{2,1,0:T(8,128)(2,1)S(1)} %get-tuple-element.55), channel_id=1, source_target_pairs={{0,8},{8,0},{1,9},{9,1},{2,10},{10,2},{3,11},{11,3},{4,12},{12,4},... | collective-permute-start | bytes 983048 | tf_op jit(solution)/shard_map/ppermute | solution.py:500
  117.2 12.2 %collective-permute-start.14 = (bf16[2,320,256]{2,1,0:T(8,128)(2,1)S(1)}, bf16[2,320,256]{2,1,0:T(8,128)(2,1)S(1)}, u32[]{:S(2)}, u32[]{:S(2)}) collective-permute-start(bf16[2,320,256]{2,1,0:T(8,128)(2,1)S(1)} %add_convert_fusion.3), channel_id=1, source_target_pairs={{64,0},{96,32},{0,64},{32,96},{65,1},{97,33},{1,65},{33,97},{66,2}... | collective-permute-start | bytes 983048 | tf_op jit(solution)/shard_map/ppermute | solution.py:504
  119.2 16.3 %collective-permute-start.16 = (bf16[2,320,256]{2,1,0:T(8,128)(2,1)S(1)}, bf16[2,320,256]{2,1,0:T(8,128)(2,1)S(1)}, u32[]{:S(2)}, u32[]{:S(2)}) collective-permute-start(bf16[2,320,256]{2,1,0:T(8,128)(2,1)S(1)} %add_convert_fusion.2), channel_id=1, source_target_pairs={{96,0},{0,32},{32,64},{64,96},{97,1},{1,33},{33,65},{65,97},{98,2}... | collective-permute-start | bytes 983048 | tf_op jit(solution)/shard_map/ppermute | solution.py:504
  120.1 15.4 %collective-permute-start.18 = (bf16[2,320,256]{2,1,0:T(8,128)(2,1)S(1)}, bf16[2,320,256]{2,1,0:T(8,128)(2,1)S(1)}, u32[]{:S(2)}, u32[]{:S(2)}) collective-permute-start(bf16[2,320,256]{2,1,0:T(8,128)(2,1)S(1)} %add_convert_fusion.1), channel_id=1, source_target_pairs={{32,0},{64,32},{96,64},{0,96},{33,1},{65,33},{97,65},{1,97},{34,2}... | collective-permute-start | bytes 983048 | tf_op jit(solution)/shard_map/ppermute | solution.py:504
  136.5 15.2 %all-to-all-start.3 = ((bf16[16,40,256]{2,1,0:T(8,128)(2,1)}), bf16[16,40,256]{2,1,0:T(8,128)(2,1)S(1)}, u32[]{:S(2)}, u32[]{:S(2)}) async-start(bf16[16,40,256]{2,1,0:T(8,128)(2,1)} %bitcast.14), calls=%async_computation.3 | async-start | bytes 655360 | tf_op jit(solution)/shard_map/all_to_all | solution.py:509
  (5 other events, 11.2 us)

commit v13 on v12

--- a/solution.py
+++ b/solution.py
@@ -87,12 +87,6 @@
         top, end = top + prev_ref[:plen], end + prev_ref[plen:]
     kv_ref[:plen] = top.astype(kv_ref.dtype)
     kv_ref[plen:] = end.astype(kv_ref.dtype)
-
-
-def one_hot(start_ref, r, block):
-    row = lax.broadcasted_iota(jnp.int32, (SLOTS, SLOTS), 1) + block * SLOTS
-    slot = lax.broadcasted_iota(jnp.int32, (SLOTS, SLOTS), 0) + start_ref[r]
-    return jnp.where((row == slot) & (row < start_ref[r + 1]), 1.0, 0.0).astype(BF16)
 
 
 def first_pass(coef, last, bound_ref, *refs):
@@ -152,7 +146,7 @@
     stat_refs, refs = refs[:NY], refs[NY:]
     if last:
         layout_hbm, out_ref, prev_ref, back_hbm, kvgrad_hbm = refs[:5]
-        acc, bias, back_ref, layout_ref, sems = refs[5:]
+        acc, bias, packed, back_ref, layout_ref, sems = refs[5:]
         bring = pltpu.make_async_copy(layout_hbm, layout_ref, sems.at[N_SEQ + 1])
     else:
         back_ref, kvgrad_ref, acc, bias = refs
@@ -215,12 +209,13 @@
     if last:
         att = [out_ref[:, r].astype(F32) * columns[r, 3:4] for r in parts]
         grad = [dq[r] + prev_ref[:, r] for r in parts]
-        back = jnp.concatenate(att + grad, 1).astype(BF16)
+        here = pl.ds(pl.multiple_of(step * SLOTS, SLOTS), SLOTS)
+        for i, part in enumerate(att + grad):
+            packed[here, i * DH : (i + 1) * DH] = part
 
         @pl.when(step == 0)
         def _():
             bring.wait()
-            back_ref[...] = jnp.zeros_like(back_ref)
 
         def leave(r):
             slots = pl.ds(pl.multiple_of(r * SLOTS, SLOTS), SLOTS)
@@ -228,16 +223,18 @@
 
         def place(r, _):
             slots = pl.ds(pl.multiple_of(r * SLOTS, SLOTS), SLOTS)
-            onehot = one_hot(layout_ref, r, step)
-            back_ref[slots] += jnp.dot(onehot, back, preferred_element_type=F32).astype(BF16)
-
-            @pl.when(layout_ref[r + 1] <= (step + 1) * SLOTS)
-            def _():
-                leave(r).start()
-
+            start = layout_ref[r]
+            even = pl.multiple_of(lax.div(start, 8) * 8, 8)
+            back_by = SLOTS + 8 - (start - even)
+            live = lax.broadcasted_iota(jnp.int32, (SLOTS, DH), 0) < layout_ref[r + 1] - start
+            for i in range(2 * HALF):
+                cols = slice(i * DH, (i + 1) * DH)
+                window = pltpu.roll(packed[pl.ds(even, SLOTS + 8), cols], back_by, 0)[:SLOTS]
+                back_ref[slots, cols] = jnp.where(live, window, 0.0).astype(BF16)
+            leave(r).start()
             return 0
 
-        base = N_SEQ + 1 + 2 * step
+        base = N_SEQ + 1 + step
         lax.fori_loop(layout_ref[base], layout_ref[base + 1], place, 0)
     else:
         for r in parts:
@@ -328,11 +325,9 @@
     past = packed[:, None] >= ends[None, :]
     source = packed + jnp.sum(jnp.where(past, slots - lengths[None, :], 0), 1)
     starts = jnp.concatenate([jnp.zeros((1,), jnp.int32), ends.astype(jnp.int32)])
-    lows = jnp.arange(live_all // SLOTS)[:, None] * SLOTS
-    first = jnp.sum(ends[None, :] <= lows, 1)
-    behind = jnp.sum((ends - lengths)[None, :] < lows + SLOTS, 1)
-    spans = jnp.stack([first, behind], 1).astype(jnp.int32).reshape(-1)
-    layout = jnp.concatenate([starts, spans])
+    lows = jnp.arange(live_all // SLOTS + 1)[:, None] * SLOTS
+    before = jnp.sum(ends[None, :] <= lows, 1).astype(jnp.int32)
+    layout = jnp.concatenate([starts, before])
     layout = jnp.pad(layout, (0, 3 * N_SEQ - layout.shape[0]))
 
     def bounds(owner):
@@ -457,6 +452,7 @@
             ],
             scratch_shapes=[pltpu.VMEM((2 * DH, keys), F32), pltpu.VMEM((8, plen), F32)]
             + [
+                pltpu.VMEM((live_all + slots, 2 * half), F32),
                 pltpu.VMEM((N_SEQ * slots, 2 * half), BF16),
                 pltpu.SMEM((3 * N_SEQ,), jnp.int32),
                 pltpu.SemaphoreType.DMA((N_SEQ + 2,)),

time: 153 us -> 153 us (level)
  no operation moved by 1% of the time
where the time goes in v13:
time: 153 us; the launch traced here: 152 us
  Pallas kernels  51 us (33%)
  starting transfers between devices  44.8 us (29%)
  waiting for transfers between devices  41.3 us (27%)
  local copies, waits for them, and re-layouts  6.63 us (4%)
  other arithmetic  3.64 us (2%)
  matrix products  3.15 us (2%)
  between operations  1.53 us (1%)
    pallas_call x2, Pallas kernels, backward(): pl.pallas_call(functools.partial(second_pass, coef, scale, last), grid=(s...  22.7 us
    ppermute x3, waiting for transfers between devices, per_device(): moved.append(lax.ppermute(piece, 'x', shift(-k)))  12.6 us
    pallas_call x2, Pallas kernels, forward(): pl.pallas_call(functools.partial(first_pass, coef, last), grid=(steps,),...  12.3 us
    pallas_call x1, Pallas kernels, per_device(): pl.pallas_call(functools.partial(weight_kernel, cuts), in_specs=[vmem] *...  8.97 us
    all_to_all x1, waiting for transfers between devices, per_device(): shares = lax.all_to_all(line, PLANE, 0, 0, tiled=True)  8.36 us
    all_to_all x1, starting transfers between devices, per_device(): lax.all_to_all(block, PLANE, 0, 0, tiled=True).reshape(2, 8 * shard, 2 * DH)  8.13 us
    ppermute x1, waiting for transfers between devices, per_device(): opposite = lax.ppermute(block, 'x', shift(2))  8 us
    unnamed x12, local copies, waits for them, and re-layouts  6.6 us
  transfers between devices with their start and end apart: 23, of which 13 were waited for; matrix products, arithmetic and copies ran while one was open for 4% of the time, Pallas kernels for 23%

profile of v13, /device:TPU:0, one launch (start us, length us, event | category | flops | bytes accessed | tf_op | source)
XLA Modules:
  0.0 151.9 jit_solution(12886512921323946932)
XLA Ops:
  2.1 8.1 %all-to-all-start = ((bf16[16,40,256]{2,1,0:T(8,128)(2,1)}), bf16[16,40,256]{2,1,0:T(8,128)(2,1)S(1)}, u32[]{:S(2)}, u32[]{:S(2)}) async-start(bf16[16,40,256]{2,1,0:T(8,128)(2,1)} %weight_copies.1), calls=%async_computation | async-start | bytes 655360 | tf_op jit(solution)/shard_map/all_to_all | solution.py:349
  16.1 3.3 %all-to-all-done = bf16[16,40,256]{2,1,0:T(8,128)(2,1)S(1)} async-done(((bf16[16,40,256]{2,1,0:T(8,128)(2,1)}), bf16[16,40,256]{2,1,0:T(8,128)(2,1)S(1)}, u32[]{:S(2)}, u32[]{:S(2)}) %all-to-all-start) | async-done | bytes 327712 | tf_op jit(solution)/shard_map/all_to_all | solution.py:349
  19.4 4.5 %all-to-all-start.1 = ((bf16[8,128,1024]{2,1,0:T(8,128)(2,1)}), bf16[8,128,1024]{2,1,0:T(8,128)(2,1)}, u32[]{:S(2)}, u32[]{:S(2)}) async-start(bf16[8,128,1024]{2,1,0:T(8,128)(2,1)} %query_halves.1), calls=%async_computation.1 | async-start | bytes 4194304 | tf_op jit(solution)/shard_map/all_to_all | solution.py:367
  25.6 2.7 %collective-permute-start.1 = (bf16[2,320,256]{2,1,0:T(8,128)(2,1)S(1)}, bf16[2,320,256]{2,1,0:T(8,128)(2,1)S(1)}, u32[]{:S(2)}, u32[]{:S(2)}) collective-permute-start(bf16[2,320,256]{2,1,0:T(8,128)(2,1)S(1)} %bitcast.29), channel_id=1, source_target_pairs={{64,0},{96,32},{0,64},{32,96},{65,1},{97,33},{1,65},{33,97},{66,2}... | collective-permute-start | bytes 983048 | tf_op jit(solution)/shard_map/ppermute | solution.py:364
  29.7 4.0 %copy-done = bf16[1,1024,5120]{2,1,0:T(8,128)(2,1)S(1)} copy-done((bf16[1,1024,5120]{2,1,0:T(8,128)(2,1)S(1)}, bf16[1,1024,5120]{2,1,0:T(8,128)(2,1)}, u32[]{:S(2)}) %copy-start) | copy-done | bytes 10485784
  35.3 8.0 %collective-permute-done.1.refs_1_ = bf16[2,320,256]{2,1,0:T(8,128)(2,1)S(1)} collective-permute-done((bf16[2,320,256]{2,1,0:T(8,128)(2,1)S(1)}, bf16[2,320,256]{2,1,0:T(8,128)(2,1)S(1)}, u32[]{:S(2)}, u32[]{:S(2)}) %collective-permute-start.1) | collective-permute-done | bytes 327712 | tf_op jit(solution)/shard_map/ppermute | solution.py:364
  45.4 1.9 %project_last.1.refs_1_.kv_ref = bf16[1152,256]{1,0:T(8,128)(2,1)S(1)} custom-call(bf16[1024,5120]{1,0:T(8,128)(2,1)S(1)} %bitcast.22, bf16[128,5120]{1,0:T(8,128)(2,1)S(1)} %bitcast.26, bf16[2,320,256]{2,1,0:T(8,128)(2,1)S(1)} %collective-permute-done.refs_0_, bf16[2,320,256]{2,1,0:T(8,128)(2,1)S(1)} %collective-permute-done.1.refs_1_, ...), custom_call_target="tpu_custom_call" | custom-call | flops 1509949440 | bytes 5898240 | tf_op jit(solution)/shard_map/project_last/pallas_call | solution.py:371
  47.3 1.9 %collective-permute-start.7 = (bf16[1152,256]{1,0:T(8,128)(2,1)S(1)}, bf16[1152,256]{1,0:T(8,128)(2,1)S(1)}, u32[]{:S(2)}, u32[]{:S(2)}) collective-permute-start(bf16[1152,256]{1,0:T(8,128)(2,1)S(1)} %project_last.1.refs_1_.kv_ref), channel_id=1, source_target_pairs={{0,1},{1,0},{2,3},{3,2},{4,5},{5,4},{6,7},{7,6},{8,9},{9,8},{10,11... | collective-permute-start | bytes 1769480 | tf_op jit(solution)/shard_map/ppermute | solution.py:394
  49.2 3.7 %all-to-all-done.1 = bf16[8,128,1024]{2,1,0:T(8,128)(2,1)} async-done(((bf16[8,128,1024]{2,1,0:T(8,128)(2,1)}), bf16[8,128,1024]{2,1,0:T(8,128)(2,1)}, u32[]{:S(2)}, u32[]{:S(2)}) %all-to-all-start.1) | async-done | bytes 2097184 | tf_op jit(solution)/shard_map/all_to_all | solution.py:367
  52.9 3.2 %fusion.1.refs_0_.refs_2_.q_ref.g_ref = bf16[640,1024]{1,0:T(8,128)(2,1)S(1)} fusion(bf16[1024,1024]{1,0:T(8,128)(2,1)} %bitcast.7, s32[640]{0:T(1024)S(1)} %get-tuple-element.34), kind=kOutput, calls=%fused_computation.2 | convolution fusion | flops 1343488000 | bytes 3410432 | tf_op jit(solution)/shard_map/dot_general | solution.py:428
  56.0 5.8 %attend_own.1 = (f32[128,2560]{1,0:T(8,128)S(1)}, f32[3,2560]{1,0:T(4,128)S(1)}) custom-call(s32[16,640]{1,0:T(8,128)S(1)} %concatenate.10.bound_ref, bf16[640,1024]{1,0:T(8,128)(2,1)S(1)} %fusion.1.refs_0_.refs_2_.q_ref.g_ref, bf16[1152,256]{1,0:T(8,128)(2,1)S(1)} %project_last.1.refs_1_.kv_ref), custom_call_target="tpu_custom_call" | custom-call | flops 1509949440 | bytes 4194304 | tf_op jit(solution)/shard_map/attend_own/pallas_call | solution.py:407
  62.8 6.5 %attend_more.1 = (bf16[640,512]{1,0:T(8,128)(2,1)S(1)}, f32[3,2560]{1,0:T(4,128)S(1)}) custom-call(s32[16,640]{1,0:T(8,128)S(1)} %concatenate.11.bound_ref, bf16[640,1024]{1,0:T(8,128)(2,1)S(1)} %fusion.1.refs_0_.refs_2_.q_ref.g_ref, bf16[1152,256]{1,0:T(8,128)(2,1)S(1)} %collective-permute-done.7.refs_1_.kv_ref, ...), custom_call_target="tpu_custom_call" | custom-call | flops 1509949440 | bytes 4194304 | tf_op jit(solution)/shard_map/attend_more/pallas_call | solution.py:407
  69.4 1.8 %collective-permute-start.10 = (f32[3,2560]{1,0:T(4,128)S(1)}, f32[3,2560]{1,0:T(4,128)S(1)}, u32[]{:S(2)}, u32[]{:S(2)}) collective-permute-start(f32[3,2560]{1,0:T(4,128)S(1)} %get-tuple-element.42.refs_0_), channel_id=1, source_target_pairs={{6,0},{0,2},{2,4},{4,6},{7,1},{1,3},{3,5},{5,7},{14,8},{8,10},{10,... | collective-permute-start | bytes 92168 | tf_op jit(solution)/shard_map/ppermute | solution.py:431
  71.2 2.7 %collective-permute-start.9 = (f32[3,2560]{1,0:T(4,128)S(1)}, f32[3,2560]{1,0:T(4,128)S(1)}, u32[]{:S(2)}, u32[]{:S(2)}) collective-permute-start(f32[3,2560]{1,0:T(4,128)S(1)} %get-tuple-element.42.refs_0_), channel_id=1, source_target_pairs={{4,0},{6,2},{0,4},{2,6},{5,1},{7,3},{1,5},{3,7},{12,8},{14,10},{8,... | collective-permute-start | bytes 92168 | tf_op jit(solution)/shard_map/ppermute | solution.py:431
  77.9 9.5 %grads_other.1 = (f32[640,512]{1,0:T(8,128)S(1)}, bf16[256,1152]{1,0:T(8,128)(2,1)S(1)}) custom-call(s32[16,640]{1,0:T(8,128)S(1)} %concatenate.11.bound_ref, bf16[640,1024]{1,0:T(8,128)(2,1)S(1)} %fusion.1.refs_0_.refs_2_.q_ref.g_ref, bf16[640,1024]{1,0:T(8,128)(2,1)S(1)} %fusion.1.refs_0_.refs_2_.q_ref.g_ref, ...), custom_call_target="tpu_custom_call" | custom-call | flops 3774873600 | bytes 8388608 | tf_op jit(solution)/shard_map/grads_other/pallas_call | solution.py:435
  89.0 13.2 %grads_own.1 = (bf16[1024,1024]{1,0:T(8,128)(2,1)}, f32[256,1152]{1,0:T(8,128)}) custom-call(s32[16,640]{1,0:T(8,128)S(1)} %concatenate.10.bound_ref, bf16[640,1024]{1,0:T(8,128)(2,1)S(1)} %fusion.1.refs_0_.refs_2_.q_ref.g_ref, bf16[640,1024]{1,0:T(8,128)(2,1)S(1)} %fusion.1.refs_0_.refs_2_.q_ref.g_ref, bf16[1152,256]{1,0:T(8,128)(2,1)S(1)} %project_last.1.refs_1_.kv_ref, ...), custom_call_target="tpu_custom_call" | custom-call | flops 3774873600 | bytes 8388608 | tf_op jit(solution)/shard_map/grads_own/pallas_call | solution.py:435
  102.1 3.9 %all-to-all-start.2 = ((bf16[8,128,1024]{2,1,0:T(8,128)(2,1)}), bf16[8,128,1024]{2,1,0:T(8,128)(2,1)S(1)}, u32[]{:S(2)}, u32[]{:S(2)}) async-start(bf16[8,128,1024]{2,1,0:T(8,128)(2,1)} %bitcast.34), calls=%async_computation.2 | async-start | bytes 4194304 | tf_op jit(solution)/shard_map/all_to_all | solution.py:473
  106.1 9.0 %weight_grad.1 = (f32[2,320,256]{2,1,0:T(8,128)S(1)}, f32[2,320,256]{2,1,0:T(8,128)S(1)}, f32[2,320,256]{2,1,0:T(8,128)S(1)}, f32[2,320,256]{2,1,0:T(8,128)}, bf...) custom-call(f32[256,1152]{1,0:T(8,128)} %get-tuple-element.46.own_re, ...), custom_call_target="tpu_custom_call" | custom-call | flops 3019898880 | bytes 11796480 | tf_op jit(solution)/shard_map/weight_grad/pallas_call | solution.py:477
  116.8 2.2 %collective-permute-start.14 = (bf16[2,320,256]{2,1,0:T(8,128)(2,1)S(1)}, bf16[2,320,256]{2,1,0:T(8,128)(2,1)S(1)}, u32[]{:S(2)}, u32[]{:S(2)}) collective-permute-start(bf16[2,320,256]{2,1,0:T(8,128)(2,1)S(1)} %add_convert_fusion.3), channel_id=1, source_target_pairs={{64,0},{96,32},{0,64},{32,96},{65,1},{97,33},{1,65},{33,97},{66,2}... | collective-permute-start | bytes 983048 | tf_op jit(solution)/shard_map/ppermute | solution.py:500
  119.7 2.8 %collective-permute-start.18 = (bf16[2,320,256]{2,1,0:T(8,128)(2,1)S(1)}, bf16[2,320,256]{2,1,0:T(8,128)(2,1)S(1)}, u32[]{:S(2)}, u32[]{:S(2)}) collective-permute-start(bf16[2,320,256]{2,1,0:T(8,128)(2,1)S(1)} %add_convert_fusion.1), channel_id=1, source_target_pairs={{32,0},{64,32},{96,64},{0,96},{33,1},{65,33},{97,65},{1,97},{34,2}... | collective-permute-start | bytes 983048 | tf_op jit(solution)/shard_map/ppermute | solution.py:500
  122.6 6.4 %collective-permute-done.14 = bf16[2,320,256]{2,1,0:T(8,128)(2,1)S(1)} collective-permute-done((bf16[2,320,256]{2,1,0:T(8,128)(2,1)S(1)}, bf16[2,320,256]{2,1,0:T(8,128)(2,1)S(1)}, u32[]{:S(2)}, u32[]{:S(2)}) %collective-permute-start.14) | collective-permute-done | bytes 327712 | tf_op jit(solution)/shard_map/ppermute | solution.py:500
  129.0 6.2 %collective-permute-done.16 = bf16[2,320,256]{2,1,0:T(8,128)(2,1)S(1)} collective-permute-done((bf16[2,320,256]{2,1,0:T(8,128)(2,1)S(1)}, bf16[2,320,256]{2,1,0:T(8,128)(2,1)S(1)}, u32[]{:S(2)}, u32[]{:S(2)}) %collective-permute-start.16) | collective-permute-done | bytes 327712 | tf_op jit(solution)/shard_map/ppermute | solution.py:500
  136.1 5.8 %all-to-all-start.3 = ((bf16[16,40,256]{2,1,0:T(8,128)(2,1)}), bf16[16,40,256]{2,1,0:T(8,128)(2,1)S(1)}, u32[]{:S(2)}, u32[]{:S(2)}) async-start(bf16[16,40,256]{2,1,0:T(8,128)(2,1)} %bitcast.10), calls=%async_computation.3 | async-start | bytes 655360 | tf_op jit(solution)/shard_map/all_to_all | solution.py:505
  142.9 8.4 %all-to-all-done.3 = bf16[16,40,256]{2,1,0:T(8,128)(2,1)S(1)} async-done(((bf16[16,40,256]{2,1,0:T(8,128)(2,1)}), bf16[16,40,256]{2,1,0:T(8,128)(2,1)S(1)}, u32[]{:S(2)}, u32[]{:S(2)}) %all-to-all-start.3) | async-done | bytes 327712 | tf_op jit(solution)/shard_map/all_to_all | solution.py:505
  (63 shorter events, 25.0 us)
Async XLA Ops:
  2.1 17.3 %all-to-all-start = ((bf16[16,40,256]{2,1,0:T(8,128)(2,1)}), bf16[16,40,256]{2,1,0:T(8,128)(2,1)S(1)}, u32[]{:S(2)}, u32[]{:S(2)}) async-start(bf16[16,40,256]{2,1,0:T(8,128)(2,1)} %weight_copies.1), calls=%async_computation | async-start | bytes 655360 | tf_op jit(solution)/shard_map/all_to_all | solution.py:349
  19.4 10.3 %copy-start.1 = (bf16[1,128,5120]{2,1,0:T(8,128)(2,1)S(1)}, bf16[1,128,5120]{2,1,0:T(8,128)(2,1)}, u32[]{:S(2)}) copy-start(bf16[1,128,5120]{2,1,0:T(8,128)(2,1)} %param.8) | copy-start | bytes 3932164
  19.4 33.5 %all-to-all-start.1 = ((bf16[8,128,1024]{2,1,0:T(8,128)(2,1)}), bf16[8,128,1024]{2,1,0:T(8,128)(2,1)}, u32[]{:S(2)}, u32[]{:S(2)}) async-start(bf16[8,128,1024]{2,1,0:T(8,128)(2,1)} %query_halves.1), calls=%async_computation.1 | async-start | bytes 4194304 | tf_op jit(solution)/shard_map/all_to_all | solution.py:367
  23.9 5.8 %collective-permute-start.5 = (bf16[2,320,256]{2,1,0:T(8,128)(2,1)S(1)}, bf16[2,320,256]{2,1,0:T(8,128)(2,1)S(1)}, u32[]{:S(2)}, u32[]{:S(2)}) collective-permute-start(bf16[2,320,256]{2,1,0:T(8,128)(2,1)S(1)} %bitcast.27), channel_id=1, source_target_pairs={{0,8},{8,0},{1,9},{9,1},{2,10},{10,2},{3,11},{11,3},{4,12},{12,4},... | collective-permute-start | bytes 983048 | tf_op jit(solution)/shard_map/ppermute | solution.py:366
  24.0 11.3 %collective-permute-start.4 = (bf16[2,320,256]{2,1,0:T(8,128)(2,1)S(1)}, bf16[2,320,256]{2,1,0:T(8,128)(2,1)S(1)}, u32[]{:S(2)}, u32[]{:S(2)}) collective-permute-start(bf16[2,320,256]{2,1,0:T(8,128)(2,1)S(1)} %bitcast.28), channel_id=1, source_target_pairs={{96,0},{0,32},{32,64},{64,96},{97,1},{1,33},{33,65},{65,97},{98,2}... | collective-permute-start | bytes 983048 | tf_op jit(solution)/shard_map/ppermute | solution.py:365
  25.6 17.8 %collective-permute-start.1 = (bf16[2,320,256]{2,1,0:T(8,128)(2,1)S(1)}, bf16[2,320,256]{2,1,0:T(8,128)(2,1)S(1)}, u32[]{:S(2)}, u32[]{:S(2)}) collective-permute-start(bf16[2,320,256]{2,1,0:T(8,128)(2,1)S(1)} %bitcast.29), channel_id=1, source_target_pairs={{64,0},{96,32},{0,64},{32,96},{65,1},{97,33},{1,65},{33,97},{66,2}... | collective-permute-start | bytes 983048 | tf_op jit(solution)/shard_map/ppermute | solution.py:364
  28.3 15.1 %collective-permute-start = (bf16[2,320,256]{2,1,0:T(8,128)(2,1)S(1)}, bf16[2,320,256]{2,1,0:T(8,128)(2,1)S(1)}, u32[]{:S(2)}, u32[]{:S(2)}) collective-permute-start(bf16[2,320,256]{2,1,0:T(8,128)(2,1)S(1)} %bitcast.30), channel_id=1, source_target_pairs={{32,0},{64,32},{96,64},{0,96},{33,1},{65,33},{97,65},{1,97},{34,2}... | collective-permute-start | bytes 983048 | tf_op jit(solution)/shard_map/ppermute | solution.py:365
  35.3 8.5 %collective-permute-start.6 = (bf16[2,320,256]{2,1,0:T(8,128)(2,1)S(1)}, bf16[2,320,256]{2,1,0:T(8,128)(2,1)S(1)}, u32[]{:S(2)}, u32[]{:S(2)}) collective-permute-start(bf16[2,320,256]{2,1,0:T(8,128)(2,1)S(1)} %collective-permute-done.4.refs_0_), channel_id=1, source_target_pairs={{0,8},{8,0},{1,9},{9,1},{2,10},{10,2},{3,11},{11,3},{4,12},{12,4},... | collective-permute-start | bytes 983048 | tf_op jit(solution)/shard_map/ppermute | solution.py:391
  43.4 1.6 %collective-permute-start.3 = (bf16[2,320,256]{2,1,0:T(8,128)(2,1)S(1)}, bf16[2,320,256]{2,1,0:T(8,128)(2,1)S(1)}, u32[]{:S(2)}, u32[]{:S(2)}) collective-permute-start(bf16[2,320,256]{2,1,0:T(8,128)(2,1)S(1)} %collective-permute-done.1.refs_1_), channel_id=1, source_target_pairs={{0,8},{8,0},{1,9},{9,1},{2,10},{10,2},{3,11},{11,3},{4,12},{12,4},... | collective-permute-start | bytes 983048 | tf_op jit(solution)/shard_map/ppermute | solution.py:391
  43.4 2.1 %collective-permute-start.2 = (bf16[2,320,256]{2,1,0:T(8,128)(2,1)S(1)}, bf16[2,320,256]{2,1,0:T(8,128)(2,1)S(1)}, u32[]{:S(2)}, u32[]{:S(2)}) collective-permute-start(bf16[2,320,256]{2,1,0:T(8,128)(2,1)S(1)} %collective-permute-done.refs_0_), channel_id=1, source_target_pairs={{0,8},{8,0},{1,9},{9,1},{2,10},{10,2},{3,11},{11,3},{4,12},{12,4},... | collective-permute-start | bytes 983048 | tf_op jit(solution)/shard_map/ppermute | solution.py:391
  47.3 15.5 %collective-permute-start.7 = (bf16[1152,256]{1,0:T(8,128)(2,1)S(1)}, bf16[1152,256]{1,0:T(8,128)(2,1)S(1)}, u32[]{:S(2)}, u32[]{:S(2)}) collective-permute-start(bf16[1152,256]{1,0:T(8,128)(2,1)S(1)} %project_last.1.refs_1_.kv_ref), channel_id=1, source_target_pairs={{0,1},{1,0},{2,3},{3,2},{4,5},{5,4},{6,7},{7,6},{8,9},{9,8},{10,11... | collective-permute-start | bytes 1769480 | tf_op jit(solution)/shard_map/ppermute | solution.py:394
  69.4 6.0 %collective-permute-start.10 = (f32[3,2560]{1,0:T(4,128)S(1)}, f32[3,2560]{1,0:T(4,128)S(1)}, u32[]{:S(2)}, u32[]{:S(2)}) collective-permute-start(f32[3,2560]{1,0:T(4,128)S(1)} %get-tuple-element.42.refs_0_), channel_id=1, source_target_pairs={{6,0},{0,2},{2,4},{4,6},{7,1},{1,3},{3,5},{5,7},{14,8},{8,10},{10,... | collective-permute-start | bytes 92168 | tf_op jit(solution)/shard_map/ppermute | solution.py:431
  71.2 5.5 %collective-permute-start.9 = (f32[3,2560]{1,0:T(4,128)S(1)}, f32[3,2560]{1,0:T(4,128)S(1)}, u32[]{:S(2)}, u32[]{:S(2)}) collective-permute-start(f32[3,2560]{1,0:T(4,128)S(1)} %get-tuple-element.42.refs_0_), channel_id=1, source_target_pairs={{4,0},{6,2},{0,4},{2,6},{5,1},{7,3},{1,5},{3,7},{12,8},{14,10},{8,... | collective-permute-start | bytes 92168 | tf_op jit(solution)/shard_map/ppermute | solution.py:431
  73.9 4.0 %collective-permute-start.8 = (f32[3,2560]{1,0:T(4,128)S(1)}, f32[3,2560]{1,0:T(4,128)S(1)}, u32[]{:S(2)}, u32[]{:S(2)}) collective-permute-start(f32[3,2560]{1,0:T(4,128)S(1)} %get-tuple-element.42.refs_0_), channel_id=1, source_target_pairs={{2,0},{4,2},{6,4},{0,6},{3,1},{5,3},{7,5},{1,7},{10,8},{12,10},{14... | collective-permute-start | bytes 92168 | tf_op jit(solution)/shard_map/ppermute | solution.py:431
  87.4 18.6 %collective-permute-start.11 = (bf16[256,1152]{1,0:T(8,128)(2,1)S(1)}, bf16[256,1152]{1,0:T(8,128)(2,1)S(1)}, u32[]{:S(2)}, u32[]{:S(2)}) collective-permute-start(bf16[256,1152]{1,0:T(8,128)(2,1)S(1)} %get-tuple-element.47), channel_id=1, source_target_pairs={{0,1},{1,0},{2,3},{3,2},{4,5},{5,4},{6,7},{7,6},{8,9},{9,8},{10,11... | collective-permute-start | bytes 1769480 | tf_op jit(solution)/shard_map/ppermute | solution.py:469
  102.1 34.0 %all-to-all-start.2 = ((bf16[8,128,1024]{2,1,0:T(8,128)(2,1)}), bf16[8,128,1024]{2,1,0:T(8,128)(2,1)S(1)}, u32[]{:S(2)}, u32[]{:S(2)}) async-start(bf16[8,128,1024]{2,1,0:T(8,128)(2,1)} %bitcast.34), calls=%async_computation.2 | async-start | bytes 4194304 | tf_op jit(solution)/shard_map/all_to_all | solution.py:473
  115.0 1.7 %collective-permute-start.13 = (bf16[2,320,256]{2,1,0:T(8,128)(2,1)S(1)}, bf16[2,320,256]{2,1,0:T(8,128)(2,1)S(1)}, u32[]{:S(2)}, u32[]{:S(2)}) collective-permute-start(bf16[2,320,256]{2,1,0:T(8,128)(2,1)S(1)} %get-tuple-element.51), channel_id=1, source_target_pairs={{0,8},{8,0},{1,9},{9,1},{2,10},{10,2},{3,11},{11,3},{4,12},{12,4},... | collective-permute-start | bytes 983048 | tf_op jit(solution)/shard_map/ppermute | solution.py:496
  115.1 3.9 %collective-permute-start.15 = (bf16[2,320,256]{2,1,0:T(8,128)(2,1)S(1)}, bf16[2,320,256]{2,1,0:T(8,128)(2,1)S(1)}, u32[]{:S(2)}, u32[]{:S(2)}) collective-permute-start(bf16[2,320,256]{2,1,0:T(8,128)(2,1)S(1)} %get-tuple-element.53), channel_id=1, source_target_pairs={{0,8},{8,0},{1,9},{9,1},{2,10},{10,2},{3,11},{11,3},{4,12},{12,4},... | collective-permute-start | bytes 983048 | tf_op jit(solution)/shard_map/ppermute | solution.py:496
  115.6 7.0 %collective-permute-start.12 = (bf16[2,320,256]{2,1,0:T(8,128)(2,1)S(1)}, bf16[2,320,256]{2,1,0:T(8,128)(2,1)S(1)}, u32[]{:S(2)}, u32[]{:S(2)}) collective-permute-start(bf16[2,320,256]{2,1,0:T(8,128)(2,1)S(1)} %get-tuple-element.49), channel_id=1, source_target_pairs={{0,8},{8,0},{1,9},{9,1},{2,10},{10,2},{3,11},{11,3},{4,12},{12,4},... | collective-permute-start | bytes 983048 | tf_op jit(solution)/shard_map/ppermute | solution.py:496
  115.7 3.9 %collective-permute-start.17 = (bf16[2,320,256]{2,1,0:T(8,128)(2,1)S(1)}, bf16[2,320,256]{2,1,0:T(8,128)(2,1)S(1)}, u32[]{:S(2)}, u32[]{:S(2)}) collective-permute-start(bf16[2,320,256]{2,1,0:T(8,128)(2,1)S(1)} %get-tuple-element.55), channel_id=1, source_target_pairs={{0,8},{8,0},{1,9},{9,1},{2,10},{10,2},{3,11},{11,3},{4,12},{12,4},... | collective-permute-start | bytes 983048 | tf_op jit(solution)/shard_map/ppermute | solution.py:496
  116.8 12.2 %collective-permute-start.14 = (bf16[2,320,256]{2,1,0:T(8,128)(2,1)S(1)}, bf16[2,320,256]{2,1,0:T(8,128)(2,1)S(1)}, u32[]{:S(2)}, u32[]{:S(2)}) collective-permute-start(bf16[2,320,256]{2,1,0:T(8,128)(2,1)S(1)} %add_convert_fusion.3), channel_id=1, source_target_pairs={{64,0},{96,32},{0,64},{32,96},{65,1},{97,33},{1,65},{33,97},{66,2}... | collective-permute-start | bytes 983048 | tf_op jit(solution)/shard_map/ppermute | solution.py:500
  119.1 16.1 %collective-permute-start.16 = (bf16[2,320,256]{2,1,0:T(8,128)(2,1)S(1)}, bf16[2,320,256]{2,1,0:T(8,128)(2,1)S(1)}, u32[]{:S(2)}, u32[]{:S(2)}) collective-permute-start(bf16[2,320,256]{2,1,0:T(8,128)(2,1)S(1)} %add_convert_fusion.2), channel_id=1, source_target_pairs={{96,0},{0,32},{32,64},{64,96},{97,1},{1,33},{33,65},{65,97},{98,2}... | collective-permute-start | bytes 983048 | tf_op jit(solution)/shard_map/ppermute | solution.py:500
  119.7 15.4 %collective-permute-start.18 = (bf16[2,320,256]{2,1,0:T(8,128)(2,1)S(1)}, bf16[2,320,256]{2,1,0:T(8,128)(2,1)S(1)}, u32[]{:S(2)}, u32[]{:S(2)}) collective-permute-start(bf16[2,320,256]{2,1,0:T(8,128)(2,1)S(1)} %add_convert_fusion.1), channel_id=1, source_target_pairs={{32,0},{64,32},{96,64},{0,96},{33,1},{65,33},{97,65},{1,97},{34,2}... | collective-permute-start | bytes 983048 | tf_op jit(solution)/shard_map/ppermute | solution.py:500
  136.1 15.2 %all-to-all-start.3 = ((bf16[16,40,256]{2,1,0:T(8,128)(2,1)}), bf16[16,40,256]{2,1,0:T(8,128)(2,1)S(1)}, u32[]{:S(2)}, u32[]{:S(2)}) async-start(bf16[16,40,256]{2,1,0:T(8,128)(2,1)} %bitcast.10), calls=%async_computation.3 | async-start | bytes 655360 | tf_op jit(solution)/shard_map/all_to_all | solution.py:505
  (5 other events, 11.2 us)
